TPU v7x, 32 devices: a whole 2x2x4 slice. The times are simulated.
32 devices in a mesh: scan: 4 (over x, core), obj: 8 (over z, y).
Axes of the slice: x: 2, y: 2, z: 4, core: 2. Of those that a mesh axis runs over, the one named last changes fastest.
Arguments:
- object_slices: float32 [2, 2, 2048, 2048], P(None, None, 'obj'), may hold values from -4 to 4
- probe: float32 [2, 2, 256, 256], replicated, may hold values from -6 to 6
- measured: bfloat16 [4, 8, 2, 256, 256], P('scan', 'obj'), may hold values from 0 to 4
- positions: int32 [4, 8, 2, 2], P('scan', 'obj'), may hold values from 0 to 1792, as said below
- counts: int32 [4, 8], P('scan', 'obj'), may hold values from 0 to 2, as said below
Outputs:
- object_grad: float32 [2, 2, 2048, 2048], P(None, None, 'obj', 'scan')
- probe_grad: float32 [2, 2, 256, 256], P(None, None, 'obj', 'scan')
Inputs may be any that keep to these rules, and one draw needn't show every extreme that they name: In every tile o the counts over the 4 batches sum to exactly 4, and some batch of every tile has 2 live patterns. `positions`: the row offset is below 256, the column at most 1792.
All inputs are finite; a program needn't handle non-finite values.
Results may differ from a plain program's by a relative error of at most 0.013.
Values may be sent and summed in bfloat16 or wider, within the bound.
No kernel may reach another device: no remote copies, remote signals or barrier semaphores. Data moves between devices by JAX's collectives and lax.ppermute only.
A program may use at most 128 MiB of HBM per device.

v0:
```python
import math

import jax
import jax.numpy as jnp
from jax import lax
from jax.sharding import PartitionSpec as P


def shifted(block, axis, distance):
    devices = range(lax.axis_size(axis))
    route = [((i - distance) % len(devices), i) for i in devices]
    return lax.ppermute(block, axis, route)


def dft_matrix(length, sign):
    index_row = jnp.arange(length, dtype=jnp.int32)
    product = index_row[:, None] * index_row[None, :] % length
    angles = product.astype(jnp.float32) * (2.0 * math.pi / length)
    factor = 1.0 / math.sqrt(length)
    real_part = jnp.cos(angles) * factor
    imag_part = sign * jnp.sin(angles) * factor
    stacked = jnp.stack([jnp.stack([real_part, -imag_part]), jnp.stack([imag_part, real_part])])
    return stacked.astype(jnp.bfloat16)


def fresnel_kernel(length):
    index_row = jnp.arange(length, dtype=jnp.int32)
    freqs = jnp.where(index_row < length // 2, index_row, index_row - length)
    squares = freqs * freqs
    summed = (squares[:, None] + squares[None, :]) % (4 * length)
    phases = summed.astype(jnp.float32) * (2.0 * math.pi / (4 * length))
    return jnp.stack([jnp.cos(phases), -jnp.sin(phases)])


def transform(field_in, matrix):
    partial_out = jnp.einsum(
        "pqab,qbc->pac", matrix, field_in.astype(jnp.bfloat16), preferred_element_type=jnp.float32
    )
    return jnp.einsum(
        "qab,pqbc->pac",
        partial_out.astype(jnp.bfloat16),
        matrix,
        preferred_element_type=jnp.float32,
    )


def complex_mul(first_op, second_op):
    return jnp.stack(
        [
            first_op[0] * second_op[0] - first_op[1] * second_op[1],
            first_op[0] * second_op[1] + first_op[1] * second_op[0],
        ]
    )


def conj_mul(first_op, second_op):
    return jnp.stack(
        [
            first_op[0] * second_op[0] + first_op[1] * second_op[1],
            first_op[0] * second_op[1] - first_op[1] * second_op[0],
        ]
    )


def pattern_terms(patches, probe, pattern_data, weight, forward, inverse, kernel):
    layers = patches.shape[0]

    def forward_mode(mode_probe):
        arrivals = [mode_probe]
        field_now = complex_mul(mode_probe, patches[0])
        spectrum = transform(field_now, forward)
        field_now = transform(complex_mul(kernel, spectrum), inverse)
        arrivals.append(field_now)
        field_now = complex_mul(field_now, patches[1])
        return (transform(field_now, forward), jnp.stack(arrivals))

    far_field, arrivals = jax.vmap(forward_mode)(probe)
    intensity = jnp.sum(far_field[:, 0] ** 2 + far_field[:, 1] ** 2, axis=0)
    misfit = (intensity - pattern_data.astype(jnp.float32)) * weight

    def back_mode(mode_far, mode_arrivals):
        adjoint = transform(misfit[None] * mode_far, inverse)
        layer_grads = [None] * layers
        for layer_idx in reversed(range(layers)):
            layer_grads[layer_idx] = conj_mul(mode_arrivals[layer_idx], adjoint)
            adjoint = conj_mul(patches[layer_idx], adjoint)
            if layer_idx > 0:
                spectrum = transform(adjoint, forward)
                adjoint = transform(conj_mul(kernel, spectrum), inverse)
        return (jnp.stack(layer_grads), adjoint)

    patch_grads, probe_grads = jax.vmap(back_mode)(far_field, arrivals)
    return (jnp.sum(patch_grads, axis=0), probe_grads)


def body(object_slices, probe, measured, positions, counts):
    layers = object_slices.shape[0]
    tile_rows = object_slices.shape[2]
    tile_cols = object_slices.shape[3]
    length = probe.shape[-1]
    slots_all = measured.shape[2]
    forward = dft_matrix(length, -1.0)
    inverse = dft_matrix(length, 1.0)
    kernel = fresnel_kernel(length)
    zero_index = jnp.zeros((), jnp.int32)
    slot_data = measured[0, 0]
    slot_pos = positions[0, 0]
    slot_weight = (jnp.arange(slots_all, dtype=jnp.int32) < counts[0, 0]).astype(jnp.float32)
    wanted = shifted(slot_pos[:, 1], "obj", 1)

    def cut_piece(col_start):
        return lax.dynamic_slice(
            object_slices,
            (zero_index, zero_index, zero_index, col_start),
            (layers, 2, length, length),
        )

    own_pieces = jax.vmap(cut_piece)(wanted)
    got_pieces = shifted(own_pieces, "obj", -1)

    def join_window(pattern_pos, piece):
        col_corner = (zero_index, zero_index, zero_index, pattern_pos[1])
        own_cols = lax.dynamic_slice(object_slices, col_corner, (layers, 2, tile_rows, length))
        column_block = jnp.concatenate([own_cols, piece], axis=2)
        row_corner = (zero_index, zero_index, pattern_pos[0], zero_index)
        return lax.dynamic_slice(column_block, row_corner, (layers, 2, length, length))

    slot_patches = jax.vmap(join_window)(slot_pos, got_pieces)

    def slot_step(probe_sum, inputs):
        pattern_data, weight, patches = inputs
        patch_grad, probe_grad = pattern_terms(
            patches, probe, pattern_data, weight, forward, inverse, kernel
        )
        return (probe_sum + probe_grad, patch_grad)

    probe_zero = jnp.zeros(probe.shape, jnp.float32)
    probe_sum, slot_grads = lax.scan(slot_step, probe_zero, (slot_data, slot_weight, slot_patches))

    def add_window(band, inputs):
        patch_grad, pattern_pos = inputs
        corner = (zero_index, zero_index, pattern_pos[0], pattern_pos[1])
        current = lax.dynamic_slice(band, corner, (layers, 2, length, length))
        return (lax.dynamic_update_slice(band, current + patch_grad, corner), None)

    band_start = jnp.zeros((layers, 2, tile_rows + length, tile_cols), jnp.float32)
    band, leftover = lax.scan(add_window, band_start, (slot_grads, slot_pos))
    rim_back = shifted(band[:, :, tile_rows:], "obj", 1)
    tile_grad = band[:, :, :tile_rows].at[:, :, :length].add(rim_back)
    object_grad = lax.psum_scatter(tile_grad, "scan", scatter_dimension=3, tiled=True)
    live_total = lax.axis_size("scan") * lax.axis_size("obj") * slots_all // 2
    factor = 1.0 / math.sqrt(live_total)
    partial_probe = lax.psum_scatter(probe_sum, "obj", scatter_dimension=2, tiled=True)
    probe_total = lax.psum_scatter(partial_probe, "scan", scatter_dimension=3, tiled=True)
    return (object_grad, probe_total * factor)


def solution(mesh):
    return jax.shard_map(
        body,
        mesh=mesh,
        in_specs=(
            P(None, None, "obj", None),
            P(),
            P("scan", "obj", None, None, None),
            P("scan", "obj", None, None),
            P("scan", "obj"),
        ),
        out_specs=(P(None, None, "obj", "scan"), P(None, None, "obj", "scan")),
        check_vma=False,
    )
```

profile of v0, /device:TPU:0, one launch (start us, length us, event | category | flops | bytes accessed | tf_op | source)
XLA Modules:
  0.0 553.0 jit_solution(14762891595575144329)
XLA Ops:
  11.2 4.6 collective-permute-done
  17.4 7.9 %while.33 = (s32[]{:T(128)}, f32[2,2,256,2048]{3,2,1,0:T(8,128)}, s32[2,4]{1,0:T(2,128)S(1)}, f32[2,2,2,256,256]{4,3,2,1,0:T(8,128)}, s32[]{:T(128)}) while((s32[]{:T(128)}, f32[2,2,256,2048]{3,2,1,0:T(8,128)}, s32[2,4]{1,0:T(2,128)S(1)}, f32[2,2,2,256,256]{4,3,2,1,0:T(8,128)}, s32[]{:T(128)}) %tuple.139), condition=%wide.while_cond.2, body=%wide.while_body.2.sunk | while | flops 2 | bytes 2097781 | solution.py:112
  18.0 3.4 bitcast_dynamic-update-slice_fusion.7
  22.0 3.4 bitcast_dynamic-update-slice_fusion.7
  36.1 7.8 %while.32 = (s32[]{:T(128)}, f32[2,2,256,2048]{3,2,1,0:T(8,128)}, s32[2,4]{1,0:T(2,128)S(1)}, f32[2,2,2,256,256]{4,3,2,1,0:T(8,128)}, s32[]{:T(128)}) while((s32[]{:T(128)}, f32[2,2,256,2048]{3,2,1,0:T(8,128)}, s32[2,4]{1,0:T(2,128)S(1)}, f32[2,2,2,256,256]{4,3,2,1,0:T(8,128)}, s32[]{:T(128)}) %tuple.160), condition=%wide.while_cond.1, body=%wide.while_body.1.sunk | while | flops 2 | bytes 2097781 | solution.py:123
  40.5 3.4 bitcast_dynamic-update-slice_fusion.6
  43.9 28.3 %collective-permute-done.1 = f32[2,2,2,256,256]{4,3,2,1,0:T(8,128)} collective-permute-done((f32[2,2,2,256,256]{4,3,2,1,0:T(8,128)}, f32[2,2,2,256,256]{4,3,2,1,0:T(8,128)}, u32[]{:S(2)}, u32[]{:S(2)}) %collective-permute-start.1) | collective-permute-done | bytes 2097184 | tf_op jit(solution)/shard_map/ppermute | solution.py:12
  72.2 4.5 pad_maximum_fusion
  78.2 8.4 %while.34 = (s32[]{:T(128)}, f32[2,2,2,512,256]{4,3,2,1,0:T(8,128)}, s32[2,5]{1,0:T(2,128)S(1)}, f32[2,2,2,256,256]{4,3,2,1,0:T(8,128)}, s32[]{:T(128)}) while((s32[]{:T(128)}, f32[2,2,2,512,256]{4,3,2,1,0:T(8,128)}, s32[2,5]{1,0:T(2,128)S(1)}, f32[2,2,2,256,256]{4,3,2,1,0:T(8,128)}, s32[]{:T(128)}) %tuple.145), condition=%wide.while_cond.3, body=%wide.while_body.3.sunk | while | flops 2 | bytes 2098309 | solution.py:126
  78.8 3.6 dynamic-slice_dynamic-update-slice_fusion.2
  83.0 3.6 dynamic-slice_dynamic-update-slice_fusion.2
  86.6 84.1 %while.35 = (s32[]{:T(128)}, f32[2,2,256,256]{2,3,1,0:T(8,128)}, f32[2,2,2,256,256]{3,4,2,1,0:T(8,128)}, f32[2,2,2,256,256]{4,3,2,1,0:T(8,128)}, f32[2,2,256,256...) while((s32[]{:T(128)}, f32[2,2,256,256]{2,3,1,0:T(8,128)}, ...), condition=%wide.region_3.4_spmd.clone.clone.clone.clone, body=%wide.region_0.3_spmd.clone.clone.clone.clone.sunk | while | flops 3237281792 | bytes 101844376 | solution.py:138
  111.8 3.3 convolution_bitcast_fusion.19
  153.9 3.3 convolution_bitcast_fusion.19
  170.8 7.9 %broadcast_in_dim.11 = f32[2,2,512,2048]{3,2,1,0:T(8,128)} broadcast(f32[]{:T(128)} %constant.104.clone.1), dimensions={} | broadcast | bytes 16777220 | tf_op jit(solution)/shard_map/broadcast_in_dim | solution.py:146
  178.6 34.3 %while.31 = (s32[]{:T(128)}, f32[2,2,512,2048]{3,2,1,0:T(8,128)}, s32[2,2]{1,0:T(2,128)S(1)}, f32[2,2,2,256,256]{3,4,2,1,0:T(8,128)}, s32[]{:T(128)}, /*index=5*/s32[]{:T(128)}, s32[]{:T(128)}, s32[]{:T(128)}) while((s32[]{:T(128)}, f32[2,2,512,2048]{3,2,1,0:T(8,128)}, s32[2,2]{1,0:T(2,128)S(1)}, f32[2,2,2,256,256]{3,4,2,1,0:T(8,128)}, ...), condition=%wide.region_5.6_spmd, body=%wide.region_4.5_spmd.sunk | while | flops 262152 | bytes 9437397 | solution.py:147
  186.1 8.2 %dynamic_update_slice.14 = f32[2,2,512,2048]{3,2,1,0:T(8,128)} dynamic-update-slice(f32[2,2,512,2048]{3,2,1,0:T(8,128)} %get-tuple-element.723, f32[2,2,256,256]{3,2,1,0:T(8,128)S(1)} %bitcast_add_fusion.2, s32[]{:T(128)} %constant.103.clone.1..sunk, s32[]{:T(128)} %constant.103.clone.1..sunk, s32[]{:T(128)S(6)} %select_n.175, s32[]{:T(128)S(6)} %select_n.176) | dynamic-update-slice | bytes 2097156 | tf_op jit(solution)/shard_map/while/body/eval_jaxpr/dynamic_update_slice | solution.py:144
  202.1 10.8 %dynamic_update_slice.14 = f32[2,2,512,2048]{3,2,1,0:T(8,128)} dynamic-update-slice(f32[2,2,512,2048]{3,2,1,0:T(8,128)} %get-tuple-element.723, f32[2,2,256,256]{3,2,1,0:T(8,128)S(1)} %bitcast_add_fusion.2, s32[]{:T(128)} %constant.103.clone.1..sunk, s32[]{:T(128)} %constant.103.clone.1..sunk, s32[]{:T(128)S(6)} %select_n.175, s32[]{:T(128)S(6)} %select_n.176) | dynamic-update-slice | bytes 2097156 | tf_op jit(solution)/shard_map/while/body/eval_jaxpr/dynamic_update_slice | solution.py:144
  212.9 7.8 %slice.170 = f32[2,2,256,2048]{3,2,1,0:T(8,128)} slice(f32[2,2,512,2048]{3,2,1,0:T(8,128)} %get-tuple-element.121), slice={[0:2], [0:2], [256:512], [0:2048]} | slice | bytes 16777216 | tf_op jit(solution)/shard_map/slice | solution.py:148
  220.7 4.6 collective-permute-start.2
  226.7 223.7 %reduce-scatter.8.cloned.1.call-done = f32[2,2,32,256]{3,2,1,0:T(8,128)} async-done(((f32[2,2,256,256]{3,2,1,0:T(8,128)}), f32[2,2,32,256]{3,2,1,0:T(8,128)}) %reduce-scatter.8.cloned.1.call-update) | async-done | bytes 131088 | tf_op jit(solution)/shard_map/reduce_scatter | solution.py:153
  452.7 11.8 %slice_add_fusion = f32[2,2,256,2048]{3,2,1,0:T(8,128)} fusion(f32[2,2,256,2048]{3,2,1,0:T(8,128)} %collective-permute-done.2, f32[2,2,512,2048]{3,2,1,0:T(8,128)} %get-tuple-element.121), kind=kLoop, calls=%fused_computation.140 | loop fusion | flops 2097152 | bytes 25165824 | tf_op jit(solution)/shard_map/add | solution.py:149
  464.5 7.0 %reduce-scatter.10.cloned.1.call-done = f32[64,128]{1,0:T(8,128)} async-done(((f32[256,128]{1,0:T(8,128)}), f32[64,128]{1,0:T(8,128)}) %reduce-scatter.10.cloned.1.call-update) | async-done | bytes 32784
  473.2 73.3 %reduce-scatter.6.cloned.1.call-done = f32[2,2,256,512]{3,2,1,0:T(8,128)} async-done(((f32[2,2,256,2048]{3,2,1,0:T(8,128)}), f32[2,2,256,512]{3,2,1,0:T(8,128)}) %reduce-scatter.6.cloned.1.call-update) | async-done | bytes 2097168 | tf_op jit(solution)/shard_map/reduce_scatter | solution.py:150
  (157 shorter events, 114.4 us)
Async XLA Ops:
  7.2 443.2 %reduce-scatter.8.cloned.1.call-start = ((), (), s32[]{:S(2)}) async-start(), calls=%async_computation.4 | async-start | bytes 1179648 | tf_op jit(solution)/shard_map/reduce_scatter | solution.py:153
  8.1 7.6 %collective-permute-start = (s32[2]{0:T(128)S(1)}, s32[2]{0:T(128)S(1)}, u32[]{:S(2)}, u32[]{:S(2)}) collective-permute-start(s32[2]{0:T(128)S(1)} %get-tuple-element.416), channel_id=1, source_target_pairs={{7,0},{0,1},{1,2},{2,3},{3,4},{4,5},{5,6},{6,7},{15,8},{8,9},{9,10... | collective-permute-start | bytes 32 | tf_op jit(solution)/shard_map/ppermute | solution.py:12
  17.4 10.6 %copy-start.9 = (f32[2,2,256,256]{3,2,1,0:T(8,128)S(1)}, f32[2,2,256,256]{3,2,1,0:T(8,128)}, u32[]{:S(2)}) copy-start(f32[2,2,256,256]{3,2,1,0:T(8,128)} %param.14) | copy-start | bytes 3145732
  25.4 46.8 %collective-permute-start.1 = (f32[2,2,2,256,256]{4,3,2,1,0:T(8,128)}, f32[2,2,2,256,256]{4,3,2,1,0:T(8,128)}, u32[]{:S(2)}, u32[]{:S(2)}) collective-permute-start(f32[2,2,2,256,256]{4,3,2,1,0:T(8,128)} %get-tuple-element.138), channel_id=1, source_target_pairs={{1,0},{2,1},{3,2},{4,3},{5,4},{6,5},{7,6},{0,7},{9,8},{10,9},{11,1... | collective-permute-start | bytes 6291464 | tf_op jit(solution)/shard_map/ppermute | solution.py:12
  88.3 7.5 %copy-start.3 = (f32[256,256]{1,0:T(8,128)}, f32[256,256]{1,0:T(8,128)S(1)}, u32[]{:S(2)}) copy-start(f32[256,256]{1,0:T(8,128)S(1)} %get-tuple-element.611) | copy-start | bytes 786436 | tf_op jit(solution)/shard_map/while
  99.8 2.4 copy-start.2
  104.5 1.0 copy-start.1
  121.6 1.2 copy-start
  123.1 1.2 copy-start.4
  124.7 1.0 copy-start.5
  125.7 1.6 copy-start.7
  127.4 1.3 copy-start.8
  130.3 7.5 %copy-start.3 = (f32[256,256]{1,0:T(8,128)}, f32[256,256]{1,0:T(8,128)S(1)}, u32[]{:S(2)}) copy-start(f32[256,256]{1,0:T(8,128)S(1)} %get-tuple-element.611) | copy-start | bytes 786436 | tf_op jit(solution)/shard_map/while
  141.9 2.4 copy-start.2
  163.7 1.2 copy-start
  165.2 1.2 copy-start.4
  166.7 1.0 copy-start.5
  167.7 1.6 copy-start.7
  169.4 1.3 copy-start.8
  170.8 7.9 %copy-start.10 = (s32[1,1,2,2]{3,2,1,0:T(2,128)S(1)}, s32[1,1,2,2]{3,2,1,0:T(2,128)}, u32[]{:S(2)}) copy-start(s32[1,1,2,2]{3,2,1,0:T(2,128)} %param.16) | copy-start | bytes 52
  212.9 12.4 %copy-start.6 = (f32[2,2,256,256]{2,3,1,0:T(8,128)S(1)}, f32[2,2,256,256]{2,3,1,0:T(8,128)}, u32[]{:S(2)}) copy-start(f32[2,2,256,256]{2,3,1,0:T(8,128)} %get-tuple-element.122) | copy-start | bytes 3145732
  220.7 232.0 %collective-permute-start.2 = (f32[2,2,256,2048]{3,2,1,0:T(8,128)}, f32[2,2,256,2048]{3,2,1,0:T(8,128)}, u32[]{:S(2)}, u32[]{:S(2)}) collective-permute-start(f32[2,2,256,2048]{3,2,1,0:T(8,128)} %slice.170), channel_id=1, source_target_pairs={{7,0},{0,1},{1,2},{2,3},{3,4},{4,5},{5,6},{6,7},{15,8},{8,9},{9,10... | collective-permute-start | bytes 25165832 | tf_op jit(solution)/shard_map/ppermute | solution.py:12
  226.6 244.9 %reduce-scatter.10.cloned.1.call-start = ((), (), s32[]{:S(2)}) async-start(), calls=%async_computation.5 | async-start | bytes 163840
  452.7 93.8 %reduce-scatter.6.cloned.1.call-start = ((), (), s32[]{:S(2)}) async-start(), calls=%async_computation.3 | async-start | bytes 10485760 | tf_op jit(solution)/shard_map/reduce_scatter | solution.py:150
  (1 other events, 1.0 us)
Sparse Core Ops, SparseCore 0:
  226.7 223.5 reduce-scatter.7
  452.9 18.5 reduce-scatter.9
  474.7 71.7 reduce-scatter.5
where the time goes:
time: 555 us; the launch traced here: 553 us
  waiting for transfers between devices  337 us (61%)
  local copies, waits for them, and re-layouts  94.5 us (17%)
  other arithmetic  58.1 us (10%)
  matrix products  31.6 us (6%)
  between operations  14.5 us (3%)
  starting transfers between devices  9.74 us (2%)
  loops' own time  7.67 us (1%)
    reduce_scatter x1, waiting for transfers between devices, body(): lax.psum_scatter(probe_sum, 'obj', scatter_dimension=2, tiled=True)  224 us
    reduce_scatter x1, waiting for transfers between devices, body(): lax.psum_scatter(tile_grad, 'scan', scatter_dimension=3, tiled=True)  73.3 us
    ppermute x3, waiting for transfers between devices, shifted(): return lax.ppermute(block, axis, route)  32.8 us
    dot_general x12, matrix products, transform(): jnp.einsum('qab,pqbc->pac', partial_out.astype(jnp.bfloat16), matrix, pre...  31.6 us
    gather x18, local copies, waits for them, and re-layouts  24.2 us
    another operation x17, other arithmetic  24.1 us
    dynamic_update_slice x2, local copies, waits for them, and re-layouts, add_window(): return (lax.dynamic_update_slice(band, current + patch_grad, corner), None)  19 us
    while x40, local copies, waits for them, and re-layouts  16.9 us
  transfers between devices with their start and end apart: 6, of which 5 were waited for; matrix products, arithmetic and copies ran while one was open for 6% of the time, Pallas kernels for 0%

commit v1 on v0

v1 whole, which is shorter than its diff:
```python
import functools
import math

import jax
import jax.numpy as jnp
import ml_dtypes
import numpy as np
from jax import lax
from jax.experimental import pallas as pl
from jax.experimental.pallas import tpu as pltpu
from jax.sharding import PartitionSpec as P

AXES = ("scan", "obj")
CORES = 2
MIB = 1 << 20


def dft_tables(length):
    index = np.arange(length)
    angles = (index[:, None] * index[None, :] % length) * (2.0 * math.pi / length)
    parts = np.stack([np.cos(angles), -np.sin(angles)]) / math.sqrt(length)
    return parts.astype(np.float32).astype(ml_dtypes.bfloat16).astype(np.float32)


def fresnel_tables(length):
    index = np.arange(length)
    freqs = np.where(index < length // 2, index, index - length)
    squares = freqs * freqs
    phases = ((squares[:, None] + squares[None, :]) % (4 * length)) * (2.0 * math.pi / (4 * length))
    return np.stack([np.cos(phases), -np.sin(phases)]).astype(np.float32)


def send(block, scan_of, obj_step):
    n_scan, n_obj = lax.axis_size("scan"), lax.axis_size("obj")
    route = []
    for s in range(n_scan):
        for o in range(n_obj):
            route.append((s * n_obj + o, scan_of(s) % n_scan * n_obj + (o + obj_step) % n_obj))
    return lax.ppermute(block, AXES, route)


def fill_table(table, infos, me, n_scan):
    for k, info in enumerate(infos):
        row = lax.rem(me - k + n_scan, n_scan)
        for j in range(5):
            table[row, j] = info[j]


def assigned(table, target, n_scan):
    idle = table[target, 0] == 0
    rank = jnp.int32(0)
    for a in range(n_scan):
        rank += jnp.where((table[a, 0] == 0) & (a < target), 1, 0)
    source = jnp.int32(target)
    seen = jnp.int32(0)
    for a in range(n_scan):
        full = table[a, 0] == 2
        source = jnp.where(idle & full & (seen == rank), a, source)
        seen += jnp.where(full, 1, 0)
    slot = jnp.where(idle, 1, 0)
    row = jnp.where(idle, table[source, 3], table[source, 1])
    col = jnp.where(idle, table[source, 4], table[source, 2])
    return source, slot, row, col


def column_block(col, length, tile_cols):
    base = jnp.minimum(lax.div(col, length), tile_cols // length - 2)
    return base, col - base * length


def cut_kernel(n_scan, *refs):
    infos = refs[:n_scan]
    object_ref, out_ref, table, wide, sem = refs[n_scan:]
    layers, _, rows, length = out_ref.shape
    me = lax.axis_index("scan")
    fill_table(table, infos, me, n_scan)
    _, _, _, col = assigned(table, me, n_scan)
    base, off = column_block(col, length, object_ref.shape[3])
    start = pl.multiple_of(base * length, length)
    copy = pltpu.make_async_copy(object_ref.at[:, :, :, pl.ds(start, 2 * length)], wide, sem)
    copy.start()
    copy.wait()
    step = 32
    lane = lax.broadcasted_iota(jnp.int32, (step, length), 1)
    keep = lane >= off
    for l in range(layers):
        for q in range(2):
            for i in range(0, rows, step):
                at = pl.ds(i, step)
                picked = jnp.where(keep, wide[l, q, at, :length], wide[l, q, at, length:])
                out_ref[l, q, at, :] = picked.astype(out_ref.dtype)


def pattern_kernel(n_scan, *refs):
    infos = refs[:n_scan]
    object_ref, piece_ref, probe_ref, own_ref = refs[n_scan : n_scan + 4]
    others = refs[n_scan + 4 : 2 * n_scan + 3]
    dft_ref, fresnel_ref = refs[2 * n_scan + 3 : 2 * n_scan + 5]
    grad_ref, egrad_ref = refs[2 * n_scan + 5 : 2 * n_scan + 7]
    (table, wide, x_ref, p_ref, a_ref, v_ref, u_ref, s_ref, far_ref, meas_ref,
     lf, li, rf, ri, sem) = refs[2 * n_scan + 7 :]
    modes, _, length, _ = probe_ref.shape
    me = lax.axis_index("scan")
    fill_table(table, infos, me, n_scan)
    source, slot, row, col = assigned(table, me, n_scan)
    base, off = column_block(col, length, object_ref.shape[3])
    start = pl.multiple_of(base * length, length)
    copy = pltpu.make_async_copy(object_ref.at[:, :, :, pl.ds(start, 2 * length)], wide, sem)
    copy.start()
    turn = lax.rem(off, length)

    @pl.when(slot == 0)
    def _():
        meas_ref[...] = own_ref[0]

    for k in range(1, n_scan):
        @pl.when((slot == 1) & (source == lax.rem(me - k + n_scan, n_scan)))
        def _():
            meas_ref[...] = others[k - 1][...]

    def put(matrix, real, imag):
        matrix[:length, :length] = real.astype(jnp.bfloat16)
        matrix[length:, length:] = real.astype(jnp.bfloat16)
        matrix[:length, length:] = imag.astype(jnp.bfloat16)
        matrix[length:, :length] = (-imag).astype(jnp.bfloat16)

    real, imag = dft_ref[0], dft_ref[1]
    put(lf, pltpu.roll(real, row, 1), -pltpu.roll(imag, row, 1))
    put(li, pltpu.roll(real, row, 0), pltpu.roll(imag, row, 0))
    put(rf, pltpu.roll(real, turn, 0), pltpu.roll(imag, turn, 0))
    put(ri, pltpu.roll(real, turn, 1), -pltpu.roll(imag, turn, 1))
    for m in range(modes):
        for q in range(2):
            p_ref[m, q] = pltpu.roll(pltpu.roll(probe_ref[m, q], row, 0), turn, 1)

    step = 32
    chunks = range(0, length, step)
    lane = lax.broadcasted_iota(jnp.int32, (step, length), 1)
    line = lax.broadcasted_iota(jnp.int32, (step, length), 0)
    keep = lane >= off

    def load_x(l):
        for q in range(2):
            for i in chunks:
                at = pl.ds(i, step)
                own = jnp.where(keep, wide[l, q, at, :length], wide[l, q, at, length:])
                x_ref[l, q, at, :] = jnp.where(line >= row - i, own, piece_ref[l, q, at, :].astype(jnp.float32))

    def put_v(m, i, real, imag):
        at = m * length
        v_ref[pl.ds(i, step), at : at + length] = real.astype(jnp.bfloat16)
        v_ref[pl.ds(length + i, step), at : at + length] = imag.astype(jnp.bfloat16)

    def transform(left, right):
        mid = jnp.dot(left[...], v_ref[...], preferred_element_type=jnp.float32).astype(jnp.bfloat16)
        for m in range(modes):
            for q in range(2):
                u_ref[m * length : (m + 1) * length, q * length : (q + 1) * length] = mid[
                    q * length : (q + 1) * length, m * length : (m + 1) * length
                ]
        s_ref[...] = jnp.dot(u_ref[...], right[...], preferred_element_type=jnp.float32)

    def get_s(ref, m, i):
        at = pl.ds(m * length + i, step)
        return ref[at, :length], ref[at, length:]

    def mul(ar, ai, br, bi):
        return ar * br - ai * bi, ar * bi + ai * br

    def cmul(ar, ai, br, bi):
        return ar * br + ai * bi, ar * bi - ai * br

    def propagate(conj):
        transform(lf, rf)
        for i in chunks:
            at = pl.ds(i, step)
            kr, ki = fresnel_ref[0, at, :], fresnel_ref[1, at, :]
            for m in range(modes):
                sr, si = get_s(s_ref, m, i)
                put_v(m, i, *(cmul if conj else mul)(kr, ki, sr, si))
        transform(li, ri)

    copy.wait()
    for l in range(2):
        load_x(l)
    for i in chunks:
        at = pl.ds(i, step)
        xr, xi = x_ref[0, 0, at, :], x_ref[0, 1, at, :]
        for m in range(modes):
            put_v(m, i, *mul(p_ref[m, 0, at, :], p_ref[m, 1, at, :], xr, xi))
    propagate(False)
    for i in chunks:
        at = pl.ds(i, step)
        xr, xi = x_ref[1, 0, at, :], x_ref[1, 1, at, :]
        for m in range(modes):
            ar, ai = get_s(s_ref, m, i)
            a_ref[m, 0, at, :] = ar
            a_ref[m, 1, at, :] = ai
            put_v(m, i, *mul(ar, ai, xr, xi))
    transform(lf, rf)
    for i in chunks:
        at = pl.ds(i, step)
        misfit = -meas_ref[at, :].astype(jnp.float32)
        for m in range(modes):
            fr, fi = get_s(s_ref, m, i)
            misfit += fr * fr + fi * fi
        for m in range(modes):
            fr, fi = get_s(s_ref, m, i)
            put_v(m, i, misfit * fr, misfit * fi)
    transform(li, ri)
    for i in chunks:
        at = pl.ds(i, step)
        xr, xi = x_ref[1, 0, at, :], x_ref[1, 1, at, :]
        gr = gi = 0.0
        for m in range(modes):
            cr, ci = get_s(s_ref, m, i)
            dr, di = cmul(a_ref[m, 0, at, :], a_ref[m, 1, at, :], cr, ci)
            gr, gi = gr + dr, gi + di
            put_v(m, i, *cmul(xr, xi, cr, ci))
        grad_ref[1, 0, at, :] = gr.astype(jnp.bfloat16)
        grad_ref[1, 1, at, :] = gi.astype(jnp.bfloat16)
    propagate(True)
    for i in chunks:
        at = pl.ds(i, step)
        xr, xi = x_ref[0, 0, at, :], x_ref[0, 1, at, :]
        gr = gi = 0.0
        for m in range(modes):
            cr, ci = get_s(s_ref, m, i)
            dr, di = cmul(p_ref[m, 0, at, :], p_ref[m, 1, at, :], cr, ci)
            gr, gi = gr + dr, gi + di
            er, ei = cmul(xr, xi, cr, ci)
            a_ref[m, 0, at, :] = er
            a_ref[m, 1, at, :] = ei
        grad_ref[0, 0, at, :] = gr.astype(jnp.bfloat16)
        grad_ref[0, 1, at, :] = gi.astype(jnp.bfloat16)
    row_back = lax.rem(length - row, length)
    turn_back = lax.rem(length - turn, length)
    for m in range(modes):
        for q in range(2):
            egrad_ref[m, q] = pltpu.roll(pltpu.roll(a_ref[m, q], row_back, 0), turn_back, 1)


def place_kernel(n_scan, steps, *refs):
    own_infos, prev_infos = refs[:n_scan], refs[n_scan : 2 * n_scan]
    patches = refs[2 * n_scan : 4 * n_scan]
    out_ref, own_table, prev_table = refs[4 * n_scan :]
    layers, _, rows, width = out_ref.shape
    length = patches[0].shape[3]
    tile_cols = width * n_scan
    me = lax.axis_index("scan")
    fill_table(own_table, own_infos, me, n_scan)
    fill_table(prev_table, prev_infos, me, n_scan)
    step = 32
    out_ref[...] = jnp.zeros(out_ref.shape, jnp.float32)
    lane = lax.broadcasted_iota(jnp.int32, (step, length), 1)
    line = lax.broadcasted_iota(jnp.int32, (step, length), 0)
    for index, patch in enumerate(patches):
        flip, jump = steps[index % n_scan]
        source = lax.rem((me ^ flip) - jump + n_scan, n_scan)
        table = own_table if index < n_scan else prev_table
        _, _, row, col = assigned(table, source, n_scan)
        base, off = column_block(col, length, tile_cols)
        top, bottom = (row, rows) if index < n_scan else (0, row)
        for block in range(width // length):
            here = me * (width // length) + block
            first, second = base == here, base + 1 == here
            left = jnp.where(first, off, 0)
            right = jnp.where(first, length, off)

            @pl.when(first | second)
            def _():
                cols = (lane >= left) & (lane < right)
                spot = slice(block * length, (block + 1) * length)
                for i in range(0, rows, step):
                    mask = cols & (line >= top - i) & (line < bottom - i)
                    at = pl.ds(i, step)
                    for l in range(layers):
                        for q in range(2):
                            value = patch[l, q, at, :].astype(jnp.float32)
                            out_ref[l, q, at, spot] += jnp.where(mask, value, 0.0)


def body(object_slices, probe, measured, positions, counts):
    layers, _, tile_rows, tile_cols = object_slices.shape
    modes, _, length, _ = probe.shape
    slots = measured.shape[2]
    n_scan, n_obj = lax.axis_size("scan"), lax.axis_size("obj")
    smem = pl.BlockSpec(memory_space=pltpu.SMEM)
    vmem = pl.BlockSpec(memory_space=pltpu.VMEM)
    hbm = pl.BlockSpec(memory_space=pl.ANY)
    info = jnp.concatenate([counts[0], positions[0, 0].reshape(-1)])
    prev_infos = [send(info, lambda s, k=k: s + k, 1) for k in range(n_scan)]
    own_infos = [info] + [send(info, lambda s, k=k: s + k, 0) for k in range(1, n_scan)]
    second = measured[0, 0, 1]
    others = [send(second, lambda s, k=k: s + k, 0) for k in range(1, n_scan)]

    piece_shape = (layers, 2, length, length)
    table = pltpu.SMEM((n_scan, 8), jnp.int32)
    wide = pltpu.VMEM((layers, 2, tile_rows, 2 * length), jnp.float32)
    piece = pl.pallas_call(
        functools.partial(cut_kernel, n_scan),
        out_shape=jax.ShapeDtypeStruct(piece_shape, jnp.bfloat16),
        in_specs=[smem] * n_scan + [hbm],
        out_specs=vmem,
        scratch_shapes=[table, wide, pltpu.SemaphoreType.DMA],
        compiler_params=pltpu.CompilerParams(vmem_limit_bytes=16 * MIB),
        name="cut",
    )(*prev_infos, object_slices)
    got = send(piece, lambda s: s, -1)

    wide_mat = pltpu.VMEM((2 * length, 2 * length), jnp.bfloat16)
    stack_mat = pltpu.VMEM((modes * length, 2 * length), jnp.float32)
    flops = 3 * 2 * 2 * modes * 8 * length**3
    grad, egrad = pl.pallas_call(
        functools.partial(pattern_kernel, n_scan),
        out_shape=[
            jax.ShapeDtypeStruct(piece_shape, jnp.bfloat16),
            jax.ShapeDtypeStruct(probe.shape, jnp.float32),
        ],
        in_specs=[smem] * n_scan + [hbm] + [vmem] * (n_scan + 4),
        out_specs=[vmem, vmem],
        scratch_shapes=[
            table,
            wide,
            pltpu.VMEM(piece_shape, jnp.float32),
            pltpu.VMEM(probe.shape, jnp.float32),
            pltpu.VMEM(probe.shape, jnp.float32),
            pltpu.VMEM((2 * length, modes * length), jnp.bfloat16),
            pltpu.VMEM((modes * length, 2 * length), jnp.bfloat16),
            stack_mat,
            stack_mat,
            pltpu.VMEM((length, length), measured.dtype),
            wide_mat,
            wide_mat,
            wide_mat,
            wide_mat,
            pltpu.SemaphoreType.DMA,
        ],
        compiler_params=pltpu.CompilerParams(vmem_limit_bytes=32 * MIB),
        cost_estimate=pl.CostEstimate(flops=flops, bytes_accessed=8 * MIB, transcendentals=0),
        name="pattern",
    )(*own_infos, object_slices, got, probe, measured[0, 0], *others, dft_tables(length), fresnel_tables(length))

    jumps = [CORES * k for k in range(n_scan // CORES)]
    own_patches = [grad] + [send(grad, lambda s, j=j: s + j, 0) for j in jumps[1:]]
    prev_patches = [send(grad, lambda s, j=j: s + j, 1) for j in jumps]
    own_other = [send(p, lambda s: s ^ 1, 0) for p in own_patches]
    prev_other = [send(p, lambda s: s ^ 1, 0) for p in prev_patches]
    steps = [(0, j) for j in jumps] + [(1, j) for j in jumps]
    object_grad = pl.pallas_call(
        functools.partial(place_kernel, n_scan, steps),
        out_shape=jax.ShapeDtypeStruct((layers, 2, tile_rows, tile_cols // n_scan), jnp.float32),
        in_specs=[smem] * (2 * n_scan) + [vmem] * (2 * n_scan),
        out_specs=vmem,
        scratch_shapes=[table, table],
        compiler_params=pltpu.CompilerParams(vmem_limit_bytes=32 * MIB),
        name="place",
    )(*own_infos, *prev_infos, *own_patches, *own_other, *prev_patches, *prev_other)

    factor = 1.0 / math.sqrt(n_scan * n_obj * slots // 2)
    partial_probe = lax.psum_scatter(egrad, "scan", scatter_dimension=3, tiled=True)
    probe_total = lax.psum_scatter(partial_probe, "obj", scatter_dimension=2, tiled=True)
    return (object_grad, probe_total * factor)


def solution(mesh):
    return jax.shard_map(
        body,
        mesh=mesh,
        in_specs=(
            P(None, None, "obj", None),
            P(),
            P("scan", "obj", None, None, None),
            P("scan", "obj", None, None),
            P("scan", "obj"),
        ),
        out_specs=(P(None, None, "obj", "scan"), P(None, None, "obj", "scan")),
        check_vma=False,
    )
```

time: 555 us -> 187 us (0.34)
  waiting for transfers between devices: 337 us -> 131 us
  local copies, waits for them, and re-layouts: 94.5 us -> 11.5 us
  other arithmetic: 58.1 us -> 0.95 us
  matrix products: 31.6 us -> 0 us
  Pallas kernels: 0 us -> 11.2 us
  loops' own time: 7.67 us -> 0 us
  starting transfers between devices: 9.74 us -> 16.6 us
    reduce_scatter x2 -> x0, waiting for transfers between devices: 297 us -> none  [the longest x1 224 us: body(): lax.psum_scatter(probe_sum, 'obj', scatter_dimension=2, tiled=True)]
    unnamed x4, waiting for transfers between devices: 7.05 us -> 88.8 us
    dot_general x12 -> x0, matrix products: 31.6 us -> none  [transform(): jnp.einsum('qab,pqbc->pac', partial_out.astype(jnp.bfloat16), matrix, pre...]
    another operation x23 -> x0, other arithmetic: 25.4 us -> none
    gather x18 -> x0, local copies, waits for them, and re-layouts: 24.2 us -> none
    dynamic_update_slice x4 -> x0, local copies, waits for them, and re-layouts: 19.2 us -> none  [the longest x2 19 us: add_window(): return (lax.dynamic_update_slice(band, current + patch_grad, corner), None)]
    while x41 -> x0, local copies, waits for them, and re-layouts: 18.3 us -> none
    add x9 -> x0, other arithmetic: 16.6 us -> none  [the longest x1 11.8 us: body(): tile_grad = band[:, :, :tile_rows].at[:, :, :length].add(rim_back)]
  transfers between devices with their start and end apart: 6 -> 20, of which waited for: 5 -> 11; matrix products, arithmetic and copies ran while one was open for 6% -> 3% of each run, Pallas kernels for 0% -> 0%
where the time goes in v1:
time: 187 us
  waiting for transfers between devices  131 us (70%)
  starting transfers between devices  16.6 us (9%)
  between operations  16.1 us (9%)
  local copies, waits for them, and re-layouts  11.5 us (6%)
  Pallas kernels  11.2 us (6%)
    unnamed x4, waiting for transfers between devices  88.8 us
    ppermute x18, waiting for transfers between devices, send(): return lax.ppermute(block, AXES, route)  41.9 us
    ppermute x18, starting transfers between devices, send(): return lax.ppermute(block, AXES, route)  16.6 us
    unnamed x20, local copies, waits for them, and re-layouts  8.44 us
    pallas_call x1, Pallas kernels, body(): pl.pallas_call(functools.partial(pattern_kernel, n_scan), out_shape=[jax....  6.84 us
  transfers between devices with their start and end apart: 20, of which 11 were waited for; matrix products, arithmetic and copies ran while one was open for 3% of the time, Pallas kernels for 0%

profile of v1, /device:TPU:0, one launch (start us, length us, event | category | flops | bytes accessed | tf_op | source)
XLA Modules:
  0.0 187.1 jit_solution(893710881359176760)
XLA Ops:
  8.7 3.3 %collective-permute-start.6 = (s32[5]{0:T(128)S(1)}, s32[5]{0:T(128)S(1)}, u32[]{:S(2)}, u32[]{:S(2)}) collective-permute-start(s32[5]{0:T(128)S(1)} %pad_add_fusion.refs_0_), channel_id=1, source_target_pairs={{0,25},{1,26},{2,27},{3,28},{4,29},{5,30},{6,31},{7,24},{8,1},{9,2... | collective-permute-start | bytes 68 | tf_op jit(solution)/shard_map/ppermute | solution.py:39
  12.0 1.5 collective-permute-start.5
  13.5 1.5 collective-permute-start.4
  15.1 1.5 collective-permute-start.3
  16.6 2.6 %collective-permute-done.5.refs_2_.refs_6_ = s32[5]{0:T(128)S(1)} collective-permute-done((s32[5]{0:T(128)S(1)}, s32[5]{0:T(128)S(1)}, u32[]{:S(2)}, u32[]{:S(2)}) %collective-permute-start.5) | collective-permute-done | bytes 52 | tf_op jit(solution)/shard_map/ppermute | solution.py:39
  20.1 1.2 collective-permute-done.3.refs_0_.refs_4_
  21.3 3.4 %copy-done = f32[2,2,256,2048]{3,2,1,0:T(8,128)S(1)} copy-done((f32[2,2,256,2048]{3,2,1,0:T(8,128)S(1)}, f32[2,2,256,2048]{3,2,1,0:T(8,128)}, u32[]{:S(2)}) %copy-start) | copy-done | bytes 8388632
  26.4 1.2 collective-permute-start.9
  27.6 1.7 collective-permute-start.2
  29.3 3.6 %collective-permute-done.2.refs_3_ = s32[5]{0:T(128)S(1)} collective-permute-done((s32[5]{0:T(128)S(1)}, s32[5]{0:T(128)S(1)}, u32[]{:S(2)}, u32[]{:S(2)}) %collective-permute-start.2) | collective-permute-done | bytes 52 | tf_op jit(solution)/shard_map/ppermute | solution.py:39
  32.9 1.1 collective-permute-start.1
  34.0 2.4 %collective-permute-done.1.refs_2_ = s32[5]{0:T(128)S(1)} collective-permute-done((s32[5]{0:T(128)S(1)}, s32[5]{0:T(128)S(1)}, u32[]{:S(2)}, u32[]{:S(2)}) %collective-permute-start.1) | collective-permute-done | bytes 52 | tf_op jit(solution)/shard_map/ppermute | solution.py:39
  37.2 2.2 %collective-permute-done.refs_1_ = s32[5]{0:T(128)S(1)} collective-permute-done((s32[5]{0:T(128)S(1)}, s32[5]{0:T(128)S(1)}, u32[]{:S(2)}, u32[]{:S(2)}) %collective-permute-start) | collective-permute-done | bytes 52 | tf_op jit(solution)/shard_map/ppermute | solution.py:39
  39.5 1.2 copy-done.3
  40.7 1.0 copy-done.5
  41.7 6.8 %pattern.1 = (bf16[2,2,256,256]{3,2,1,0:T(8,128)(2,1)S(1)}, f32[2,2,256,256]{3,2,1,0:T(8,128)S(1)}) custom-call(s32[5]{0:T(128)S(1)} %pad_add_fusion.refs_0_, s32[5]{0:T(128)S(1)} %collective-permute-done.refs_1_, s32[5]{0:T(128)S(1)} %collective-permute-done.1.refs_2_, s32[5]{0:T(128)S(1)} %collective-permute-done.2.refs_3_, ...), custom_call_target="tpu_custom_call" | custom-call | flops 3221225472 | bytes 8388608 | tf_op jit(solution)/shard_map/pattern/pallas_call | solution.py:314
  48.6 2.1 %collective-permute-start.15 = (bf16[2,2,256,256]{3,2,1,0:T(8,128)(2,1)S(1)}, bf16[2,2,256,256]{3,2,1,0:T(8,128)(2,1)S(1)}, u32[]{:S(2)}, u32[]{:S(2)}) collective-permute-start(bf16[2,2,256,256]{3,2,1,0:T(8,128)(2,1)S(1)} %get-tuple-element.4.refs_8_), channel_id=1, source_target_pairs={{0,17},{1,18},{2,19},{3,20},{4,21},{5,22},{6,23},{7,16},{8,25},{9,... | collective-permute-start | bytes 1572872 | tf_op jit(solution)/shard_map/ppermute | solution.py:39
  51.7 1.3 copy.11
  53.2 14.7 %collective-permute-done.15.refs_13_ = bf16[2,2,256,256]{3,2,1,0:T(8,128)(2,1)S(1)} collective-permute-done((bf16[2,2,256,256]{3,2,1,0:T(8,128)(2,1)S(1)}, bf16[2,2,256,256]{3,2,1,0:T(8,128)(2,1)S(1)}, u32[]{:S(2)}, u32[]{:S(2)}) %collective-permute-start.15) | collective-permute-done | bytes 524320 | tf_op jit(solution)/shard_map/ppermute | solution.py:39
  67.9 8.5 %collective-permute-done.14.refs_12_ = bf16[2,2,256,256]{3,2,1,0:T(8,128)(2,1)S(1)} collective-permute-done((bf16[2,2,256,256]{3,2,1,0:T(8,128)(2,1)S(1)}, bf16[2,2,256,256]{3,2,1,0:T(8,128)(2,1)S(1)}, u32[]{:S(2)}, u32[]{:S(2)}) %collective-permute-start.14) | collective-permute-done | bytes 524320 | tf_op jit(solution)/shard_map/ppermute | solution.py:39
  76.4 5.7 %collective-permute-done.11.refs_9_ = bf16[2,2,256,256]{3,2,1,0:T(8,128)(2,1)S(1)} collective-permute-done((bf16[2,2,256,256]{3,2,1,0:T(8,128)(2,1)S(1)}, bf16[2,2,256,256]{3,2,1,0:T(8,128)(2,1)S(1)}, u32[]{:S(2)}, u32[]{:S(2)}) %collective-permute-start.11) | collective-permute-done | bytes 524320 | tf_op jit(solution)/shard_map/ppermute | solution.py:39
  83.4 14.8 %all-reduce.5.cloned.1.call-done = f32[2,2,256,256]{2,1,0,3:T(2,128)} async-done(((f32[2,2,256,256]{2,1,0,3:T(2,128)}), f32[2,2,256,256]{2,1,0,3:T(2,128)}) %all-reduce.5.cloned.1.call-update) | async-done | bytes 1048592
  101.4 73.9 %all-reduce.7.cloned.1.call-done = f32[2,2,256,64]{3,1,0,2:T(2,128)} async-done(((f32[2,2,256,64]{3,1,0,2:T(2,128)}), f32[2,2,256,64]{3,1,0,2:T(2,128)}) %all-reduce.7.cloned.1.call-update) | async-done | bytes 262160
  176.9 3.3 %place.1 = f32[2,2,256,512]{3,2,1,0:T(8,128)} custom-call(s32[5]{0:T(128)S(1)} %pad_add_fusion.refs_0_, s32[5]{0:T(128)S(1)} %collective-permute-done.refs_1_, s32[5]{0:T(128)S(1)} %collective-permute-done.1.refs_2_, s32[5]{0:T(128)S(1)} %collective-permute-done.2.refs_3_, s32[5]{0:T(128)S(1)} %collective-permute-done.3.refs_0_.refs_4_, ...), custom_call_target="tpu_custom_call" | custom-call | tf_op jit(solution)/shard_map/place/pallas_call | solution.py:350
  (47 shorter events, 10.1 us)
Async XLA Ops:
  7.2 91.0 %all-reduce.5.cloned.1.call-start = ((), (), s32[]{:S(2)}) async-start(), calls=%async_computation | async-start | bytes 2097152
  8.7 7.9 %collective-permute-start.6 = (s32[5]{0:T(128)S(1)}, s32[5]{0:T(128)S(1)}, u32[]{:S(2)}, u32[]{:S(2)}) collective-permute-start(s32[5]{0:T(128)S(1)} %pad_add_fusion.refs_0_), channel_id=1, source_target_pairs={{0,25},{1,26},{2,27},{3,28},{4,29},{5,30},{6,31},{7,24},{8,1},{9,2... | collective-permute-start | bytes 68 | tf_op jit(solution)/shard_map/ppermute | solution.py:39
  12.0 7.1 %collective-permute-start.5 = (s32[5]{0:T(128)S(1)}, s32[5]{0:T(128)S(1)}, u32[]{:S(2)}, u32[]{:S(2)}) collective-permute-start(s32[5]{0:T(128)S(1)} %pad_add_fusion.refs_0_), channel_id=1, source_target_pairs={{0,17},{1,18},{2,19},{3,20},{4,21},{5,22},{6,23},{7,16},{8,25},{9,... | collective-permute-start | bytes 68 | tf_op jit(solution)/shard_map/ppermute | solution.py:39
  13.5 6.6 %collective-permute-start.4 = (s32[5]{0:T(128)S(1)}, s32[5]{0:T(128)S(1)}, u32[]{:S(2)}, u32[]{:S(2)}) collective-permute-start(s32[5]{0:T(128)S(1)} %pad_add_fusion.refs_0_), channel_id=1, source_target_pairs={{0,9},{1,10},{2,11},{3,12},{4,13},{5,14},{6,15},{7,8},{8,17},{9,18... | collective-permute-start | bytes 68 | tf_op jit(solution)/shard_map/ppermute | solution.py:39
  15.1 6.2 %collective-permute-start.3 = (s32[5]{0:T(128)S(1)}, s32[5]{0:T(128)S(1)}, u32[]{:S(2)}, u32[]{:S(2)}) collective-permute-start(s32[5]{0:T(128)S(1)} %pad_add_fusion.refs_0_), channel_id=1, source_target_pairs={{0,1},{1,2},{2,3},{3,4},{4,5},{5,6},{6,7},{7,0},{8,9},{9,10},{10,1... | collective-permute-start | bytes 68 | tf_op jit(solution)/shard_map/ppermute | solution.py:39
  24.7 14.8 %copy-start.1 = (f32[2,2,256,2048]{3,2,1,0:T(8,128)S(1)}, f32[2,2,256,2048]{3,2,1,0:T(8,128)}, u32[]{:S(2)}) copy-start(f32[2,2,256,2048]{3,2,1,0:T(8,128)} %refs_4_.3) | copy-start | bytes 25165828
  24.7 14.8 %copy-start.4 = (f32[2,256,256]{2,1,0:T(8,128)S(1)}, f32[2,256,256]{2,1,0:T(8,128)}, u32[]{:S(2)}) copy-start(f32[2,256,256]{2,1,0:T(8,128)} %constant.7.clone.refs_12_) | copy-start | bytes 1572868
  25.7 56.4 %copy-start.7 = (u32[32]{0:T(128)S(1)}, u32[32]{0:T(128)}, u32[]{:S(2)}) copy-start(u32[32]{0:T(128)} %constant.13) | copy-start | bytes 388
  25.7 13.7 %collective-permute-start.7 = (bf16[2,2,256,256]{3,2,1,0:T(8,128)(2,1)S(1)}, bf16[2,2,256,256]{3,2,1,0:T(8,128)(2,1)S(1)}, u32[]{:S(2)}, u32[]{:S(2)}) collective-permute-start(bf16[2,2,256,256]{3,2,1,0:T(8,128)(2,1)S(1)} %cut.1), channel_id=1, source_target_pairs={{0,7},{1,0},{2,1},{3,2},{4,3},{5,4},{6,5},{7,6},{8,15},{9,8},{10,9... | collective-permute-start | bytes 1572872 | tf_op jit(solution)/shard_map/ppermute | solution.py:39
  26.3 13.1 %collective-permute-start.10 = (bf16[256,256]{1,0:T(8,128)(2,1)S(1)}, bf16[256,256]{1,0:T(8,128)(2,1)S(1)}, u32[]{:S(2)}, u32[]{:S(2)}) collective-permute-start(bf16[256,256]{1,0:T(8,128)(2,1)S(1)} %slice_bitcast_fusion), channel_id=1, source_target_pairs={{0,24},{1,25},{2,26},{3,27},{4,28},{5,29},{6,30},{7,31},{8,0},{9,1... | collective-permute-start | bytes 393224 | tf_op jit(solution)/shard_map/ppermute | solution.py:39
  26.4 13.1 %collective-permute-start.9 = (bf16[256,256]{1,0:T(8,128)(2,1)S(1)}, bf16[256,256]{1,0:T(8,128)(2,1)S(1)}, u32[]{:S(2)}, u32[]{:S(2)}) collective-permute-start(bf16[256,256]{1,0:T(8,128)(2,1)S(1)} %slice_bitcast_fusion), channel_id=1, source_target_pairs={{0,16},{1,17},{2,18},{3,19},{4,20},{5,21},{6,22},{7,23},{8,24},{9,... | collective-permute-start | bytes 393224 | tf_op jit(solution)/shard_map/ppermute | solution.py:39
  27.6 11.9 %collective-permute-start.8 = (bf16[256,256]{1,0:T(8,128)(2,1)S(1)}, bf16[256,256]{1,0:T(8,128)(2,1)S(1)}, u32[]{:S(2)}, u32[]{:S(2)}) collective-permute-start(bf16[256,256]{1,0:T(8,128)(2,1)S(1)} %slice_bitcast_fusion), channel_id=1, source_target_pairs={{0,8},{1,9},{2,10},{3,11},{4,12},{5,13},{6,14},{7,15},{8,16},{9,17... | collective-permute-start | bytes 393224 | tf_op jit(solution)/shard_map/ppermute | solution.py:39
  27.6 5.3 %collective-permute-start.2 = (s32[5]{0:T(128)S(1)}, s32[5]{0:T(128)S(1)}, u32[]{:S(2)}, u32[]{:S(2)}) collective-permute-start(s32[5]{0:T(128)S(1)} %pad_add_fusion.refs_0_), channel_id=1, source_target_pairs={{0,24},{1,25},{2,26},{3,27},{4,28},{5,29},{6,30},{7,31},{8,0},{9,1... | collective-permute-start | bytes 68 | tf_op jit(solution)/shard_map/ppermute | solution.py:39
  32.9 3.5 %collective-permute-start.1 = (s32[5]{0:T(128)S(1)}, s32[5]{0:T(128)S(1)}, u32[]{:S(2)}, u32[]{:S(2)}) collective-permute-start(s32[5]{0:T(128)S(1)} %pad_add_fusion.refs_0_), channel_id=1, source_target_pairs={{0,16},{1,17},{2,18},{3,19},{4,20},{5,21},{6,22},{7,23},{8,24},{9,... | collective-permute-start | bytes 68 | tf_op jit(solution)/shard_map/ppermute | solution.py:39
  36.5 3.0 %collective-permute-start = (s32[5]{0:T(128)S(1)}, s32[5]{0:T(128)S(1)}, u32[]{:S(2)}, u32[]{:S(2)}) collective-permute-start(s32[5]{0:T(128)S(1)} %pad_add_fusion.refs_0_), channel_id=1, source_target_pairs={{0,8},{1,9},{2,10},{3,11},{4,12},{5,13},{6,14},{7,15},{8,16},{9,17... | collective-permute-start | bytes 68 | tf_op jit(solution)/shard_map/ppermute | solution.py:39
  41.7 58.5 %copy-start.6 = (u32[32]{0:T(128)S(1)}, u32[32]{0:T(128)}, u32[]{:S(2)}) copy-start(u32[32]{0:T(128)} %constant.17) | copy-start | bytes 388
  48.6 19.3 %collective-permute-start.15 = (bf16[2,2,256,256]{3,2,1,0:T(8,128)(2,1)S(1)}, bf16[2,2,256,256]{3,2,1,0:T(8,128)(2,1)S(1)}, u32[]{:S(2)}, u32[]{:S(2)}) collective-permute-start(bf16[2,2,256,256]{3,2,1,0:T(8,128)(2,1)S(1)} %get-tuple-element.4.refs_8_), channel_id=1, source_target_pairs={{0,17},{1,18},{2,19},{3,20},{4,21},{5,22},{6,23},{7,16},{8,25},{9,... | collective-permute-start | bytes 1572872 | tf_op jit(solution)/shard_map/ppermute | solution.py:39
  50.7 25.7 %collective-permute-start.14 = (bf16[2,2,256,256]{3,2,1,0:T(8,128)(2,1)S(1)}, bf16[2,2,256,256]{3,2,1,0:T(8,128)(2,1)S(1)}, u32[]{:S(2)}, u32[]{:S(2)}) collective-permute-start(bf16[2,2,256,256]{3,2,1,0:T(8,128)(2,1)S(1)} %get-tuple-element.4.refs_8_), channel_id=1, source_target_pairs={{0,1},{1,2},{2,3},{3,4},{4,5},{5,6},{6,7},{7,0},{8,9},{9,10},{10,1... | collective-permute-start | bytes 1572872 | tf_op jit(solution)/shard_map/ppermute | solution.py:39
  50.7 31.4 %collective-permute-start.11 = (bf16[2,2,256,256]{3,2,1,0:T(8,128)(2,1)S(1)}, bf16[2,2,256,256]{3,2,1,0:T(8,128)(2,1)S(1)}, u32[]{:S(2)}, u32[]{:S(2)}) collective-permute-start(bf16[2,2,256,256]{3,2,1,0:T(8,128)(2,1)S(1)} %get-tuple-element.4.refs_8_), channel_id=1, source_target_pairs={{0,16},{1,17},{2,18},{3,19},{4,20},{5,21},{6,22},{7,23},{8,24},{9,... | collective-permute-start | bytes 1572872 | tf_op jit(solution)/shard_map/ppermute | solution.py:39
  53.0 122.3 %all-reduce.7.cloned.1.call-start = ((), (), s32[]{:S(2)}) async-start(), calls=%async_computation.1 | async-start | bytes 1048576
  53.1 123.8 %collective-permute-start.12 = (bf16[2,2,256,256]{3,2,1,0:T(8,128)(2,1)S(1)}, bf16[2,2,256,256]{3,2,1,0:T(8,128)(2,1)S(1)}, u32[]{:S(2)}, u32[]{:S(2)}) collective-permute-start(bf16[2,2,256,256]{3,2,1,0:T(8,128)(2,1)S(1)} %get-tuple-element.4.refs_8_), channel_id=1, source_target_pairs={{0,8},{1,9},{2,10},{3,11},{4,12},{5,13},{6,14},{7,15},{8,0},{9,1},... | collective-permute-start | bytes 1572872 | tf_op jit(solution)/shard_map/ppermute | solution.py:39
  67.9 109.0 %collective-permute-start.17 = (bf16[2,2,256,256]{3,2,1,0:T(8,128)(2,1)S(1)}, bf16[2,2,256,256]{3,2,1,0:T(8,128)(2,1)S(1)}, u32[]{:S(2)}, u32[]{:S(2)}) collective-permute-start(bf16[2,2,256,256]{3,2,1,0:T(8,128)(2,1)S(1)} %collective-permute-done.15.refs_13_), channel_id=1, source_target_pairs={{0,8},{1,9},{2,10},{3,11},{4,12},{5,13},{6,14},{7,15},{8,0},{9,1},... | collective-permute-start | bytes 1572872 | tf_op jit(solution)/shard_map/ppermute | solution.py:39
  76.4 100.5 %collective-permute-start.16 = (bf16[2,2,256,256]{3,2,1,0:T(8,128)(2,1)S(1)}, bf16[2,2,256,256]{3,2,1,0:T(8,128)(2,1)}, u32[]{:S(2)}, u32[]{:S(2)}) collective-permute-start(bf16[2,2,256,256]{3,2,1,0:T(8,128)(2,1)S(1)} %collective-permute-done.14.refs_12_), channel_id=1, source_target_pairs={{0,8},{1,9},{2,10},{3,11},{4,12},{5,13},{6,14},{7,15},{8,0},{9,1},... | collective-permute-start | bytes 1572872 | tf_op jit(solution)/shard_map/ppermute | solution.py:39
  82.1 94.8 %collective-permute-start.13 = (bf16[2,2,256,256]{3,2,1,0:T(8,128)(2,1)S(1)}, bf16[2,2,256,256]{3,2,1,0:T(8,128)(2,1)}, u32[]{:S(2)}, u32[]{:S(2)}) collective-permute-start(bf16[2,2,256,256]{3,2,1,0:T(8,128)(2,1)S(1)} %collective-permute-done.11.refs_9_), channel_id=1, source_target_pairs={{0,8},{1,9},{2,10},{3,11},{4,12},{5,13},{6,14},{7,15},{8,0},{9,1},... | collective-permute-start | bytes 1572872 | tf_op jit(solution)/shard_map/ppermute | solution.py:39
  (4 other events, 7.2 us)
Sparse Core Ops, SparseCore 0:
  53.2 44.9 all-reduce.4
  102.6 72.7 all-reduce.6

commit v2 on v0

v2 whole, which is shorter than its diff:
```python
import functools
import math

import jax
import jax.numpy as jnp
import ml_dtypes
import numpy as np
from jax import lax
from jax.experimental import pallas as pl
from jax.experimental.pallas import tpu as pltpu
from jax.sharding import PartitionSpec as P

AXES = ("scan", "obj")
CORES = 2
MIB = 1 << 20


def dft_tables(length):
    index = np.arange(length)
    angles = (index[:, None] * index[None, :] % length) * (2.0 * math.pi / length)
    parts = np.stack([np.cos(angles), -np.sin(angles)]) / math.sqrt(length)
    return parts.astype(np.float32).astype(ml_dtypes.bfloat16).astype(np.float32)


def fresnel_tables(length):
    index = np.arange(length)
    freqs = np.where(index < length // 2, index, index - length)
    squares = freqs * freqs
    phases = ((squares[:, None] + squares[None, :]) % (4 * length)) * (2.0 * math.pi / (4 * length))
    return np.stack([np.cos(phases), -np.sin(phases)]).astype(np.float32)


def send(block, scan_of, obj_step):
    n_scan, n_obj = lax.axis_size("scan"), lax.axis_size("obj")
    route = []
    for s in range(n_scan):
        for o in range(n_obj):
            route.append((s * n_obj + o, scan_of(s) % n_scan * n_obj + (o + obj_step) % n_obj))
    return lax.ppermute(block, AXES, route)


def assigned(info, tile, target, n_scan, n_obj):
    def entry(a, j):
        return info[a * n_obj + tile, 0, j]

    idle = entry(target, 0) == 0
    counts = [entry(a, 0) for a in range(n_scan)]
    rank = jnp.int32(0)
    for a in range(n_scan):
        rank += jnp.where((counts[a] == 0) & (a < target), 1, 0)
    source = jnp.int32(target)
    seen = jnp.int32(0)
    for a in range(n_scan):
        full = counts[a] == 2
        source = jnp.where(idle & full & (seen == rank), a, source)
        seen += jnp.where(full, 1, 0)
    slot = jnp.where(idle, 1, 0)
    return source, slot, entry(source, 1 + 2 * slot), entry(source, 2 + 2 * slot)


def column_block(col, length, tile_cols):
    base = jnp.minimum(lax.div(col, length), tile_cols // length - 2)
    return base, col - base * length


STEP = 32


def lanes(length):
    return lax.broadcasted_iota(jnp.int32, (STEP, length), 1)


def lines(length):
    return lax.broadcasted_iota(jnp.int32, (STEP, length), 0)


def mul(ar, ai, br, bi):
    return ar * br - ai * bi, ar * bi + ai * br


def cmul(ar, ai, br, bi):
    return ar * br + ai * bi, ar * bi - ai * br


def fetch_columns(object_ref, wide, sem, base, length):
    start = pl.multiple_of(base * length, length)
    copy = pltpu.make_async_copy(object_ref.at[:, :, :, pl.ds(start, 2 * length)], wide, sem)
    copy.start()
    return copy


def pick_columns(wide, l, q, at, off, length):
    return jnp.where(lanes(length) >= off, wide[l, q, at, :length], wide[l, q, at, length:])


def cut_kernel(sizes, info, object_ref, piece0, piece1, wide, sem):
    n_scan, n_obj, tile_cols = sizes
    _, rows, length = piece0.shape
    tile = lax.rem(lax.axis_index("obj") + n_obj - 1, n_obj)
    _, _, _, col = assigned(info, tile, lax.axis_index("scan"), n_scan, n_obj)
    base, off = column_block(col, length, tile_cols)
    fetch_columns(object_ref, wide, sem, base, length).wait()
    for l, piece in enumerate((piece0, piece1)):
        for q in range(2):
            for i in range(0, rows, STEP):
                at = pl.ds(i, STEP)
                piece[q, at, :] = pick_columns(wide, l, q, at, off, length).astype(piece.dtype)


def prep_kernel(sizes, info, object_ref, probe_ref, dft_ref, mats, p_ref, xo_ref, wide, sem):
    n_scan, n_obj, tile_cols = sizes
    modes, _, length, _ = probe_ref.shape
    _, _, row, col = assigned(info, lax.axis_index("obj"), lax.axis_index("scan"), n_scan, n_obj)
    base, off = column_block(col, length, tile_cols)
    copy = fetch_columns(object_ref, wide, sem, base, length)
    turn = lax.rem(off, length)

    def put(k, real, imag):
        mats[k, :length, :length] = real.astype(jnp.bfloat16)
        mats[k, length:, length:] = real.astype(jnp.bfloat16)
        mats[k, :length, length:] = imag.astype(jnp.bfloat16)
        mats[k, length:, :length] = (-imag).astype(jnp.bfloat16)

    real, imag = dft_ref[0], dft_ref[1]
    put(0, pltpu.roll(real, row, 1), -pltpu.roll(imag, row, 1))
    put(1, pltpu.roll(real, turn, 0), pltpu.roll(imag, turn, 0))
    put(2, pltpu.roll(real, row, 0), pltpu.roll(imag, row, 0))
    put(3, pltpu.roll(real, turn, 1), -pltpu.roll(imag, turn, 1))
    for m in range(modes):
        for q in range(2):
            p_ref[m, q] = pltpu.roll(pltpu.roll(probe_ref[m, q], row, 0), turn, 1)
    copy.wait()
    for l in range(xo_ref.shape[0]):
        for q in range(2):
            for i in range(0, length, STEP):
                at = pl.ds(i, STEP)
                xo_ref[l, q, at, :] = pick_columns(wide, l, q, at, off, length)


def put_v(v_ref, length, m, i, real, imag):
    spot = slice(m * length, (m + 1) * length)
    v_ref[pl.ds(i, STEP), spot] = real.astype(jnp.bfloat16)
    v_ref[pl.ds(length + i, STEP), spot] = imag.astype(jnp.bfloat16)


def get_s(s_ref, length, m, i):
    at = pl.ds(m * length + i, STEP)
    return s_ref[at, :length], s_ref[at, length:]


def transform(mats, inverse, v_ref, u_ref, s_ref):
    length = mats.shape[1] // 2
    mid = jnp.dot(mats[2 * inverse], v_ref[...], preferred_element_type=jnp.float32).astype(jnp.bfloat16)
    for m in range(v_ref.shape[1] // length):
        for q in range(2):
            u_ref[m * length : (m + 1) * length, q * length : (q + 1) * length] = mid[
                q * length : (q + 1) * length, m * length : (m + 1) * length
            ]
    s_ref[...] = jnp.dot(u_ref[...], mats[2 * inverse + 1], preferred_element_type=jnp.float32)


def propagate(product, mats, fresnel_ref, v_in, v_ref, u_ref, s_ref):
    length = mats.shape[1] // 2
    transform(mats, 0, v_in, u_ref, s_ref)
    for i in range(0, length, STEP):
        at = pl.ds(i, STEP)
        kr, ki = fresnel_ref[0, at, :], fresnel_ref[1, at, :]
        for m in range(v_ref.shape[1] // length):
            put_v(v_ref, length, m, i, *product(kr, ki, *get_s(s_ref, length, m, i)))
    transform(mats, 1, v_ref, u_ref, s_ref)


def join(own, piece_ref, q, i, row, length):
    piece = piece_ref[q, pl.ds(i, STEP), :].astype(jnp.float32)
    return jnp.where(lines(length) >= row - i, own, piece)


def first_kernel(sizes, info, mats, fresnel_ref, p_ref, xo_ref, piece, a_ref, x_ref, v_ref, u_ref, s_ref):
    n_scan, n_obj, tile_cols = sizes
    modes, _, length, _ = p_ref.shape
    _, _, row, _ = assigned(info, lax.axis_index("obj"), lax.axis_index("scan"), n_scan, n_obj)
    for i in range(0, length, STEP):
        at = pl.ds(i, STEP)
        xr = join(xo_ref[0, 0, at, :], piece, 0, i, row, length)
        xi = join(xo_ref[0, 1, at, :], piece, 1, i, row, length)
        x_ref[0, at, :] = xr
        x_ref[1, at, :] = xi
        for m in range(modes):
            put_v(v_ref, length, m, i, *mul(p_ref[m, 0, at, :], p_ref[m, 1, at, :], xr, xi))
    propagate(mul, mats, fresnel_ref, v_ref, v_ref, u_ref, s_ref)
    for i in range(0, length, STEP):
        at = pl.ds(i, STEP)
        for m in range(modes):
            a_ref[m, 0, at, :], a_ref[m, 1, at, :] = get_s(s_ref, length, m, i)


def second_kernel(sizes, *refs):
    n_scan, n_obj, tile_cols = sizes
    info, mats, a_ref, xo_ref, piece, own_ref = refs[:6]
    others = refs[6 : 5 + n_scan]
    grad_ref, v_out, v_ref, u_ref, s_ref, x_ref, meas_ref = refs[5 + n_scan :]
    modes, _, length, _ = a_ref.shape
    me = lax.axis_index("scan")
    source, slot, row, _ = assigned(info, lax.axis_index("obj"), me, n_scan, n_obj)

    @pl.when(slot == 0)
    def _():
        meas_ref[...] = own_ref[0]

    for k in range(1, n_scan):
        @pl.when((slot == 1) & (source == lax.rem(me - k + n_scan, n_scan)))
        def _():
            meas_ref[...] = others[k - 1][...]

    for i in range(0, length, STEP):
        at = pl.ds(i, STEP)
        xr = join(xo_ref[1, 0, at, :], piece, 0, i, row, length)
        xi = join(xo_ref[1, 1, at, :], piece, 1, i, row, length)
        x_ref[0, at, :] = xr
        x_ref[1, at, :] = xi
        for m in range(modes):
            put_v(v_ref, length, m, i, *mul(a_ref[m, 0, at, :], a_ref[m, 1, at, :], xr, xi))
    transform(mats, 0, v_ref, u_ref, s_ref)
    for i in range(0, length, STEP):
        misfit = -meas_ref[pl.ds(i, STEP), :].astype(jnp.float32)
        for m in range(modes):
            fr, fi = get_s(s_ref, length, m, i)
            misfit += fr * fr + fi * fi
        for m in range(modes):
            fr, fi = get_s(s_ref, length, m, i)
            put_v(v_ref, length, m, i, misfit * fr, misfit * fi)
    transform(mats, 1, v_ref, u_ref, s_ref)
    for i in range(0, length, STEP):
        at = pl.ds(i, STEP)
        gr = gi = 0.0
        for m in range(modes):
            cr, ci = get_s(s_ref, length, m, i)
            dr, di = cmul(a_ref[m, 0, at, :], a_ref[m, 1, at, :], cr, ci)
            gr, gi = gr + dr, gi + di
            put_v(v_out, length, m, i, *cmul(x_ref[0, at, :], x_ref[1, at, :], cr, ci))
        grad_ref[0, at, :] = gr.astype(grad_ref.dtype)
        grad_ref[1, at, :] = gi.astype(grad_ref.dtype)


def third_kernel(sizes, info, mats, fresnel_ref, v_in, x_ref, p_ref, grad_ref, e_ref, v_ref, u_ref, s_ref, b_ref):
    n_scan, n_obj, tile_cols = sizes
    modes, _, length, _ = p_ref.shape
    _, _, row, col = assigned(info, lax.axis_index("obj"), lax.axis_index("scan"), n_scan, n_obj)
    _, off = column_block(col, length, tile_cols)
    propagate(cmul, mats, fresnel_ref, v_in, v_ref, u_ref, s_ref)
    for i in range(0, length, STEP):
        at = pl.ds(i, STEP)
        gr = gi = 0.0
        for m in range(modes):
            cr, ci = get_s(s_ref, length, m, i)
            dr, di = cmul(p_ref[m, 0, at, :], p_ref[m, 1, at, :], cr, ci)
            gr, gi = gr + dr, gi + di
            b_ref[m, 0, at, :], b_ref[m, 1, at, :] = cmul(x_ref[0, at, :], x_ref[1, at, :], cr, ci)
        grad_ref[0, at, :] = gr.astype(grad_ref.dtype)
        grad_ref[1, at, :] = gi.astype(grad_ref.dtype)
    row_back = lax.rem(length - row, length)
    col_back = lax.rem(2 * length - off, length)
    per_row, per_col = length // n_obj, length // n_scan
    lane = lax.broadcasted_iota(jnp.int32, (length, 128), 1)
    for m in range(modes):
        for q in range(2):
            b_ref[m, q] = pltpu.roll(pltpu.roll(b_ref[m, q], row_back, 0), col_back, 1)
        for s in range(n_scan):
            first, shift = s * per_col // 128 * 128, s * per_col % 128
            real = b_ref[m, 0, :, first : first + 128]
            imag = b_ref[m, 1, :, first : first + 128]
            real = pltpu.roll(real, (128 - shift) % 128, 1) if shift else real
            imag = pltpu.roll(imag, (per_col - shift) % 128, 1) if shift != per_col else imag
            both = jnp.where(lane < per_col, real, imag)[:, : 2 * per_col]
            for o in range(n_obj):
                e_ref[s * n_obj + o, m] = both[o * per_row : (o + 1) * per_row].astype(e_ref.dtype)


def place_kernel(sizes, steps, factor, *refs):
    n_scan, n_obj, tile_cols = sizes
    info, chunks = refs[:2]
    out_ref, probe_out = refs[-2:]
    patches = refs[2:-2]
    layers, _, rows, width = out_ref.shape
    length = patches[0].shape[2]
    me = lax.axis_index("scan")
    here = lax.axis_index("obj")
    out_ref[...] = jnp.zeros(out_ref.shape, jnp.float32)
    lane, line = lanes(length), lines(length)
    for index in range(2 * n_scan):
        previous, member = divmod(index, n_scan)
        flip, jump = steps[member]
        source = lax.rem((me ^ flip) - jump + n_scan, n_scan)
        tile = lax.rem(here + n_obj - previous, n_obj)
        _, _, row, col = assigned(info, tile, source, n_scan, n_obj)
        base, off = column_block(col, length, tile_cols)
        top, bottom = (0, row) if previous else (row, rows)
        for block in range(width // length):
            column = me * (width // length) + block
            first, second = base == column, base + 1 == column
            left = jnp.where(first, off, 0)
            right = jnp.where(first, length, off)

            @pl.when(first | second)
            def _():
                cols = (lane >= left) & (lane < right)
                spot = slice(block * length, (block + 1) * length)
                for i in range(0, rows, STEP):
                    mask = cols & (line >= top - i) & (line < bottom - i)
                    at = pl.ds(i, STEP)
                    for l in range(layers):
                        for q in range(2):
                            value = patches[index * layers + l][q, at, :].astype(jnp.float32)
                            out_ref[l, q, at, spot] += jnp.where(mask, value, 0.0)

    per_col = probe_out.shape[3]
    for m in range(probe_out.shape[0]):
        total = chunks[0, m].astype(jnp.float32)
        for d in range(1, n_scan * n_obj):
            total += chunks[d, m].astype(jnp.float32)
        total *= factor
        probe_out[m, 0] = total[:, :per_col]
        probe_out[m, 1] = total[:, per_col:]


def body(object_slices, probe, measured, positions, counts):
    layers, _, tile_rows, tile_cols = object_slices.shape
    modes, _, length, _ = probe.shape
    slots = measured.shape[2]
    n_scan, n_obj = lax.axis_size("scan"), lax.axis_size("obj")
    devices = n_scan * n_obj
    sizes = (n_scan, n_obj, tile_cols)
    smem = pl.BlockSpec(memory_space=pltpu.SMEM)
    vmem = pl.BlockSpec(memory_space=pltpu.VMEM)
    hbm = pl.BlockSpec(memory_space=pltpu.HBM)
    params = pltpu.CompilerParams(vmem_limit_bytes=20 * MIB)
    real, half = jnp.float32, jnp.bfloat16

    def call(kernel, outs, ins, scratch, name, flops, *args):
        return pl.pallas_call(
            kernel,
            out_shape=[jax.ShapeDtypeStruct(*o) for o in outs],
            in_specs=ins,
            out_specs=[vmem] * len(outs),
            scratch_shapes=scratch,
            compiler_params=params,
            cost_estimate=pl.CostEstimate(flops=flops, bytes_accessed=4 * MIB, transcendentals=0),
            name=name,
        )(*args)

    def kernel_of(function):
        return functools.partial(function, sizes)

    info = jnp.concatenate([counts[0], positions[0, 0].reshape(-1)])
    info = jnp.broadcast_to(jnp.pad(info, (0, 123)), (devices, 1, 128))
    info = lax.all_to_all(info, AXES, 0, 0, tiled=True)
    second = measured[0, 0, 1]
    others = [send(second, lambda s, k=k: s + k, 0) for k in range(1, n_scan)]

    piece_shape = (2, length, length)
    field_shape = (modes, 2, length, length)
    wide = [pltpu.VMEM((layers, 2, tile_rows, 2 * length), real), pltpu.SemaphoreType.DMA]
    vus = [
        pltpu.VMEM((2 * length, modes * length), half),
        pltpu.VMEM((modes * length, 2 * length), half),
        pltpu.VMEM((modes * length, 2 * length), real),
    ]
    pair_flops = 2 * 2 * modes * 8 * length**3
    pieces = call(
        kernel_of(cut_kernel), [(piece_shape, half)] * 2, [smem, hbm], wide, "cut", MIB, info, object_slices
    )
    pieces = [send(piece, lambda s: s, -1) for piece in pieces]
    mats, turned, own_part = call(
        kernel_of(prep_kernel),
        [((4, 2 * length, 2 * length), half), (field_shape, real), ((layers, *piece_shape), real)],
        [smem, hbm, vmem, vmem],
        wide,
        "prep",
        MIB,
        info,
        object_slices,
        probe,
        dft_tables(length),
    )
    fresnel = fresnel_tables(length)
    arrived, patch = call(
        kernel_of(first_kernel),
        [(field_shape, real), (piece_shape, real)],
        [smem] + [vmem] * 5,
        vus,
        "first",
        pair_flops,
        info,
        mats,
        fresnel,
        turned,
        own_part,
        pieces[0],
    )
    grad1, carried = call(
        kernel_of(second_kernel),
        [(piece_shape, half), ((2 * length, modes * length), half)],
        [smem] + [vmem] * (4 + n_scan),
        vus + [pltpu.VMEM(piece_shape, real), pltpu.VMEM((length, length), measured.dtype)],
        "second",
        pair_flops,
        info,
        mats,
        arrived,
        own_part,
        pieces[1],
        measured[0, 0],
        *others,
    )
    chunk_shape = (devices, modes, length // n_obj, 2 * (length // n_scan))
    grad0, chunks = call(
        kernel_of(third_kernel),
        [(piece_shape, half), (chunk_shape, half)],
        [smem] + [vmem] * 5,
        vus + [pltpu.VMEM(field_shape, real)],
        "third",
        pair_flops,
        info,
        mats,
        fresnel,
        carried,
        patch,
        turned,
    )

    jumps = [CORES * k for k in range(n_scan // CORES)]
    held = []
    for l, grad in enumerate((grad0, grad1)):
        own = [grad] + [send(grad, lambda s, j=j: s + j, 0) for j in jumps[1:]]
        passed = [send(grad, lambda s: s, 1)]
        if l == 0:
            passed += [send(passed[0], lambda s, j=j: s + j, 0) for j in jumps[1:]]
        else:
            passed += [send(patch_grad, lambda s: s, 1) for patch_grad in own[1:]]
        own += [send(p, lambda s: s ^ 1, 0) for p in own]
        passed += [send(p, lambda s: s ^ 1, 0) for p in passed]
        held.append(own + passed)
    chunks = lax.all_to_all(chunks, AXES, 0, 0, tiled=True)
    steps = [(0, j) for j in jumps] + [(1, j) for j in jumps]
    factor = 1.0 / math.sqrt(n_scan * n_obj * slots // 2)
    object_grad, probe_grad = call(
        functools.partial(place_kernel, sizes, steps, factor),
        [
            ((layers, 2, tile_rows, tile_cols // n_scan), real),
            ((modes, 2, length // n_obj, length // n_scan), real),
        ],
        [smem, vmem] + [vmem] * (2 * n_scan * layers),
        [],
        "place",
        MIB,
        info,
        chunks,
        *[held[l][index] for index in range(2 * n_scan) for l in range(layers)],
    )
    return (object_grad, probe_grad)


def solution(mesh):
    return jax.shard_map(
        body,
        mesh=mesh,
        in_specs=(
            P(None, None, "obj", None),
            P(),
            P("scan", "obj", None, None, None),
            P("scan", "obj", None, None),
            P("scan", "obj"),
        ),
        out_specs=(P(None, None, "obj", "scan"), P(None, None, "obj", "scan")),
        check_vma=False,
    )
```

time: 555 us -> 89.6 us (0.16)
  waiting for transfers between devices: 337 us -> 30.9 us
  local copies, waits for them, and re-layouts: 94.5 us -> 12.5 us
  other arithmetic: 58.1 us -> 0.08 us
  matrix products: 31.6 us -> 0 us
  Pallas kernels: 0 us -> 15.5 us
  blocking collectives: 0 us -> 14.2 us
  between operations: 14.5 us -> 1.4 us
  loops' own time: 7.67 us -> 0 us
    reduce_scatter x2 -> x0, waiting for transfers between devices: 297 us -> none  [the longest x1 224 us: body(): lax.psum_scatter(probe_sum, 'obj', scatter_dimension=2, tiled=True)]
    dot_general x12 -> x0, matrix products: 31.6 us -> none  [transform(): jnp.einsum('qab,pqbc->pac', partial_out.astype(jnp.bfloat16), matrix, pre...]
    another operation x23 -> x0, other arithmetic: 25.4 us -> none
    gather x18 -> x0, local copies, waits for them, and re-layouts: 24.2 us -> none
    dynamic_update_slice x4 -> x0, local copies, waits for them, and re-layouts: 19.2 us -> none  [the longest x2 19 us: add_window(): return (lax.dynamic_update_slice(band, current + patch_grad, corner), None)]
    while x41 -> x0, local copies, waits for them, and re-layouts: 18.3 us -> none
    add x9 -> x0, other arithmetic: 16.6 us -> none  [the longest x1 11.8 us: body(): tile_grad = band[:, :, :tile_rows].at[:, :, :length].add(rim_back)]
    pallas_call x0 -> x6, Pallas kernels: none -> 15.5 us  [call(): pl.pallas_call(kernel, out_shape=[jax.ShapeDtypeStruct(*o) for o in outs]...]
  transfers between devices with their start and end apart: 6 -> 20, of which waited for: 5 -> 6; matrix products, arithmetic and copies ran while one was open for 6% -> 0% of each run, Pallas kernels for 0% -> 5%
where the time goes in v2:
time: 89.6 us; the launch traced here: 89.3 us
  waiting for transfers between devices  30.9 us (34%)
  Pallas kernels  15.5 us (17%)
  starting transfers between devices  14.6 us (16%)
  blocking collectives  14.2 us (16%)
  local copies, waits for them, and re-layouts  12.5 us (14%)
  between operations  1.4 us (2%)
    ppermute x19, waiting for transfers between devices, send(): return lax.ppermute(block, AXES, route)  30.9 us
    pallas_call x6, Pallas kernels, call(): pl.pallas_call(kernel, out_shape=[jax.ShapeDtypeStruct(*o) for o in outs]...  15.5 us
    all_to_all x1, blocking collectives, body(): info = lax.all_to_all(info, AXES, 0, 0, tiled=True)  14.2 us
    unnamed x30, local copies, waits for them, and re-layouts  11.7 us
    ppermute x19, starting transfers between devices, send(): return lax.ppermute(block, AXES, route)  10.9 us
    all_to_all x1, starting transfers between devices, body(): chunks = lax.all_to_all(chunks, AXES, 0, 0, tiled=True)  3.74 us
  transfers between devices with their start and end apart: 20, of which 6 were waited for; matrix products, arithmetic and copies ran while one was open for 0% of the time, Pallas kernels for 5%

profile of v2, /device:TPU:0, one launch (start us, length us, event | category | flops | bytes accessed | tf_op | source)
XLA Modules:
  0.0 89.3 jit_solution(1165797772899892129)
XLA Ops:
  2.1 14.2 %all_to_all.10.info.refs_0_ = s32[32,1,128]{2,1,0:T(1,128)S(1)} all-to-all(s32[32,1,128]{2,1,0:T(1,128)S(1)} %broadcast_in_dim.3), channel_id=1, replica_groups=mesh['scan'=4,'obj'=8] {'scan','obj'}, dimensions={0} | all-to-all | bytes 32768 | tf_op jit(solution)/shard_map/all_to_all | solution.py:356
  16.4 3.4 %copy-done = f32[2,2,256,2048]{3,2,1,0:T(8,128)S(1)} copy-done((f32[2,2,256,2048]{3,2,1,0:T(8,128)S(1)}, f32[2,2,256,2048]{3,2,1,0:T(8,128)}, u32[]{:S(2)}) %copy-start) | copy-done | bytes 8388632
  19.7 1.3 %cut.1 = (bf16[2,256,256]{2,1,0:T(8,128)(2,1)S(1)}, bf16[2,256,256]{2,1,0:T(8,128)(2,1)S(1)}) custom-call(s32[32,1,128]{2,1,0:T(1,128)S(1)} %all_to_all.10.info.refs_0_, f32[2,2,256,2048]{3,2,1,0:T(8,128)S(1)} %copy-done), custom_call_target="tpu_custom_call" | custom-call | flops 1048576 | bytes 4194304 | tf_op jit(solution)/shard_map/cut/pallas_call | solution.py:340
  21.8 1.4 %collective-permute-start.1 = (bf16[2,256,256]{2,1,0:T(8,128)(2,1)S(1)}, bf16[2,256,256]{2,1,0:T(8,128)(2,1)S(1)}, u32[]{:S(2)}, u32[]{:S(2)}) collective-permute-start(bf16[2,256,256]{2,1,0:T(8,128)(2,1)S(1)} %get-tuple-element.18), channel_id=1, source_target_pairs={{0,7},{1,0},{2,1},{3,2},{4,3},{5,4},{6,5},{7,6},{8,15},{9,8},{10,9... | collective-permute-start | bytes 786440 | tf_op jit(solution)/shard_map/ppermute | solution.py:39
  24.2 2.3 %prep.1 = (bf16[4,512,512]{2,1,0:T(8,128)(2,1)S(1)}, f32[2,2,256,256]{3,2,1,0:T(8,128)S(1)}, f32[2,2,256,256]{3,2,1,0:T(8,128)S(1)}) custom-call(s32[32,1,128]{2,1,0:T(1,128)S(1)} %all_to_all.10.info.refs_0_, f32[2,2,256,2048]{3,2,1,0:T(8,128)S(1)} %copy-done, f32[2,2,256,256]{3,2,1,0:T(8,128)S(1)} %copy-done.2, f32[2,256,256]{2,1,0:T(8,128)S(1)} %copy-done.4), custom_call_target="tpu_custom_call" | custom-call | flops 1048576 | bytes 4194304 | tf_op jit(solution)/shard_map/prep/pallas_call | solution.py:340
  26.4 3.9 %collective-permute-done.piece = bf16[2,256,256]{2,1,0:T(8,128)(2,1)S(1)} collective-permute-done((bf16[2,256,256]{2,1,0:T(8,128)(2,1)S(1)}, bf16[2,256,256]{2,1,0:T(8,128)(2,1)S(1)}, u32[]{:S(2)}, u32[]{:S(2)}) %collective-permute-start) | collective-permute-done | bytes 262176 | tf_op jit(solution)/shard_map/ppermute | solution.py:39
  30.4 2.3 %first.1 = (f32[2,2,256,256]{3,2,1,0:T(8,128)S(1)}, f32[2,256,256]{2,1,0:T(8,128)S(1)}) custom-call(s32[32,1,128]{2,1,0:T(1,128)S(1)} %all_to_all.10.info.refs_0_, bf16[4,512,512]{2,1,0:T(8,128)(2,1)S(1)} %get-tuple-element.13.mats.refs_1_, f32[2,256,256]{2,1,0:T(8,128)S(1)} %copy-done.1, f32[2,2,256,256]{3,2,1,0:T(8,128)S(1)} %get-tuple-element.14.p_ref, ...), custom_call_target="tpu_custom_call" | custom-call | flops 1073741824 | bytes 4194304 | tf_op jit(solution)/shard_map/first/pallas_call | solution.py:340
  32.7 2.0 %collective-permute-done.1.refs_4_ = bf16[2,256,256]{2,1,0:T(8,128)(2,1)S(1)} collective-permute-done((bf16[2,256,256]{2,1,0:T(8,128)(2,1)S(1)}, bf16[2,256,256]{2,1,0:T(8,128)(2,1)S(1)}, u32[]{:S(2)}, u32[]{:S(2)}) %collective-permute-start.1) | collective-permute-done | bytes 262176 | tf_op jit(solution)/shard_map/ppermute | solution.py:39
  34.7 2.5 %second.1 = (bf16[2,256,256]{2,1,0:T(8,128)(2,1)S(1)}, bf16[512,512]{1,0:T(8,128)(2,1)S(1)}) custom-call(s32[32,1,128]{2,1,0:T(1,128)S(1)} %all_to_all.10.info.refs_0_, bf16[4,512,512]{2,1,0:T(8,128)(2,1)S(1)} %get-tuple-element.13.mats.refs_1_, f32[2,2,256,256]{3,2,1,0:T(8,128)S(1)} %get-tuple-element.17.refs_2_, ...), custom_call_target="tpu_custom_call" | custom-call | flops 1073741824 | bytes 4194304 | tf_op jit(solution)/shard_map/second/pallas_call | solution.py:340
  37.2 3.7 %third.1 = (bf16[2,256,256]{2,1,0:T(8,128)(2,1)S(1)}, bf16[32,2,32,128]{3,2,1,0:T(8,128)(2,1)}) custom-call(s32[32,1,128]{2,1,0:T(1,128)S(1)} %all_to_all.10.info.refs_0_, bf16[4,512,512]{2,1,0:T(8,128)(2,1)S(1)} %get-tuple-element.13.mats.refs_1_, f32[2,256,256]{2,1,0:T(8,128)S(1)} %copy-done.1, bf16[512,512]{1,0:T(8,128)(2,1)S(1)} %get-tuple-element.19.v_in, ...), custom_call_target="tpu_custom_call" | custom-call | flops 1073741824 | bytes 4194304 | tf_op jit(solution)/shard_map/third/pallas_call | solution.py:340
  40.9 3.7 %all-to-all-start.1 = ((bf16[32,2,32,128]{3,2,1,0:T(8,128)(2,1)}), bf16[32,2,32,128]{3,2,1,0:T(8,128)(2,1)S(1)}, u32[]{:S(2)}, u32[]{:S(2)}) async-start(bf16[32,2,32,128]{3,2,1,0:T(8,128)(2,1)} %get-tuple-element.21), calls=%async_computation.1 | async-start | bytes 1048576 | tf_op jit(solution)/shard_map/all_to_all | solution.py:443
  44.7 1.8 %collective-permute-start.11 = (bf16[2,256,256]{2,1,0:T(8,128)(2,1)S(1)}, bf16[2,256,256]{2,1,0:T(8,128)(2,1)S(1)}, u32[]{:S(2)}, u32[]{:S(2)}) collective-permute-start(bf16[2,256,256]{2,1,0:T(8,128)(2,1)S(1)} %get-tuple-element.22.refs_2_), channel_id=1, source_target_pairs={{0,1},{1,2},{2,3},{3,4},{4,5},{5,6},{6,7},{7,0},{8,9},{9,10},{10,1... | collective-permute-start | bytes 786440 | tf_op jit(solution)/shard_map/ppermute | solution.py:39
  46.5 1.5 %collective-permute-start.5 = (bf16[2,256,256]{2,1,0:T(8,128)(2,1)S(1)}, bf16[2,256,256]{2,1,0:T(8,128)(2,1)S(1)}, u32[]{:S(2)}, u32[]{:S(2)}) collective-permute-start(bf16[2,256,256]{2,1,0:T(8,128)(2,1)S(1)} %get-tuple-element.22.refs_2_), channel_id=1, source_target_pairs={{0,16},{1,17},{2,18},{3,19},{4,20},{5,21},{6,22},{7,23},{8,24},{9,... | collective-permute-start | bytes 786440 | tf_op jit(solution)/shard_map/ppermute | solution.py:39
  48.5 1.5 %collective-permute-start.12 = (bf16[2,256,256]{2,1,0:T(8,128)(2,1)S(1)}, bf16[2,256,256]{2,1,0:T(8,128)(2,1)S(1)}, u32[]{:S(2)}, u32[]{:S(2)}) collective-permute-start(bf16[2,256,256]{2,1,0:T(8,128)(2,1)S(1)} %get-tuple-element.23.refs_3_), channel_id=1, source_target_pairs={{0,1},{1,2},{2,3},{3,4},{4,5},{5,6},{6,7},{7,0},{8,9},{9,10},{10,1... | collective-permute-start | bytes 786440 | tf_op jit(solution)/shard_map/ppermute | solution.py:39
  50.0 14.8 %collective-permute-done.11.refs_10_ = bf16[2,256,256]{2,1,0:T(8,128)(2,1)S(1)} collective-permute-done((bf16[2,256,256]{2,1,0:T(8,128)(2,1)S(1)}, bf16[2,256,256]{2,1,0:T(8,128)(2,1)S(1)}, u32[]{:S(2)}, u32[]{:S(2)}) %collective-permute-start.11) | collective-permute-done | bytes 262176 | tf_op jit(solution)/shard_map/ppermute | solution.py:39
  65.3 1.5 %collective-permute-start.13 = (bf16[2,256,256]{2,1,0:T(8,128)(2,1)S(1)}, bf16[2,256,256]{2,1,0:T(8,128)(2,1)S(1)}, u32[]{:S(2)}, u32[]{:S(2)}) collective-permute-start(bf16[2,256,256]{2,1,0:T(8,128)(2,1)S(1)} %collective-permute-done.11.refs_10_), channel_id=1, source_target_pairs={{0,16},{1,17},{2,18},{3,19},{4,20},{5,21},{6,22},{7,23},{8,24},{9,... | collective-permute-start | bytes 786440 | tf_op jit(solution)/shard_map/ppermute | solution.py:39
  66.8 3.1 %collective-permute-done.12.refs_11_ = bf16[2,256,256]{2,1,0:T(8,128)(2,1)S(1)} collective-permute-done((bf16[2,256,256]{2,1,0:T(8,128)(2,1)S(1)}, bf16[2,256,256]{2,1,0:T(8,128)(2,1)S(1)}, u32[]{:S(2)}, u32[]{:S(2)}) %collective-permute-start.12) | collective-permute-done | bytes 262176 | tf_op jit(solution)/shard_map/ppermute | solution.py:39
  70.6 3.1 %collective-permute-done.13.refs_12_ = bf16[2,256,256]{2,1,0:T(8,128)(2,1)S(1)} collective-permute-done((bf16[2,256,256]{2,1,0:T(8,128)(2,1)S(1)}, bf16[2,256,256]{2,1,0:T(8,128)(2,1)S(1)}, u32[]{:S(2)}, u32[]{:S(2)}) %collective-permute-start.13) | collective-permute-done | bytes 262176 | tf_op jit(solution)/shard_map/ppermute | solution.py:39
  73.6 3.9 %collective-permute-done.14.refs_13_ = bf16[2,256,256]{2,1,0:T(8,128)(2,1)S(1)} collective-permute-done((bf16[2,256,256]{2,1,0:T(8,128)(2,1)S(1)}, bf16[2,256,256]{2,1,0:T(8,128)(2,1)S(1)}, u32[]{:S(2)}, u32[]{:S(2)}) %collective-permute-start.14) | collective-permute-done | bytes 262176 | tf_op jit(solution)/shard_map/ppermute | solution.py:39
  81.1 0.9 %copy-done.6 = bf16[2,256,256]{2,1,0:T(8,128)(2,1)S(1)} copy-done((bf16[2,256,256]{2,1,0:T(8,128)(2,1)S(1)}, bf16[2,256,256]{2,1,0:T(8,128)(2,1)}, u32[]{:S(2)}) %copy-start.6) | copy-done | bytes 262168
  82.1 0.9 %copy-done.8 = bf16[2,256,256]{2,1,0:T(8,128)(2,1)S(1)} copy-done((bf16[2,256,256]{2,1,0:T(8,128)(2,1)S(1)}, bf16[2,256,256]{2,1,0:T(8,128)(2,1)}, u32[]{:S(2)}) %copy-start.8) | copy-done | bytes 262168
  83.0 0.9 %copy-done.10 = bf16[2,256,256]{2,1,0:T(8,128)(2,1)S(1)} copy-done((bf16[2,256,256]{2,1,0:T(8,128)(2,1)S(1)}, bf16[2,256,256]{2,1,0:T(8,128)(2,1)}, u32[]{:S(2)}) %copy-start.10) | copy-done | bytes 262168
  84.0 0.9 %copy-done.12 = bf16[2,256,256]{2,1,0:T(8,128)(2,1)S(1)} copy-done((bf16[2,256,256]{2,1,0:T(8,128)(2,1)S(1)}, bf16[2,256,256]{2,1,0:T(8,128)(2,1)}, u32[]{:S(2)}) %copy-start.12) | copy-done | bytes 262168
  85.9 3.4 %place.1 = (f32[2,2,256,512]{3,2,1,0:T(8,128)}, f32[2,2,32,64]{3,2,1,0:T(8,128)}) custom-call(s32[32,1,128]{2,1,0:T(1,128)S(1)} %all_to_all.10.info.refs_0_, bf16[32,2,32,128]{3,2,1,0:T(8,128)(2,1)S(1)} %all-to-all-done.1.refs_1_, bf16[2,256,256]{2,1,0:T(8,128)(2,1)S(1)} %get-tuple-element.22.refs_2_, bf16[2,256,256]{2,1,0:T(8,128)(2,1)S(1)} %get-tuple-element.23.refs_3_, ...), custom_call_target="tpu_custom_call" | custom-call | flops 1048576 | bytes 4194304 | tf_op jit(solution)/shard_map/place/pallas_call | solution.py:340
  (58 shorter events, 8.7 us)
Async XLA Ops:
  19.7 3.4 %copy-start.3 = (bf16[1,1,2,256,256]{4,3,2,1,0:T(8,128)(2,1)S(1)}, bf16[1,1,2,256,256]{4,3,2,1,0:T(8,128)(2,1)}, u32[]{:S(2)}) copy-start(bf16[1,1,2,256,256]{4,3,2,1,0:T(8,128)(2,1)} %param.9) | copy-start | bytes 786436
  19.7 4.4 %copy-start.2 = (f32[2,2,256,256]{3,2,1,0:T(8,128)S(1)}, f32[2,2,256,256]{3,2,1,0:T(8,128)}, u32[]{:S(2)}) copy-start(f32[2,2,256,256]{3,2,1,0:T(8,128)} %probe_ref.1) | copy-start | bytes 3145732
  19.7 4.4 %copy-start.4 = (f32[2,256,256]{2,1,0:T(8,128)S(1)}, f32[2,256,256]{2,1,0:T(8,128)}, u32[]{:S(2)}) copy-start(f32[2,256,256]{2,1,0:T(8,128)} %constant.6.clone.dft_ref) | copy-start | bytes 1572868
  21.1 9.3 %collective-permute-start = (bf16[2,256,256]{2,1,0:T(8,128)(2,1)S(1)}, bf16[2,256,256]{2,1,0:T(8,128)(2,1)S(1)}, u32[]{:S(2)}, u32[]{:S(2)}) collective-permute-start(bf16[2,256,256]{2,1,0:T(8,128)(2,1)S(1)} %get-tuple-element.16), channel_id=1, source_target_pairs={{0,7},{1,0},{2,1},{3,2},{4,3},{5,4},{6,5},{7,6},{8,15},{9,8},{10,9... | collective-permute-start | bytes 786440 | tf_op jit(solution)/shard_map/ppermute | solution.py:39
  21.8 12.9 %collective-permute-start.1 = (bf16[2,256,256]{2,1,0:T(8,128)(2,1)S(1)}, bf16[2,256,256]{2,1,0:T(8,128)(2,1)S(1)}, u32[]{:S(2)}, u32[]{:S(2)}) collective-permute-start(bf16[2,256,256]{2,1,0:T(8,128)(2,1)S(1)} %get-tuple-element.18), channel_id=1, source_target_pairs={{0,7},{1,0},{2,1},{3,2},{4,3},{5,4},{6,5},{7,6},{8,15},{9,8},{10,9... | collective-permute-start | bytes 786440 | tf_op jit(solution)/shard_map/ppermute | solution.py:39
  23.2 7.2 %copy-start.1 = (f32[2,256,256]{2,1,0:T(8,128)S(1)}, f32[2,256,256]{2,1,0:T(8,128)}, u32[]{:S(2)}) copy-start(f32[2,256,256]{2,1,0:T(8,128)} %constant.7.clone.fresnel_ref) | copy-start | bytes 1572868
  23.2 9.5 %collective-permute-start.4 = (bf16[256,256]{1,0:T(8,128)(2,1)S(1)}, bf16[256,256]{1,0:T(8,128)(2,1)S(1)}, u32[]{:S(2)}, u32[]{:S(2)}) collective-permute-start(bf16[256,256]{1,0:T(8,128)(2,1)S(1)} %slice_bitcast_fusion), channel_id=1, source_target_pairs={{0,24},{1,25},{2,26},{3,27},{4,28},{5,29},{6,30},{7,31},{8,0},{9,1... | collective-permute-start | bytes 393224 | tf_op jit(solution)/shard_map/ppermute | solution.py:39
  23.2 9.4 %collective-permute-start.3 = (bf16[256,256]{1,0:T(8,128)(2,1)S(1)}, bf16[256,256]{1,0:T(8,128)(2,1)S(1)}, u32[]{:S(2)}, u32[]{:S(2)}) collective-permute-start(bf16[256,256]{1,0:T(8,128)(2,1)S(1)} %slice_bitcast_fusion), channel_id=1, source_target_pairs={{0,16},{1,17},{2,18},{3,19},{4,20},{5,21},{6,22},{7,23},{8,24},{9,... | collective-permute-start | bytes 393224 | tf_op jit(solution)/shard_map/ppermute | solution.py:39
  24.1 8.5 %collective-permute-start.2 = (bf16[256,256]{1,0:T(8,128)(2,1)S(1)}, bf16[256,256]{1,0:T(8,128)(2,1)S(1)}, u32[]{:S(2)}, u32[]{:S(2)}) collective-permute-start(bf16[256,256]{1,0:T(8,128)(2,1)S(1)} %slice_bitcast_fusion), channel_id=1, source_target_pairs={{0,8},{1,9},{2,10},{3,11},{4,12},{5,13},{6,14},{7,15},{8,16},{9,17... | collective-permute-start | bytes 393224 | tf_op jit(solution)/shard_map/ppermute | solution.py:39
  40.9 40.2 %all-to-all-start.1 = ((bf16[32,2,32,128]{3,2,1,0:T(8,128)(2,1)}), bf16[32,2,32,128]{3,2,1,0:T(8,128)(2,1)S(1)}, u32[]{:S(2)}, u32[]{:S(2)}) async-start(bf16[32,2,32,128]{3,2,1,0:T(8,128)(2,1)} %get-tuple-element.21), calls=%async_computation.1 | async-start | bytes 1048576 | tf_op jit(solution)/shard_map/all_to_all | solution.py:443
  44.7 20.2 %collective-permute-start.11 = (bf16[2,256,256]{2,1,0:T(8,128)(2,1)S(1)}, bf16[2,256,256]{2,1,0:T(8,128)(2,1)S(1)}, u32[]{:S(2)}, u32[]{:S(2)}) collective-permute-start(bf16[2,256,256]{2,1,0:T(8,128)(2,1)S(1)} %get-tuple-element.22.refs_2_), channel_id=1, source_target_pairs={{0,1},{1,2},{2,3},{3,4},{4,5},{5,6},{6,7},{7,0},{8,9},{9,10},{10,1... | collective-permute-start | bytes 786440 | tf_op jit(solution)/shard_map/ppermute | solution.py:39
  46.5 18.4 %collective-permute-start.7 = (bf16[2,256,256]{2,1,0:T(8,128)(2,1)S(1)}, bf16[2,256,256]{2,1,0:T(8,128)(2,1)S(1)}, u32[]{:S(2)}, u32[]{:S(2)}) collective-permute-start(bf16[2,256,256]{2,1,0:T(8,128)(2,1)S(1)} %get-tuple-element.22.refs_2_), channel_id=1, source_target_pairs={{0,8},{1,9},{2,10},{3,11},{4,12},{5,13},{6,14},{7,15},{8,0},{9,1},... | collective-permute-start | bytes 786440 | tf_op jit(solution)/shard_map/ppermute | solution.py:39
  46.5 18.9 %collective-permute-start.5 = (bf16[2,256,256]{2,1,0:T(8,128)(2,1)S(1)}, bf16[2,256,256]{2,1,0:T(8,128)(2,1)S(1)}, u32[]{:S(2)}, u32[]{:S(2)}) collective-permute-start(bf16[2,256,256]{2,1,0:T(8,128)(2,1)S(1)} %get-tuple-element.22.refs_2_), channel_id=1, source_target_pairs={{0,16},{1,17},{2,18},{3,19},{4,20},{5,21},{6,22},{7,23},{8,24},{9,... | collective-permute-start | bytes 786440 | tf_op jit(solution)/shard_map/ppermute | solution.py:39
  47.9 18.9 %collective-permute-start.6 = (bf16[2,256,256]{2,1,0:T(8,128)(2,1)S(1)}, bf16[2,256,256]{2,1,0:T(8,128)(2,1)S(1)}, u32[]{:S(2)}, u32[]{:S(2)}) collective-permute-start(bf16[2,256,256]{2,1,0:T(8,128)(2,1)S(1)} %get-tuple-element.23.refs_3_), channel_id=1, source_target_pairs={{0,16},{1,17},{2,18},{3,19},{4,20},{5,21},{6,22},{7,23},{8,24},{9,... | collective-permute-start | bytes 786440 | tf_op jit(solution)/shard_map/ppermute | solution.py:39
  48.5 21.5 %collective-permute-start.12 = (bf16[2,256,256]{2,1,0:T(8,128)(2,1)S(1)}, bf16[2,256,256]{2,1,0:T(8,128)(2,1)S(1)}, u32[]{:S(2)}, u32[]{:S(2)}) collective-permute-start(bf16[2,256,256]{2,1,0:T(8,128)(2,1)S(1)} %get-tuple-element.23.refs_3_), channel_id=1, source_target_pairs={{0,1},{1,2},{2,3},{3,4},{4,5},{5,6},{6,7},{7,0},{8,9},{9,10},{10,1... | collective-permute-start | bytes 786440 | tf_op jit(solution)/shard_map/ppermute | solution.py:39
  64.8 5.2 %collective-permute-start.8 = (bf16[2,256,256]{2,1,0:T(8,128)(2,1)S(1)}, bf16[2,256,256]{2,1,0:T(8,128)(2,1)S(1)}, u32[]{:S(2)}, u32[]{:S(2)}) collective-permute-start(bf16[2,256,256]{2,1,0:T(8,128)(2,1)S(1)} %get-tuple-element.23.refs_3_), channel_id=1, source_target_pairs={{0,8},{1,9},{2,10},{3,11},{4,12},{5,13},{6,14},{7,15},{8,0},{9,1},... | collective-permute-start | bytes 786440 | tf_op jit(solution)/shard_map/ppermute | solution.py:39
  64.8 5.7 %collective-permute-start.15 = (bf16[2,256,256]{2,1,0:T(8,128)(2,1)S(1)}, bf16[2,256,256]{2,1,0:T(8,128)(2,1)S(1)}, u32[]{:S(2)}, u32[]{:S(2)}) collective-permute-start(bf16[2,256,256]{2,1,0:T(8,128)(2,1)S(1)} %collective-permute-done.11.refs_10_), channel_id=1, source_target_pairs={{0,8},{1,9},{2,10},{3,11},{4,12},{5,13},{6,14},{7,15},{8,0},{9,1},... | collective-permute-start | bytes 786440 | tf_op jit(solution)/shard_map/ppermute | solution.py:39
  65.3 8.3 %collective-permute-start.13 = (bf16[2,256,256]{2,1,0:T(8,128)(2,1)S(1)}, bf16[2,256,256]{2,1,0:T(8,128)(2,1)S(1)}, u32[]{:S(2)}, u32[]{:S(2)}) collective-permute-start(bf16[2,256,256]{2,1,0:T(8,128)(2,1)S(1)} %collective-permute-done.11.refs_10_), channel_id=1, source_target_pairs={{0,16},{1,17},{2,18},{3,19},{4,20},{5,21},{6,22},{7,23},{8,24},{9,... | collective-permute-start | bytes 786440 | tf_op jit(solution)/shard_map/ppermute | solution.py:39
  66.8 10.7 %collective-permute-start.14 = (bf16[2,256,256]{2,1,0:T(8,128)(2,1)S(1)}, bf16[2,256,256]{2,1,0:T(8,128)(2,1)S(1)}, u32[]{:S(2)}, u32[]{:S(2)}) collective-permute-start(bf16[2,256,256]{2,1,0:T(8,128)(2,1)S(1)} %collective-permute-done.6.refs_5_), channel_id=1, source_target_pairs={{0,1},{1,2},{2,3},{3,4},{4,5},{5,6},{6,7},{7,0},{8,9},{9,10},{10,1... | collective-permute-start | bytes 786440 | tf_op jit(solution)/shard_map/ppermute | solution.py:39
  70.0 9.0 %collective-permute-start.10 = (bf16[2,256,256]{2,1,0:T(8,128)(2,1)S(1)}, bf16[2,256,256]{2,1,0:T(8,128)(2,1)S(1)}, u32[]{:S(2)}, u32[]{:S(2)}) collective-permute-start(bf16[2,256,256]{2,1,0:T(8,128)(2,1)S(1)} %collective-permute-done.6.refs_5_), channel_id=1, source_target_pairs={{0,8},{1,9},{2,10},{3,11},{4,12},{5,13},{6,14},{7,15},{8,0},{9,1},... | collective-permute-start | bytes 786440 | tf_op jit(solution)/shard_map/ppermute | solution.py:39
  70.0 7.6 %collective-permute-start.9 = (bf16[2,256,256]{2,1,0:T(8,128)(2,1)S(1)}, bf16[2,256,256]{2,1,0:T(8,128)(2,1)S(1)}, u32[]{:S(2)}, u32[]{:S(2)}) collective-permute-start(bf16[2,256,256]{2,1,0:T(8,128)(2,1)S(1)} %collective-permute-done.5.refs_4_), channel_id=1, source_target_pairs={{0,8},{1,9},{2,10},{3,11},{4,12},{5,13},{6,14},{7,15},{8,0},{9,1},... | collective-permute-start | bytes 786440 | tf_op jit(solution)/shard_map/ppermute | solution.py:39
  70.5 7.8 %collective-permute-start.16 = (bf16[2,256,256]{2,1,0:T(8,128)(2,1)S(1)}, bf16[2,256,256]{2,1,0:T(8,128)(2,1)S(1)}, u32[]{:S(2)}, u32[]{:S(2)}) collective-permute-start(bf16[2,256,256]{2,1,0:T(8,128)(2,1)S(1)} %collective-permute-done.12.refs_11_), channel_id=1, source_target_pairs={{0,8},{1,9},{2,10},{3,11},{4,12},{5,13},{6,14},{7,15},{8,0},{9,1},... | collective-permute-start | bytes 786440 | tf_op jit(solution)/shard_map/ppermute | solution.py:39
  73.6 6.1 %collective-permute-start.17 = (bf16[2,256,256]{2,1,0:T(8,128)(2,1)S(1)}, bf16[2,256,256]{2,1,0:T(8,128)(2,1)S(1)}, u32[]{:S(2)}, u32[]{:S(2)}) collective-permute-start(bf16[2,256,256]{2,1,0:T(8,128)(2,1)S(1)} %collective-permute-done.13.refs_12_), channel_id=1, source_target_pairs={{0,8},{1,9},{2,10},{3,11},{4,12},{5,13},{6,14},{7,15},{8,0},{9,1},... | collective-permute-start | bytes 786440 | tf_op jit(solution)/shard_map/ppermute | solution.py:39
  77.6 2.8 %collective-permute-start.18 = (bf16[2,256,256]{2,1,0:T(8,128)(2,1)S(1)}, bf16[2,256,256]{2,1,0:T(8,128)(2,1)S(1)}, u32[]{:S(2)}, u32[]{:S(2)}) collective-permute-start(bf16[2,256,256]{2,1,0:T(8,128)(2,1)S(1)} %collective-permute-done.14.refs_13_), channel_id=1, source_target_pairs={{0,8},{1,9},{2,10},{3,11},{4,12},{5,13},{6,14},{7,15},{8,0},{9,1},... | collective-permute-start | bytes 786440 | tf_op jit(solution)/shard_map/ppermute | solution.py:39
  (11 other events, 11.7 us)

commit v3 on v2

--- a/solution.py
+++ b/solution.py
@@ -13,6 +13,7 @@
 AXES = ("scan", "obj")
 CORES = 2
 MIB = 1 << 20
+SMALL, LARGE = 20, 58
 
 
 def dft_tables(length):
@@ -30,32 +31,40 @@
     return np.stack([np.cos(phases), -np.sin(phases)]).astype(np.float32)
 
 
-def send(block, scan_of, obj_step):
+def send(block, move):
     n_scan, n_obj = lax.axis_size("scan"), lax.axis_size("obj")
     route = []
     for s in range(n_scan):
         for o in range(n_obj):
-            route.append((s * n_obj + o, scan_of(s) % n_scan * n_obj + (o + obj_step) % n_obj))
+            goal = move(s, o)
+            if goal is not None:
+                route.append((s * n_obj + o, goal[0] % n_scan * n_obj + goal[1] % n_obj))
     return lax.ppermute(block, AXES, route)
 
 
-def assigned(info, tile, target, n_scan, n_obj):
+OWN, PREVIOUS = 0, 1
+
+
+def live(info, tile, rank, n_scan):
     def entry(a, j):
-        return info[a * n_obj + tile, 0, j]
-
-    idle = entry(target, 0) == 0
-    counts = [entry(a, 0) for a in range(n_scan)]
-    rank = jnp.int32(0)
+        return info[a, 0, 8 * tile + j]
+
+    source, slot = jnp.int32(0), jnp.int32(0)
+    before = jnp.int32(0)
     for a in range(n_scan):
-        rank += jnp.where((counts[a] == 0) & (a < target), 1, 0)
-    source = jnp.int32(target)
-    seen = jnp.int32(0)
-    for a in range(n_scan):
-        full = counts[a] == 2
-        source = jnp.where(idle & full & (seen == rank), a, source)
-        seen += jnp.where(full, 1, 0)
-    slot = jnp.where(idle, 1, 0)
+        count = entry(a, 0)
+        here = (rank >= before) & (rank < before + count)
+        source = jnp.where(here, a, source)
+        slot = jnp.where(here, rank - before, slot)
+        before += count
     return source, slot, entry(source, 1 + 2 * slot), entry(source, 2 + 2 * slot)
+
+
+def place_of(n_scan):
+    me = lax.axis_index("scan")
+    core = lax.rem(me, CORES)
+    chip = lax.div(me, CORES)
+    return chip, core, chip + core * (n_scan // CORES)
 
 
 def column_block(col, length, tile_cols):
@@ -94,10 +103,10 @@
 
 
 def cut_kernel(sizes, info, object_ref, piece0, piece1, wide, sem):
-    n_scan, n_obj, tile_cols = sizes
+    n_scan, _, tile_cols = sizes
     _, rows, length = piece0.shape
-    tile = lax.rem(lax.axis_index("obj") + n_obj - 1, n_obj)
-    _, _, _, col = assigned(info, tile, lax.axis_index("scan"), n_scan, n_obj)
+    _, core, rank = place_of(n_scan)
+    _, _, _, col = live(info, 1 - core, rank, n_scan)
     base, off = column_block(col, length, tile_cols)
     fetch_columns(object_ref, wide, sem, base, length).wait()
     for l, piece in enumerate((piece0, piece1)):
@@ -107,10 +116,26 @@
                 piece[q, at, :] = pick_columns(wide, l, q, at, off, length).astype(piece.dtype)
 
 
+def choose_kernel(sizes, steps, info, *refs):
+    n_scan, _, _ = sizes
+    sources = refs[:n_scan]
+    out_ref, sem = refs[n_scan:]
+    me = lax.axis_index("scan")
+    _, _, rank = place_of(n_scan)
+    source, slot, _, _ = live(info, OWN, rank, n_scan)
+    for (flip, jump), candidate in zip(steps, sources):
+        @pl.when(source == lax.rem((me ^ flip) - jump + n_scan, n_scan))
+        def _():
+            copy = pltpu.make_async_copy(candidate.at[slot], out_ref, sem)
+            copy.start()
+            copy.wait()
+
+
 def prep_kernel(sizes, info, object_ref, probe_ref, dft_ref, mats, p_ref, xo_ref, wide, sem):
-    n_scan, n_obj, tile_cols = sizes
+    n_scan, _, tile_cols = sizes
     modes, _, length, _ = probe_ref.shape
-    _, _, row, col = assigned(info, lax.axis_index("obj"), lax.axis_index("scan"), n_scan, n_obj)
+    _, core, rank = place_of(n_scan)
+    _, _, row, col = live(info, core, rank, n_scan)
     base, off = column_block(col, length, tile_cols)
     copy = fetch_columns(object_ref, wide, sem, base, length)
     turn = lax.rem(off, length)
@@ -170,19 +195,26 @@
     transform(mats, 1, v_ref, u_ref, s_ref)
 
 
-def join(own, piece_ref, q, i, row, length):
+def own_rows(sizes, info, length):
+    n_scan, _, _ = sizes
+    _, core, rank = place_of(n_scan)
+    _, _, row, _ = live(info, core, rank, n_scan)
+    return jnp.where(core == 0, row, 0), jnp.where(core == 0, length, row)
+
+
+def join(own, piece_ref, q, i, bounds, length):
     piece = piece_ref[q, pl.ds(i, STEP), :].astype(jnp.float32)
-    return jnp.where(lines(length) >= row - i, own, piece)
+    line = lines(length)
+    return jnp.where((line >= bounds[0] - i) & (line < bounds[1] - i), own, piece)
 
 
 def first_kernel(sizes, info, mats, fresnel_ref, p_ref, xo_ref, piece, a_ref, x_ref, v_ref, u_ref, s_ref):
-    n_scan, n_obj, tile_cols = sizes
     modes, _, length, _ = p_ref.shape
-    _, _, row, _ = assigned(info, lax.axis_index("obj"), lax.axis_index("scan"), n_scan, n_obj)
-    for i in range(0, length, STEP):
-        at = pl.ds(i, STEP)
-        xr = join(xo_ref[0, 0, at, :], piece, 0, i, row, length)
-        xi = join(xo_ref[0, 1, at, :], piece, 1, i, row, length)
+    bounds = own_rows(sizes, info, length)
+    for i in range(0, length, STEP):
+        at = pl.ds(i, STEP)
+        xr = join(xo_ref[0, 0, at, :], piece, 0, i, bounds, length)
+        xi = join(xo_ref[0, 1, at, :], piece, 1, i, bounds, length)
         x_ref[0, at, :] = xr
         x_ref[1, at, :] = xi
         for m in range(modes):
@@ -194,35 +226,23 @@
             a_ref[m, 0, at, :], a_ref[m, 1, at, :] = get_s(s_ref, length, m, i)
 
 
-def second_kernel(sizes, *refs):
-    n_scan, n_obj, tile_cols = sizes
-    info, mats, a_ref, xo_ref, piece, own_ref = refs[:6]
-    others = refs[6 : 5 + n_scan]
-    grad_ref, v_out, v_ref, u_ref, s_ref, x_ref, meas_ref = refs[5 + n_scan :]
+def second_kernel(sizes, info, mats, a_ref, xo_ref, piece, meas_here, meas_sent, grad_ref, v_out, v_ref, u_ref, s_ref, x_ref):
     modes, _, length, _ = a_ref.shape
-    me = lax.axis_index("scan")
-    source, slot, row, _ = assigned(info, lax.axis_index("obj"), me, n_scan, n_obj)
-
-    @pl.when(slot == 0)
-    def _():
-        meas_ref[...] = own_ref[0]
-
-    for k in range(1, n_scan):
-        @pl.when((slot == 1) & (source == lax.rem(me - k + n_scan, n_scan)))
-        def _():
-            meas_ref[...] = others[k - 1][...]
-
-    for i in range(0, length, STEP):
-        at = pl.ds(i, STEP)
-        xr = join(xo_ref[1, 0, at, :], piece, 0, i, row, length)
-        xi = join(xo_ref[1, 1, at, :], piece, 1, i, row, length)
+    bounds = own_rows(sizes, info, length)
+    _, core, _ = place_of(sizes[0])
+    for i in range(0, length, STEP):
+        at = pl.ds(i, STEP)
+        xr = join(xo_ref[1, 0, at, :], piece, 0, i, bounds, length)
+        xi = join(xo_ref[1, 1, at, :], piece, 1, i, bounds, length)
         x_ref[0, at, :] = xr
         x_ref[1, at, :] = xi
         for m in range(modes):
             put_v(v_ref, length, m, i, *mul(a_ref[m, 0, at, :], a_ref[m, 1, at, :], xr, xi))
     transform(mats, 0, v_ref, u_ref, s_ref)
     for i in range(0, length, STEP):
-        misfit = -meas_ref[pl.ds(i, STEP), :].astype(jnp.float32)
+        at = pl.ds(i, STEP)
+        here, sent = meas_here[at, :].astype(jnp.float32), meas_sent[at, :].astype(jnp.float32)
+        misfit = -jnp.where(core == 0, here, sent)
         for m in range(modes):
             fr, fi = get_s(s_ref, length, m, i)
             misfit += fr * fr + fi * fi
@@ -242,10 +262,12 @@
         grad_ref[1, at, :] = gi.astype(grad_ref.dtype)
 
 
-def third_kernel(sizes, info, mats, fresnel_ref, v_in, x_ref, p_ref, grad_ref, e_ref, v_ref, u_ref, s_ref, b_ref):
+def third_kernel(sizes, info, mats, fresnel_ref, v_in, x_ref, p_ref, grad_ref, keep_ref, give_ref, v_ref, u_ref, s_ref, b_ref):
     n_scan, n_obj, tile_cols = sizes
     modes, _, length, _ = p_ref.shape
-    _, _, row, col = assigned(info, lax.axis_index("obj"), lax.axis_index("scan"), n_scan, n_obj)
+    chip, core, rank = place_of(n_scan)
+    chips = n_scan // CORES
+    _, _, row, col = live(info, core, rank, n_scan)
     _, off = column_block(col, length, tile_cols)
     propagate(cmul, mats, fresnel_ref, v_in, v_ref, u_ref, s_ref)
     for i in range(0, length, STEP):
@@ -272,32 +294,62 @@
             real = pltpu.roll(real, (128 - shift) % 128, 1) if shift else real
             imag = pltpu.roll(imag, (per_col - shift) % 128, 1) if shift != per_col else imag
             both = jnp.where(lane < per_col, real, imag)[:, : 2 * per_col]
-            for o in range(n_obj):
-                e_ref[s * n_obj + o, m] = both[o * per_row : (o + 1) * per_row].astype(e_ref.dtype)
-
-
-def place_kernel(sizes, steps, factor, *refs):
-    n_scan, n_obj, tile_cols = sizes
-    info, chunks = refs[:2]
-    out_ref, probe_out = refs[-2:]
-    patches = refs[2:-2]
-    layers, _, rows, width = out_ref.shape
+            apart = lax.rem(s // CORES - chip + chips, chips)
+            for mine, ref in ((core, keep_ref), (1 - core, give_ref)):
+                @pl.when(mine == s % CORES)
+                def _():
+                    for o in range(n_obj):
+                        ref[o, apart, m] = both[o * per_row : (o + 1) * per_row].astype(ref.dtype)
+
+
+def place_kernel(sizes, kinds, factor, *refs):
+    n_scan, _, tile_cols = sizes
+    chips = n_scan // CORES
+    layers = refs[-4].shape[0]
+    info = refs[0]
+    shares = refs[1 : 1 + chips]
+    patches = refs[1 + chips : -4]
+    out_ref, probe_out, held, sems = refs[-4:]
+    _, _, rows, width = out_ref.shape
     length = patches[0].shape[2]
     me = lax.axis_index("scan")
-    here = lax.axis_index("obj")
+    chip, core, _ = place_of(n_scan)
+    blocks = width // length
+    first_block = me * blocks
+    spots = []
+    for index, (kind, flip, jump) in enumerate(kinds):
+        other = core ^ flip
+        tile = other ^ kind
+        rank = lax.rem(chip - jump + chips, chips) + other * chips
+        _, _, row, col = live(info, tile, rank, n_scan)
+        base, off = column_block(col, length, tile_cols)
+        top, bottom = jnp.where(tile == OWN, row, 0), jnp.where(tile == OWN, rows, row)
+        meets = (base + 1 >= first_block) & (base < first_block + blocks)
+        copies = [
+            pltpu.make_async_copy(patches[index * layers + l], held.at[index, l], sems.at[index, l])
+            for l in range(layers)
+        ]
+        spots.append((base, off, top, bottom, meets, copies))
+
+        @pl.when(meets)
+        def _():
+            for copy in copies:
+                copy.start()
+
     out_ref[...] = jnp.zeros(out_ref.shape, jnp.float32)
+    per_col = probe_out.shape[3]
+    for m in range(probe_out.shape[0]):
+        total = sum(share[m].astype(jnp.float32) for share in shares) * factor
+        probe_out[m, 0] = total[:, :per_col]
+        probe_out[m, 1] = total[:, per_col:]
     lane, line = lanes(length), lines(length)
-    for index in range(2 * n_scan):
-        previous, member = divmod(index, n_scan)
-        flip, jump = steps[member]
-        source = lax.rem((me ^ flip) - jump + n_scan, n_scan)
-        tile = lax.rem(here + n_obj - previous, n_obj)
-        _, _, row, col = assigned(info, tile, source, n_scan, n_obj)
-        base, off = column_block(col, length, tile_cols)
-        top, bottom = (0, row) if previous else (row, rows)
-        for block in range(width // length):
-            column = me * (width // length) + block
-            first, second = base == column, base + 1 == column
+    for index, (base, off, top, bottom, meets, copies) in enumerate(spots):
+        @pl.when(meets)
+        def _():
+            for copy in copies:
+                copy.wait()
+        for block in range(blocks):
+            first, second = base == first_block + block, base + 1 == first_block + block
             left = jnp.where(first, off, 0)
             right = jnp.where(first, length, off)
 
@@ -310,17 +362,8 @@
                     at = pl.ds(i, STEP)
                     for l in range(layers):
                         for q in range(2):
-                            value = patches[index * layers + l][q, at, :].astype(jnp.float32)
+                            value = held[index, l, q, at, :].astype(jnp.float32)
                             out_ref[l, q, at, spot] += jnp.where(mask, value, 0.0)
-
-    per_col = probe_out.shape[3]
-    for m in range(probe_out.shape[0]):
-        total = chunks[0, m].astype(jnp.float32)
-        for d in range(1, n_scan * n_obj):
-            total += chunks[d, m].astype(jnp.float32)
-        total *= factor
-        probe_out[m, 0] = total[:, :per_col]
-        probe_out[m, 1] = total[:, per_col:]
 
 
 def body(object_slices, probe, measured, positions, counts):
@@ -328,34 +371,41 @@
     modes, _, length, _ = probe.shape
     slots = measured.shape[2]
     n_scan, n_obj = lax.axis_size("scan"), lax.axis_size("obj")
-    devices = n_scan * n_obj
+    chips = n_scan // CORES
     sizes = (n_scan, n_obj, tile_cols)
     smem = pl.BlockSpec(memory_space=pltpu.SMEM)
     vmem = pl.BlockSpec(memory_space=pltpu.VMEM)
     hbm = pl.BlockSpec(memory_space=pltpu.HBM)
-    params = pltpu.CompilerParams(vmem_limit_bytes=20 * MIB)
     real, half = jnp.float32, jnp.bfloat16
 
-    def call(kernel, outs, ins, scratch, name, flops, *args):
+    def call(kernel, outs, ins, scratch, name, flops, limit, *args):
         return pl.pallas_call(
-            kernel,
+            functools.partial(kernel[0], sizes, *kernel[1:]),
             out_shape=[jax.ShapeDtypeStruct(*o) for o in outs],
             in_specs=ins,
             out_specs=[vmem] * len(outs),
             scratch_shapes=scratch,
-            compiler_params=params,
+            compiler_params=pltpu.CompilerParams(vmem_limit_bytes=limit * MIB),
             cost_estimate=pl.CostEstimate(flops=flops, bytes_accessed=4 * MIB, transcendentals=0),
             name=name,
         )(*args)
 
-    def kernel_of(function):
-        return functools.partial(function, sizes)
-
-    info = jnp.concatenate([counts[0], positions[0, 0].reshape(-1)])
-    info = jnp.broadcast_to(jnp.pad(info, (0, 123)), (devices, 1, 128))
-    info = lax.all_to_all(info, AXES, 0, 0, tiled=True)
-    second = measured[0, 0, 1]
-    others = [send(second, lambda s, k=k: s + k, 0) for k in range(1, n_scan)]
+    def across(block):
+        return send(block, lambda s, o: (s ^ 1, o))
+
+    def along(block, jump):
+        return send(block, lambda s, o: (s + CORES * jump, o)) if jump else block
+
+    def outward(block, sign):
+        return send(block, lambda s, o: (s, o + (sign if s % CORES == 0 else -sign)))
+
+    info = jnp.concatenate([counts[0], positions[0, 0].reshape(-1), jnp.zeros((3,), jnp.int32)])
+    both = jnp.concatenate([info, send(info, lambda s, o: (s, o + 1))])
+    info = lax.all_to_all(jnp.broadcast_to(both, (n_scan, 1, 16)), "scan", 0, 0, tiled=True)
+
+    steps = [(0, CORES * j) for j in range(chips)] + [(1, CORES * j) for j in range(chips)]
+    gathered = [along(measured[0, 0], j) for j in range(chips)]
+    gathered += [across(block) for block in gathered]
 
     piece_shape = (2, length, length)
     field_shape = (modes, 2, length, length)
@@ -367,16 +417,29 @@
     ]
     pair_flops = 2 * 2 * modes * 8 * length**3
     pieces = call(
-        kernel_of(cut_kernel), [(piece_shape, half)] * 2, [smem, hbm], wide, "cut", MIB, info, object_slices
-    )
-    pieces = [send(piece, lambda s: s, -1) for piece in pieces]
+        (cut_kernel,), [(piece_shape, half)] * 2, [smem, hbm], wide, "cut", MIB, LARGE, info, object_slices
+    )
+    pieces = [outward(piece, -1) for piece in pieces]
+    (chosen,) = call(
+        (choose_kernel, steps),
+        [((length, length), measured.dtype)],
+        [smem] + [hbm] * n_scan,
+        [pltpu.SemaphoreType.DMA],
+        "choose",
+        MIB,
+        LARGE,
+        info,
+        *gathered,
+    )
+    passed = send(chosen, lambda s, o: (s, o + 1) if s % CORES else None)
     mats, turned, own_part = call(
-        kernel_of(prep_kernel),
+        (prep_kernel,),
         [((4, 2 * length, 2 * length), half), (field_shape, real), ((layers, *piece_shape), real)],
         [smem, hbm, vmem, vmem],
         wide,
         "prep",
         MIB,
+        LARGE,
         info,
         object_slices,
         probe,
@@ -384,12 +447,13 @@
     )
     fresnel = fresnel_tables(length)
     arrived, patch = call(
-        kernel_of(first_kernel),
+        (first_kernel,),
         [(field_shape, real), (piece_shape, real)],
         [smem] + [vmem] * 5,
         vus,
         "first",
         pair_flops,
+        SMALL,
         info,
         mats,
         fresnel,
@@ -398,28 +462,30 @@
         pieces[0],
     )
     grad1, carried = call(
-        kernel_of(second_kernel),
+        (second_kernel,),
         [(piece_shape, half), ((2 * length, modes * length), half)],
-        [smem] + [vmem] * (4 + n_scan),
-        vus + [pltpu.VMEM(piece_shape, real), pltpu.VMEM((length, length), measured.dtype)],
+        [smem] + [vmem] * 6,
+        vus + [pltpu.VMEM(piece_shape, real)],
         "second",
         pair_flops,
+        SMALL,
         info,
         mats,
         arrived,
         own_part,
         pieces[1],
-        measured[0, 0],
-        *others,
-    )
-    chunk_shape = (devices, modes, length // n_obj, 2 * (length // n_scan))
-    grad0, chunks = call(
-        kernel_of(third_kernel),
-        [(piece_shape, half), (chunk_shape, half)],
+        chosen,
+        passed,
+    )
+    chunk_shape = (n_obj, chips, modes, length // n_obj, 2 * (length // n_scan))
+    grad0, keep, give = call(
+        (third_kernel,),
+        [(piece_shape, half), (chunk_shape, half), (chunk_shape, half)],
         [smem] + [vmem] * 5,
         vus + [pltpu.VMEM(field_shape, real)],
         "third",
         pair_flops,
+        SMALL,
         info,
         mats,
         fresnel,
@@ -428,33 +494,33 @@
         turned,
     )
 
-    jumps = [CORES * k for k in range(n_scan // CORES)]
     held = []
-    for l, grad in enumerate((grad0, grad1)):
-        own = [grad] + [send(grad, lambda s, j=j: s + j, 0) for j in jumps[1:]]
-        passed = [send(grad, lambda s: s, 1)]
-        if l == 0:
-            passed += [send(passed[0], lambda s, j=j: s + j, 0) for j in jumps[1:]]
-        else:
-            passed += [send(patch_grad, lambda s: s, 1) for patch_grad in own[1:]]
-        own += [send(p, lambda s: s ^ 1, 0) for p in own]
-        passed += [send(p, lambda s: s ^ 1, 0) for p in passed]
-        held.append(own + passed)
-    chunks = lax.all_to_all(chunks, AXES, 0, 0, tiled=True)
-    steps = [(0, j) for j in jumps] + [(1, j) for j in jumps]
+    for grad in (grad0, grad1):
+        here = [along(grad, j) for j in range(chips)]
+        there = [outward(block, 1) for block in here]
+        held.append(here + there + [across(block) for block in here + there])
+    kinds = [(kind, flip, jump) for flip in range(2) for kind in range(2) for jump in range(chips)]
+    chunks = (keep.astype(real) + across(give).astype(real)).astype(half)
+    chunks = lax.all_to_all(chunks, "obj", 0, 0, tiled=True)
+    chunks = jnp.sum(chunks.astype(real), axis=0).astype(half)
+    shares = [along(chunks[j], j) for j in range(chips)]
     factor = 1.0 / math.sqrt(n_scan * n_obj * slots // 2)
     object_grad, probe_grad = call(
-        functools.partial(place_kernel, sizes, steps, factor),
+        (place_kernel, kinds, factor),
         [
             ((layers, 2, tile_rows, tile_cols // n_scan), real),
             ((modes, 2, length // n_obj, length // n_scan), real),
         ],
-        [smem, vmem] + [vmem] * (2 * n_scan * layers),
-        [],
+        [smem] + [vmem] * chips + [hbm] * (2 * n_scan * layers),
+        [
+            pltpu.VMEM((2 * n_scan, layers, *piece_shape), half),
+            pltpu.SemaphoreType.DMA((2 * n_scan, layers)),
+        ],
         "place",
         MIB,
+        LARGE,
         info,
-        chunks,
+        *shares,
         *[held[l][index] for index in range(2 * n_scan) for l in range(layers)],
     )
     return (object_grad, probe_grad)

time: 89.6 us -> 88.1 us (0.983)
  starting transfers between devices: 14.6 us -> 26.7 us
  waiting for transfers between devices: 30.9 us -> 22.4 us
  blocking collectives: 14.2 us -> 6.56 us
  Pallas kernels: 15.5 us -> 21.9 us
  local copies, waits for them, and re-layouts: 12.5 us -> 7.34 us
  other arithmetic: 0.08 us -> 0.98 us
    ppermute x19 -> x23, starting transfers between devices: 10.9 us -> 22.2 us  [send(): return lax.ppermute(block, AXES, route)]
    ppermute x19 -> x23, waiting for transfers between devices: 30.9 us -> 22.4 us  [send(): return lax.ppermute(block, AXES, route)]
    all_to_all x1, blocking collectives: 14.2 us -> 6.56 us  [body(): lax.all_to_all(jnp.broadcast_to(both, (n_scan, 1, 16)), 'scan', 0, 0, til...]
    pallas_call x6 -> x7, Pallas kernels: 15.5 us -> 21.9 us  [call(): pl.pallas_call(functools.partial(kernel[0], sizes, *kernel[1:]), out_shap...]
    unnamed x30 -> x50, local copies, waits for them, and re-layouts: 11.7 us -> 5.97 us
  transfers between devices with their start and end apart: 20 -> 24, of which waited for: 6 -> 7; matrix products, arithmetic and copies ran while one was open for 0% -> 3% of each run, Pallas kernels for 5% -> 14%
where the time goes in v3:
time: 88.1 us; the launch traced here: 87.5 us
  starting transfers between devices  26.7 us (30%)
  waiting for transfers between devices  22.4 us (25%)
  Pallas kernels  21.9 us (25%)
  local copies, waits for them, and re-layouts  7.34 us (8%)
  blocking collectives  6.56 us (7%)
  between operations  1.65 us (2%)
  other arithmetic  0.98 us (1%)
    ppermute x23, waiting for transfers between devices, send(): return lax.ppermute(block, AXES, route)  22.4 us
    ppermute x23, starting transfers between devices, send(): return lax.ppermute(block, AXES, route)  22.2 us
    pallas_call x7, Pallas kernels, call(): pl.pallas_call(functools.partial(kernel[0], sizes, *kernel[1:]), out_shap...  21.9 us
    all_to_all x1, blocking collectives, body(): lax.all_to_all(jnp.broadcast_to(both, (n_scan, 1, 16)), 'scan', 0, 0, til...  6.56 us
    unnamed x50, local copies, waits for them, and re-layouts  5.97 us
    all_to_all x1, starting transfers between devices, body(): chunks = lax.all_to_all(chunks, 'obj', 0, 0, tiled=True)  4.48 us
  transfers between devices with their start and end apart: 24, of which 7 were waited for; matrix products, arithmetic and copies ran while one was open for 3% of the time, Pallas kernels for 14%

profile of v3, /device:TPU:0, one launch (start us, length us, event | category | flops | bytes accessed | tf_op | source)
XLA Modules:
  0.0 87.5 jit_solution(13050445865765087927)
XLA Ops:
  0.6 3.0 %collective-permute-start.3 = (bf16[2,256,256]{2,1,0:T(8,128)(2,1)}, bf16[2,256,256]{2,1,0:T(8,128)(2,1)S(1)}, u32[]{:S(2)}, u32[]{:S(2)}) collective-permute-start(bf16[2,256,256]{2,1,0:T(8,128)(2,1)} %bitcast.8), channel_id=1, source_target_pairs={{0,16},{1,17},{2,18},{3,19},{4,20},{5,21},{6,22},{7,23},{8,24},{9,... | collective-permute-start | bytes 786440 | tf_op jit(solution)/shard_map/ppermute | solution.py:42
  5.1 1.5 %collective-permute-start = (s32[8]{0:T(128)S(1)}, s32[8]{0:T(128)S(1)}, u32[]{:S(2)}, u32[]{:S(2)}) collective-permute-start(s32[8]{0:T(128)S(1)} %pad_add_fusion), channel_id=1, source_target_pairs={{0,1},{1,2},{2,3},{3,4},{4,5},{5,6},{6,7},{7,0},{8,9},{9,10},{10,1... | collective-permute-start | bytes 104 | tf_op jit(solution)/shard_map/ppermute | solution.py:42
  6.7 3.5 %collective-permute-done.3.refs_1_ = bf16[2,256,256]{2,1,0:T(8,128)(2,1)S(1)} collective-permute-done((bf16[2,256,256]{2,1,0:T(8,128)(2,1)}, bf16[2,256,256]{2,1,0:T(8,128)(2,1)S(1)}, u32[]{:S(2)}, u32[]{:S(2)}) %collective-permute-start.3) | collective-permute-done | bytes 262176 | tf_op jit(solution)/shard_map/ppermute | solution.py:42
  11.5 6.6 %all_to_all.10.info.refs_0_ = s32[4,1,16]{2,1,0:T(1,128)} all-to-all(s32[4,1,16]{2,1,0:T(1,128)S(1)} %broadcast_in_dim.3), channel_id=1, replica_groups=mesh['scan'=4,'obj'=8] {'scan'}, dimensions={0} | all-to-all | bytes 512 | tf_op jit(solution)/shard_map/all_to_all | solution.py:404
  18.0 3.2 %cut.1 = (bf16[2,256,256]{2,1,0:T(8,128)(2,1)}, bf16[2,256,256]{2,1,0:T(8,128)(2,1)}) custom-call(s32[4,1,16]{2,1,0:T(1,128)} %all_to_all.10.info.refs_0_, f32[2,2,256,2048]{3,2,1,0:T(8,128)} %object_ref.3), custom_call_target="tpu_custom_call" | custom-call | flops 1048576 | bytes 4194304 | tf_op jit(solution)/shard_map/cut/pallas_call | solution.py:382
  21.2 3.7 %collective-permute-start.1 = (bf16[2,256,256]{2,1,0:T(8,128)(2,1)}, bf16[2,256,256]{2,1,0:T(8,128)(2,1)S(1)}, u32[]{:S(2)}, u32[]{:S(2)}) collective-permute-start(bf16[2,256,256]{2,1,0:T(8,128)(2,1)} %get-tuple-element.17), channel_id=1, source_target_pairs={{0,7},{1,0},{2,1},{3,2},{4,3},{5,4},{6,5},{7,6},{8,9},{9,10},{10,1... | collective-permute-start | bytes 786440 | tf_op jit(solution)/shard_map/ppermute | solution.py:42
  26.8 2.3 %choose.1.meas_here = bf16[256,256]{1,0:T(8,128)(2,1)} custom-call(s32[4,1,16]{2,1,0:T(1,128)} %all_to_all.10.info.refs_0_, bf16[2,256,256]{2,1,0:T(8,128)(2,1)} %bitcast.10, bf16[2,256,256]{2,1,0:T(8,128)(2,1)} %copy-done.10, bf16[2,256,256]{2,1,0:T(8,128)(2,1)} %copy-done.11, bf16[2,256,256]{2,1,0:T(8,128)(2,1)} %copy-done.12), custom_call_target="tpu_custom_call" | custom-call | flops 1048576 | bytes 4194304 | tf_op jit(solution)/shard_map/choose/pallas_call | solution.py:382
  29.9 5.0 %prep.1 = (bf16[4,512,512]{2,1,0:T(8,128)(2,1)}, f32[2,2,256,256]{3,2,1,0:T(8,128)}, f32[2,2,256,256]{3,2,1,0:T(8,128)}) custom-call(s32[4,1,16]{2,1,0:T(1,128)} %all_to_all.10.info.refs_0_, f32[2,2,256,2048]{3,2,1,0:T(8,128)} %object_ref.3, f32[2,2,256,256]{3,2,1,0:T(8,128)} %probe_ref.1, f32[2,256,256]{2,1,0:T(8,128)} %constant.9.clone.dft_ref), custom_call_target="tpu_custom_call" | custom-call | flops 1048576 | bytes 4194304 | tf_op jit(solution)/shard_map/prep/pallas_call | solution.py:382
  34.9 1.6 %copy-done = bf16[4,512,512]{2,1,0:T(8,128)(2,1)S(1)} copy-done((bf16[4,512,512]{2,1,0:T(8,128)(2,1)S(1)}, bf16[4,512,512]{2,1,0:T(8,128)(2,1)}, u32[]{:S(2)}) %copy-start) | copy-done | bytes 2097176
  36.5 1.2 %copy-done.1 = f32[2,2,256,256]{3,2,1,0:T(8,128)S(1)} copy-done((f32[2,2,256,256]{3,2,1,0:T(8,128)S(1)}, f32[2,2,256,256]{3,2,1,0:T(8,128)}, u32[]{:S(2)}) %copy-start.1) | copy-done | bytes 1048600
  39.0 2.1 %first.1 = (f32[2,2,256,256]{3,2,1,0:T(8,128)S(1)}, f32[2,256,256]{2,1,0:T(8,128)S(1)}) custom-call(s32[4,1,16]{2,1,0:T(1,128)S(1)} %copy-done.9, bf16[4,512,512]{2,1,0:T(8,128)(2,1)S(1)} %copy-done, f32[2,256,256]{2,1,0:T(8,128)S(1)} %copy-done.5, f32[2,2,256,256]{3,2,1,0:T(8,128)S(1)} %copy-done.1, f32[2,2,256,256]{3,2,1,0:T(8,128)S(1)} %copy-done.3, ...), custom_call_target="tpu_custom_call" | custom-call | flops 1073741824 | bytes 4194304 | tf_op jit(solution)/shard_map/first/pallas_call | solution.py:382
  41.1 2.2 %second.1 = (bf16[2,256,256]{2,1,0:T(8,128)(2,1)S(1)}, bf16[512,512]{1,0:T(8,128)(2,1)S(1)}) custom-call(s32[4,1,16]{2,1,0:T(1,128)S(1)} %copy-done.9, bf16[4,512,512]{2,1,0:T(8,128)(2,1)S(1)} %copy-done, f32[2,2,256,256]{3,2,1,0:T(8,128)S(1)} %get-tuple-element.18.a_ref, f32[2,2,256,256]{3,2,1,0:T(8,128)S(1)} %copy-done.4, ...), custom_call_target="tpu_custom_call" | custom-call | flops 1073741824 | bytes 4194304 | tf_op jit(solution)/shard_map/second/pallas_call | solution.py:382
  43.4 3.3 %third.1 = (bf16[2,256,256]{2,1,0:T(8,128)(2,1)S(1)}, bf16[8,2,2,32,128]{4,3,2,1,0:T(8,128)(2,1)S(1)}, bf16[8,2,2,32,128]{4,3,2,1,0:T(8,128)(2,1)S(1)}) custom-call(s32[4,1,16]{2,1,0:T(1,128)S(1)} %copy-done.9, bf16[4,512,512]{2,1,0:T(8,128)(2,1)S(1)} %copy-done, f32[2,256,256]{2,1,0:T(8,128)S(1)} %copy-done.5, bf16[512,512]{1,0:T(8,128)(2,1)S(1)} %get-tuple-element.20.v_in, ...), custom_call_target="tpu_custom_call" | custom-call | flops 1073741824 | bytes 4194304 | tf_op jit(solution)/shard_map/third/pallas_call | solution.py:382
  47.3 1.5 %collective-permute-start.11 = (bf16[2,256,256]{2,1,0:T(8,128)(2,1)S(1)}, bf16[2,256,256]{2,1,0:T(8,128)(2,1)S(1)}, u32[]{:S(2)}, u32[]{:S(2)}) collective-permute-start(bf16[2,256,256]{2,1,0:T(8,128)(2,1)S(1)} %get-tuple-element.24.refs_3_), channel_id=1, source_target_pairs={{0,1},{1,2},{2,3},{3,4},{4,5},{5,6},{6,7},{7,0},{8,15},{9,8},{10,9... | collective-permute-start | bytes 786440 | tf_op jit(solution)/shard_map/ppermute | solution.py:42
  49.0 1.8 %collective-permute-start.10 = (bf16[2,256,256]{2,1,0:T(8,128)(2,1)S(1)}, bf16[2,256,256]{2,1,0:T(8,128)(2,1)S(1)}, u32[]{:S(2)}, u32[]{:S(2)}) collective-permute-start(bf16[2,256,256]{2,1,0:T(8,128)(2,1)S(1)} %get-tuple-element.25.refs_4_), channel_id=1, source_target_pairs={{0,16},{1,17},{2,18},{3,19},{4,20},{5,21},{6,22},{7,23},{8,24},{9,... | collective-permute-start | bytes 786440 | tf_op jit(solution)/shard_map/ppermute | solution.py:42
  51.6 4.5 %all-to-all-start.1 = ((bf16[8,2,2,32,128]{4,3,2,1,0:T(8,128)(2,1)}), bf16[8,2,2,32,128]{4,3,2,1,0:T(8,128)(2,1)S(1)}, u32[]{:S(2)}, u32[]{:S(2)}) async-start(bf16[8,2,2,32,128]{4,3,2,1,0:T(8,128)(2,1)} %add_convert_fusion), calls=%async_computation.1 | async-start | bytes 524288 | tf_op jit(solution)/shard_map/all_to_all | solution.py:504
  56.1 2.1 %collective-permute-start.12 = (bf16[2,256,256]{2,1,0:T(8,128)(2,1)S(1)}, bf16[2,256,256]{2,1,0:T(8,128)(2,1)S(1)}, u32[]{:S(2)}, u32[]{:S(2)}) collective-permute-start(bf16[2,256,256]{2,1,0:T(8,128)(2,1)S(1)} %get-tuple-element.25.refs_4_), channel_id=1, source_target_pairs={{0,1},{1,2},{2,3},{3,4},{4,5},{5,6},{6,7},{7,0},{8,15},{9,8},{10,9... | collective-permute-start | bytes 786440 | tf_op jit(solution)/shard_map/ppermute | solution.py:42
  58.2 2.9 %collective-permute-start.19 = (bf16[2,256,256]{2,1,0:T(8,128)(2,1)S(1)}, bf16[2,256,256]{2,1,0:T(8,128)(2,1)S(1)}, u32[]{:S(2)}, u32[]{:S(2)}) collective-permute-start(bf16[2,256,256]{2,1,0:T(8,128)(2,1)S(1)} %collective-permute-done.11.refs_7_), channel_id=1, source_target_pairs={{0,8},{1,9},{2,10},{3,11},{4,12},{5,13},{6,14},{7,15},{8,0},{9,1},... | collective-permute-start | bytes 786440 | tf_op jit(solution)/shard_map/ppermute | solution.py:42
  61.1 2.2 %collective-permute-done.10.refs_6_ = bf16[2,256,256]{2,1,0:T(8,128)(2,1)S(1)} collective-permute-done((bf16[2,256,256]{2,1,0:T(8,128)(2,1)S(1)}, bf16[2,256,256]{2,1,0:T(8,128)(2,1)S(1)}, u32[]{:S(2)}, u32[]{:S(2)}) %collective-permute-start.10) | collective-permute-done | bytes 262176 | tf_op jit(solution)/shard_map/ppermute | solution.py:42
  63.8 8.0 %collective-permute-done.12.refs_8_ = bf16[2,256,256]{2,1,0:T(8,128)(2,1)S(1)} collective-permute-done((bf16[2,256,256]{2,1,0:T(8,128)(2,1)S(1)}, bf16[2,256,256]{2,1,0:T(8,128)(2,1)S(1)}, u32[]{:S(2)}, u32[]{:S(2)}) %collective-permute-start.12) | collective-permute-done | bytes 262176 | tf_op jit(solution)/shard_map/ppermute | solution.py:42
  72.3 2.3 %collective-permute-done.13.refs_9_ = bf16[2,256,256]{2,1,0:T(8,128)(2,1)S(1)} collective-permute-done((bf16[2,256,256]{2,1,0:T(8,128)(2,1)S(1)}, bf16[2,256,256]{2,1,0:T(8,128)(2,1)S(1)}, u32[]{:S(2)}, u32[]{:S(2)}) %collective-permute-start.13) | collective-permute-done | bytes 262176 | tf_op jit(solution)/shard_map/ppermute | solution.py:42
  75.8 1.6 %collective-permute-done.14.refs_10_ = bf16[2,256,256]{2,1,0:T(8,128)(2,1)S(1)} collective-permute-done((bf16[2,256,256]{2,1,0:T(8,128)(2,1)S(1)}, bf16[2,256,256]{2,1,0:T(8,128)(2,1)S(1)}, u32[]{:S(2)}, u32[]{:S(2)}) %collective-permute-start.14) | collective-permute-done | bytes 262176 | tf_op jit(solution)/shard_map/ppermute | solution.py:42
  79.5 3.5 %collective-permute-done.8.refs_2_ = bf16[2,32,128]{2,1,0:T(8,128)(2,1)S(1)} collective-permute-done((bf16[2,32,128]{2,1,0:T(8,128)(2,1)S(1)}, bf16[2,32,128]{2,1,0:T(8,128)(2,1)S(1)}, u32[]{:S(2)}, u32[]{:S(2)}) %collective-permute-start.8) | collective-permute-done | bytes 16416 | tf_op jit(solution)/shard_map/ppermute | solution.py:42
  83.7 3.9 %place.1 = (f32[2,2,256,512]{3,2,1,0:T(8,128)}, f32[2,2,32,64]{3,2,1,0:T(8,128)}) custom-call(s32[4,1,16]{2,1,0:T(1,128)} %all_to_all.10.info.refs_0_, bf16[2,32,128]{2,1,0:T(8,128)(2,1)} %get-tuple-element.27.refs_1_, bf16[2,32,128]{2,1,0:T(8,128)(2,1)} %copy-done.24, bf16[2,256,256]{2,1,0:T(8,128)(2,1)} %copy-done.8, bf16[2,256,256]{2,1,0:T(8,128)(2,1)} %copy-done.7, ...), custom_call_target="tpu_custom_call" | custom-call | flops 1048576 | bytes 4194304 | tf_op jit(solution)/shard_map/place/pallas_call | solution.py:382
  (90 shorter events, 12.5 us)
Async XLA Ops:
  0.6 9.5 %collective-permute-start.3 = (bf16[2,256,256]{2,1,0:T(8,128)(2,1)}, bf16[2,256,256]{2,1,0:T(8,128)(2,1)S(1)}, u32[]{:S(2)}, u32[]{:S(2)}) collective-permute-start(bf16[2,256,256]{2,1,0:T(8,128)(2,1)} %bitcast.8), channel_id=1, source_target_pairs={{0,16},{1,17},{2,18},{3,19},{4,20},{5,21},{6,22},{7,23},{8,24},{9,... | collective-permute-start | bytes 786440 | tf_op jit(solution)/shard_map/ppermute | solution.py:42
  3.6 21.7 %collective-permute-start.4 = (bf16[2,256,256]{2,1,0:T(8,128)(2,1)}, bf16[2,256,256]{2,1,0:T(8,128)(2,1)S(1)}, u32[]{:S(2)}, u32[]{:S(2)}) collective-permute-start(bf16[2,256,256]{2,1,0:T(8,128)(2,1)} %bitcast.9), channel_id=1, source_target_pairs={{0,8},{1,9},{2,10},{3,11},{4,12},{5,13},{6,14},{7,15},{8,0},{9,1},... | collective-permute-start | bytes 786440 | tf_op jit(solution)/shard_map/ppermute | solution.py:42
  5.1 6.2 %collective-permute-start = (s32[8]{0:T(128)S(1)}, s32[8]{0:T(128)S(1)}, u32[]{:S(2)}, u32[]{:S(2)}) collective-permute-start(s32[8]{0:T(128)S(1)} %pad_add_fusion), channel_id=1, source_target_pairs={{0,1},{1,2},{2,3},{3,4},{4,5},{5,6},{6,7},{7,0},{8,9},{9,10},{10,1... | collective-permute-start | bytes 104 | tf_op jit(solution)/shard_map/ppermute | solution.py:42
  10.2 15.2 %collective-permute-start.5 = (bf16[2,256,256]{2,1,0:T(8,128)(2,1)S(1)}, bf16[2,256,256]{2,1,0:T(8,128)(2,1)S(1)}, u32[]{:S(2)}, u32[]{:S(2)}) collective-permute-start(bf16[2,256,256]{2,1,0:T(8,128)(2,1)S(1)} %collective-permute-done.3.refs_1_), channel_id=1, source_target_pairs={{0,8},{1,9},{2,10},{3,11},{4,12},{5,13},{6,14},{7,15},{8,0},{9,1},... | collective-permute-start | bytes 786440 | tf_op jit(solution)/shard_map/ppermute | solution.py:42
  21.2 13.7 %collective-permute-start.1 = (bf16[2,256,256]{2,1,0:T(8,128)(2,1)}, bf16[2,256,256]{2,1,0:T(8,128)(2,1)S(1)}, u32[]{:S(2)}, u32[]{:S(2)}) collective-permute-start(bf16[2,256,256]{2,1,0:T(8,128)(2,1)} %get-tuple-element.17), channel_id=1, source_target_pairs={{0,7},{1,0},{2,1},{3,2},{4,3},{5,4},{6,5},{7,6},{8,9},{9,10},{10,1... | collective-permute-start | bytes 786440 | tf_op jit(solution)/shard_map/ppermute | solution.py:42
  24.9 16.2 %collective-permute-start.2 = (bf16[2,256,256]{2,1,0:T(8,128)(2,1)}, bf16[2,256,256]{2,1,0:T(8,128)(2,1)S(1)}, u32[]{:S(2)}, u32[]{:S(2)}) collective-permute-start(bf16[2,256,256]{2,1,0:T(8,128)(2,1)} %get-tuple-element.19), channel_id=1, source_target_pairs={{0,7},{1,0},{2,1},{3,2},{4,3},{5,4},{6,5},{7,6},{8,9},{9,10},{10,1... | collective-permute-start | bytes 786440 | tf_op jit(solution)/shard_map/ppermute | solution.py:42
  29.0 12.0 %collective-permute-start.6 = (bf16[256,256]{1,0:T(8,128)(2,1)}, bf16[256,256]{1,0:T(8,128)(2,1)S(1)}, u32[]{:S(2)}, u32[]{:S(2)}) collective-permute-start(bf16[256,256]{1,0:T(8,128)(2,1)} %choose.1.meas_here), channel_id=1, source_target_pairs={{8,9},{9,10},{10,11},{11,12},{12,13},{13,14},{14,15},{15,8},{24,25... | collective-permute-start | bytes 393224 | tf_op jit(solution)/shard_map/ppermute | solution.py:42
  46.7 4.1 %collective-permute-start.7 = (bf16[8,2,2,32,128]{4,3,2,1,0:T(8,128)(2,1)S(1)}, bf16[8,2,2,32,128]{4,3,2,1,0:T(8,128)(2,1)S(1)}, u32[]{:S(2)}, u32[]{:S(2)}) collective-permute-start(bf16[8,2,2,32,128]{4,3,2,1,0:T(8,128)(2,1)S(1)} %get-tuple-element.23), channel_id=1, source_target_pairs={{0,8},{1,9},{2,10},{3,11},{4,12},{5,13},{6,14},{7,15},{8,0},{9,1},... | collective-permute-start | bytes 786440 | tf_op jit(solution)/shard_map/ppermute | solution.py:42
  46.8 9.3 %collective-permute-start.15 = (bf16[2,256,256]{2,1,0:T(8,128)(2,1)S(1)}, bf16[2,256,256]{2,1,0:T(8,128)(2,1)S(1)}, u32[]{:S(2)}, u32[]{:S(2)}) collective-permute-start(bf16[2,256,256]{2,1,0:T(8,128)(2,1)S(1)} %get-tuple-element.24.refs_3_), channel_id=1, source_target_pairs={{0,8},{1,9},{2,10},{3,11},{4,12},{5,13},{6,14},{7,15},{8,0},{9,1},... | collective-permute-start | bytes 786440 | tf_op jit(solution)/shard_map/ppermute | solution.py:42
  47.3 10.9 %collective-permute-start.11 = (bf16[2,256,256]{2,1,0:T(8,128)(2,1)S(1)}, bf16[2,256,256]{2,1,0:T(8,128)(2,1)S(1)}, u32[]{:S(2)}, u32[]{:S(2)}) collective-permute-start(bf16[2,256,256]{2,1,0:T(8,128)(2,1)S(1)} %get-tuple-element.24.refs_3_), channel_id=1, source_target_pairs={{0,1},{1,2},{2,3},{3,4},{4,5},{5,6},{6,7},{7,0},{8,15},{9,8},{10,9... | collective-permute-start | bytes 786440 | tf_op jit(solution)/shard_map/ppermute | solution.py:42
  48.8 12.3 %collective-permute-start.9 = (bf16[2,256,256]{2,1,0:T(8,128)(2,1)S(1)}, bf16[2,256,256]{2,1,0:T(8,128)(2,1)S(1)}, u32[]{:S(2)}, u32[]{:S(2)}) collective-permute-start(bf16[2,256,256]{2,1,0:T(8,128)(2,1)S(1)} %get-tuple-element.24.refs_3_), channel_id=1, source_target_pairs={{0,16},{1,17},{2,18},{3,19},{4,20},{5,21},{6,22},{7,23},{8,24},{9,... | collective-permute-start | bytes 786440 | tf_op jit(solution)/shard_map/ppermute | solution.py:42
  49.0 14.3 %collective-permute-start.10 = (bf16[2,256,256]{2,1,0:T(8,128)(2,1)S(1)}, bf16[2,256,256]{2,1,0:T(8,128)(2,1)S(1)}, u32[]{:S(2)}, u32[]{:S(2)}) collective-permute-start(bf16[2,256,256]{2,1,0:T(8,128)(2,1)S(1)} %get-tuple-element.25.refs_4_), channel_id=1, source_target_pairs={{0,16},{1,17},{2,18},{3,19},{4,20},{5,21},{6,22},{7,23},{8,24},{9,... | collective-permute-start | bytes 786440 | tf_op jit(solution)/shard_map/ppermute | solution.py:42
  51.6 27.1 %all-to-all-start.1 = ((bf16[8,2,2,32,128]{4,3,2,1,0:T(8,128)(2,1)}), bf16[8,2,2,32,128]{4,3,2,1,0:T(8,128)(2,1)S(1)}, u32[]{:S(2)}, u32[]{:S(2)}) async-start(bf16[8,2,2,32,128]{4,3,2,1,0:T(8,128)(2,1)} %add_convert_fusion), calls=%async_computation.1 | async-start | bytes 524288 | tf_op jit(solution)/shard_map/all_to_all | solution.py:504
  56.1 7.2 %collective-permute-start.16 = (bf16[2,256,256]{2,1,0:T(8,128)(2,1)S(1)}, bf16[2,256,256]{2,1,0:T(8,128)(2,1)S(1)}, u32[]{:S(2)}, u32[]{:S(2)}) collective-permute-start(bf16[2,256,256]{2,1,0:T(8,128)(2,1)S(1)} %get-tuple-element.25.refs_4_), channel_id=1, source_target_pairs={{0,8},{1,9},{2,10},{3,11},{4,12},{5,13},{6,14},{7,15},{8,0},{9,1},... | collective-permute-start | bytes 786440 | tf_op jit(solution)/shard_map/ppermute | solution.py:42
  56.1 15.7 %collective-permute-start.12 = (bf16[2,256,256]{2,1,0:T(8,128)(2,1)S(1)}, bf16[2,256,256]{2,1,0:T(8,128)(2,1)S(1)}, u32[]{:S(2)}, u32[]{:S(2)}) collective-permute-start(bf16[2,256,256]{2,1,0:T(8,128)(2,1)S(1)} %get-tuple-element.25.refs_4_), channel_id=1, source_target_pairs={{0,1},{1,2},{2,3},{3,4},{4,5},{5,6},{6,7},{7,0},{8,15},{9,8},{10,9... | collective-permute-start | bytes 786440 | tf_op jit(solution)/shard_map/ppermute | solution.py:42
  58.2 13.6 %collective-permute-start.19 = (bf16[2,256,256]{2,1,0:T(8,128)(2,1)S(1)}, bf16[2,256,256]{2,1,0:T(8,128)(2,1)S(1)}, u32[]{:S(2)}, u32[]{:S(2)}) collective-permute-start(bf16[2,256,256]{2,1,0:T(8,128)(2,1)S(1)} %collective-permute-done.11.refs_7_), channel_id=1, source_target_pairs={{0,8},{1,9},{2,10},{3,11},{4,12},{5,13},{6,14},{7,15},{8,0},{9,1},... | collective-permute-start | bytes 786440 | tf_op jit(solution)/shard_map/ppermute | solution.py:42
  61.1 13.5 %collective-permute-start.13 = (bf16[2,256,256]{2,1,0:T(8,128)(2,1)S(1)}, bf16[2,256,256]{2,1,0:T(8,128)(2,1)S(1)}, u32[]{:S(2)}, u32[]{:S(2)}) collective-permute-start(bf16[2,256,256]{2,1,0:T(8,128)(2,1)S(1)} %collective-permute-done.9.refs_5_), channel_id=1, source_target_pairs={{0,1},{1,2},{2,3},{3,4},{4,5},{5,6},{6,7},{7,0},{8,15},{9,8},{10,9... | collective-permute-start | bytes 786440 | tf_op jit(solution)/shard_map/ppermute | solution.py:42
  63.3 14.2 %collective-permute-start.14 = (bf16[2,256,256]{2,1,0:T(8,128)(2,1)S(1)}, bf16[2,256,256]{2,1,0:T(8,128)(2,1)S(1)}, u32[]{:S(2)}, u32[]{:S(2)}) collective-permute-start(bf16[2,256,256]{2,1,0:T(8,128)(2,1)S(1)} %collective-permute-done.10.refs_6_), channel_id=1, source_target_pairs={{0,1},{1,2},{2,3},{3,4},{4,5},{5,6},{6,7},{7,0},{8,15},{9,8},{10,9... | collective-permute-start | bytes 786440 | tf_op jit(solution)/shard_map/ppermute | solution.py:42
  63.3 16.0 %collective-permute-start.17 = (bf16[2,256,256]{2,1,0:T(8,128)(2,1)S(1)}, bf16[2,256,256]{2,1,0:T(8,128)(2,1)S(1)}, u32[]{:S(2)}, u32[]{:S(2)}) collective-permute-start(bf16[2,256,256]{2,1,0:T(8,128)(2,1)S(1)} %collective-permute-done.9.refs_5_), channel_id=1, source_target_pairs={{0,8},{1,9},{2,10},{3,11},{4,12},{5,13},{6,14},{7,15},{8,0},{9,1},... | collective-permute-start | bytes 786440 | tf_op jit(solution)/shard_map/ppermute | solution.py:42
  71.8 7.7 %collective-permute-start.18 = (bf16[2,256,256]{2,1,0:T(8,128)(2,1)S(1)}, bf16[2,256,256]{2,1,0:T(8,128)(2,1)S(1)}, u32[]{:S(2)}, u32[]{:S(2)}) collective-permute-start(bf16[2,256,256]{2,1,0:T(8,128)(2,1)S(1)} %collective-permute-done.10.refs_6_), channel_id=1, source_target_pairs={{0,8},{1,9},{2,10},{3,11},{4,12},{5,13},{6,14},{7,15},{8,0},{9,1},... | collective-permute-start | bytes 786440 | tf_op jit(solution)/shard_map/ppermute | solution.py:42
  71.8 7.7 %collective-permute-start.20 = (bf16[2,256,256]{2,1,0:T(8,128)(2,1)S(1)}, bf16[2,256,256]{2,1,0:T(8,128)(2,1)}, u32[]{:S(2)}, u32[]{:S(2)}) collective-permute-start(bf16[2,256,256]{2,1,0:T(8,128)(2,1)S(1)} %collective-permute-done.12.refs_8_), channel_id=1, source_target_pairs={{0,8},{1,9},{2,10},{3,11},{4,12},{5,13},{6,14},{7,15},{8,0},{9,1},... | collective-permute-start | bytes 786440 | tf_op jit(solution)/shard_map/ppermute | solution.py:42
  74.6 8.4 %collective-permute-start.21 = (bf16[2,256,256]{2,1,0:T(8,128)(2,1)S(1)}, bf16[2,256,256]{2,1,0:T(8,128)(2,1)}, u32[]{:S(2)}, u32[]{:S(2)}) collective-permute-start(bf16[2,256,256]{2,1,0:T(8,128)(2,1)S(1)} %collective-permute-done.13.refs_9_), channel_id=1, source_target_pairs={{0,8},{1,9},{2,10},{3,11},{4,12},{5,13},{6,14},{7,15},{8,0},{9,1},... | collective-permute-start | bytes 786440 | tf_op jit(solution)/shard_map/ppermute | solution.py:42
  77.4 5.6 %collective-permute-start.22 = (bf16[2,256,256]{2,1,0:T(8,128)(2,1)S(1)}, bf16[2,256,256]{2,1,0:T(8,128)(2,1)}, u32[]{:S(2)}, u32[]{:S(2)}) collective-permute-start(bf16[2,256,256]{2,1,0:T(8,128)(2,1)S(1)} %collective-permute-done.14.refs_10_), channel_id=1, source_target_pairs={{0,8},{1,9},{2,10},{3,11},{4,12},{5,13},{6,14},{7,15},{8,0},{9,1},... | collective-permute-start | bytes 786440 | tf_op jit(solution)/shard_map/ppermute | solution.py:42
  79.3 3.7 %collective-permute-start.8 = (bf16[2,32,128]{2,1,0:T(8,128)(2,1)S(1)}, bf16[2,32,128]{2,1,0:T(8,128)(2,1)S(1)}, u32[]{:S(2)}, u32[]{:S(2)}) collective-permute-start(bf16[2,32,128]{2,1,0:T(8,128)(2,1)S(1)} %get-tuple-element.26), channel_id=1, source_target_pairs={{0,16},{1,17},{2,18},{3,19},{4,20},{5,21},{6,22},{7,23},{8,24},{9,... | collective-permute-start | bytes 49160 | tf_op jit(solution)/shard_map/ppermute | solution.py:42
  (25 other events, 242.4 us)

commit v4 on v3

--- a/solution.py
+++ b/solution.py
@@ -91,29 +91,40 @@
     return ar * br + ai * bi, ar * bi - ai * br
 
 
-def fetch_columns(object_ref, wide, sem, base, length):
+def fetch_columns(object_ref, wide, sems, base, length):
+    layers, _, rows, _ = wide.shape
     start = pl.multiple_of(base * length, length)
-    copy = pltpu.make_async_copy(object_ref.at[:, :, :, pl.ds(start, 2 * length)], wide, sem)
-    copy.start()
-    return copy
+    copies = []
+    for l in range(layers):
+        for q in range(2):
+            for h in range(2):
+                at = pl.ds(h * (rows // 2), rows // 2)
+                copy = pltpu.make_async_copy(
+                    object_ref.at[l, q, at, pl.ds(start, 2 * length)], wide.at[l, q, at], sems.at[l, q, h]
+                )
+                copy.start()
+                copies.append(copy)
+    return copies
 
 
 def pick_columns(wide, l, q, at, off, length):
     return jnp.where(lanes(length) >= off, wide[l, q, at, :length], wide[l, q, at, length:])
 
 
-def cut_kernel(sizes, info, object_ref, piece0, piece1, wide, sem):
+def pick_kernel(sizes, own, info, object_ref, out_ref, wide, sems):
     n_scan, _, tile_cols = sizes
-    _, rows, length = piece0.shape
+    layers, _, rows, length = out_ref.shape
     _, core, rank = place_of(n_scan)
-    _, _, _, col = live(info, 1 - core, rank, n_scan)
+    _, _, _, col = live(info, core if own else 1 - core, rank, n_scan)
     base, off = column_block(col, length, tile_cols)
-    fetch_columns(object_ref, wide, sem, base, length).wait()
-    for l, piece in enumerate((piece0, piece1)):
+    copies = fetch_columns(object_ref, wide, sems, base, length)
+    for l in range(layers):
         for q in range(2):
             for i in range(0, rows, STEP):
+                if i % (rows // 2) == 0:
+                    copies.pop(0).wait()
                 at = pl.ds(i, STEP)
-                piece[q, at, :] = pick_columns(wide, l, q, at, off, length).astype(piece.dtype)
+                out_ref[l, q, at, :] = pick_columns(wide, l, q, at, off, length).astype(out_ref.dtype)
 
 
 def choose_kernel(sizes, steps, info, *refs):
@@ -131,13 +142,12 @@
             copy.wait()
 
 
-def prep_kernel(sizes, info, object_ref, probe_ref, dft_ref, mats, p_ref, xo_ref, wide, sem):
+def prep_kernel(sizes, info, probe_ref, dft_ref, mats, p_ref):
     n_scan, _, tile_cols = sizes
     modes, _, length, _ = probe_ref.shape
     _, core, rank = place_of(n_scan)
     _, _, row, col = live(info, core, rank, n_scan)
-    base, off = column_block(col, length, tile_cols)
-    copy = fetch_columns(object_ref, wide, sem, base, length)
+    _, off = column_block(col, length, tile_cols)
     turn = lax.rem(off, length)
 
     def put(k, real, imag):
@@ -154,12 +164,6 @@
     for m in range(modes):
         for q in range(2):
             p_ref[m, q] = pltpu.roll(pltpu.roll(probe_ref[m, q], row, 0), turn, 1)
-    copy.wait()
-    for l in range(xo_ref.shape[0]):
-        for q in range(2):
-            for i in range(0, length, STEP):
-                at = pl.ds(i, STEP)
-                xo_ref[l, q, at, :] = pick_columns(wide, l, q, at, off, length)
 
 
 def put_v(v_ref, length, m, i, real, imag):
@@ -202,42 +206,41 @@
     return jnp.where(core == 0, row, 0), jnp.where(core == 0, length, row)
 
 
-def join(own, piece_ref, q, i, bounds, length):
-    piece = piece_ref[q, pl.ds(i, STEP), :].astype(jnp.float32)
-    line = lines(length)
-    return jnp.where((line >= bounds[0] - i) & (line < bounds[1] - i), own, piece)
-
-
-def first_kernel(sizes, info, mats, fresnel_ref, p_ref, xo_ref, piece, a_ref, x_ref, v_ref, u_ref, s_ref):
+def join(own, piece, i, bounds):
+    line = lines(own.shape[1])
+    return jnp.where((line >= bounds[0] - i) & (line < bounds[1] - i), own, piece.astype(jnp.float32))
+
+
+def pattern_kernel(
+    sizes, info, mats, fresnel_ref, p_ref, xo_ref, piece, meas_here, meas_sent,
+    grad_ref, keep_ref, give_ref, v_ref, u_ref, s_ref, x_ref, a_ref,
+):
+    n_scan, n_obj, tile_cols = sizes
     modes, _, length, _ = p_ref.shape
     bounds = own_rows(sizes, info, length)
+    chip, core, rank = place_of(n_scan)
+    chips = n_scan // CORES
+    _, _, row, col = live(info, core, rank, n_scan)
+    _, off = column_block(col, length, tile_cols)
+    for l in range(x_ref.shape[0]):
+        for q in range(2):
+            for i in range(0, length, STEP):
+                at = pl.ds(i, STEP)
+                x_ref[l, q, at, :] = join(xo_ref[l, q, at, :], piece[l, q, at, :], i, bounds)
     for i in range(0, length, STEP):
         at = pl.ds(i, STEP)
-        xr = join(xo_ref[0, 0, at, :], piece, 0, i, bounds, length)
-        xi = join(xo_ref[0, 1, at, :], piece, 1, i, bounds, length)
-        x_ref[0, at, :] = xr
-        x_ref[1, at, :] = xi
+        xr, xi = x_ref[0, 0, at, :], x_ref[0, 1, at, :]
         for m in range(modes):
             put_v(v_ref, length, m, i, *mul(p_ref[m, 0, at, :], p_ref[m, 1, at, :], xr, xi))
     propagate(mul, mats, fresnel_ref, v_ref, v_ref, u_ref, s_ref)
     for i in range(0, length, STEP):
         at = pl.ds(i, STEP)
+        xr, xi = x_ref[1, 0, at, :], x_ref[1, 1, at, :]
         for m in range(modes):
-            a_ref[m, 0, at, :], a_ref[m, 1, at, :] = get_s(s_ref, length, m, i)
-
-
-def second_kernel(sizes, info, mats, a_ref, xo_ref, piece, meas_here, meas_sent, grad_ref, v_out, v_ref, u_ref, s_ref, x_ref):
-    modes, _, length, _ = a_ref.shape
-    bounds = own_rows(sizes, info, length)
-    _, core, _ = place_of(sizes[0])
-    for i in range(0, length, STEP):
-        at = pl.ds(i, STEP)
-        xr = join(xo_ref[1, 0, at, :], piece, 0, i, bounds, length)
-        xi = join(xo_ref[1, 1, at, :], piece, 1, i, bounds, length)
-        x_ref[0, at, :] = xr
-        x_ref[1, at, :] = xi
-        for m in range(modes):
-            put_v(v_ref, length, m, i, *mul(a_ref[m, 0, at, :], a_ref[m, 1, at, :], xr, xi))
+            ar, ai = get_s(s_ref, length, m, i)
+            a_ref[m, 0, at, :] = ar
+            a_ref[m, 1, at, :] = ai
+            put_v(v_ref, length, m, i, *mul(ar, ai, xr, xi))
     transform(mats, 0, v_ref, u_ref, s_ref)
     for i in range(0, length, STEP):
         at = pl.ds(i, STEP)
@@ -257,19 +260,10 @@
             cr, ci = get_s(s_ref, length, m, i)
             dr, di = cmul(a_ref[m, 0, at, :], a_ref[m, 1, at, :], cr, ci)
             gr, gi = gr + dr, gi + di
-            put_v(v_out, length, m, i, *cmul(x_ref[0, at, :], x_ref[1, at, :], cr, ci))
-        grad_ref[0, at, :] = gr.astype(grad_ref.dtype)
-        grad_ref[1, at, :] = gi.astype(grad_ref.dtype)
-
-
-def third_kernel(sizes, info, mats, fresnel_ref, v_in, x_ref, p_ref, grad_ref, keep_ref, give_ref, v_ref, u_ref, s_ref, b_ref):
-    n_scan, n_obj, tile_cols = sizes
-    modes, _, length, _ = p_ref.shape
-    chip, core, rank = place_of(n_scan)
-    chips = n_scan // CORES
-    _, _, row, col = live(info, core, rank, n_scan)
-    _, off = column_block(col, length, tile_cols)
-    propagate(cmul, mats, fresnel_ref, v_in, v_ref, u_ref, s_ref)
+            put_v(v_ref, length, m, i, *cmul(x_ref[1, 0, at, :], x_ref[1, 1, at, :], cr, ci))
+        grad_ref[1, 0, at, :] = gr.astype(grad_ref.dtype)
+        grad_ref[1, 1, at, :] = gi.astype(grad_ref.dtype)
+    propagate(cmul, mats, fresnel_ref, v_ref, v_ref, u_ref, s_ref)
     for i in range(0, length, STEP):
         at = pl.ds(i, STEP)
         gr = gi = 0.0
@@ -277,20 +271,20 @@
             cr, ci = get_s(s_ref, length, m, i)
             dr, di = cmul(p_ref[m, 0, at, :], p_ref[m, 1, at, :], cr, ci)
             gr, gi = gr + dr, gi + di
-            b_ref[m, 0, at, :], b_ref[m, 1, at, :] = cmul(x_ref[0, at, :], x_ref[1, at, :], cr, ci)
-        grad_ref[0, at, :] = gr.astype(grad_ref.dtype)
-        grad_ref[1, at, :] = gi.astype(grad_ref.dtype)
+            a_ref[m, 0, at, :], a_ref[m, 1, at, :] = cmul(x_ref[0, 0, at, :], x_ref[0, 1, at, :], cr, ci)
+        grad_ref[0, 0, at, :] = gr.astype(grad_ref.dtype)
+        grad_ref[0, 1, at, :] = gi.astype(grad_ref.dtype)
     row_back = lax.rem(length - row, length)
     col_back = lax.rem(2 * length - off, length)
     per_row, per_col = length // n_obj, length // n_scan
     lane = lax.broadcasted_iota(jnp.int32, (length, 128), 1)
     for m in range(modes):
         for q in range(2):
-            b_ref[m, q] = pltpu.roll(pltpu.roll(b_ref[m, q], row_back, 0), col_back, 1)
+            a_ref[m, q] = pltpu.roll(pltpu.roll(a_ref[m, q], row_back, 0), col_back, 1)
         for s in range(n_scan):
             first, shift = s * per_col // 128 * 128, s * per_col % 128
-            real = b_ref[m, 0, :, first : first + 128]
-            imag = b_ref[m, 1, :, first : first + 128]
+            real = a_ref[m, 0, :, first : first + 128]
+            imag = a_ref[m, 1, :, first : first + 128]
             real = pltpu.roll(real, (128 - shift) % 128, 1) if shift else real
             imag = pltpu.roll(imag, (per_col - shift) % 128, 1) if shift != per_col else imag
             both = jnp.where(lane < per_col, real, imag)[:, : 2 * per_col]
@@ -311,7 +305,7 @@
     patches = refs[1 + chips : -4]
     out_ref, probe_out, held, sems = refs[-4:]
     _, _, rows, width = out_ref.shape
-    length = patches[0].shape[2]
+    length = patches[0].shape[3]
     me = lax.axis_index("scan")
     chip, core, _ = place_of(n_scan)
     blocks = width // length
@@ -326,7 +320,7 @@
         top, bottom = jnp.where(tile == OWN, row, 0), jnp.where(tile == OWN, rows, row)
         meets = (base + 1 >= first_block) & (base < first_block + blocks)
         copies = [
-            pltpu.make_async_copy(patches[index * layers + l], held.at[index, l], sems.at[index, l])
+            pltpu.make_async_copy(patches[index].at[l], held.at[index, l], sems.at[index, l])
             for l in range(layers)
         ]
         spots.append((base, off, top, bottom, meets, copies))
@@ -403,23 +397,21 @@
     both = jnp.concatenate([info, send(info, lambda s, o: (s, o + 1))])
     info = lax.all_to_all(jnp.broadcast_to(both, (n_scan, 1, 16)), "scan", 0, 0, tiled=True)
 
+    measured, info = lax.optimization_barrier((measured, info))
     steps = [(0, CORES * j) for j in range(chips)] + [(1, CORES * j) for j in range(chips)]
     gathered = [along(measured[0, 0], j) for j in range(chips)]
     gathered += [across(block) for block in gathered]
 
-    piece_shape = (2, length, length)
+    patch_shape = (layers, 2, length, length)
     field_shape = (modes, 2, length, length)
-    wide = [pltpu.VMEM((layers, 2, tile_rows, 2 * length), real), pltpu.SemaphoreType.DMA]
-    vus = [
-        pltpu.VMEM((2 * length, modes * length), half),
-        pltpu.VMEM((modes * length, 2 * length), half),
-        pltpu.VMEM((modes * length, 2 * length), real),
-    ]
-    pair_flops = 2 * 2 * modes * 8 * length**3
-    pieces = call(
-        (cut_kernel,), [(piece_shape, half)] * 2, [smem, hbm], wide, "cut", MIB, LARGE, info, object_slices
-    )
-    pieces = [outward(piece, -1) for piece in pieces]
+    wide = [pltpu.VMEM((layers, 2, tile_rows, 2 * length), real), pltpu.SemaphoreType.DMA((layers, 2, 2))]
+    (piece,) = call(
+        (pick_kernel, False), [(patch_shape, half)], [smem, hbm], wide, "cut", MIB, LARGE, info, object_slices
+    )
+    piece = outward(piece, -1)
+    (own_part,) = call(
+        (pick_kernel, True), [(patch_shape, real)], [smem, hbm], wide, "own", MIB, LARGE, info, object_slices
+    )
     (chosen,) = call(
         (choose_kernel, steps),
         [((length, length), measured.dtype)],
@@ -432,73 +424,46 @@
         *gathered,
     )
     passed = send(chosen, lambda s, o: (s, o + 1) if s % CORES else None)
-    mats, turned, own_part = call(
+    mats, turned = call(
         (prep_kernel,),
-        [((4, 2 * length, 2 * length), half), (field_shape, real), ((layers, *piece_shape), real)],
-        [smem, hbm, vmem, vmem],
-        wide,
+        [((4, 2 * length, 2 * length), half), (field_shape, real)],
+        [smem, vmem, vmem],
+        [],
         "prep",
         MIB,
-        LARGE,
+        SMALL,
         info,
-        object_slices,
         probe,
         dft_tables(length),
     )
-    fresnel = fresnel_tables(length)
-    arrived, patch = call(
-        (first_kernel,),
-        [(field_shape, real), (piece_shape, real)],
-        [smem] + [vmem] * 5,
-        vus,
-        "first",
-        pair_flops,
+    chunk_shape = (n_obj, chips, modes, length // n_obj, 2 * (length // n_scan))
+    grad, keep, give = call(
+        (pattern_kernel,),
+        [(patch_shape, half), (chunk_shape, half), (chunk_shape, half)],
+        [smem] + [vmem] * 7,
+        [
+            pltpu.VMEM((2 * length, modes * length), half),
+            pltpu.VMEM((modes * length, 2 * length), half),
+            pltpu.VMEM((modes * length, 2 * length), real),
+            pltpu.VMEM(patch_shape, real),
+            pltpu.VMEM(field_shape, real),
+        ],
+        "pattern",
+        3 * 2 * 2 * modes * 8 * length**3,
         SMALL,
         info,
         mats,
-        fresnel,
+        fresnel_tables(length),
         turned,
         own_part,
-        pieces[0],
-    )
-    grad1, carried = call(
-        (second_kernel,),
-        [(piece_shape, half), ((2 * length, modes * length), half)],
-        [smem] + [vmem] * 6,
-        vus + [pltpu.VMEM(piece_shape, real)],
-        "second",
-        pair_flops,
-        SMALL,
-        info,
-        mats,
-        arrived,
-        own_part,
-        pieces[1],
+        piece,
         chosen,
         passed,
     )
-    chunk_shape = (n_obj, chips, modes, length // n_obj, 2 * (length // n_scan))
-    grad0, keep, give = call(
-        (third_kernel,),
-        [(piece_shape, half), (chunk_shape, half), (chunk_shape, half)],
-        [smem] + [vmem] * 5,
-        vus + [pltpu.VMEM(field_shape, real)],
-        "third",
-        pair_flops,
-        SMALL,
-        info,
-        mats,
-        fresnel,
-        carried,
-        patch,
-        turned,
-    )
-
-    held = []
-    for grad in (grad0, grad1):
-        here = [along(grad, j) for j in range(chips)]
-        there = [outward(block, 1) for block in here]
-        held.append(here + there + [across(block) for block in here + there])
+
+    here = [along(grad, j) for j in range(chips)]
+    there = [outward(block, 1) for block in here]
+    held = here + there + [across(block) for block in here + there]
     kinds = [(kind, flip, jump) for flip in range(2) for kind in range(2) for jump in range(chips)]
     chunks = (keep.astype(real) + across(give).astype(real)).astype(half)
     chunks = lax.all_to_all(chunks, "obj", 0, 0, tiled=True)
@@ -511,9 +476,9 @@
             ((layers, 2, tile_rows, tile_cols // n_scan), real),
             ((modes, 2, length // n_obj, length // n_scan), real),
         ],
-        [smem] + [vmem] * chips + [hbm] * (2 * n_scan * layers),
+        [smem] + [vmem] * chips + [hbm] * (2 * n_scan),
         [
-            pltpu.VMEM((2 * n_scan, layers, *piece_shape), half),
+            pltpu.VMEM((2 * n_scan, layers, *patch_shape[1:]), half),
             pltpu.SemaphoreType.DMA((2 * n_scan, layers)),
         ],
         "place",
@@ -521,7 +486,7 @@
         LARGE,
         info,
         *shares,
-        *[held[l][index] for index in range(2 * n_scan) for l in range(layers)],
+        *held,
     )
     return (object_grad, probe_grad)
 

time: 88.1 us -> 82.5 us (0.936)
  waiting for transfers between devices: 22.4 us -> 27.8 us
  starting transfers between devices: 26.7 us -> 21.3 us
  local copies, waits for them, and re-layouts: 7.34 us -> 4.09 us
  Pallas kernels: 21.9 us -> 18.9 us
    ppermute x23 -> x15, starting transfers between devices: 22.2 us -> 14.3 us  [send(): return lax.ppermute(block, AXES, route)]
    ppermute x23 -> x15, waiting for transfers between devices: 22.4 us -> 27.8 us  [send(): return lax.ppermute(block, AXES, route)]
    unnamed x50 -> x34, local copies, waits for them, and re-layouts: 5.97 us -> 2.71 us
    pallas_call x7 -> x6, Pallas kernels: 21.9 us -> 18.9 us  [call(): pl.pallas_call(functools.partial(kernel[0], sizes, *kernel[1:]), out_shap...]
    all_to_all x1, starting transfers between devices: 4.48 us -> 6.93 us  [body(): chunks = lax.all_to_all(chunks, 'obj', 0, 0, tiled=True)]
  transfers between devices with their start and end apart: 24 -> 16, of which waited for: 7 -> 6; matrix products, arithmetic and copies ran while one was open for 3% -> 2% of each run, Pallas kernels for 14% -> 13%
where the time goes in v4:
time: 82.5 us; the launch traced here: 81.2 us
  waiting for transfers between devices  27.8 us (34%)
  starting transfers between devices  21.3 us (26%)
  Pallas kernels  18.9 us (23%)
  blocking collectives  6.55 us (8%)
  local copies, waits for them, and re-layouts  4.09 us (5%)
  between operations  1.53 us (2%)
  other arithmetic  1.04 us (1%)
    ppermute x15, waiting for transfers between devices, send(): return lax.ppermute(block, AXES, route)  27.8 us
    pallas_call x6, Pallas kernels, call(): pl.pallas_call(functools.partial(kernel[0], sizes, *kernel[1:]), out_shap...  18.9 us
    ppermute x15, starting transfers between devices, send(): return lax.ppermute(block, AXES, route)  14.3 us
    all_to_all x1, starting transfers between devices, body(): chunks = lax.all_to_all(chunks, 'obj', 0, 0, tiled=True)  6.93 us
    all_to_all x1, blocking collectives, body(): lax.all_to_all(jnp.broadcast_to(both, (n_scan, 1, 16)), 'scan', 0, 0, til...  6.55 us
    unnamed x34, local copies, waits for them, and re-layouts  2.71 us
  transfers between devices with their start and end apart: 16, of which 6 were waited for; matrix products, arithmetic and copies ran while one was open for 2% of the time, Pallas kernels for 13%

profile of v4, /device:TPU:0, one launch (start us, length us, event | category | flops | bytes accessed | tf_op | source)
XLA Modules:
  0.0 81.2 jit_solution(8570370812231837379)
XLA Ops:
  1.3 0.8 reshape_squeeze.3
  2.1 3.0 %collective-permute-start = (s32[8]{0:T(128)S(1)}, s32[8]{0:T(128)S(1)}, u32[]{:S(2)}, u32[]{:S(2)}) collective-permute-start(s32[8]{0:T(128)S(1)} %pad_add_fusion), channel_id=1, source_target_pairs={{0,1},{1,2},{2,3},{3,4},{4,5},{5,6},{6,7},{7,0},{8,9},{9,10},{10,1... | collective-permute-start | bytes 104 | tf_op jit(solution)/shard_map/ppermute | solution.py:42
  5.1 4.6 %collective-permute-done = s32[8]{0:T(128)S(1)} collective-permute-done((s32[8]{0:T(128)S(1)}, s32[8]{0:T(128)S(1)}, u32[]{:S(2)}, u32[]{:S(2)}) %collective-permute-start) | collective-permute-done | bytes 64 | tf_op jit(solution)/shard_map/ppermute | solution.py:42
  9.7 6.5 %all_to_all.10.info.refs_0_ = s32[4,1,16]{2,1,0:T(1,128)} all-to-all(s32[4,1,16]{2,1,0:T(1,128)S(1)} %broadcast_in_dim.3), channel_id=1, replica_groups=mesh['scan'=4,'obj'=8] {'scan'}, dimensions={0} | all-to-all | bytes 512 | tf_op jit(solution)/shard_map/all_to_all | solution.py:398
  16.5 3.1 %cut.1 = bf16[2,2,256,256]{3,2,1,0:T(8,128)(2,1)} custom-call(s32[4,1,16]{2,1,0:T(1,128)} %all_to_all.10.info.refs_0_, f32[2,2,256,2048]{3,2,1,0:T(8,128)} %object_ref.3), custom_call_target="tpu_custom_call" | custom-call | flops 1048576 | bytes 4194304 | tf_op jit(solution)/shard_map/cut/pallas_call | solution.py:376
  19.6 2.1 %collective-permute-start.1 = (bf16[2,2,256,256]{3,2,1,0:T(8,128)(2,1)}, bf16[2,2,256,256]{3,2,1,0:T(8,128)(2,1)S(1)}, u32[]{:S(2)}, u32[]{:S(2)}) collective-permute-start(bf16[2,2,256,256]{3,2,1,0:T(8,128)(2,1)} %cut.1), channel_id=1, source_target_pairs={{0,7},{1,0},{2,1},{3,2},{4,3},{5,4},{6,5},{7,6},{8,9},{9,10},{10,1... | collective-permute-start | bytes 1572872 | tf_op jit(solution)/shard_map/ppermute | solution.py:42
  21.7 3.0 %collective-permute-done.2.refs_1_ = bf16[2,256,256]{2,1,0:T(8,128)(2,1)S(1)} collective-permute-done((bf16[2,256,256]{2,1,0:T(8,128)(2,1)}, bf16[2,256,256]{2,1,0:T(8,128)(2,1)S(1)}, u32[]{:S(2)}, u32[]{:S(2)}) %collective-permute-start.2) | collective-permute-done | bytes 262176 | tf_op jit(solution)/shard_map/ppermute | solution.py:42
  24.7 1.5 %collective-permute-done.4.refs_3_ = bf16[2,256,256]{2,1,0:T(8,128)(2,1)S(1)} collective-permute-done((bf16[2,256,256]{2,1,0:T(8,128)(2,1)S(1)}, bf16[2,256,256]{2,1,0:T(8,128)(2,1)S(1)}, u32[]{:S(2)}, u32[]{:S(2)}) %collective-permute-start.4) | collective-permute-done | bytes 262176 | tf_op jit(solution)/shard_map/ppermute | solution.py:42
  26.9 2.3 %choose.1.meas_here = bf16[256,256]{1,0:T(8,128)(2,1)} custom-call(s32[4,1,16]{2,1,0:T(1,128)} %all_to_all.10.info.refs_0_, bf16[2,256,256]{2,1,0:T(8,128)(2,1)} %bitcast.9, bf16[2,256,256]{2,1,0:T(8,128)(2,1)} %copy-done.13, bf16[2,256,256]{2,1,0:T(8,128)(2,1)} %copy-done.14, bf16[2,256,256]{2,1,0:T(8,128)(2,1)} %copy-done.15), custom_call_target="tpu_custom_call" | custom-call | flops 1048576 | bytes 4194304 | tf_op jit(solution)/shard_map/choose/pallas_call | solution.py:376
  29.3 0.8 collective-permute-start.5
  30.1 3.3 %own.1.xo_ref = f32[2,2,256,256]{3,2,1,0:T(8,128)} custom-call(s32[4,1,16]{2,1,0:T(1,128)} %all_to_all.10.info.refs_0_, f32[2,2,256,2048]{3,2,1,0:T(8,128)} %object_ref.3), custom_call_target="tpu_custom_call" | custom-call | flops 1048576 | bytes 4194304 | tf_op jit(solution)/shard_map/own/pallas_call | solution.py:376
  33.4 1.5 %prep.1 = (bf16[4,512,512]{2,1,0:T(8,128)(2,1)S(1)}, f32[2,2,256,256]{3,2,1,0:T(8,128)S(1)}) custom-call(s32[4,1,16]{2,1,0:T(1,128)S(1)} %copy-done.5, f32[2,2,256,256]{3,2,1,0:T(8,128)S(1)} %copy-done.1, f32[2,256,256]{2,1,0:T(8,128)S(1)} %copy-done.2), custom_call_target="tpu_custom_call" | custom-call | flops 1048576 | bytes 4194304 | tf_op jit(solution)/shard_map/prep/pallas_call | solution.py:376
  35.0 1.2 %copy-done = f32[2,2,256,256]{3,2,1,0:T(8,128)S(1)} copy-done((f32[2,2,256,256]{3,2,1,0:T(8,128)S(1)}, f32[2,2,256,256]{3,2,1,0:T(8,128)}, u32[]{:S(2)}) %copy-start) | copy-done | bytes 1048600
  36.2 6.2 %pattern.1 = (bf16[2,2,256,256]{3,2,1,0:T(8,128)(2,1)S(1)}, bf16[8,2,2,32,128]{4,3,2,1,0:T(8,128)(2,1)S(1)}, bf16[8,2,2,32,128]{4,3,2,1,0:T(8,128)(2,1)S(1)}) custom-call(s32[4,1,16]{2,1,0:T(1,128)S(1)} %copy-done.5, bf16[4,512,512]{2,1,0:T(8,128)(2,1)S(1)} %get-tuple-element.10.mats, f32[2,256,256]{2,1,0:T(8,128)S(1)} %copy-done.6, ...), custom_call_target="tpu_custom_call" | custom-call | flops 3221225472 | bytes 4194304 | tf_op jit(solution)/shard_map/pattern/pallas_call | solution.py:376
  42.4 1.6 %collective-permute-start.8 = (bf16[2,2,256,256]{3,2,1,0:T(8,128)(2,1)S(1)}, bf16[2,2,256,256]{3,2,1,0:T(8,128)(2,1)S(1)}, u32[]{:S(2)}, u32[]{:S(2)}) collective-permute-start(bf16[2,2,256,256]{3,2,1,0:T(8,128)(2,1)S(1)} %get-tuple-element.15.refs_3_), channel_id=1, source_target_pairs={{0,16},{1,17},{2,18},{3,19},{4,20},{5,21},{6,22},{7,23},{8,24},{9,... | collective-permute-start | bytes 1572872 | tf_op jit(solution)/shard_map/ppermute | solution.py:42
  44.0 1.7 %collective-permute-start.6 = (bf16[8,2,2,32,128]{4,3,2,1,0:T(8,128)(2,1)S(1)}, bf16[8,2,2,32,128]{4,3,2,1,0:T(8,128)(2,1)S(1)}, u32[]{:S(2)}, u32[]{:S(2)}) collective-permute-start(bf16[8,2,2,32,128]{4,3,2,1,0:T(8,128)(2,1)S(1)} %get-tuple-element.14), channel_id=1, source_target_pairs={{0,8},{1,9},{2,10},{3,11},{4,12},{5,13},{6,14},{7,15},{8,0},{9,1},... | collective-permute-start | bytes 786440 | tf_op jit(solution)/shard_map/ppermute | solution.py:42
  45.7 9.5 %collective-permute-done.8.refs_4_ = bf16[2,2,256,256]{3,2,1,0:T(8,128)(2,1)S(1)} collective-permute-done((bf16[2,2,256,256]{3,2,1,0:T(8,128)(2,1)S(1)}, bf16[2,2,256,256]{3,2,1,0:T(8,128)(2,1)S(1)}, u32[]{:S(2)}, u32[]{:S(2)}) %collective-permute-start.8) | collective-permute-done | bytes 524320 | tf_op jit(solution)/shard_map/ppermute | solution.py:42
  55.3 0.8 %add_convert_fusion = bf16[8,2,2,32,128]{4,3,2,1,0:T(8,128)(2,1)} fusion(bf16[8,2,2,32,128]{4,3,2,1,0:T(8,128)(2,1)S(1)} %collective-permute-done.6, bf16[8,2,2,32,128]{4,3,2,1,0:T(8,128)(2,1)S(1)} %get-tuple-element.13), kind=kLoop, calls=%fused_computation | loop fusion | flops 524288 | bytes 786432 | tf_op jit(solution)/shard_map/convert_element_type | solution.py:468
  56.1 6.9 %all-to-all-start.1 = ((bf16[8,2,2,32,128]{4,3,2,1,0:T(8,128)(2,1)}), bf16[8,2,2,32,128]{4,3,2,1,0:T(8,128)(2,1)S(1)}, u32[]{:S(2)}, u32[]{:S(2)}) async-start(bf16[8,2,2,32,128]{4,3,2,1,0:T(8,128)(2,1)} %add_convert_fusion), calls=%async_computation.1 | async-start | bytes 524288 | tf_op jit(solution)/shard_map/all_to_all | solution.py:469
  63.9 7.0 %collective-permute-done.10.refs_6_ = bf16[2,2,256,256]{3,2,1,0:T(8,128)(2,1)S(1)} collective-permute-done((bf16[2,2,256,256]{3,2,1,0:T(8,128)(2,1)S(1)}, bf16[2,2,256,256]{3,2,1,0:T(8,128)(2,1)S(1)}, u32[]{:S(2)}, u32[]{:S(2)}) %collective-permute-start.10) | collective-permute-done | bytes 524320 | tf_op jit(solution)/shard_map/ppermute | solution.py:42
  70.9 2.6 %collective-permute-start.14 = (bf16[2,2,256,256]{3,2,1,0:T(8,128)(2,1)S(1)}, bf16[2,2,256,256]{3,2,1,0:T(8,128)(2,1)}, u32[]{:S(2)}, u32[]{:S(2)}) collective-permute-start(bf16[2,2,256,256]{3,2,1,0:T(8,128)(2,1)S(1)} %collective-permute-done.10.refs_6_), channel_id=1, source_target_pairs={{0,8},{1,9},{2,10},{3,11},{4,12},{5,13},{6,14},{7,15},{8,0},{9,1},... | collective-permute-start | bytes 1572872 | tf_op jit(solution)/shard_map/ppermute | solution.py:42
  74.1 1.5 %collective-permute-start.7 = (bf16[2,32,128]{2,1,0:T(8,128)(2,1)S(1)}, bf16[2,32,128]{2,1,0:T(8,128)(2,1)S(1)}, u32[]{:S(2)}, u32[]{:S(2)}) collective-permute-start(bf16[2,32,128]{2,1,0:T(8,128)(2,1)S(1)} %get-tuple-element.16), channel_id=1, source_target_pairs={{0,16},{1,17},{2,18},{3,19},{4,20},{5,21},{6,22},{7,23},{8,24},{9,... | collective-permute-start | bytes 49160 | tf_op jit(solution)/shard_map/ppermute | solution.py:42
  75.6 2.2 %collective-permute-done.7.refs_2_ = bf16[2,32,128]{2,1,0:T(8,128)(2,1)S(1)} collective-permute-done((bf16[2,32,128]{2,1,0:T(8,128)(2,1)S(1)}, bf16[2,32,128]{2,1,0:T(8,128)(2,1)S(1)}, u32[]{:S(2)}, u32[]{:S(2)}) %collective-permute-start.7) | collective-permute-done | bytes 16416 | tf_op jit(solution)/shard_map/ppermute | solution.py:42
  78.7 2.6 %place.1 = (f32[2,2,256,512]{3,2,1,0:T(8,128)}, f32[2,2,32,64]{3,2,1,0:T(8,128)}) custom-call(s32[4,1,16]{2,1,0:T(1,128)} %all_to_all.10.info.refs_0_, bf16[2,32,128]{2,1,0:T(8,128)(2,1)} %get-tuple-element.17.refs_1_, bf16[2,32,128]{2,1,0:T(8,128)(2,1)} %copy-done.16, bf16[2,2,256,256]{3,2,1,0:T(8,128)(2,1)} %copy-done.3, ...), custom_call_target="tpu_custom_call" | custom-call | flops 1048576 | bytes 4194304 | tf_op jit(solution)/shard_map/place/pallas_call | solution.py:376
  (57 shorter events, 3.4 us)
Async XLA Ops:
  2.1 7.5 %collective-permute-start = (s32[8]{0:T(128)S(1)}, s32[8]{0:T(128)S(1)}, u32[]{:S(2)}, u32[]{:S(2)}) collective-permute-start(s32[8]{0:T(128)S(1)} %pad_add_fusion), channel_id=1, source_target_pairs={{0,1},{1,2},{2,3},{3,4},{4,5},{5,6},{6,7},{7,0},{8,9},{9,10},{10,1... | collective-permute-start | bytes 104 | tf_op jit(solution)/shard_map/ppermute | solution.py:42
  16.3 5.4 %copy-start.12 = (bf16[1,1,2,256,256]{4,3,2,1,0:T(8,128)(2,1)S(1)}, bf16[1,1,2,256,256]{4,3,2,1,0:T(8,128)(2,1)}, u32[]{:S(2)}) copy-start(bf16[1,1,2,256,256]{4,3,2,1,0:T(8,128)(2,1)} %param.9) | copy-start | bytes 786436
  16.3 8.4 %collective-permute-start.2 = (bf16[2,256,256]{2,1,0:T(8,128)(2,1)}, bf16[2,256,256]{2,1,0:T(8,128)(2,1)S(1)}, u32[]{:S(2)}, u32[]{:S(2)}) collective-permute-start(bf16[2,256,256]{2,1,0:T(8,128)(2,1)} %bitcast.8), channel_id=1, source_target_pairs={{0,16},{1,17},{2,18},{3,19},{4,20},{5,21},{6,22},{7,23},{8,24},{9,... | collective-permute-start | bytes 786440 | tf_op jit(solution)/shard_map/ppermute | solution.py:42
  19.6 15.4 %collective-permute-start.1 = (bf16[2,2,256,256]{3,2,1,0:T(8,128)(2,1)}, bf16[2,2,256,256]{3,2,1,0:T(8,128)(2,1)S(1)}, u32[]{:S(2)}, u32[]{:S(2)}) collective-permute-start(bf16[2,2,256,256]{3,2,1,0:T(8,128)(2,1)} %cut.1), channel_id=1, source_target_pairs={{0,7},{1,0},{2,1},{3,2},{4,3},{5,4},{6,5},{7,6},{8,9},{9,10},{10,1... | collective-permute-start | bytes 1572872 | tf_op jit(solution)/shard_map/ppermute | solution.py:42
  21.7 3.0 %collective-permute-start.3 = (bf16[2,256,256]{2,1,0:T(8,128)(2,1)S(1)}, bf16[2,256,256]{2,1,0:T(8,128)(2,1)S(1)}, u32[]{:S(2)}, u32[]{:S(2)}) collective-permute-start(bf16[2,256,256]{2,1,0:T(8,128)(2,1)S(1)} %bitcast.10), channel_id=1, source_target_pairs={{0,8},{1,9},{2,10},{3,11},{4,12},{5,13},{6,14},{7,15},{8,0},{9,1},... | collective-permute-start | bytes 786440 | tf_op jit(solution)/shard_map/ppermute | solution.py:42
  24.7 1.5 %collective-permute-start.4 = (bf16[2,256,256]{2,1,0:T(8,128)(2,1)S(1)}, bf16[2,256,256]{2,1,0:T(8,128)(2,1)S(1)}, u32[]{:S(2)}, u32[]{:S(2)}) collective-permute-start(bf16[2,256,256]{2,1,0:T(8,128)(2,1)S(1)} %collective-permute-done.2.refs_1_), channel_id=1, source_target_pairs={{0,8},{1,9},{2,10},{3,11},{4,12},{5,13},{6,14},{7,15},{8,0},{9,1},... | collective-permute-start | bytes 786440 | tf_op jit(solution)/shard_map/ppermute | solution.py:42
  29.2 4.2 %copy-start.1 = (f32[2,2,256,256]{3,2,1,0:T(8,128)S(1)}, f32[2,2,256,256]{3,2,1,0:T(8,128)}, u32[]{:S(2)}) copy-start(f32[2,2,256,256]{3,2,1,0:T(8,128)} %probe_ref.1) | copy-start | bytes 3145732
  29.2 5.7 %copy-start.4 = (bf16[256,256]{1,0:T(8,128)(2,1)S(1)}, bf16[256,256]{1,0:T(8,128)(2,1)}, u32[]{:S(2)}) copy-start(bf16[256,256]{1,0:T(8,128)(2,1)} %choose.1.meas_here) | copy-start | bytes 393220
  29.3 5.7 %copy-start.6 = (f32[2,256,256]{2,1,0:T(8,128)S(1)}, f32[2,256,256]{2,1,0:T(8,128)}, u32[]{:S(2)}) copy-start(f32[2,256,256]{2,1,0:T(8,128)} %constant.10.clone.fresnel_ref) | copy-start | bytes 1572868
  29.3 5.7 %collective-permute-start.5 = (bf16[256,256]{1,0:T(8,128)(2,1)}, bf16[256,256]{1,0:T(8,128)(2,1)S(1)}, u32[]{:S(2)}, u32[]{:S(2)}) collective-permute-start(bf16[256,256]{1,0:T(8,128)(2,1)} %choose.1.meas_here), channel_id=1, source_target_pairs={{8,9},{9,10},{10,11},{11,12},{12,13},{13,14},{14,15},{15,8},{24,25... | collective-permute-start | bytes 393224 | tf_op jit(solution)/shard_map/ppermute | solution.py:42
  42.4 35.5 %copy-start.3 = (bf16[2,2,256,256]{3,2,1,0:T(8,128)(2,1)}, bf16[2,2,256,256]{3,2,1,0:T(8,128)(2,1)S(1)}, u32[]{:S(2)}) copy-start(bf16[2,2,256,256]{3,2,1,0:T(8,128)(2,1)S(1)} %get-tuple-element.15.refs_3_) | copy-start | bytes 1572868
  42.4 12.8 %collective-permute-start.8 = (bf16[2,2,256,256]{3,2,1,0:T(8,128)(2,1)S(1)}, bf16[2,2,256,256]{3,2,1,0:T(8,128)(2,1)S(1)}, u32[]{:S(2)}, u32[]{:S(2)}) collective-permute-start(bf16[2,2,256,256]{3,2,1,0:T(8,128)(2,1)S(1)} %get-tuple-element.15.refs_3_), channel_id=1, source_target_pairs={{0,16},{1,17},{2,18},{3,19},{4,20},{5,21},{6,22},{7,23},{8,24},{9,... | collective-permute-start | bytes 1572872 | tf_op jit(solution)/shard_map/ppermute | solution.py:42
  44.0 11.3 %collective-permute-start.6 = (bf16[8,2,2,32,128]{4,3,2,1,0:T(8,128)(2,1)S(1)}, bf16[8,2,2,32,128]{4,3,2,1,0:T(8,128)(2,1)S(1)}, u32[]{:S(2)}, u32[]{:S(2)}) collective-permute-start(bf16[8,2,2,32,128]{4,3,2,1,0:T(8,128)(2,1)S(1)} %get-tuple-element.14), channel_id=1, source_target_pairs={{0,8},{1,9},{2,10},{3,11},{4,12},{5,13},{6,14},{7,15},{8,0},{9,1},... | collective-permute-start | bytes 786440 | tf_op jit(solution)/shard_map/ppermute | solution.py:42
  45.7 17.8 %collective-permute-start.9 = (bf16[2,2,256,256]{3,2,1,0:T(8,128)(2,1)S(1)}, bf16[2,2,256,256]{3,2,1,0:T(8,128)(2,1)S(1)}, u32[]{:S(2)}, u32[]{:S(2)}) collective-permute-start(bf16[2,2,256,256]{3,2,1,0:T(8,128)(2,1)S(1)} %get-tuple-element.15.refs_3_), channel_id=1, source_target_pairs={{0,1},{1,2},{2,3},{3,4},{4,5},{5,6},{6,7},{7,0},{8,15},{9,8},{10,9... | collective-permute-start | bytes 1572872 | tf_op jit(solution)/shard_map/ppermute | solution.py:42
  55.2 22.7 %copy-start.7 = (bf16[2,2,256,256]{3,2,1,0:T(8,128)(2,1)}, bf16[2,2,256,256]{3,2,1,0:T(8,128)(2,1)S(1)}, u32[]{:S(2)}) copy-start(bf16[2,2,256,256]{3,2,1,0:T(8,128)(2,1)S(1)} %collective-permute-done.8.refs_4_) | copy-start | bytes 1572868
  55.2 15.7 %collective-permute-start.10 = (bf16[2,2,256,256]{3,2,1,0:T(8,128)(2,1)S(1)}, bf16[2,2,256,256]{3,2,1,0:T(8,128)(2,1)S(1)}, u32[]{:S(2)}, u32[]{:S(2)}) collective-permute-start(bf16[2,2,256,256]{3,2,1,0:T(8,128)(2,1)S(1)} %collective-permute-done.8.refs_4_), channel_id=1, source_target_pairs={{0,1},{1,2},{2,3},{3,4},{4,5},{5,6},{6,7},{7,0},{8,15},{9,8},{10,9... | collective-permute-start | bytes 1572872 | tf_op jit(solution)/shard_map/ppermute | solution.py:42
  56.1 17.4 %all-to-all-start.1 = ((bf16[8,2,2,32,128]{4,3,2,1,0:T(8,128)(2,1)}), bf16[8,2,2,32,128]{4,3,2,1,0:T(8,128)(2,1)S(1)}, u32[]{:S(2)}, u32[]{:S(2)}) async-start(bf16[8,2,2,32,128]{4,3,2,1,0:T(8,128)(2,1)} %add_convert_fusion), calls=%async_computation.1 | async-start | bytes 524288 | tf_op jit(solution)/shard_map/all_to_all | solution.py:469
  63.0 12.6 %collective-permute-start.11 = (bf16[2,2,256,256]{3,2,1,0:T(8,128)(2,1)S(1)}, bf16[2,2,256,256]{3,2,1,0:T(8,128)(2,1)S(1)}, u32[]{:S(2)}, u32[]{:S(2)}) collective-permute-start(bf16[2,2,256,256]{3,2,1,0:T(8,128)(2,1)S(1)} %get-tuple-element.15.refs_3_), channel_id=1, source_target_pairs={{0,8},{1,9},{2,10},{3,11},{4,12},{5,13},{6,14},{7,15},{8,0},{9,1},... | collective-permute-start | bytes 1572872 | tf_op jit(solution)/shard_map/ppermute | solution.py:42
  63.4 14.5 %collective-permute-start.12 = (bf16[2,2,256,256]{3,2,1,0:T(8,128)(2,1)S(1)}, bf16[2,2,256,256]{3,2,1,0:T(8,128)(2,1)S(1)}, u32[]{:S(2)}, u32[]{:S(2)}) collective-permute-start(bf16[2,2,256,256]{3,2,1,0:T(8,128)(2,1)S(1)} %collective-permute-done.8.refs_4_), channel_id=1, source_target_pairs={{0,8},{1,9},{2,10},{3,11},{4,12},{5,13},{6,14},{7,15},{8,0},{9,1},... | collective-permute-start | bytes 1572872 | tf_op jit(solution)/shard_map/ppermute | solution.py:42
  63.5 14.4 %copy-start.8 = (bf16[2,2,256,256]{3,2,1,0:T(8,128)(2,1)}, bf16[2,2,256,256]{3,2,1,0:T(8,128)(2,1)S(1)}, u32[]{:S(2)}) copy-start(bf16[2,2,256,256]{3,2,1,0:T(8,128)(2,1)S(1)} %collective-permute-done.9.refs_5_) | copy-start | bytes 1572868
  63.6 14.3 %collective-permute-start.13 = (bf16[2,2,256,256]{3,2,1,0:T(8,128)(2,1)S(1)}, bf16[2,2,256,256]{3,2,1,0:T(8,128)(2,1)}, u32[]{:S(2)}, u32[]{:S(2)}) collective-permute-start(bf16[2,2,256,256]{3,2,1,0:T(8,128)(2,1)S(1)} %collective-permute-done.9.refs_5_), channel_id=1, source_target_pairs={{0,8},{1,9},{2,10},{3,11},{4,12},{5,13},{6,14},{7,15},{8,0},{9,1},... | collective-permute-start | bytes 1572872 | tf_op jit(solution)/shard_map/ppermute | solution.py:42
  70.9 7.0 %copy-start.9 = (bf16[2,2,256,256]{3,2,1,0:T(8,128)(2,1)}, bf16[2,2,256,256]{3,2,1,0:T(8,128)(2,1)S(1)}, u32[]{:S(2)}) copy-start(bf16[2,2,256,256]{3,2,1,0:T(8,128)(2,1)S(1)} %collective-permute-done.10.refs_6_) | copy-start | bytes 1572868
  70.9 7.0 %collective-permute-start.14 = (bf16[2,2,256,256]{3,2,1,0:T(8,128)(2,1)S(1)}, bf16[2,2,256,256]{3,2,1,0:T(8,128)(2,1)}, u32[]{:S(2)}, u32[]{:S(2)}) collective-permute-start(bf16[2,2,256,256]{3,2,1,0:T(8,128)(2,1)S(1)} %collective-permute-done.10.refs_6_), channel_id=1, source_target_pairs={{0,8},{1,9},{2,10},{3,11},{4,12},{5,13},{6,14},{7,15},{8,0},{9,1},... | collective-permute-start | bytes 1572872 | tf_op jit(solution)/shard_map/ppermute | solution.py:42
  74.1 3.7 %collective-permute-start.7 = (bf16[2,32,128]{2,1,0:T(8,128)(2,1)S(1)}, bf16[2,32,128]{2,1,0:T(8,128)(2,1)S(1)}, u32[]{:S(2)}, u32[]{:S(2)}) collective-permute-start(bf16[2,32,128]{2,1,0:T(8,128)(2,1)S(1)} %get-tuple-element.16), channel_id=1, source_target_pairs={{0,16},{1,17},{2,18},{3,19},{4,20},{5,21},{6,22},{7,23},{8,24},{9,... | collective-permute-start | bytes 49160 | tf_op jit(solution)/shard_map/ppermute | solution.py:42
  (9 other events, 17.0 us)

commit v5 on v4

--- a/solution.py
+++ b/solution.py
@@ -13,7 +13,7 @@
 AXES = ("scan", "obj")
 CORES = 2
 MIB = 1 << 20
-SMALL, LARGE = 20, 58
+SMALL, LARGE = 20, 56
 
 
 def dft_tables(length):
@@ -399,8 +399,10 @@
 
     measured, info = lax.optimization_barrier((measured, info))
     steps = [(0, CORES * j) for j in range(chips)] + [(1, CORES * j) for j in range(chips)]
-    gathered = [along(measured[0, 0], j) for j in range(chips)]
-    gathered += [across(block) for block in gathered]
+    def shifted(block, flip, jump):
+        return send(block, lambda s, o: ((s ^ flip) + jump, o)) if flip or jump else block
+
+    gathered = [shifted(measured[0, 0], flip, jump) for flip, jump in steps]
 
     patch_shape = (layers, 2, length, length)
     field_shape = (modes, 2, length, length)
@@ -412,18 +414,6 @@
     (own_part,) = call(
         (pick_kernel, True), [(patch_shape, real)], [smem, hbm], wide, "own", MIB, LARGE, info, object_slices
     )
-    (chosen,) = call(
-        (choose_kernel, steps),
-        [((length, length), measured.dtype)],
-        [smem] + [hbm] * n_scan,
-        [pltpu.SemaphoreType.DMA],
-        "choose",
-        MIB,
-        LARGE,
-        info,
-        *gathered,
-    )
-    passed = send(chosen, lambda s, o: (s, o + 1) if s % CORES else None)
     mats, turned = call(
         (prep_kernel,),
         [((4, 2 * length, 2 * length), half), (field_shape, real)],
@@ -436,6 +426,19 @@
         probe,
         dft_tables(length),
     )
+    gathered, mats, own_part = lax.optimization_barrier((gathered, mats, own_part))
+    (chosen,) = call(
+        (choose_kernel, steps),
+        [((length, length), measured.dtype)],
+        [smem] + [hbm] * n_scan,
+        [pltpu.SemaphoreType.DMA],
+        "choose",
+        MIB,
+        LARGE,
+        info,
+        *gathered,
+    )
+    passed = send(chosen, lambda s, o: (s, o + 1) if s % CORES else None)
     chunk_shape = (n_obj, chips, modes, length // n_obj, 2 * (length // n_scan))
     grad, keep, give = call(
         (pattern_kernel,),
@@ -461,12 +464,13 @@
         passed,
     )
 
-    here = [along(grad, j) for j in range(chips)]
-    there = [outward(block, 1) for block in here]
+    here = [grad] + [along(grad, j) for j in range(1, chips)]
+    chunks = (keep.astype(real) + across(give).astype(real)).astype(half)
+    chunks = lax.all_to_all(chunks, "obj", 0, 0, tiled=True)
+    late, chunks = lax.optimization_barrier((here[1:], chunks))
+    there = [outward(block, 1) for block in here[:1] + late]
     held = here + there + [across(block) for block in here + there]
     kinds = [(kind, flip, jump) for flip in range(2) for kind in range(2) for jump in range(chips)]
-    chunks = (keep.astype(real) + across(give).astype(real)).astype(half)
-    chunks = lax.all_to_all(chunks, "obj", 0, 0, tiled=True)
     chunks = jnp.sum(chunks.astype(real), axis=0).astype(half)
     shares = [along(chunks[j], j) for j in range(chips)]
     factor = 1.0 / math.sqrt(n_scan * n_obj * slots // 2)

time: 82.5 us -> 96.6 us (1.17)
  starting transfers between devices: 21.3 us -> 32.9 us
  waiting for transfers between devices: 27.8 us -> 30 us
  Pallas kernels: 18.9 us -> 20.4 us
    ppermute x15, starting transfers between devices: 14.3 us -> 29.5 us  [send(): return lax.ppermute(block, AXES, route)]
    all_to_all x1, starting transfers between devices: 6.93 us -> 3.41 us  [body(): chunks = lax.all_to_all(chunks, 'obj', 0, 0, tiled=True)]
    all_to_all x1, waiting for transfers between devices: 0.01 us -> 1.63 us  [body(): chunks = lax.all_to_all(chunks, 'obj', 0, 0, tiled=True)]
    pallas_call x6, Pallas kernels: 18.9 us -> 20.4 us  [call(): pl.pallas_call(functools.partial(kernel[0], sizes, *kernel[1:]), out_shap...]
    unnamed x34 -> x36, local copies, waits for them, and re-layouts: 2.71 us -> 2.37 us
  transfers between devices with their start and end apart: 16 -> 16, of which waited for: 6 -> 8; matrix products, arithmetic and copies ran while one was open for 2% -> 1% of each run, Pallas kernels for 13% -> 7%
where the time goes in v5:
time: 96.6 us; the launch traced here: 96.2 us
  starting transfers between devices  32.9 us (34%)
  waiting for transfers between devices  30 us (31%)
  Pallas kernels  20.4 us (21%)
  blocking collectives  6.56 us (7%)
  local copies, waits for them, and re-layouts  3.74 us (4%)
  between operations  1.53 us (2%)
  other arithmetic  0.98 us (1%)
    ppermute x15, starting transfers between devices, send(): return lax.ppermute(block, AXES, route)  29.5 us
    ppermute x15, waiting for transfers between devices, send(): return lax.ppermute(block, AXES, route)  28.4 us
    pallas_call x6, Pallas kernels, call(): pl.pallas_call(functools.partial(kernel[0], sizes, *kernel[1:]), out_shap...  20.4 us
    all_to_all x1, blocking collectives, body(): lax.all_to_all(jnp.broadcast_to(both, (n_scan, 1, 16)), 'scan', 0, 0, til...  6.56 us
    all_to_all x1, starting transfers between devices, body(): chunks = lax.all_to_all(chunks, 'obj', 0, 0, tiled=True)  3.41 us
    unnamed x36, local copies, waits for them, and re-layouts  2.37 us
  transfers between devices with their start and end apart: 16, of which 8 were waited for; matrix products, arithmetic and copies ran while one was open for 1% of the time, Pallas kernels for 7%

profile of v5, /device:TPU:0, one launch (start us, length us, event | category | flops | bytes accessed | tf_op | source)
XLA Modules:
  0.0 96.2 jit_solution(6635465236475678223)
XLA Ops:
  2.1 3.0 %collective-permute-start = (s32[8]{0:T(128)S(1)}, s32[8]{0:T(128)S(1)}, u32[]{:S(2)}, u32[]{:S(2)}) collective-permute-start(s32[8]{0:T(128)S(1)} %pad_add_fusion), channel_id=1, source_target_pairs={{0,1},{1,2},{2,3},{3,4},{4,5},{5,6},{6,7},{7,0},{8,9},{9,10},{10,1... | collective-permute-start | bytes 104 | tf_op jit(solution)/shard_map/ppermute | solution.py:42
  5.1 4.6 %collective-permute-done = s32[8]{0:T(128)S(1)} collective-permute-done((s32[8]{0:T(128)S(1)}, s32[8]{0:T(128)S(1)}, u32[]{:S(2)}, u32[]{:S(2)}) %collective-permute-start) | collective-permute-done | bytes 64 | tf_op jit(solution)/shard_map/ppermute | solution.py:42
  9.7 6.6 %all_to_all.10.info.refs_0_ = s32[4,1,16]{2,1,0:T(1,128)} all-to-all(s32[4,1,16]{2,1,0:T(1,128)S(1)} %broadcast_in_dim.3), channel_id=1, replica_groups=mesh['scan'=4,'obj'=8] {'scan'}, dimensions={0} | all-to-all | bytes 512 | tf_op jit(solution)/shard_map/all_to_all | solution.py:398
  16.3 3.2 %cut.1 = bf16[2,2,256,256]{3,2,1,0:T(8,128)(2,1)} custom-call(s32[4,1,16]{2,1,0:T(1,128)} %all_to_all.10.info.refs_0_, f32[2,2,256,2048]{3,2,1,0:T(8,128)} %object_ref.3), custom_call_target="tpu_custom_call" | custom-call | flops 1048576 | bytes 4194304 | tf_op jit(solution)/shard_map/cut/pallas_call | solution.py:376
  19.5 2.1 %collective-permute-start.4 = (bf16[2,2,256,256]{3,2,1,0:T(8,128)(2,1)}, bf16[2,2,256,256]{3,2,1,0:T(8,128)(2,1)S(1)}, u32[]{:S(2)}, u32[]{:S(2)}) collective-permute-start(bf16[2,2,256,256]{3,2,1,0:T(8,128)(2,1)} %cut.1), channel_id=1, source_target_pairs={{0,7},{1,0},{2,1},{3,2},{4,3},{5,4},{6,5},{7,6},{8,9},{9,10},{10,1... | collective-permute-start | bytes 1572872 | tf_op jit(solution)/shard_map/ppermute | solution.py:42
  22.0 1.8 %collective-permute-start.1 = (bf16[2,256,256]{2,1,0:T(8,128)(2,1)S(1)}, bf16[2,256,256]{2,1,0:T(8,128)(2,1)S(1)}, u32[]{:S(2)}, u32[]{:S(2)}) collective-permute-start(bf16[2,256,256]{2,1,0:T(8,128)(2,1)S(1)} %bitcast.11), channel_id=1, source_target_pairs={{0,16},{1,17},{2,18},{3,19},{4,20},{5,21},{6,22},{7,23},{8,24},{9,... | collective-permute-start | bytes 786440 | tf_op jit(solution)/shard_map/ppermute | solution.py:42
  23.8 3.3 %own.1.xo_ref = f32[2,2,256,256]{3,2,1,0:T(8,128)} custom-call(s32[4,1,16]{2,1,0:T(1,128)} %all_to_all.10.info.refs_0_, f32[2,2,256,2048]{3,2,1,0:T(8,128)} %object_ref.3), custom_call_target="tpu_custom_call" | custom-call | flops 1048576 | bytes 4194304 | tf_op jit(solution)/shard_map/own/pallas_call | solution.py:376
  27.2 1.5 %prep.1 = (bf16[4,512,512]{2,1,0:T(8,128)(2,1)S(1)}, f32[2,2,256,256]{3,2,1,0:T(8,128)S(1)}) custom-call(s32[4,1,16]{2,1,0:T(1,128)S(1)} %copy-done.5, f32[2,2,256,256]{3,2,1,0:T(8,128)S(1)} %copy-done.1, f32[2,256,256]{2,1,0:T(8,128)S(1)} %copy-done.2), custom_call_target="tpu_custom_call" | custom-call | flops 1048576 | bytes 4194304 | tf_op jit(solution)/shard_map/prep/pallas_call | solution.py:376
  28.7 1.6 %collective-permute-done.3.refs_3_ = bf16[2,256,256]{2,1,0:T(8,128)(2,1)S(1)} collective-permute-done((bf16[2,256,256]{2,1,0:T(8,128)(2,1)S(1)}, bf16[2,256,256]{2,1,0:T(8,128)(2,1)S(1)}, u32[]{:S(2)}, u32[]{:S(2)}) %collective-permute-start.3) | collective-permute-done | bytes 262176 | tf_op jit(solution)/shard_map/ppermute | solution.py:42
  30.3 3.3 %collective-permute-done.1.refs_1_ = bf16[2,256,256]{2,1,0:T(8,128)(2,1)S(1)} collective-permute-done((bf16[2,256,256]{2,1,0:T(8,128)(2,1)S(1)}, bf16[2,256,256]{2,1,0:T(8,128)(2,1)S(1)}, u32[]{:S(2)}, u32[]{:S(2)}) %collective-permute-start.1) | collective-permute-done | bytes 262176 | tf_op jit(solution)/shard_map/ppermute | solution.py:42
  34.3 2.3 %choose.1.meas_here = bf16[256,256]{1,0:T(8,128)(2,1)} custom-call(s32[4,1,16]{2,1,0:T(1,128)} %all_to_all.10.info.refs_0_, bf16[2,256,256]{2,1,0:T(8,128)(2,1)} %bitcast.8, bf16[2,256,256]{2,1,0:T(8,128)(2,1)} %copy-done.16, bf16[2,256,256]{2,1,0:T(8,128)(2,1)} %copy-done.15, bf16[2,256,256]{2,1,0:T(8,128)(2,1)} %copy-done.14), custom_call_target="tpu_custom_call" | custom-call | flops 1048576 | bytes 4194304 | tf_op jit(solution)/shard_map/choose/pallas_call | solution.py:376
  38.2 6.2 %pattern.1 = (bf16[2,2,256,256]{3,2,1,0:T(8,128)(2,1)S(1)}, bf16[8,2,2,32,128]{4,3,2,1,0:T(8,128)(2,1)S(1)}, bf16[8,2,2,32,128]{4,3,2,1,0:T(8,128)(2,1)S(1)}) custom-call(s32[4,1,16]{2,1,0:T(1,128)S(1)} %copy-done.6, bf16[4,512,512]{2,1,0:T(8,128)(2,1)S(1)} %get-tuple-element.20.mats, f32[2,256,256]{2,1,0:T(8,128)S(1)} %copy-done.7, ...), custom_call_target="tpu_custom_call" | custom-call | flops 3221225472 | bytes 4194304 | tf_op jit(solution)/shard_map/pattern/pallas_call | solution.py:376
  44.4 9.1 %collective-permute-start.7 = (bf16[8,2,2,32,128]{4,3,2,1,0:T(8,128)(2,1)S(1)}, bf16[8,2,2,32,128]{4,3,2,1,0:T(8,128)(2,1)S(1)}, u32[]{:S(2)}, u32[]{:S(2)}) collective-permute-start(bf16[8,2,2,32,128]{4,3,2,1,0:T(8,128)(2,1)S(1)} %get-tuple-element.29), channel_id=1, source_target_pairs={{0,8},{1,9},{2,10},{3,11},{4,12},{5,13},{6,14},{7,15},{8,0},{9,1},... | collective-permute-start | bytes 786440 | tf_op jit(solution)/shard_map/ppermute | solution.py:42
  53.5 1.2 %collective-permute-start.6 = (bf16[2,2,256,256]{3,2,1,0:T(8,128)(2,1)S(1)}, bf16[2,2,256,256]{3,2,1,0:T(8,128)(2,1)S(1)}, u32[]{:S(2)}, u32[]{:S(2)}) collective-permute-start(bf16[2,2,256,256]{3,2,1,0:T(8,128)(2,1)S(1)} %get-tuple-element.27.refs_3_), channel_id=1, source_target_pairs={{0,16},{1,17},{2,18},{3,19},{4,20},{5,21},{6,22},{7,23},{8,24},{9,... | collective-permute-start | bytes 1572872 | tf_op jit(solution)/shard_map/ppermute | solution.py:42
  55.5 3.4 %all-to-all-start.1 = ((bf16[8,2,2,32,128]{4,3,2,1,0:T(8,128)(2,1)}), bf16[8,2,2,32,128]{4,3,2,1,0:T(8,128)(2,1)S(1)}, u32[]{:S(2)}, u32[]{:S(2)}) async-start(bf16[8,2,2,32,128]{4,3,2,1,0:T(8,128)(2,1)} %add_convert_fusion), calls=%async_computation.1 | async-start | bytes 524288 | tf_op jit(solution)/shard_map/all_to_all | solution.py:469
  58.9 1.9 %collective-permute-start.9 = (bf16[2,2,256,256]{3,2,1,0:T(8,128)(2,1)S(1)}, bf16[2,2,256,256]{3,2,1,0:T(8,128)(2,1)S(1)}, u32[]{:S(2)}, u32[]{:S(2)}) collective-permute-start(bf16[2,2,256,256]{3,2,1,0:T(8,128)(2,1)S(1)} %get-tuple-element.27.refs_3_), channel_id=1, source_target_pairs={{0,1},{1,2},{2,3},{3,4},{4,5},{5,6},{6,7},{7,0},{8,15},{9,8},{10,9... | collective-permute-start | bytes 1572872 | tf_op jit(solution)/shard_map/ppermute | solution.py:42
  60.8 6.6 %collective-permute-done.6.refs_4_ = bf16[2,2,256,256]{3,2,1,0:T(8,128)(2,1)S(1)} collective-permute-done((bf16[2,2,256,256]{3,2,1,0:T(8,128)(2,1)S(1)}, bf16[2,2,256,256]{3,2,1,0:T(8,128)(2,1)S(1)}, u32[]{:S(2)}, u32[]{:S(2)}) %collective-permute-start.6) | collective-permute-done | bytes 524320 | tf_op jit(solution)/shard_map/ppermute | solution.py:42
  67.4 1.6 %all-to-all-done.1 = bf16[8,2,2,32,128]{4,3,2,1,0:T(8,128)(2,1)S(1)} async-done(((bf16[8,2,2,32,128]{4,3,2,1,0:T(8,128)(2,1)}), bf16[8,2,2,32,128]{4,3,2,1,0:T(8,128)(2,1)S(1)}, u32[]{:S(2)}, u32[]{:S(2)}) %all-to-all-start.1) | async-done | bytes 262176 | tf_op jit(solution)/shard_map/all_to_all | solution.py:469
  69.0 6.5 %collective-permute-start.10 = (bf16[2,2,256,256]{3,2,1,0:T(8,128)(2,1)S(1)}, bf16[2,2,256,256]{3,2,1,0:T(8,128)(2,1)S(1)}, u32[]{:S(2)}, u32[]{:S(2)}) collective-permute-start(bf16[2,2,256,256]{3,2,1,0:T(8,128)(2,1)S(1)} %collective-permute-done.6.refs_4_), channel_id=1, source_target_pairs={{0,1},{1,2},{2,3},{3,4},{4,5},{5,6},{6,7},{7,0},{8,15},{9,8},{10,9... | collective-permute-start | bytes 1572872 | tf_op jit(solution)/shard_map/ppermute | solution.py:42
  76.1 4.2 %collective-permute-done.9.refs_5_ = bf16[2,2,256,256]{3,2,1,0:T(8,128)(2,1)S(1)} collective-permute-done((bf16[2,2,256,256]{3,2,1,0:T(8,128)(2,1)S(1)}, bf16[2,2,256,256]{3,2,1,0:T(8,128)(2,1)S(1)}, u32[]{:S(2)}, u32[]{:S(2)}) %collective-permute-start.9) | collective-permute-done | bytes 524320 | tf_op jit(solution)/shard_map/ppermute | solution.py:42
  80.2 5.6 %collective-permute-done.10.refs_6_ = bf16[2,2,256,256]{3,2,1,0:T(8,128)(2,1)S(1)} collective-permute-done((bf16[2,2,256,256]{3,2,1,0:T(8,128)(2,1)S(1)}, bf16[2,2,256,256]{3,2,1,0:T(8,128)(2,1)S(1)}, u32[]{:S(2)}, u32[]{:S(2)}) %collective-permute-start.10) | collective-permute-done | bytes 524320 | tf_op jit(solution)/shard_map/ppermute | solution.py:42
  85.8 1.2 %collective-permute-start.14 = (bf16[2,2,256,256]{3,2,1,0:T(8,128)(2,1)S(1)}, bf16[2,2,256,256]{3,2,1,0:T(8,128)(2,1)}, u32[]{:S(2)}, u32[]{:S(2)}) collective-permute-start(bf16[2,2,256,256]{3,2,1,0:T(8,128)(2,1)S(1)} %collective-permute-done.10.refs_6_), channel_id=1, source_target_pairs={{0,8},{1,9},{2,10},{3,11},{4,12},{5,13},{6,14},{7,15},{8,0},{9,1},... | collective-permute-start | bytes 1572872 | tf_op jit(solution)/shard_map/ppermute | solution.py:42
  88.9 2.6 %collective-permute-done.8.refs_2_ = bf16[2,32,128]{2,1,0:T(8,128)(2,1)S(1)} collective-permute-done((bf16[2,32,128]{2,1,0:T(8,128)(2,1)S(1)}, bf16[2,32,128]{2,1,0:T(8,128)(2,1)S(1)}, u32[]{:S(2)}, u32[]{:S(2)}) %collective-permute-start.8) | collective-permute-done | bytes 16416 | tf_op jit(solution)/shard_map/ppermute | solution.py:42
  92.2 3.9 %place.1 = (f32[2,2,256,512]{3,2,1,0:T(8,128)}, f32[2,2,32,64]{3,2,1,0:T(8,128)}) custom-call(s32[4,1,16]{2,1,0:T(1,128)} %all_to_all.10.info.refs_0_, bf16[2,32,128]{2,1,0:T(8,128)(2,1)} %get-tuple-element.33.refs_1_, bf16[2,32,128]{2,1,0:T(8,128)(2,1)} %copy-done.17, bf16[2,2,256,256]{3,2,1,0:T(8,128)(2,1)} %copy-done.3, ...), custom_call_target="tpu_custom_call" | custom-call | flops 1048576 | bytes 4194304 | tf_op jit(solution)/shard_map/place/pallas_call | solution.py:376
  (59 shorter events, 7.5 us)
Async XLA Ops:
  2.1 7.5 %collective-permute-start = (s32[8]{0:T(128)S(1)}, s32[8]{0:T(128)S(1)}, u32[]{:S(2)}, u32[]{:S(2)}) collective-permute-start(s32[8]{0:T(128)S(1)} %pad_add_fusion), channel_id=1, source_target_pairs={{0,1},{1,2},{2,3},{3,4},{4,5},{5,6},{6,7},{7,0},{8,9},{9,10},{10,1... | collective-permute-start | bytes 104 | tf_op jit(solution)/shard_map/ppermute | solution.py:42
  19.5 17.8 %collective-permute-start.4 = (bf16[2,2,256,256]{3,2,1,0:T(8,128)(2,1)}, bf16[2,2,256,256]{3,2,1,0:T(8,128)(2,1)S(1)}, u32[]{:S(2)}, u32[]{:S(2)}) collective-permute-start(bf16[2,2,256,256]{3,2,1,0:T(8,128)(2,1)} %cut.1), channel_id=1, source_target_pairs={{0,7},{1,0},{2,1},{3,2},{4,3},{5,4},{6,5},{7,6},{8,9},{9,10},{10,1... | collective-permute-start | bytes 1572872 | tf_op jit(solution)/shard_map/ppermute | solution.py:42
  21.6 5.5 %copy-start.5 = (s32[4,1,16]{2,1,0:T(1,128)S(1)}, s32[4,1,16]{2,1,0:T(1,128)}, u32[]{:S(2)}) copy-start(s32[4,1,16]{2,1,0:T(1,128)} %all_to_all.10.info.refs_0_) | copy-start | bytes 772
  21.6 8.7 %collective-permute-start.3 = (bf16[2,256,256]{2,1,0:T(8,128)(2,1)S(1)}, bf16[2,256,256]{2,1,0:T(8,128)(2,1)S(1)}, u32[]{:S(2)}, u32[]{:S(2)}) collective-permute-start(bf16[2,256,256]{2,1,0:T(8,128)(2,1)S(1)} %bitcast.9), channel_id=1, source_target_pairs={{0,24},{1,25},{2,26},{3,27},{4,28},{5,29},{6,30},{7,31},{8,16},{9,... | collective-permute-start | bytes 786440 | tf_op jit(solution)/shard_map/ppermute | solution.py:42
  21.7 8.6 %collective-permute-start.2 = (bf16[2,256,256]{2,1,0:T(8,128)(2,1)S(1)}, bf16[2,256,256]{2,1,0:T(8,128)(2,1)S(1)}, u32[]{:S(2)}, u32[]{:S(2)}) collective-permute-start(bf16[2,256,256]{2,1,0:T(8,128)(2,1)S(1)} %bitcast.10), channel_id=1, source_target_pairs={{0,8},{1,9},{2,10},{3,11},{4,12},{5,13},{6,14},{7,15},{8,0},{9,1},... | collective-permute-start | bytes 786440 | tf_op jit(solution)/shard_map/ppermute | solution.py:42
  22.0 11.6 %collective-permute-start.1 = (bf16[2,256,256]{2,1,0:T(8,128)(2,1)S(1)}, bf16[2,256,256]{2,1,0:T(8,128)(2,1)S(1)}, u32[]{:S(2)}, u32[]{:S(2)}) collective-permute-start(bf16[2,256,256]{2,1,0:T(8,128)(2,1)S(1)} %bitcast.11), channel_id=1, source_target_pairs={{0,16},{1,17},{2,18},{3,19},{4,20},{5,21},{6,22},{7,23},{8,24},{9,... | collective-permute-start | bytes 786440 | tf_op jit(solution)/shard_map/ppermute | solution.py:42
  27.1 10.1 %copy-start = (f32[2,2,256,256]{3,2,1,0:T(8,128)S(1)}, f32[2,2,256,256]{3,2,1,0:T(8,128)}, u32[]{:S(2)}) copy-start(f32[2,2,256,256]{3,2,1,0:T(8,128)} %own.1.xo_ref) | copy-start | bytes 3145732
  27.2 10.1 %copy-start.6 = (s32[4,1,16]{2,1,0:T(1,128)S(1)}, s32[4,1,16]{2,1,0:T(1,128)}, u32[]{:S(2)}) copy-start(s32[4,1,16]{2,1,0:T(1,128)} %all_to_all.10.info.refs_0_) | copy-start | bytes 772
  27.2 10.1 %copy-start.7 = (f32[2,256,256]{2,1,0:T(8,128)S(1)}, f32[2,256,256]{2,1,0:T(8,128)}, u32[]{:S(2)}) copy-start(f32[2,256,256]{2,1,0:T(8,128)} %constant.10.clone.fresnel_ref) | copy-start | bytes 1572868
  36.6 0.7 collective-permute-start.5
  44.4 47.1 %copy-start.3 = (bf16[2,2,256,256]{3,2,1,0:T(8,128)(2,1)}, bf16[2,2,256,256]{3,2,1,0:T(8,128)(2,1)S(1)}, u32[]{:S(2)}) copy-start(bf16[2,2,256,256]{3,2,1,0:T(8,128)(2,1)S(1)} %get-tuple-element.27.refs_3_) | copy-start | bytes 1572868
  44.4 10.3 %collective-permute-start.7 = (bf16[8,2,2,32,128]{4,3,2,1,0:T(8,128)(2,1)S(1)}, bf16[8,2,2,32,128]{4,3,2,1,0:T(8,128)(2,1)S(1)}, u32[]{:S(2)}, u32[]{:S(2)}) collective-permute-start(bf16[8,2,2,32,128]{4,3,2,1,0:T(8,128)(2,1)S(1)} %get-tuple-element.29), channel_id=1, source_target_pairs={{0,8},{1,9},{2,10},{3,11},{4,12},{5,13},{6,14},{7,15},{8,0},{9,1},... | collective-permute-start | bytes 786440 | tf_op jit(solution)/shard_map/ppermute | solution.py:42
  53.5 13.9 %collective-permute-start.6 = (bf16[2,2,256,256]{3,2,1,0:T(8,128)(2,1)S(1)}, bf16[2,2,256,256]{3,2,1,0:T(8,128)(2,1)S(1)}, u32[]{:S(2)}, u32[]{:S(2)}) collective-permute-start(bf16[2,2,256,256]{3,2,1,0:T(8,128)(2,1)S(1)} %get-tuple-element.27.refs_3_), channel_id=1, source_target_pairs={{0,16},{1,17},{2,18},{3,19},{4,20},{5,21},{6,22},{7,23},{8,24},{9,... | collective-permute-start | bytes 1572872 | tf_op jit(solution)/shard_map/ppermute | solution.py:42
  55.5 13.6 %all-to-all-start.1 = ((bf16[8,2,2,32,128]{4,3,2,1,0:T(8,128)(2,1)}), bf16[8,2,2,32,128]{4,3,2,1,0:T(8,128)(2,1)S(1)}, u32[]{:S(2)}, u32[]{:S(2)}) async-start(bf16[8,2,2,32,128]{4,3,2,1,0:T(8,128)(2,1)} %add_convert_fusion), calls=%async_computation.1 | async-start | bytes 524288 | tf_op jit(solution)/shard_map/all_to_all | solution.py:469
  58.9 21.3 %collective-permute-start.9 = (bf16[2,2,256,256]{3,2,1,0:T(8,128)(2,1)S(1)}, bf16[2,2,256,256]{3,2,1,0:T(8,128)(2,1)S(1)}, u32[]{:S(2)}, u32[]{:S(2)}) collective-permute-start(bf16[2,2,256,256]{3,2,1,0:T(8,128)(2,1)S(1)} %get-tuple-element.27.refs_3_), channel_id=1, source_target_pairs={{0,1},{1,2},{2,3},{3,4},{4,5},{5,6},{6,7},{7,0},{8,15},{9,8},{10,9... | collective-permute-start | bytes 1572872 | tf_op jit(solution)/shard_map/ppermute | solution.py:42
  67.4 24.1 %copy-start.8 = (bf16[2,2,256,256]{3,2,1,0:T(8,128)(2,1)}, bf16[2,2,256,256]{3,2,1,0:T(8,128)(2,1)S(1)}, u32[]{:S(2)}) copy-start(bf16[2,2,256,256]{3,2,1,0:T(8,128)(2,1)S(1)} %collective-permute-done.6.refs_4_) | copy-start | bytes 1572868
  69.0 16.8 %collective-permute-start.10 = (bf16[2,2,256,256]{3,2,1,0:T(8,128)(2,1)S(1)}, bf16[2,2,256,256]{3,2,1,0:T(8,128)(2,1)S(1)}, u32[]{:S(2)}, u32[]{:S(2)}) collective-permute-start(bf16[2,2,256,256]{3,2,1,0:T(8,128)(2,1)S(1)} %collective-permute-done.6.refs_4_), channel_id=1, source_target_pairs={{0,1},{1,2},{2,3},{3,4},{4,5},{5,6},{6,7},{7,0},{8,15},{9,8},{10,9... | collective-permute-start | bytes 1572872 | tf_op jit(solution)/shard_map/ppermute | solution.py:42
  75.5 13.3 %collective-permute-start.11 = (bf16[2,2,256,256]{3,2,1,0:T(8,128)(2,1)S(1)}, bf16[2,2,256,256]{3,2,1,0:T(8,128)(2,1)S(1)}, u32[]{:S(2)}, u32[]{:S(2)}) collective-permute-start(bf16[2,2,256,256]{3,2,1,0:T(8,128)(2,1)S(1)} %get-tuple-element.27.refs_3_), channel_id=1, source_target_pairs={{0,8},{1,9},{2,10},{3,11},{4,12},{5,13},{6,14},{7,15},{8,0},{9,1},... | collective-permute-start | bytes 1572872 | tf_op jit(solution)/shard_map/ppermute | solution.py:42
  75.6 15.9 %collective-permute-start.12 = (bf16[2,2,256,256]{3,2,1,0:T(8,128)(2,1)S(1)}, bf16[2,2,256,256]{3,2,1,0:T(8,128)(2,1)S(1)}, u32[]{:S(2)}, u32[]{:S(2)}) collective-permute-start(bf16[2,2,256,256]{3,2,1,0:T(8,128)(2,1)S(1)} %collective-permute-done.6.refs_4_), channel_id=1, source_target_pairs={{0,8},{1,9},{2,10},{3,11},{4,12},{5,13},{6,14},{7,15},{8,0},{9,1},... | collective-permute-start | bytes 1572872 | tf_op jit(solution)/shard_map/ppermute | solution.py:42
  80.2 11.2 %copy-start.9 = (bf16[2,2,256,256]{3,2,1,0:T(8,128)(2,1)}, bf16[2,2,256,256]{3,2,1,0:T(8,128)(2,1)S(1)}, u32[]{:S(2)}) copy-start(bf16[2,2,256,256]{3,2,1,0:T(8,128)(2,1)S(1)} %collective-permute-done.9.refs_5_) | copy-start | bytes 1572868
  80.2 11.2 %collective-permute-start.13 = (bf16[2,2,256,256]{3,2,1,0:T(8,128)(2,1)S(1)}, bf16[2,2,256,256]{3,2,1,0:T(8,128)(2,1)}, u32[]{:S(2)}, u32[]{:S(2)}) collective-permute-start(bf16[2,2,256,256]{3,2,1,0:T(8,128)(2,1)S(1)} %collective-permute-done.9.refs_5_), channel_id=1, source_target_pairs={{0,8},{1,9},{2,10},{3,11},{4,12},{5,13},{6,14},{7,15},{8,0},{9,1},... | collective-permute-start | bytes 1572872 | tf_op jit(solution)/shard_map/ppermute | solution.py:42
  85.8 5.6 %copy-start.10 = (bf16[2,2,256,256]{3,2,1,0:T(8,128)(2,1)}, bf16[2,2,256,256]{3,2,1,0:T(8,128)(2,1)S(1)}, u32[]{:S(2)}) copy-start(bf16[2,2,256,256]{3,2,1,0:T(8,128)(2,1)S(1)} %collective-permute-done.10.refs_6_) | copy-start | bytes 1572868
  85.8 5.6 %collective-permute-start.14 = (bf16[2,2,256,256]{3,2,1,0:T(8,128)(2,1)S(1)}, bf16[2,2,256,256]{3,2,1,0:T(8,128)(2,1)}, u32[]{:S(2)}, u32[]{:S(2)}) collective-permute-start(bf16[2,2,256,256]{3,2,1,0:T(8,128)(2,1)S(1)} %collective-permute-done.10.refs_6_), channel_id=1, source_target_pairs={{0,8},{1,9},{2,10},{3,11},{4,12},{5,13},{6,14},{7,15},{8,0},{9,1},... | collective-permute-start | bytes 1572872 | tf_op jit(solution)/shard_map/ppermute | solution.py:42
  87.7 3.7 %collective-permute-start.8 = (bf16[2,32,128]{2,1,0:T(8,128)(2,1)S(1)}, bf16[2,32,128]{2,1,0:T(8,128)(2,1)S(1)}, u32[]{:S(2)}, u32[]{:S(2)}) collective-permute-start(bf16[2,32,128]{2,1,0:T(8,128)(2,1)S(1)} %get-tuple-element.32), channel_id=1, source_target_pairs={{0,16},{1,17},{2,18},{3,19},{4,20},{5,21},{6,22},{7,23},{8,24},{9,... | collective-permute-start | bytes 49160 | tf_op jit(solution)/shard_map/ppermute | solution.py:42
  (10 other events, 28.6 us)

commit v6 on v5

--- a/solution.py
+++ b/solution.py
@@ -45,26 +45,23 @@
 OWN, PREVIOUS = 0, 1
 
 
-def live(info, tile, rank, n_scan):
+def assigned(info, tile, target, n_scan):
     def entry(a, j):
         return info[a, 0, 8 * tile + j]
 
-    source, slot = jnp.int32(0), jnp.int32(0)
-    before = jnp.int32(0)
+    idle = entry(target, 0) == 0
+    counts = [entry(a, 0) for a in range(n_scan)]
+    rank = jnp.int32(0)
     for a in range(n_scan):
-        count = entry(a, 0)
-        here = (rank >= before) & (rank < before + count)
-        source = jnp.where(here, a, source)
-        slot = jnp.where(here, rank - before, slot)
-        before += count
+        rank += jnp.where((counts[a] == 0) & (a < target), 1, 0)
+    source = jnp.int32(target)
+    seen = jnp.int32(0)
+    for a in range(n_scan):
+        full = counts[a] == 2
+        source = jnp.where(idle & full & (seen == rank), a, source)
+        seen += jnp.where(full, 1, 0)
+    slot = jnp.where(idle, 1, 0)
     return source, slot, entry(source, 1 + 2 * slot), entry(source, 2 + 2 * slot)
-
-
-def place_of(n_scan):
-    me = lax.axis_index("scan")
-    core = lax.rem(me, CORES)
-    chip = lax.div(me, CORES)
-    return chip, core, chip + core * (n_scan // CORES)
 
 
 def column_block(col, length, tile_cols):
@@ -114,8 +111,7 @@
 def pick_kernel(sizes, own, info, object_ref, out_ref, wide, sems):
     n_scan, _, tile_cols = sizes
     layers, _, rows, length = out_ref.shape
-    _, core, rank = place_of(n_scan)
-    _, _, _, col = live(info, core if own else 1 - core, rank, n_scan)
+    _, _, _, col = assigned(info, OWN if own else PREVIOUS, lax.axis_index("scan"), n_scan)
     base, off = column_block(col, length, tile_cols)
     copies = fetch_columns(object_ref, wide, sems, base, length)
     for l in range(layers):
@@ -127,26 +123,10 @@
                 out_ref[l, q, at, :] = pick_columns(wide, l, q, at, off, length).astype(out_ref.dtype)
 
 
-def choose_kernel(sizes, steps, info, *refs):
-    n_scan, _, _ = sizes
-    sources = refs[:n_scan]
-    out_ref, sem = refs[n_scan:]
-    me = lax.axis_index("scan")
-    _, _, rank = place_of(n_scan)
-    source, slot, _, _ = live(info, OWN, rank, n_scan)
-    for (flip, jump), candidate in zip(steps, sources):
-        @pl.when(source == lax.rem((me ^ flip) - jump + n_scan, n_scan))
-        def _():
-            copy = pltpu.make_async_copy(candidate.at[slot], out_ref, sem)
-            copy.start()
-            copy.wait()
-
-
 def prep_kernel(sizes, info, probe_ref, dft_ref, mats, p_ref):
     n_scan, _, tile_cols = sizes
     modes, _, length, _ = probe_ref.shape
-    _, core, rank = place_of(n_scan)
-    _, _, row, col = live(info, core, rank, n_scan)
+    _, _, row, col = assigned(info, OWN, lax.axis_index("scan"), n_scan)
     _, off = column_block(col, length, tile_cols)
     turn = lax.rem(off, length)
 
@@ -199,34 +179,35 @@
     transform(mats, 1, v_ref, u_ref, s_ref)
 
 
-def own_rows(sizes, info, length):
-    n_scan, _, _ = sizes
-    _, core, rank = place_of(n_scan)
-    _, _, row, _ = live(info, core, rank, n_scan)
-    return jnp.where(core == 0, row, 0), jnp.where(core == 0, length, row)
-
-
-def join(own, piece, i, bounds):
-    line = lines(own.shape[1])
-    return jnp.where((line >= bounds[0] - i) & (line < bounds[1] - i), own, piece.astype(jnp.float32))
-
-
-def pattern_kernel(
-    sizes, info, mats, fresnel_ref, p_ref, xo_ref, piece, meas_here, meas_sent,
-    grad_ref, keep_ref, give_ref, v_ref, u_ref, s_ref, x_ref, a_ref,
-):
+def join(own, piece, i, row):
+    return jnp.where(lines(own.shape[1]) >= row - i, own, piece.astype(jnp.float32))
+
+
+def pattern_kernel(sizes, *refs):
     n_scan, n_obj, tile_cols = sizes
+    info, mats, fresnel_ref, p_ref, xo_ref, piece, own_ref = refs[:7]
+    others = refs[7 : 6 + n_scan]
+    grad_ref, keep_ref, give_ref, v_ref, u_ref, s_ref, x_ref, a_ref, meas_ref = refs[6 + n_scan :]
     modes, _, length, _ = p_ref.shape
-    bounds = own_rows(sizes, info, length)
-    chip, core, rank = place_of(n_scan)
-    chips = n_scan // CORES
-    _, _, row, col = live(info, core, rank, n_scan)
+    me = lax.axis_index("scan")
+    core, chip, chips = lax.rem(me, CORES), lax.div(me, CORES), n_scan // CORES
+    source, slot, row, col = assigned(info, OWN, me, n_scan)
     _, off = column_block(col, length, tile_cols)
+
+    @pl.when(slot == 0)
+    def _():
+        meas_ref[...] = own_ref[0]
+
+    for k in range(1, n_scan):
+        @pl.when((slot == 1) & (source == lax.rem(me - k + n_scan, n_scan)))
+        def _():
+            meas_ref[...] = others[k - 1][...]
+
     for l in range(x_ref.shape[0]):
         for q in range(2):
             for i in range(0, length, STEP):
                 at = pl.ds(i, STEP)
-                x_ref[l, q, at, :] = join(xo_ref[l, q, at, :], piece[l, q, at, :], i, bounds)
+                x_ref[l, q, at, :] = join(xo_ref[l, q, at, :], piece[l, q, at, :], i, row)
     for i in range(0, length, STEP):
         at = pl.ds(i, STEP)
         xr, xi = x_ref[0, 0, at, :], x_ref[0, 1, at, :]
@@ -243,9 +224,7 @@
             put_v(v_ref, length, m, i, *mul(ar, ai, xr, xi))
     transform(mats, 0, v_ref, u_ref, s_ref)
     for i in range(0, length, STEP):
-        at = pl.ds(i, STEP)
-        here, sent = meas_here[at, :].astype(jnp.float32), meas_sent[at, :].astype(jnp.float32)
-        misfit = -jnp.where(core == 0, here, sent)
+        misfit = -meas_ref[pl.ds(i, STEP), :].astype(jnp.float32)
         for m in range(modes):
             fr, fi = get_s(s_ref, length, m, i)
             misfit += fr * fr + fi * fi
@@ -296,7 +275,7 @@
                         ref[o, apart, m] = both[o * per_row : (o + 1) * per_row].astype(ref.dtype)
 
 
-def place_kernel(sizes, kinds, factor, *refs):
+def place_kernel(sizes, kinds, parts, factor, *refs):
     n_scan, _, tile_cols = sizes
     chips = n_scan // CORES
     layers = refs[-4].shape[0]
@@ -305,23 +284,22 @@
     patches = refs[1 + chips : -4]
     out_ref, probe_out, held, sems = refs[-4:]
     _, _, rows, width = out_ref.shape
-    length = patches[0].shape[3]
+    length = patches[0].shape[-1]
     me = lax.axis_index("scan")
-    chip, core, _ = place_of(n_scan)
     blocks = width // length
     first_block = me * blocks
     spots = []
-    for index, (kind, flip, jump) in enumerate(kinds):
-        other = core ^ flip
-        tile = other ^ kind
-        rank = lax.rem(chip - jump + chips, chips) + other * chips
-        _, _, row, col = live(info, tile, rank, n_scan)
+    for index, (tile, flip, jump) in enumerate(kinds):
+        source = lax.rem((me ^ flip) - CORES * jump + n_scan, n_scan)
+        _, _, row, col = assigned(info, tile, source, n_scan)
         base, off = column_block(col, length, tile_cols)
-        top, bottom = jnp.where(tile == OWN, row, 0), jnp.where(tile == OWN, rows, row)
+        top, bottom = (row, rows) if tile == OWN else (0, row)
         meets = (base + 1 >= first_block) & (base < first_block + blocks)
         copies = [
-            pltpu.make_async_copy(patches[index].at[l], held.at[index, l], sems.at[index, l])
-            for l in range(layers)
+            pltpu.make_async_copy(
+                patches[number] if part is None else patches[number].at[part], held.at[index, l], sems.at[index, l]
+            )
+            for l, (number, part) in enumerate(parts[index])
         ]
         spots.append((base, off, top, bottom, meets, copies))
 
@@ -391,18 +369,15 @@
         return send(block, lambda s, o: (s + CORES * jump, o)) if jump else block
 
     def outward(block, sign):
-        return send(block, lambda s, o: (s, o + (sign if s % CORES == 0 else -sign)))
+        return send(block, lambda s, o: (s, o + sign))
 
     info = jnp.concatenate([counts[0], positions[0, 0].reshape(-1), jnp.zeros((3,), jnp.int32)])
     both = jnp.concatenate([info, send(info, lambda s, o: (s, o + 1))])
     info = lax.all_to_all(jnp.broadcast_to(both, (n_scan, 1, 16)), "scan", 0, 0, tiled=True)
 
     measured, info = lax.optimization_barrier((measured, info))
-    steps = [(0, CORES * j) for j in range(chips)] + [(1, CORES * j) for j in range(chips)]
-    def shifted(block, flip, jump):
-        return send(block, lambda s, o: ((s ^ flip) + jump, o)) if flip or jump else block
-
-    gathered = [shifted(measured[0, 0], flip, jump) for flip, jump in steps]
+    second = measured[0, 0, 1]
+    others = [send(second, lambda s, o, k=k: (s + k, o)) for k in range(1, n_scan)]
 
     patch_shape = (layers, 2, length, length)
     field_shape = (modes, 2, length, length)
@@ -426,30 +401,18 @@
         probe,
         dft_tables(length),
     )
-    gathered, mats, own_part = lax.optimization_barrier((gathered, mats, own_part))
-    (chosen,) = call(
-        (choose_kernel, steps),
-        [((length, length), measured.dtype)],
-        [smem] + [hbm] * n_scan,
-        [pltpu.SemaphoreType.DMA],
-        "choose",
-        MIB,
-        LARGE,
-        info,
-        *gathered,
-    )
-    passed = send(chosen, lambda s, o: (s, o + 1) if s % CORES else None)
     chunk_shape = (n_obj, chips, modes, length // n_obj, 2 * (length // n_scan))
     grad, keep, give = call(
         (pattern_kernel,),
         [(patch_shape, half), (chunk_shape, half), (chunk_shape, half)],
-        [smem] + [vmem] * 7,
+        [smem] + [vmem] * (5 + n_scan),
         [
             pltpu.VMEM((2 * length, modes * length), half),
             pltpu.VMEM((modes * length, 2 * length), half),
             pltpu.VMEM((modes * length, 2 * length), real),
             pltpu.VMEM(patch_shape, real),
             pltpu.VMEM(field_shape, real),
+            pltpu.VMEM((length, length), measured.dtype),
         ],
         "pattern",
         3 * 2 * 2 * modes * 8 * length**3,
@@ -460,27 +423,41 @@
         turned,
         own_part,
         piece,
-        chosen,
-        passed,
+        measured[0, 0],
+        *others,
     )
 
     here = [grad] + [along(grad, j) for j in range(1, chips)]
     chunks = (keep.astype(real) + across(give).astype(real)).astype(half)
+    first, chunks = lax.optimization_barrier((grad, chunks))
+    there = outward(first, 1)
+    x_first = [outward(block[1], 1) for block in here[1:]]
+    obj_first = [along(there[0], j) for j in range(1, chips)]
+    held = here + [there] + x_first + obj_first
+    held += [across(block) for block in held]
+    kinds, parts = [], []
+    for flip in range(2):
+        start = flip * (len(held) // 2)
+        for j in range(chips):
+            kinds.append((OWN, flip, j))
+            parts.append([(start + j, l) for l in range(layers)])
+        for j in range(chips):
+            kinds.append((PREVIOUS, flip, j))
+            if j == 0:
+                parts.append([(start + chips, l) for l in range(layers)])
+            else:
+                parts.append([(start + 2 * chips - 1 + j, None), (start + chips + j, None)])
     chunks = lax.all_to_all(chunks, "obj", 0, 0, tiled=True)
-    late, chunks = lax.optimization_barrier((here[1:], chunks))
-    there = [outward(block, 1) for block in here[:1] + late]
-    held = here + there + [across(block) for block in here + there]
-    kinds = [(kind, flip, jump) for flip in range(2) for kind in range(2) for jump in range(chips)]
     chunks = jnp.sum(chunks.astype(real), axis=0).astype(half)
     shares = [along(chunks[j], j) for j in range(chips)]
     factor = 1.0 / math.sqrt(n_scan * n_obj * slots // 2)
     object_grad, probe_grad = call(
-        (place_kernel, kinds, factor),
+        (place_kernel, kinds, parts, factor),
         [
             ((layers, 2, tile_rows, tile_cols // n_scan), real),
             ((modes, 2, length // n_obj, length // n_scan), real),
         ],
-        [smem] + [vmem] * chips + [hbm] * (2 * n_scan),
+        [smem] + [vmem] * chips + [hbm] * len(held),
         [
             pltpu.VMEM((2 * n_scan, layers, *patch_shape[1:]), half),
             pltpu.SemaphoreType.DMA((2 * n_scan, layers)),

time: 96.6 us -> 80.6 us (0.83)
  starting transfers between devices: 32.9 us -> 14.9 us
  waiting for transfers between devices: 30 us -> 34.2 us
  Pallas kernels: 20.4 us -> 18.2 us
    ppermute x15 -> x16, starting transfers between devices: 29.5 us -> 8.43 us  [send(): return lax.ppermute(block, AXES, route)]
    ppermute x15 -> x16, waiting for transfers between devices: 28.4 us -> 34.2 us  [send(): return lax.ppermute(block, AXES, route)]
    all_to_all x1, starting transfers between devices: 3.41 us -> 6.43 us  [body(): chunks = lax.all_to_all(chunks, 'obj', 0, 0, tiled=True)]
    pallas_call x6 -> x5, Pallas kernels: 20.4 us -> 18.2 us  [call(): pl.pallas_call(functools.partial(kernel[0], sizes, *kernel[1:]), out_shap...]
    all_to_all x1, waiting for transfers between devices: 1.63 us -> 0.01 us  [body(): chunks = lax.all_to_all(chunks, 'obj', 0, 0, tiled=True)]
    unnamed x36 -> x26, local copies, waits for them, and re-layouts: 2.37 us -> 2.19 us
  transfers between devices with their start and end apart: 16 -> 17, of which waited for: 8 -> 9; matrix products, arithmetic and copies ran while one was open for 1% -> 2% of each run, Pallas kernels for 7% -> 6%
where the time goes in v6:
time: 80.6 us; the launch traced here: 80.2 us
  waiting for transfers between devices  34.2 us (42%)
  Pallas kernels  18.2 us (23%)
  starting transfers between devices  14.9 us (18%)
  blocking collectives  6.75 us (8%)
  local copies, waits for them, and re-layouts  3.6 us (4%)
  between operations  1.51 us (2%)
  other arithmetic  0.98 us (1%)
    ppermute x16, waiting for transfers between devices, send(): return lax.ppermute(block, AXES, route)  34.2 us
    pallas_call x5, Pallas kernels, call(): pl.pallas_call(functools.partial(kernel[0], sizes, *kernel[1:]), out_shap...  18.2 us
    ppermute x16, starting transfers between devices, send(): return lax.ppermute(block, AXES, route)  8.43 us
    all_to_all x1, blocking collectives, body(): lax.all_to_all(jnp.broadcast_to(both, (n_scan, 1, 16)), 'scan', 0, 0, til...  6.75 us
    all_to_all x1, starting transfers between devices, body(): chunks = lax.all_to_all(chunks, 'obj', 0, 0, tiled=True)  6.43 us
    unnamed x26, local copies, waits for them, and re-layouts  2.19 us
  transfers between devices with their start and end apart: 17, of which 9 were waited for; matrix products, arithmetic and copies ran while one was open for 2% of the time, Pallas kernels for 6%

profile of v6, /device:TPU:0, one launch (start us, length us, event | category | flops | bytes accessed | tf_op | source)
XLA Modules:
  0.0 80.2 jit_solution(1033020146252751303)
XLA Ops:
  1.3 0.8 reshape_squeeze.3
  2.1 3.0 %collective-permute-start = (s32[8]{0:T(128)S(1)}, s32[8]{0:T(128)S(1)}, u32[]{:S(2)}, u32[]{:S(2)}) collective-permute-start(s32[8]{0:T(128)S(1)} %pad_add_fusion), channel_id=1, source_target_pairs={{0,1},{1,2},{2,3},{3,4},{4,5},{5,6},{6,7},{7,0},{8,9},{9,10},{10,1... | collective-permute-start | bytes 104 | tf_op jit(solution)/shard_map/ppermute | solution.py:42
  5.1 4.6 %collective-permute-done = s32[8]{0:T(128)S(1)} collective-permute-done((s32[8]{0:T(128)S(1)}, s32[8]{0:T(128)S(1)}, u32[]{:S(2)}, u32[]{:S(2)}) %collective-permute-start) | collective-permute-done | bytes 64 | tf_op jit(solution)/shard_map/ppermute | solution.py:42
  9.7 6.8 %all_to_all.10.info.refs_0_ = s32[4,1,16]{2,1,0:T(1,128)} all-to-all(s32[4,1,16]{2,1,0:T(1,128)S(1)} %broadcast_in_dim.3), channel_id=1, replica_groups=mesh['scan'=4,'obj'=8] {'scan'}, dimensions={0} | all-to-all | bytes 512 | tf_op jit(solution)/shard_map/all_to_all | solution.py:376
  16.5 3.3 %cut.1 = bf16[2,2,256,256]{3,2,1,0:T(8,128)(2,1)} custom-call(s32[4,1,16]{2,1,0:T(1,128)} %all_to_all.10.info.refs_0_, f32[2,2,256,2048]{3,2,1,0:T(8,128)} %object_ref.3), custom_call_target="tpu_custom_call" | custom-call | flops 1048576 | bytes 4194304 | tf_op jit(solution)/shard_map/cut/pallas_call | solution.py:354
  19.7 2.1 %collective-permute-start.1 = (bf16[2,2,256,256]{3,2,1,0:T(8,128)(2,1)}, bf16[2,2,256,256]{3,2,1,0:T(8,128)(2,1)S(1)}, u32[]{:S(2)}, u32[]{:S(2)}) collective-permute-start(bf16[2,2,256,256]{3,2,1,0:T(8,128)(2,1)} %cut.1), channel_id=1, source_target_pairs={{0,7},{1,0},{2,1},{3,2},{4,3},{5,4},{6,5},{7,6},{8,15},{9,8},{10,9... | collective-permute-start | bytes 1572872 | tf_op jit(solution)/shard_map/ppermute | solution.py:42
  21.9 1.0 %collective-permute-start.3 = (bf16[256,256]{1,0:T(8,128)(2,1)S(1)}, bf16[256,256]{1,0:T(8,128)(2,1)S(1)}, u32[]{:S(2)}, u32[]{:S(2)}) collective-permute-start(bf16[256,256]{1,0:T(8,128)(2,1)S(1)} %slice_bitcast_fusion.2), channel_id=1, source_target_pairs={{0,16},{1,17},{2,18},{3,19},{4,20},{5,21},{6,22},{7,23},{8,24},{9,... | collective-permute-start | bytes 393224 | tf_op jit(solution)/shard_map/ppermute | solution.py:42
  23.0 3.3 %own.1.refs_4_ = f32[2,2,256,256]{3,2,1,0:T(8,128)} custom-call(s32[4,1,16]{2,1,0:T(1,128)} %all_to_all.10.info.refs_0_, f32[2,2,256,2048]{3,2,1,0:T(8,128)} %object_ref.3), custom_call_target="tpu_custom_call" | custom-call | flops 1048576 | bytes 4194304 | tf_op jit(solution)/shard_map/own/pallas_call | solution.py:354
  26.3 1.5 %prep.1 = (bf16[4,512,512]{2,1,0:T(8,128)(2,1)S(1)}, f32[2,2,256,256]{3,2,1,0:T(8,128)S(1)}) custom-call(s32[4,1,16]{2,1,0:T(1,128)S(1)} %copy-done.5, f32[2,2,256,256]{3,2,1,0:T(8,128)S(1)} %copy-done.1, f32[2,256,256]{2,1,0:T(8,128)S(1)} %copy-done.2), custom_call_target="tpu_custom_call" | custom-call | flops 1048576 | bytes 4194304 | tf_op jit(solution)/shard_map/prep/pallas_call | solution.py:354
  27.8 1.8 %collective-permute-done.3.refs_8_ = bf16[256,256]{1,0:T(8,128)(2,1)S(1)} collective-permute-done((bf16[256,256]{1,0:T(8,128)(2,1)S(1)}, bf16[256,256]{1,0:T(8,128)(2,1)S(1)}, u32[]{:S(2)}, u32[]{:S(2)}) %collective-permute-start.3) | collective-permute-done | bytes 131104 | tf_op jit(solution)/shard_map/ppermute | solution.py:42
  30.1 3.4 %collective-permute-done.1.refs_5_ = bf16[2,2,256,256]{3,2,1,0:T(8,128)(2,1)S(1)} collective-permute-done((bf16[2,2,256,256]{3,2,1,0:T(8,128)(2,1)}, bf16[2,2,256,256]{3,2,1,0:T(8,128)(2,1)S(1)}, u32[]{:S(2)}, u32[]{:S(2)}) %collective-permute-start.1) | collective-permute-done | bytes 524320 | tf_op jit(solution)/shard_map/ppermute | solution.py:42
  33.5 1.2 %copy-done = f32[2,2,256,256]{3,2,1,0:T(8,128)S(1)} copy-done((f32[2,2,256,256]{3,2,1,0:T(8,128)S(1)}, f32[2,2,256,256]{3,2,1,0:T(8,128)}, u32[]{:S(2)}) %copy-start) | copy-done | bytes 1048600
  34.7 6.3 %pattern.1 = (bf16[2,2,256,256]{3,2,1,0:T(8,128)(2,1)S(1)}, bf16[8,2,2,32,128]{4,3,2,1,0:T(8,128)(2,1)S(1)}, bf16[8,2,2,32,128]{4,3,2,1,0:T(8,128)(2,1)S(1)}) custom-call(s32[4,1,16]{2,1,0:T(1,128)S(1)} %copy-done.5, bf16[4,512,512]{2,1,0:T(8,128)(2,1)S(1)} %get-tuple-element.12.refs_1_, f32[2,256,256]{2,1,0:T(8,128)S(1)} %copy-done.6, ...), custom_call_target="tpu_custom_call" | custom-call | flops 3221225472 | bytes 4194304 | tf_op jit(solution)/shard_map/pattern/pallas_call | solution.py:354
  41.4 1.3 %collective-permute-done.5 = bf16[8,2,2,32,128]{4,3,2,1,0:T(8,128)(2,1)S(1)} collective-permute-done((bf16[8,2,2,32,128]{4,3,2,1,0:T(8,128)(2,1)S(1)}, bf16[8,2,2,32,128]{4,3,2,1,0:T(8,128)(2,1)S(1)}, u32[]{:S(2)}, u32[]{:S(2)}) %collective-permute-start.5) | collective-permute-done | bytes 262176 | tf_op jit(solution)/shard_map/ppermute | solution.py:42
  42.6 0.8 add_convert_fusion
  43.6 6.4 %all-to-all-start.1 = ((bf16[8,2,2,32,128]{4,3,2,1,0:T(8,128)(2,1)}), bf16[8,2,2,32,128]{4,3,2,1,0:T(8,128)(2,1)S(1)}, u32[]{:S(2)}, u32[]{:S(2)}) async-start(bf16[8,2,2,32,128]{4,3,2,1,0:T(8,128)(2,1)} %add_convert_fusion), calls=%async_computation.1 | async-start | bytes 524288 | tf_op jit(solution)/shard_map/all_to_all | solution.py:450
  50.0 5.5 %collective-permute-done.7.refs_4_ = bf16[2,2,256,256]{3,2,1,0:T(8,128)(2,1)S(1)} collective-permute-done((bf16[2,2,256,256]{3,2,1,0:T(8,128)(2,1)S(1)}, bf16[2,2,256,256]{3,2,1,0:T(8,128)(2,1)S(1)}, u32[]{:S(2)}, u32[]{:S(2)}) %collective-permute-start.7) | collective-permute-done | bytes 524320 | tf_op jit(solution)/shard_map/ppermute | solution.py:42
  55.6 5.3 %collective-permute-done.8.refs_5_ = bf16[2,2,256,256]{3,2,1,0:T(8,128)(2,1)S(1)} collective-permute-done((bf16[2,2,256,256]{3,2,1,0:T(8,128)(2,1)S(1)}, bf16[2,2,256,256]{3,2,1,0:T(8,128)(2,1)S(1)}, u32[]{:S(2)}, u32[]{:S(2)}) %collective-permute-start.8) | collective-permute-done | bytes 524320 | tf_op jit(solution)/shard_map/ppermute | solution.py:42
  61.0 0.6 collective-permute-start.10
  61.6 8.8 %collective-permute-done.9.refs_6_ = bf16[2,256,256]{2,1,0:T(8,128)(2,1)} collective-permute-done((bf16[2,256,256]{2,1,0:T(8,128)(2,1)S(1)}, bf16[2,256,256]{2,1,0:T(8,128)(2,1)}, u32[]{:S(2)}, u32[]{:S(2)}) %collective-permute-start.9) | collective-permute-done | bytes 262176 | tf_op jit(solution)/shard_map/ppermute | solution.py:42
  71.0 0.6 slice_bitcast_fusion.3
  71.6 0.6 collective-permute-start.6
  72.2 3.1 %collective-permute-done.6.refs_2_ = bf16[2,32,128]{2,1,0:T(8,128)(2,1)S(1)} collective-permute-done((bf16[2,32,128]{2,1,0:T(8,128)(2,1)S(1)}, bf16[2,32,128]{2,1,0:T(8,128)(2,1)S(1)}, u32[]{:S(2)}, u32[]{:S(2)}) %collective-permute-start.6) | collective-permute-done | bytes 16416 | tf_op jit(solution)/shard_map/ppermute | solution.py:42
  76.3 3.9 %place.1 = (f32[2,2,256,512]{3,2,1,0:T(8,128)}, f32[2,2,32,64]{3,2,1,0:T(8,128)}) custom-call(s32[4,1,16]{2,1,0:T(1,128)} %all_to_all.10.info.refs_0_, bf16[2,32,128]{2,1,0:T(8,128)(2,1)} %get-tuple-element.21.refs_1_, bf16[2,32,128]{2,1,0:T(8,128)(2,1)} %copy-done.12, bf16[2,2,256,256]{3,2,1,0:T(8,128)(2,1)} %copy-done.3, ...), custom_call_target="tpu_custom_call" | custom-call | flops 1048576 | bytes 4194304 | tf_op jit(solution)/shard_map/place/pallas_call | solution.py:354
  (53 shorter events, 2.9 us)
Async XLA Ops:
  2.1 7.5 %collective-permute-start = (s32[8]{0:T(128)S(1)}, s32[8]{0:T(128)S(1)}, u32[]{:S(2)}, u32[]{:S(2)}) collective-permute-start(s32[8]{0:T(128)S(1)} %pad_add_fusion), channel_id=1, source_target_pairs={{0,1},{1,2},{2,3},{3,4},{4,5},{5,6},{6,7},{7,0},{8,9},{9,10},{10,1... | collective-permute-start | bytes 104 | tf_op jit(solution)/shard_map/ppermute | solution.py:42
  16.5 5.3 %copy-start.4 = (bf16[1,1,2,256,256]{4,3,2,1,0:T(8,128)(2,1)S(1)}, bf16[1,1,2,256,256]{4,3,2,1,0:T(8,128)(2,1)}, u32[]{:S(2)}) copy-start(bf16[1,1,2,256,256]{4,3,2,1,0:T(8,128)(2,1)} %param.9) | copy-start | bytes 786436
  19.7 13.8 %collective-permute-start.1 = (bf16[2,2,256,256]{3,2,1,0:T(8,128)(2,1)}, bf16[2,2,256,256]{3,2,1,0:T(8,128)(2,1)S(1)}, u32[]{:S(2)}, u32[]{:S(2)}) collective-permute-start(bf16[2,2,256,256]{3,2,1,0:T(8,128)(2,1)} %cut.1), channel_id=1, source_target_pairs={{0,7},{1,0},{2,1},{3,2},{4,3},{5,4},{6,5},{7,6},{8,15},{9,8},{10,9... | collective-permute-start | bytes 1572872 | tf_op jit(solution)/shard_map/ppermute | solution.py:42
  21.8 4.4 %copy-start.1 = (f32[2,2,256,256]{3,2,1,0:T(8,128)S(1)}, f32[2,2,256,256]{3,2,1,0:T(8,128)}, u32[]{:S(2)}) copy-start(f32[2,2,256,256]{3,2,1,0:T(8,128)} %probe_ref.1) | copy-start | bytes 3145732
  21.8 4.4 %copy-start.2 = (f32[2,256,256]{2,1,0:T(8,128)S(1)}, f32[2,256,256]{2,1,0:T(8,128)}, u32[]{:S(2)}) copy-start(f32[2,256,256]{2,1,0:T(8,128)} %constant.9.clone.dft_ref) | copy-start | bytes 1572868
  21.9 11.6 %copy-start.6 = (f32[2,256,256]{2,1,0:T(8,128)S(1)}, f32[2,256,256]{2,1,0:T(8,128)}, u32[]{:S(2)}) copy-start(f32[2,256,256]{2,1,0:T(8,128)} %constant.10.clone.refs_2_) | copy-start | bytes 1572868
  21.9 5.9 %collective-permute-start.4 = (bf16[256,256]{1,0:T(8,128)(2,1)S(1)}, bf16[256,256]{1,0:T(8,128)(2,1)S(1)}, u32[]{:S(2)}, u32[]{:S(2)}) collective-permute-start(bf16[256,256]{1,0:T(8,128)(2,1)S(1)} %slice_bitcast_fusion.2), channel_id=1, source_target_pairs={{0,24},{1,25},{2,26},{3,27},{4,28},{5,29},{6,30},{7,31},{8,0},{9,1... | collective-permute-start | bytes 393224 | tf_op jit(solution)/shard_map/ppermute | solution.py:42
  21.9 7.6 %collective-permute-start.3 = (bf16[256,256]{1,0:T(8,128)(2,1)S(1)}, bf16[256,256]{1,0:T(8,128)(2,1)S(1)}, u32[]{:S(2)}, u32[]{:S(2)}) collective-permute-start(bf16[256,256]{1,0:T(8,128)(2,1)S(1)} %slice_bitcast_fusion.2), channel_id=1, source_target_pairs={{0,16},{1,17},{2,18},{3,19},{4,20},{5,21},{6,22},{7,23},{8,24},{9,... | collective-permute-start | bytes 393224 | tf_op jit(solution)/shard_map/ppermute | solution.py:42
  22.9 7.2 %collective-permute-start.2 = (bf16[256,256]{1,0:T(8,128)(2,1)S(1)}, bf16[256,256]{1,0:T(8,128)(2,1)S(1)}, u32[]{:S(2)}, u32[]{:S(2)}) collective-permute-start(bf16[256,256]{1,0:T(8,128)(2,1)S(1)} %slice_bitcast_fusion.2), channel_id=1, source_target_pairs={{0,8},{1,9},{2,10},{3,11},{4,12},{5,13},{6,14},{7,15},{8,16},{9,17... | collective-permute-start | bytes 393224 | tf_op jit(solution)/shard_map/ppermute | solution.py:42
  41.0 34.3 %copy-start.3 = (bf16[2,2,256,256]{3,2,1,0:T(8,128)(2,1)}, bf16[2,2,256,256]{3,2,1,0:T(8,128)(2,1)S(1)}, u32[]{:S(2)}) copy-start(bf16[2,2,256,256]{3,2,1,0:T(8,128)(2,1)S(1)} %get-tuple-element.19.refs_3_) | copy-start | bytes 1572868
  41.0 1.6 %collective-permute-start.5 = (bf16[8,2,2,32,128]{4,3,2,1,0:T(8,128)(2,1)S(1)}, bf16[8,2,2,32,128]{4,3,2,1,0:T(8,128)(2,1)S(1)}, u32[]{:S(2)}, u32[]{:S(2)}) collective-permute-start(bf16[8,2,2,32,128]{4,3,2,1,0:T(8,128)(2,1)S(1)} %get-tuple-element.17), channel_id=1, source_target_pairs={{0,8},{1,9},{2,10},{3,11},{4,12},{5,13},{6,14},{7,15},{8,0},{9,1},... | collective-permute-start | bytes 786440 | tf_op jit(solution)/shard_map/ppermute | solution.py:42
  41.1 14.3 %collective-permute-start.7 = (bf16[2,2,256,256]{3,2,1,0:T(8,128)(2,1)S(1)}, bf16[2,2,256,256]{3,2,1,0:T(8,128)(2,1)S(1)}, u32[]{:S(2)}, u32[]{:S(2)}) collective-permute-start(bf16[2,2,256,256]{3,2,1,0:T(8,128)(2,1)S(1)} %get-tuple-element.19.refs_3_), channel_id=1, source_target_pairs={{0,16},{1,17},{2,18},{3,19},{4,20},{5,21},{6,22},{7,23},{8,24},{9,... | collective-permute-start | bytes 1572872 | tf_op jit(solution)/shard_map/ppermute | solution.py:42
  43.4 17.5 %collective-permute-start.8 = (bf16[2,2,256,256]{3,2,1,0:T(8,128)(2,1)S(1)}, bf16[2,2,256,256]{3,2,1,0:T(8,128)(2,1)S(1)}, u32[]{:S(2)}, u32[]{:S(2)}) collective-permute-start(bf16[2,2,256,256]{3,2,1,0:T(8,128)(2,1)S(1)} %get-tuple-element.19.refs_3_), channel_id=1, source_target_pairs={{0,1},{1,2},{2,3},{3,4},{4,5},{5,6},{6,7},{7,0},{8,9},{9,10},{10,1... | collective-permute-start | bytes 1572872 | tf_op jit(solution)/shard_map/ppermute | solution.py:42
  43.4 28.1 %collective-permute-start.11 = (bf16[2,2,256,256]{3,2,1,0:T(8,128)(2,1)S(1)}, bf16[2,2,256,256]{3,2,1,0:T(8,128)(2,1)S(1)}, u32[]{:S(2)}, u32[]{:S(2)}) collective-permute-start(bf16[2,2,256,256]{3,2,1,0:T(8,128)(2,1)S(1)} %get-tuple-element.19.refs_3_), channel_id=1, source_target_pairs={{0,8},{1,9},{2,10},{3,11},{4,12},{5,13},{6,14},{7,15},{8,0},{9,1},... | collective-permute-start | bytes 1572872 | tf_op jit(solution)/shard_map/ppermute | solution.py:42
  43.6 27.4 %all-to-all-start.1 = ((bf16[8,2,2,32,128]{4,3,2,1,0:T(8,128)(2,1)}), bf16[8,2,2,32,128]{4,3,2,1,0:T(8,128)(2,1)S(1)}, u32[]{:S(2)}, u32[]{:S(2)}) async-start(bf16[8,2,2,32,128]{4,3,2,1,0:T(8,128)(2,1)} %add_convert_fusion), calls=%async_computation.1 | async-start | bytes 524288 | tf_op jit(solution)/shard_map/all_to_all | solution.py:450
  55.5 19.9 %copy-start.7 = (bf16[2,2,256,256]{3,2,1,0:T(8,128)(2,1)}, bf16[2,2,256,256]{3,2,1,0:T(8,128)(2,1)S(1)}, u32[]{:S(2)}) copy-start(bf16[2,2,256,256]{3,2,1,0:T(8,128)(2,1)S(1)} %collective-permute-done.7.refs_4_) | copy-start | bytes 1572868
  55.5 14.9 %collective-permute-start.9 = (bf16[2,256,256]{2,1,0:T(8,128)(2,1)S(1)}, bf16[2,256,256]{2,1,0:T(8,128)(2,1)}, u32[]{:S(2)}, u32[]{:S(2)}) collective-permute-start(bf16[2,256,256]{2,1,0:T(8,128)(2,1)S(1)} %slice_bitcast_fusion.1), channel_id=1, source_target_pairs={{0,1},{1,2},{2,3},{3,4},{4,5},{5,6},{6,7},{7,0},{8,9},{9,10},{10,1... | collective-permute-start | bytes 786440 | tf_op jit(solution)/shard_map/ppermute | solution.py:42
  55.6 19.8 %collective-permute-start.12 = (bf16[2,2,256,256]{3,2,1,0:T(8,128)(2,1)S(1)}, bf16[2,2,256,256]{3,2,1,0:T(8,128)(2,1)S(1)}, u32[]{:S(2)}, u32[]{:S(2)}) collective-permute-start(bf16[2,2,256,256]{3,2,1,0:T(8,128)(2,1)S(1)} %collective-permute-done.7.refs_4_), channel_id=1, source_target_pairs={{0,8},{1,9},{2,10},{3,11},{4,12},{5,13},{6,14},{7,15},{8,0},{9,1},... | collective-permute-start | bytes 1572872 | tf_op jit(solution)/shard_map/ppermute | solution.py:42
  61.0 14.4 %copy-start.8 = (bf16[2,2,256,256]{3,2,1,0:T(8,128)(2,1)}, bf16[2,2,256,256]{3,2,1,0:T(8,128)(2,1)S(1)}, u32[]{:S(2)}) copy-start(bf16[2,2,256,256]{3,2,1,0:T(8,128)(2,1)S(1)} %collective-permute-done.8.refs_5_) | copy-start | bytes 1572868
  61.0 9.4 %collective-permute-start.10 = (bf16[2,256,256]{2,1,0:T(8,128)(2,1)S(1)}, bf16[2,256,256]{2,1,0:T(8,128)(2,1)}, u32[]{:S(2)}, u32[]{:S(2)}) collective-permute-start(bf16[2,256,256]{2,1,0:T(8,128)(2,1)S(1)} %slice_bitcast_fusion), channel_id=1, source_target_pairs={{0,16},{1,17},{2,18},{3,19},{4,20},{5,21},{6,22},{7,23},{8,24},{9,... | collective-permute-start | bytes 786440 | tf_op jit(solution)/shard_map/ppermute | solution.py:42
  61.6 13.7 %collective-permute-start.13 = (bf16[2,2,256,256]{3,2,1,0:T(8,128)(2,1)S(1)}, bf16[2,2,256,256]{3,2,1,0:T(8,128)(2,1)S(1)}, u32[]{:S(2)}, u32[]{:S(2)}) collective-permute-start(bf16[2,2,256,256]{3,2,1,0:T(8,128)(2,1)S(1)} %collective-permute-done.8.refs_5_), channel_id=1, source_target_pairs={{0,8},{1,9},{2,10},{3,11},{4,12},{5,13},{6,14},{7,15},{8,0},{9,1},... | collective-permute-start | bytes 1572872 | tf_op jit(solution)/shard_map/ppermute | solution.py:42
  70.4 4.9 %collective-permute-start.14 = (bf16[2,256,256]{2,1,0:T(8,128)(2,1)}, bf16[2,256,256]{2,1,0:T(8,128)(2,1)}, u32[]{:S(2)}, u32[]{:S(2)}) collective-permute-start(bf16[2,256,256]{2,1,0:T(8,128)(2,1)} %collective-permute-done.9.refs_6_), channel_id=1, source_target_pairs={{0,8},{1,9},{2,10},{3,11},{4,12},{5,13},{6,14},{7,15},{8,0},{9,1},... | collective-permute-start | bytes 786440 | tf_op jit(solution)/shard_map/ppermute | solution.py:42
  70.4 4.9 %collective-permute-start.15 = (bf16[2,256,256]{2,1,0:T(8,128)(2,1)}, bf16[2,256,256]{2,1,0:T(8,128)(2,1)}, u32[]{:S(2)}, u32[]{:S(2)}) collective-permute-start(bf16[2,256,256]{2,1,0:T(8,128)(2,1)} %collective-permute-done.10.refs_7_), channel_id=1, source_target_pairs={{0,8},{1,9},{2,10},{3,11},{4,12},{5,13},{6,14},{7,15},{8,0},{9,1},... | collective-permute-start | bytes 786440 | tf_op jit(solution)/shard_map/ppermute | solution.py:42
  71.6 3.7 %collective-permute-start.6 = (bf16[2,32,128]{2,1,0:T(8,128)(2,1)S(1)}, bf16[2,32,128]{2,1,0:T(8,128)(2,1)S(1)}, u32[]{:S(2)}, u32[]{:S(2)}) collective-permute-start(bf16[2,32,128]{2,1,0:T(8,128)(2,1)S(1)} %get-tuple-element.20), channel_id=1, source_target_pairs={{0,16},{1,17},{2,18},{3,19},{4,20},{5,21},{6,22},{7,23},{8,24},{9,... | collective-permute-start | bytes 49160 | tf_op jit(solution)/shard_map/ppermute | solution.py:42
  (6 other events, 11.8 us)

commit v7 on v6

--- a/solution.py
+++ b/solution.py
@@ -13,7 +13,7 @@
 AXES = ("scan", "obj")
 CORES = 2
 MIB = 1 << 20
-SMALL, LARGE = 20, 56
+SMALL, MIDDLE, LARGE = 20, 48, 56
 
 
 def dft_tables(length):
@@ -272,16 +272,15 @@
                 @pl.when(mine == s % CORES)
                 def _():
                     for o in range(n_obj):
-                        ref[o, apart, m] = both[o * per_row : (o + 1) * per_row].astype(ref.dtype)
+                        ref[apart, o, m] = both[o * per_row : (o + 1) * per_row].astype(ref.dtype)
 
 
 def place_kernel(sizes, kinds, parts, factor, *refs):
-    n_scan, _, tile_cols = sizes
-    chips = n_scan // CORES
+    n_scan, n_obj, tile_cols = sizes
     layers = refs[-4].shape[0]
     info = refs[0]
-    shares = refs[1 : 1 + chips]
-    patches = refs[1 + chips : -4]
+    chunks = refs[1]
+    patches = refs[2:-4]
     out_ref, probe_out, held, sems = refs[-4:]
     _, _, rows, width = out_ref.shape
     length = patches[0].shape[-1]
@@ -311,7 +310,7 @@
     out_ref[...] = jnp.zeros(out_ref.shape, jnp.float32)
     per_col = probe_out.shape[3]
     for m in range(probe_out.shape[0]):
-        total = sum(share[m].astype(jnp.float32) for share in shares) * factor
+        total = sum(chunks[o, m].astype(jnp.float32) for o in range(n_obj)) * factor
         probe_out[m, 0] = total[:, :per_col]
         probe_out[m, 1] = total[:, per_col:]
     lane, line = lanes(length), lines(length)
@@ -387,7 +386,7 @@
     )
     piece = outward(piece, -1)
     (own_part,) = call(
-        (pick_kernel, True), [(patch_shape, real)], [smem, hbm], wide, "own", MIB, LARGE, info, object_slices
+        (pick_kernel, True), [(patch_shape, real)], [smem, hbm], wide, "own", MIB, MIDDLE, info, object_slices
     )
     mats, turned = call(
         (prep_kernel,),
@@ -401,7 +400,7 @@
         probe,
         dft_tables(length),
     )
-    chunk_shape = (n_obj, chips, modes, length // n_obj, 2 * (length // n_scan))
+    chunk_shape = (chips, n_obj, modes, length // n_obj, 2 * (length // n_scan))
     grad, keep, give = call(
         (pattern_kernel,),
         [(patch_shape, half), (chunk_shape, half), (chunk_shape, half)],
@@ -429,9 +428,11 @@
 
     here = [grad] + [along(grad, j) for j in range(1, chips)]
     chunks = (keep.astype(real) + across(give).astype(real)).astype(half)
-    first, chunks = lax.optimization_barrier((grad, chunks))
-    there = outward(first, 1)
-    x_first = [outward(block[1], 1) for block in here[1:]]
+    chunks = sum((along(chunks[j], j).astype(real) for j in range(1, chips)), chunks[0].astype(real)).astype(half)
+    there = outward(grad, 1)
+    late, chunks = lax.optimization_barrier((here[1:], chunks))
+    here = here[:1] + late
+    x_first = [outward(block[1], 1) for block in late]
     obj_first = [along(there[0], j) for j in range(1, chips)]
     held = here + [there] + x_first + obj_first
     held += [across(block) for block in held]
@@ -448,8 +449,6 @@
             else:
                 parts.append([(start + 2 * chips - 1 + j, None), (start + chips + j, None)])
     chunks = lax.all_to_all(chunks, "obj", 0, 0, tiled=True)
-    chunks = jnp.sum(chunks.astype(real), axis=0).astype(half)
-    shares = [along(chunks[j], j) for j in range(chips)]
     factor = 1.0 / math.sqrt(n_scan * n_obj * slots // 2)
     object_grad, probe_grad = call(
         (place_kernel, kinds, parts, factor),
@@ -457,7 +456,7 @@
             ((layers, 2, tile_rows, tile_cols // n_scan), real),
             ((modes, 2, length // n_obj, length // n_scan), real),
         ],
-        [smem] + [vmem] * chips + [hbm] * len(held),
+        [smem, vmem] + [hbm] * len(held),
         [
             pltpu.VMEM((2 * n_scan, layers, *patch_shape[1:]), half),
             pltpu.SemaphoreType.DMA((2 * n_scan, layers)),
@@ -466,7 +465,7 @@
         MIB,
         LARGE,
         info,
-        *shares,
+        chunks,
         *held,
     )
     return (object_grad, probe_grad)

time: 80.6 us -> 87.9 us (1.091)
  waiting for transfers between devices: 34.2 us -> 46 us
  local copies, waits for them, and re-layouts: 3.6 us -> 1.81 us
  starting transfers between devices: 14.9 us -> 13.4 us
    all_to_all x1, waiting for transfers between devices: 0.01 us -> 7.85 us  [body(): chunks = lax.all_to_all(chunks, 'obj', 0, 0, tiled=True)]
    ppermute x16, waiting for transfers between devices: 34.2 us -> 38.2 us  [send(): return lax.ppermute(block, AXES, route)]
    all_to_all x1, starting transfers between devices: 6.43 us -> 3.37 us  [body(): chunks = lax.all_to_all(chunks, 'obj', 0, 0, tiled=True)]
    ppermute x16, starting transfers between devices: 8.43 us -> 10 us  [send(): return lax.ppermute(block, AXES, route)]
    unnamed x26, local copies, waits for them, and re-layouts: 2.19 us -> 0.99 us
  transfers between devices with their start and end apart: 17 -> 17, of which waited for: 9 -> 11; matrix products, arithmetic and copies ran while one was open for 2% -> 1% of each run, Pallas kernels for 6% -> 4%
where the time goes in v7:
time: 87.9 us; the launch traced here: 87.7 us
  waiting for transfers between devices  46 us (52%)
  Pallas kernels  17.4 us (20%)
  starting transfers between devices  13.4 us (15%)
  blocking collectives  6.62 us (8%)
  local copies, waits for them, and re-layouts  1.81 us (2%)
  between operations  1.54 us (2%)
  other arithmetic  0.92 us (1%)
    ppermute x16, waiting for transfers between devices, send(): return lax.ppermute(block, AXES, route)  38.2 us
    pallas_call x5, Pallas kernels, call(): pl.pallas_call(functools.partial(kernel[0], sizes, *kernel[1:]), out_shap...  17.4 us
    ppermute x16, starting transfers between devices, send(): return lax.ppermute(block, AXES, route)  10 us
    all_to_all x1, waiting for transfers between devices, body(): chunks = lax.all_to_all(chunks, 'obj', 0, 0, tiled=True)  7.85 us
    all_to_all x1, blocking collectives, body(): lax.all_to_all(jnp.broadcast_to(both, (n_scan, 1, 16)), 'scan', 0, 0, til...  6.62 us
    all_to_all x1, starting transfers between devices, body(): chunks = lax.all_to_all(chunks, 'obj', 0, 0, tiled=True)  3.37 us
  transfers between devices with their start and end apart: 17, of which 11 were waited for; matrix products, arithmetic and copies ran while one was open for 1% of the time, Pallas kernels for 4%

profile of v7, /device:TPU:0, one launch (start us, length us, event | category | flops | bytes accessed | tf_op | source)
XLA Modules:
  0.0 87.7 jit_solution(12868488987828579437)
XLA Ops:
  1.3 0.8 reshape_squeeze.3
  2.1 3.0 %collective-permute-start = (s32[8]{0:T(128)S(1)}, s32[8]{0:T(128)S(1)}, u32[]{:S(2)}, u32[]{:S(2)}) collective-permute-start(s32[8]{0:T(128)S(1)} %pad_add_fusion), channel_id=1, source_target_pairs={{0,1},{1,2},{2,3},{3,4},{4,5},{5,6},{6,7},{7,0},{8,9},{9,10},{10,1... | collective-permute-start | bytes 104 | tf_op jit(solution)/shard_map/ppermute | solution.py:42
  5.1 4.6 %collective-permute-done = s32[8]{0:T(128)S(1)} collective-permute-done((s32[8]{0:T(128)S(1)}, s32[8]{0:T(128)S(1)}, u32[]{:S(2)}, u32[]{:S(2)}) %collective-permute-start) | collective-permute-done | bytes 64 | tf_op jit(solution)/shard_map/ppermute | solution.py:42
  9.7 6.6 %all_to_all.10.info.refs_0_ = s32[4,1,16]{2,1,0:T(1,128)} all-to-all(s32[4,1,16]{2,1,0:T(1,128)S(1)} %broadcast_in_dim.3), channel_id=1, replica_groups=mesh['scan'=4,'obj'=8] {'scan'}, dimensions={0} | all-to-all | bytes 512 | tf_op jit(solution)/shard_map/all_to_all | solution.py:375
  16.3 3.2 %cut.1 = bf16[2,2,256,256]{3,2,1,0:T(8,128)(2,1)} custom-call(s32[4,1,16]{2,1,0:T(1,128)} %all_to_all.10.info.refs_0_, f32[2,2,256,2048]{3,2,1,0:T(8,128)} %object_ref.3), custom_call_target="tpu_custom_call" | custom-call | flops 1048576 | bytes 4194304 | tf_op jit(solution)/shard_map/cut/pallas_call | solution.py:353
  19.6 2.1 %collective-permute-start.1 = (bf16[2,2,256,256]{3,2,1,0:T(8,128)(2,1)}, bf16[2,2,256,256]{3,2,1,0:T(8,128)(2,1)S(1)}, u32[]{:S(2)}, u32[]{:S(2)}) collective-permute-start(bf16[2,2,256,256]{3,2,1,0:T(8,128)(2,1)} %cut.1), channel_id=1, source_target_pairs={{0,7},{1,0},{2,1},{3,2},{4,3},{5,4},{6,5},{7,6},{8,15},{9,8},{10,9... | collective-permute-start | bytes 1572872 | tf_op jit(solution)/shard_map/ppermute | solution.py:42
  21.8 1.3 %collective-permute-start.3 = (bf16[256,256]{1,0:T(8,128)(2,1)S(1)}, bf16[256,256]{1,0:T(8,128)(2,1)S(1)}, u32[]{:S(2)}, u32[]{:S(2)}) collective-permute-start(bf16[256,256]{1,0:T(8,128)(2,1)S(1)} %slice_bitcast_fusion.4), channel_id=1, source_target_pairs={{0,16},{1,17},{2,18},{3,19},{4,20},{5,21},{6,22},{7,23},{8,24},{9,... | collective-permute-start | bytes 393224 | tf_op jit(solution)/shard_map/ppermute | solution.py:42
  23.1 2.2 %own.1.refs_4_ = f32[2,2,256,256]{3,2,1,0:T(8,128)S(1)} custom-call(s32[4,1,16]{2,1,0:T(1,128)S(1)} %copy-done.4, f32[2,2,256,2048]{3,2,1,0:T(8,128)} %object_ref.3), custom_call_target="tpu_custom_call" | custom-call | flops 1048576 | bytes 4194304 | tf_op jit(solution)/shard_map/own/pallas_call | solution.py:353
  25.3 1.5 %prep.1 = (bf16[4,512,512]{2,1,0:T(8,128)(2,1)S(1)}, f32[2,2,256,256]{3,2,1,0:T(8,128)S(1)}) custom-call(s32[4,1,16]{2,1,0:T(1,128)S(1)} %copy-done.4, f32[2,2,256,256]{3,2,1,0:T(8,128)S(1)} %copy-done, f32[2,256,256]{2,1,0:T(8,128)S(1)} %copy-done.1), custom_call_target="tpu_custom_call" | custom-call | flops 1048576 | bytes 4194304 | tf_op jit(solution)/shard_map/prep/pallas_call | solution.py:353
  26.9 3.1 %collective-permute-done.3.refs_8_ = bf16[256,256]{1,0:T(8,128)(2,1)S(1)} collective-permute-done((bf16[256,256]{1,0:T(8,128)(2,1)S(1)}, bf16[256,256]{1,0:T(8,128)(2,1)S(1)}, u32[]{:S(2)}, u32[]{:S(2)}) %collective-permute-start.3) | collective-permute-done | bytes 131104 | tf_op jit(solution)/shard_map/ppermute | solution.py:42
  30.2 3.4 %collective-permute-done.1.refs_5_ = bf16[2,2,256,256]{3,2,1,0:T(8,128)(2,1)S(1)} collective-permute-done((bf16[2,2,256,256]{3,2,1,0:T(8,128)(2,1)}, bf16[2,2,256,256]{3,2,1,0:T(8,128)(2,1)S(1)}, u32[]{:S(2)}, u32[]{:S(2)}) %collective-permute-start.1) | collective-permute-done | bytes 524320 | tf_op jit(solution)/shard_map/ppermute | solution.py:42
  33.7 6.3 %pattern.1 = (bf16[2,2,256,256]{3,2,1,0:T(8,128)(2,1)S(1)}, bf16[2,8,2,32,128]{4,3,2,1,0:T(8,128)(2,1)S(1)}, bf16[2,8,2,32,128]{4,3,2,1,0:T(8,128)(2,1)S(1)}) custom-call(s32[4,1,16]{2,1,0:T(1,128)S(1)} %copy-done.4, bf16[4,512,512]{2,1,0:T(8,128)(2,1)S(1)} %get-tuple-element.12.refs_1_, f32[2,256,256]{2,1,0:T(8,128)S(1)} %copy-done.5, ...), custom_call_target="tpu_custom_call" | custom-call | flops 3221225472 | bytes 4194304 | tf_op jit(solution)/shard_map/pattern/pallas_call | solution.py:353
  40.1 1.5 %collective-permute-done.6 = bf16[2,8,2,32,128]{4,3,2,1,0:T(8,128)(2,1)S(1)} collective-permute-done((bf16[2,8,2,32,128]{4,3,2,1,0:T(8,128)(2,1)S(1)}, bf16[2,8,2,32,128]{4,3,2,1,0:T(8,128)(2,1)S(1)}, u32[]{:S(2)}, u32[]{:S(2)}) %collective-permute-start.6) | collective-permute-done | bytes 262176 | tf_op jit(solution)/shard_map/ppermute | solution.py:42
  41.8 2.0 %collective-permute-start.5 = (bf16[2,2,256,256]{3,2,1,0:T(8,128)(2,1)S(1)}, bf16[2,2,256,256]{3,2,1,0:T(8,128)(2,1)S(1)}, u32[]{:S(2)}, u32[]{:S(2)}) collective-permute-start(bf16[2,2,256,256]{3,2,1,0:T(8,128)(2,1)S(1)} %get-tuple-element.15.refs_2_), channel_id=1, source_target_pairs={{0,16},{1,17},{2,18},{3,19},{4,20},{5,21},{6,22},{7,23},{8,24},{9,... | collective-permute-start | bytes 1572872 | tf_op jit(solution)/shard_map/ppermute | solution.py:42
  43.8 4.3 %collective-permute-done.7 = bf16[8,2,32,128]{3,2,1,0:T(8,128)(2,1)S(1)} collective-permute-done((bf16[8,2,32,128]{3,2,1,0:T(8,128)(2,1)S(1)}, bf16[8,2,32,128]{3,2,1,0:T(8,128)(2,1)S(1)}, u32[]{:S(2)}, u32[]{:S(2)}) %collective-permute-start.7) | collective-permute-done | bytes 131104 | tf_op jit(solution)/shard_map/ppermute | solution.py:42
  48.1 0.7 fusion
  48.8 8.6 %collective-permute-done.8.refs_4_ = bf16[2,2,256,256]{3,2,1,0:T(8,128)(2,1)S(1)} collective-permute-done((bf16[2,2,256,256]{3,2,1,0:T(8,128)(2,1)S(1)}, bf16[2,2,256,256]{3,2,1,0:T(8,128)(2,1)S(1)}, u32[]{:S(2)}, u32[]{:S(2)}) %collective-permute-start.8) | collective-permute-done | bytes 524320 | tf_op jit(solution)/shard_map/ppermute | solution.py:42
  57.5 1.0 %collective-permute-done.5.refs_3_ = bf16[2,2,256,256]{3,2,1,0:T(8,128)(2,1)S(1)} collective-permute-done((bf16[2,2,256,256]{3,2,1,0:T(8,128)(2,1)S(1)}, bf16[2,2,256,256]{3,2,1,0:T(8,128)(2,1)S(1)}, u32[]{:S(2)}, u32[]{:S(2)}) %collective-permute-start.5) | collective-permute-done | bytes 524320 | tf_op jit(solution)/shard_map/ppermute | solution.py:42
  59.1 0.7 collective-permute-start.9
  59.9 5.7 %collective-permute-done.10.refs_6_ = bf16[2,256,256]{2,1,0:T(8,128)(2,1)S(1)} collective-permute-done((bf16[2,256,256]{2,1,0:T(8,128)(2,1)S(1)}, bf16[2,256,256]{2,1,0:T(8,128)(2,1)S(1)}, u32[]{:S(2)}, u32[]{:S(2)}) %collective-permute-start.10) | collective-permute-done | bytes 262176 | tf_op jit(solution)/shard_map/ppermute | solution.py:42
  65.5 5.8 %collective-permute-done.9.refs_5_ = bf16[2,256,256]{2,1,0:T(8,128)(2,1)} collective-permute-done((bf16[2,256,256]{2,1,0:T(8,128)(2,1)S(1)}, bf16[2,256,256]{2,1,0:T(8,128)(2,1)}, u32[]{:S(2)}, u32[]{:S(2)}) %collective-permute-start.9) | collective-permute-done | bytes 262176 | tf_op jit(solution)/shard_map/ppermute | solution.py:42
  71.3 3.4 %all-to-all-start.1 = ((bf16[8,2,32,128]{3,2,1,0:T(8,128)(2,1)}), bf16[8,2,32,128]{3,2,1,0:T(8,128)(2,1)S(1)}, u32[]{:S(2)}, u32[]{:S(2)}) async-start(bf16[8,2,32,128]{3,2,1,0:T(8,128)(2,1)} %fusion), calls=%async_computation.1 | async-start | bytes 262144 | tf_op jit(solution)/shard_map/all_to_all | solution.py:451
  74.7 7.8 %all-to-all-done.1.refs_1_ = bf16[8,2,32,128]{3,2,1,0:T(8,128)(2,1)S(1)} async-done(((bf16[8,2,32,128]{3,2,1,0:T(8,128)(2,1)}), bf16[8,2,32,128]{3,2,1,0:T(8,128)(2,1)S(1)}, u32[]{:S(2)}, u32[]{:S(2)}) %all-to-all-start.1) | async-done | bytes 131104 | tf_op jit(solution)/shard_map/all_to_all | solution.py:451
  83.6 4.1 %place.1 = (f32[2,2,256,512]{3,2,1,0:T(8,128)}, f32[2,2,32,64]{3,2,1,0:T(8,128)}) custom-call(s32[4,1,16]{2,1,0:T(1,128)} %all_to_all.10.info.refs_0_, bf16[8,2,32,128]{3,2,1,0:T(8,128)(2,1)} %copy-done.8, bf16[2,2,256,256]{3,2,1,0:T(8,128)(2,1)} %copy-done.2, bf16[2,2,256,256]{3,2,1,0:T(8,128)(2,1)} %copy-done.7, bf16[2,2,256,256]{3,2,1,0:T(8,128)(2,1)} %copy-done.6, ...), custom_call_target="tpu_custom_call" | custom-call | flops 1048576 | bytes 4194304 | tf_op jit(solution)/shard_map/place/pallas_call | solution.py:353
  (53 shorter events, 2.5 us)
Async XLA Ops:
  2.1 7.5 %collective-permute-start = (s32[8]{0:T(128)S(1)}, s32[8]{0:T(128)S(1)}, u32[]{:S(2)}, u32[]{:S(2)}) collective-permute-start(s32[8]{0:T(128)S(1)} %pad_add_fusion), channel_id=1, source_target_pairs={{0,1},{1,2},{2,3},{3,4},{4,5},{5,6},{6,7},{7,0},{8,9},{9,10},{10,1... | collective-permute-start | bytes 104 | tf_op jit(solution)/shard_map/ppermute | solution.py:42
  16.3 6.8 %copy-start.4 = (s32[4,1,16]{2,1,0:T(1,128)S(1)}, s32[4,1,16]{2,1,0:T(1,128)}, u32[]{:S(2)}) copy-start(s32[4,1,16]{2,1,0:T(1,128)} %all_to_all.10.info.refs_0_) | copy-start | bytes 772
  19.6 14.1 %collective-permute-start.1 = (bf16[2,2,256,256]{3,2,1,0:T(8,128)(2,1)}, bf16[2,2,256,256]{3,2,1,0:T(8,128)(2,1)S(1)}, u32[]{:S(2)}, u32[]{:S(2)}) collective-permute-start(bf16[2,2,256,256]{3,2,1,0:T(8,128)(2,1)} %cut.1), channel_id=1, source_target_pairs={{0,7},{1,0},{2,1},{3,2},{4,3},{5,4},{6,5},{7,6},{8,15},{9,8},{10,9... | collective-permute-start | bytes 1572872 | tf_op jit(solution)/shard_map/ppermute | solution.py:42
  21.7 11.9 %copy-start.5 = (f32[2,256,256]{2,1,0:T(8,128)S(1)}, f32[2,256,256]{2,1,0:T(8,128)}, u32[]{:S(2)}) copy-start(f32[2,256,256]{2,1,0:T(8,128)} %constant.7.clone.refs_2_) | copy-start | bytes 1572868
  21.7 5.1 %collective-permute-start.4 = (bf16[256,256]{1,0:T(8,128)(2,1)S(1)}, bf16[256,256]{1,0:T(8,128)(2,1)S(1)}, u32[]{:S(2)}, u32[]{:S(2)}) collective-permute-start(bf16[256,256]{1,0:T(8,128)(2,1)S(1)} %slice_bitcast_fusion.4), channel_id=1, source_target_pairs={{0,24},{1,25},{2,26},{3,27},{4,28},{5,29},{6,30},{7,31},{8,0},{9,1... | collective-permute-start | bytes 393224 | tf_op jit(solution)/shard_map/ppermute | solution.py:42
  21.8 8.2 %collective-permute-start.3 = (bf16[256,256]{1,0:T(8,128)(2,1)S(1)}, bf16[256,256]{1,0:T(8,128)(2,1)S(1)}, u32[]{:S(2)}, u32[]{:S(2)}) collective-permute-start(bf16[256,256]{1,0:T(8,128)(2,1)S(1)} %slice_bitcast_fusion.4), channel_id=1, source_target_pairs={{0,16},{1,17},{2,18},{3,19},{4,20},{5,21},{6,22},{7,23},{8,24},{9,... | collective-permute-start | bytes 393224 | tf_op jit(solution)/shard_map/ppermute | solution.py:42
  23.1 7.2 %collective-permute-start.2 = (bf16[256,256]{1,0:T(8,128)(2,1)S(1)}, bf16[256,256]{1,0:T(8,128)(2,1)S(1)}, u32[]{:S(2)}, u32[]{:S(2)}) collective-permute-start(bf16[256,256]{1,0:T(8,128)(2,1)S(1)} %slice_bitcast_fusion.4), channel_id=1, source_target_pairs={{0,8},{1,9},{2,10},{3,11},{4,12},{5,13},{6,14},{7,15},{8,16},{9,17... | collective-permute-start | bytes 393224 | tf_op jit(solution)/shard_map/ppermute | solution.py:42
  40.0 42.6 %copy-start.2 = (bf16[2,2,256,256]{3,2,1,0:T(8,128)(2,1)}, bf16[2,2,256,256]{3,2,1,0:T(8,128)(2,1)S(1)}, u32[]{:S(2)}) copy-start(bf16[2,2,256,256]{3,2,1,0:T(8,128)(2,1)S(1)} %get-tuple-element.15.refs_2_) | copy-start | bytes 1572868
  40.0 1.6 %collective-permute-start.6 = (bf16[2,8,2,32,128]{4,3,2,1,0:T(8,128)(2,1)S(1)}, bf16[2,8,2,32,128]{4,3,2,1,0:T(8,128)(2,1)S(1)}, u32[]{:S(2)}, u32[]{:S(2)}) collective-permute-start(bf16[2,8,2,32,128]{4,3,2,1,0:T(8,128)(2,1)S(1)} %get-tuple-element.17), channel_id=1, source_target_pairs={{0,8},{1,9},{2,10},{3,11},{4,12},{5,13},{6,14},{7,15},{8,0},{9,1},... | collective-permute-start | bytes 786440 | tf_op jit(solution)/shard_map/ppermute | solution.py:42
  40.1 17.3 %collective-permute-start.8 = (bf16[2,2,256,256]{3,2,1,0:T(8,128)(2,1)S(1)}, bf16[2,2,256,256]{3,2,1,0:T(8,128)(2,1)S(1)}, u32[]{:S(2)}, u32[]{:S(2)}) collective-permute-start(bf16[2,2,256,256]{3,2,1,0:T(8,128)(2,1)S(1)} %get-tuple-element.15.refs_2_), channel_id=1, source_target_pairs={{0,1},{1,2},{2,3},{3,4},{4,5},{5,6},{6,7},{7,0},{8,9},{9,10},{10,1... | collective-permute-start | bytes 1572872 | tf_op jit(solution)/shard_map/ppermute | solution.py:42
  41.7 6.4 %collective-permute-start.7 = (bf16[8,2,32,128]{3,2,1,0:T(8,128)(2,1)S(1)}, bf16[8,2,32,128]{3,2,1,0:T(8,128)(2,1)S(1)}, u32[]{:S(2)}, u32[]{:S(2)}) collective-permute-start(bf16[8,2,32,128]{3,2,1,0:T(8,128)(2,1)S(1)} %slice_bitcast_fusion.2), channel_id=1, source_target_pairs={{0,16},{1,17},{2,18},{3,19},{4,20},{5,21},{6,22},{7,23},{8,24},{9,... | collective-permute-start | bytes 393224 | tf_op jit(solution)/shard_map/ppermute | solution.py:42
  41.8 16.7 %collective-permute-start.5 = (bf16[2,2,256,256]{3,2,1,0:T(8,128)(2,1)S(1)}, bf16[2,2,256,256]{3,2,1,0:T(8,128)(2,1)S(1)}, u32[]{:S(2)}, u32[]{:S(2)}) collective-permute-start(bf16[2,2,256,256]{3,2,1,0:T(8,128)(2,1)S(1)} %get-tuple-element.15.refs_2_), channel_id=1, source_target_pairs={{0,16},{1,17},{2,18},{3,19},{4,20},{5,21},{6,22},{7,23},{8,24},{9,... | collective-permute-start | bytes 1572872 | tf_op jit(solution)/shard_map/ppermute | solution.py:42
  43.8 30.9 %collective-permute-start.11 = (bf16[2,2,256,256]{3,2,1,0:T(8,128)(2,1)S(1)}, bf16[2,2,256,256]{3,2,1,0:T(8,128)(2,1)S(1)}, u32[]{:S(2)}, u32[]{:S(2)}) collective-permute-start(bf16[2,2,256,256]{3,2,1,0:T(8,128)(2,1)S(1)} %get-tuple-element.15.refs_2_), channel_id=1, source_target_pairs={{0,8},{1,9},{2,10},{3,11},{4,12},{5,13},{6,14},{7,15},{8,0},{9,1},... | collective-permute-start | bytes 1572872 | tf_op jit(solution)/shard_map/ppermute | solution.py:42
  57.4 25.2 %copy-start.6 = (bf16[2,2,256,256]{3,2,1,0:T(8,128)(2,1)}, bf16[2,2,256,256]{3,2,1,0:T(8,128)(2,1)S(1)}, u32[]{:S(2)}) copy-start(bf16[2,2,256,256]{3,2,1,0:T(8,128)(2,1)S(1)} %collective-permute-done.8.refs_4_) | copy-start | bytes 1572868
  57.4 8.1 %collective-permute-start.10 = (bf16[2,256,256]{2,1,0:T(8,128)(2,1)S(1)}, bf16[2,256,256]{2,1,0:T(8,128)(2,1)S(1)}, u32[]{:S(2)}, u32[]{:S(2)}) collective-permute-start(bf16[2,256,256]{2,1,0:T(8,128)(2,1)S(1)} %slice_bitcast_fusion), channel_id=1, source_target_pairs={{0,16},{1,17},{2,18},{3,19},{4,20},{5,21},{6,22},{7,23},{8,24},{9,... | collective-permute-start | bytes 786440 | tf_op jit(solution)/shard_map/ppermute | solution.py:42
  58.5 24.1 %copy-start.7 = (bf16[2,2,256,256]{3,2,1,0:T(8,128)(2,1)}, bf16[2,2,256,256]{3,2,1,0:T(8,128)(2,1)S(1)}, u32[]{:S(2)}) copy-start(bf16[2,2,256,256]{3,2,1,0:T(8,128)(2,1)S(1)} %collective-permute-done.5.refs_3_) | copy-start | bytes 1572868
  58.6 24.0 %collective-permute-start.13 = (bf16[2,2,256,256]{3,2,1,0:T(8,128)(2,1)S(1)}, bf16[2,2,256,256]{3,2,1,0:T(8,128)(2,1)S(1)}, u32[]{:S(2)}, u32[]{:S(2)}) collective-permute-start(bf16[2,2,256,256]{3,2,1,0:T(8,128)(2,1)S(1)} %collective-permute-done.8.refs_4_), channel_id=1, source_target_pairs={{0,8},{1,9},{2,10},{3,11},{4,12},{5,13},{6,14},{7,15},{8,0},{9,1},... | collective-permute-start | bytes 1572872 | tf_op jit(solution)/shard_map/ppermute | solution.py:42
  58.6 23.9 %collective-permute-start.12 = (bf16[2,2,256,256]{3,2,1,0:T(8,128)(2,1)S(1)}, bf16[2,2,256,256]{3,2,1,0:T(8,128)(2,1)S(1)}, u32[]{:S(2)}, u32[]{:S(2)}) collective-permute-start(bf16[2,2,256,256]{3,2,1,0:T(8,128)(2,1)S(1)} %collective-permute-done.5.refs_3_), channel_id=1, source_target_pairs={{0,8},{1,9},{2,10},{3,11},{4,12},{5,13},{6,14},{7,15},{8,0},{9,1},... | collective-permute-start | bytes 1572872 | tf_op jit(solution)/shard_map/ppermute | solution.py:42
  59.1 12.2 %collective-permute-start.9 = (bf16[2,256,256]{2,1,0:T(8,128)(2,1)S(1)}, bf16[2,256,256]{2,1,0:T(8,128)(2,1)}, u32[]{:S(2)}, u32[]{:S(2)}) collective-permute-start(bf16[2,256,256]{2,1,0:T(8,128)(2,1)S(1)} %slice_bitcast_fusion.1), channel_id=1, source_target_pairs={{0,1},{1,2},{2,3},{3,4},{4,5},{5,6},{6,7},{7,0},{8,9},{9,10},{10,1... | collective-permute-start | bytes 786440 | tf_op jit(solution)/shard_map/ppermute | solution.py:42
  65.5 17.1 %copy-start.12 = (bf16[2,256,256]{2,1,0:T(8,128)(2,1)}, bf16[2,256,256]{2,1,0:T(8,128)(2,1)S(1)}, u32[]{:S(2)}) copy-start(bf16[2,256,256]{2,1,0:T(8,128)(2,1)S(1)} %collective-permute-done.10.refs_6_) | copy-start | bytes 786436
  65.5 17.1 %collective-permute-start.15 = (bf16[2,256,256]{2,1,0:T(8,128)(2,1)S(1)}, bf16[2,256,256]{2,1,0:T(8,128)(2,1)}, u32[]{:S(2)}, u32[]{:S(2)}) collective-permute-start(bf16[2,256,256]{2,1,0:T(8,128)(2,1)S(1)} %collective-permute-done.10.refs_6_), channel_id=1, source_target_pairs={{0,8},{1,9},{2,10},{3,11},{4,12},{5,13},{6,14},{7,15},{8,0},{9,1},... | collective-permute-start | bytes 786440 | tf_op jit(solution)/shard_map/ppermute | solution.py:42
  71.3 11.3 %collective-permute-start.14 = (bf16[2,256,256]{2,1,0:T(8,128)(2,1)}, bf16[2,256,256]{2,1,0:T(8,128)(2,1)}, u32[]{:S(2)}, u32[]{:S(2)}) collective-permute-start(bf16[2,256,256]{2,1,0:T(8,128)(2,1)} %collective-permute-done.9.refs_5_), channel_id=1, source_target_pairs={{0,8},{1,9},{2,10},{3,11},{4,12},{5,13},{6,14},{7,15},{8,0},{9,1},... | collective-permute-start | bytes 786440 | tf_op jit(solution)/shard_map/ppermute | solution.py:42
  71.3 11.3 %all-to-all-start.1 = ((bf16[8,2,32,128]{3,2,1,0:T(8,128)(2,1)}), bf16[8,2,32,128]{3,2,1,0:T(8,128)(2,1)S(1)}, u32[]{:S(2)}, u32[]{:S(2)}) async-start(bf16[8,2,32,128]{3,2,1,0:T(8,128)(2,1)} %fusion), calls=%async_computation.1 | async-start | bytes 262144 | tf_op jit(solution)/shard_map/all_to_all | solution.py:451
  74.7 7.9 %copy-start.9 = (bf16[2,2,256,256]{3,2,1,0:T(8,128)(2,1)}, bf16[2,2,256,256]{3,2,1,0:T(8,128)(2,1)S(1)}, u32[]{:S(2)}) copy-start(bf16[2,2,256,256]{3,2,1,0:T(8,128)(2,1)S(1)} %collective-permute-done.11.refs_7_) | copy-start | bytes 1572868
  (6 other events, 15.1 us)

commit v8 on v7

--- a/solution.py
+++ b/solution.py
@@ -275,7 +275,7 @@
                         ref[apart, o, m] = both[o * per_row : (o + 1) * per_row].astype(ref.dtype)
 
 
-def place_kernel(sizes, kinds, parts, factor, *refs):
+def place_kernel(sizes, kinds, factor, *refs):
     n_scan, n_obj, tile_cols = sizes
     layers = refs[-4].shape[0]
     info = refs[0]
@@ -295,10 +295,8 @@
         top, bottom = (row, rows) if tile == OWN else (0, row)
         meets = (base + 1 >= first_block) & (base < first_block + blocks)
         copies = [
-            pltpu.make_async_copy(
-                patches[number] if part is None else patches[number].at[part], held.at[index, l], sems.at[index, l]
-            )
-            for l, (number, part) in enumerate(parts[index])
+            pltpu.make_async_copy(patches[index].at[l], held.at[index, l], sems.at[index, l])
+            for l in range(layers)
         ]
         spots.append((base, off, top, bottom, meets, copies))
 
@@ -426,32 +424,19 @@
         *others,
     )
 
-    here = [grad] + [along(grad, j) for j in range(1, chips)]
+    here = [along(grad, j) for j in range(1, chips)]
+    there = [send(grad, lambda s, o, j=j: (s + CORES * j, o + 1)) for j in range(chips)]
     chunks = (keep.astype(real) + across(give).astype(real)).astype(half)
     chunks = sum((along(chunks[j], j).astype(real) for j in range(1, chips)), chunks[0].astype(real)).astype(half)
-    there = outward(grad, 1)
-    late, chunks = lax.optimization_barrier((here[1:], chunks))
-    here = here[:1] + late
-    x_first = [outward(block[1], 1) for block in late]
-    obj_first = [along(there[0], j) for j in range(1, chips)]
-    held = here + [there] + x_first + obj_first
+    here, there, _ = lax.optimization_barrier((here, there, chunks))
+    chunks = lax.all_to_all(chunks, "obj", 0, 0, tiled=True)
+    there, chunks = lax.optimization_barrier((there, chunks))
+    held = [grad] + here + there
     held += [across(block) for block in held]
-    kinds, parts = [], []
-    for flip in range(2):
-        start = flip * (len(held) // 2)
-        for j in range(chips):
-            kinds.append((OWN, flip, j))
-            parts.append([(start + j, l) for l in range(layers)])
-        for j in range(chips):
-            kinds.append((PREVIOUS, flip, j))
-            if j == 0:
-                parts.append([(start + chips, l) for l in range(layers)])
-            else:
-                parts.append([(start + 2 * chips - 1 + j, None), (start + chips + j, None)])
-    chunks = lax.all_to_all(chunks, "obj", 0, 0, tiled=True)
+    kinds = [(tile, flip, j) for flip in range(2) for tile in (OWN, PREVIOUS) for j in range(chips)]
     factor = 1.0 / math.sqrt(n_scan * n_obj * slots // 2)
     object_grad, probe_grad = call(
-        (place_kernel, kinds, parts, factor),
+        (place_kernel, kinds, factor),
         [
             ((layers, 2, tile_rows, tile_cols // n_scan), real),
             ((modes, 2, length // n_obj, length // n_scan), real),

time: 87.9 us -> 80.9 us (0.920)
  waiting for transfers between devices: 46 us -> 26.9 us
  starting transfers between devices: 13.4 us -> 25.5 us
    all_to_all x1, starting transfers between devices: 3.37 us -> 15.6 us  [body(): chunks = lax.all_to_all(chunks, 'obj', 0, 0, tiled=True)]
    ppermute x16 -> x14, waiting for transfers between devices: 38.2 us -> 26.1 us  [send(): return lax.ppermute(block, AXES, route)]
    all_to_all x1, waiting for transfers between devices: 7.85 us -> 0.79 us  [body(): chunks = lax.all_to_all(chunks, 'obj', 0, 0, tiled=True)]
    ppermute x16 -> x14, starting transfers between devices: 10 us -> 9.86 us  [send(): return lax.ppermute(block, AXES, route)]
  transfers between devices with their start and end apart: 17 -> 15, of which waited for: 11 -> 11; matrix products, arithmetic and copies ran while one was open for 1% -> 1% of each run, Pallas kernels for 4% -> 5%
where the time goes in v8:
time: 80.9 us; the launch traced here: 80.8 us
  waiting for transfers between devices  26.9 us (33%)
  starting transfers between devices  25.5 us (32%)
  Pallas kernels  17.5 us (22%)
  blocking collectives  6.76 us (8%)
  local copies, waits for them, and re-layouts  1.64 us (2%)
  between operations  1.49 us (2%)
  other arithmetic  0.92 us (1%)
    ppermute x14, waiting for transfers between devices, send(): return lax.ppermute(block, AXES, route)  26.1 us
    pallas_call x5, Pallas kernels, call(): pl.pallas_call(functools.partial(kernel[0], sizes, *kernel[1:]), out_shap...  17.5 us
    all_to_all x1, starting transfers between devices, body(): chunks = lax.all_to_all(chunks, 'obj', 0, 0, tiled=True)  15.6 us
    ppermute x14, starting transfers between devices, send(): return lax.ppermute(block, AXES, route)  9.86 us
    all_to_all x1, blocking collectives, body(): lax.all_to_all(jnp.broadcast_to(both, (n_scan, 1, 16)), 'scan', 0, 0, til...  6.76 us
  transfers between devices with their start and end apart: 15, of which 11 were waited for; matrix products, arithmetic and copies ran while one was open for 1% of the time, Pallas kernels for 5%

profile of v8, /device:TPU:0, one launch (start us, length us, event | category | flops | bytes accessed | tf_op | source)
XLA Modules:
  0.0 80.8 jit_solution(6246203641888269641)
XLA Ops:
  1.3 0.8 reshape_squeeze.3
  2.1 3.0 %collective-permute-start = (s32[8]{0:T(128)S(1)}, s32[8]{0:T(128)S(1)}, u32[]{:S(2)}, u32[]{:S(2)}) collective-permute-start(s32[8]{0:T(128)S(1)} %pad_add_fusion), channel_id=1, source_target_pairs={{0,1},{1,2},{2,3},{3,4},{4,5},{5,6},{6,7},{7,0},{8,9},{9,10},{10,1... | collective-permute-start | bytes 104 | tf_op jit(solution)/shard_map/ppermute | solution.py:42
  5.1 4.6 %collective-permute-done = s32[8]{0:T(128)S(1)} collective-permute-done((s32[8]{0:T(128)S(1)}, s32[8]{0:T(128)S(1)}, u32[]{:S(2)}, u32[]{:S(2)}) %collective-permute-start) | collective-permute-done | bytes 64 | tf_op jit(solution)/shard_map/ppermute | solution.py:42
  9.7 6.8 %all_to_all.10.info.refs_0_ = s32[4,1,16]{2,1,0:T(1,128)} all-to-all(s32[4,1,16]{2,1,0:T(1,128)S(1)} %broadcast_in_dim.3), channel_id=1, replica_groups=mesh['scan'=4,'obj'=8] {'scan'}, dimensions={0} | all-to-all | bytes 512 | tf_op jit(solution)/shard_map/all_to_all | solution.py:373
  16.5 3.2 %cut.1 = bf16[2,2,256,256]{3,2,1,0:T(8,128)(2,1)} custom-call(s32[4,1,16]{2,1,0:T(1,128)} %all_to_all.10.info.refs_0_, f32[2,2,256,2048]{3,2,1,0:T(8,128)} %object_ref.3), custom_call_target="tpu_custom_call" | custom-call | flops 1048576 | bytes 4194304 | tf_op jit(solution)/shard_map/cut/pallas_call | solution.py:351
  19.7 2.1 %collective-permute-start.1 = (bf16[2,2,256,256]{3,2,1,0:T(8,128)(2,1)}, bf16[2,2,256,256]{3,2,1,0:T(8,128)(2,1)S(1)}, u32[]{:S(2)}, u32[]{:S(2)}) collective-permute-start(bf16[2,2,256,256]{3,2,1,0:T(8,128)(2,1)} %cut.1), channel_id=1, source_target_pairs={{0,7},{1,0},{2,1},{3,2},{4,3},{5,4},{6,5},{7,6},{8,15},{9,8},{10,9... | collective-permute-start | bytes 1572872 | tf_op jit(solution)/shard_map/ppermute | solution.py:42
  21.9 1.0 %collective-permute-start.3 = (bf16[256,256]{1,0:T(8,128)(2,1)S(1)}, bf16[256,256]{1,0:T(8,128)(2,1)S(1)}, u32[]{:S(2)}, u32[]{:S(2)}) collective-permute-start(bf16[256,256]{1,0:T(8,128)(2,1)S(1)} %slice_bitcast_fusion.2), channel_id=1, source_target_pairs={{0,16},{1,17},{2,18},{3,19},{4,20},{5,21},{6,22},{7,23},{8,24},{9,... | collective-permute-start | bytes 393224 | tf_op jit(solution)/shard_map/ppermute | solution.py:42
  22.9 2.2 %own.1.refs_4_ = f32[2,2,256,256]{3,2,1,0:T(8,128)S(1)} custom-call(s32[4,1,16]{2,1,0:T(1,128)S(1)} %copy-done.4, f32[2,2,256,2048]{3,2,1,0:T(8,128)} %object_ref.3), custom_call_target="tpu_custom_call" | custom-call | flops 1048576 | bytes 4194304 | tf_op jit(solution)/shard_map/own/pallas_call | solution.py:351
  25.2 1.5 %prep.1 = (bf16[4,512,512]{2,1,0:T(8,128)(2,1)S(1)}, f32[2,2,256,256]{3,2,1,0:T(8,128)S(1)}) custom-call(s32[4,1,16]{2,1,0:T(1,128)S(1)} %copy-done.4, f32[2,2,256,256]{3,2,1,0:T(8,128)S(1)} %copy-done, f32[2,256,256]{2,1,0:T(8,128)S(1)} %copy-done.1), custom_call_target="tpu_custom_call" | custom-call | flops 1048576 | bytes 4194304 | tf_op jit(solution)/shard_map/prep/pallas_call | solution.py:351
  26.7 2.9 %collective-permute-done.3.refs_8_ = bf16[256,256]{1,0:T(8,128)(2,1)S(1)} collective-permute-done((bf16[256,256]{1,0:T(8,128)(2,1)S(1)}, bf16[256,256]{1,0:T(8,128)(2,1)S(1)}, u32[]{:S(2)}, u32[]{:S(2)}) %collective-permute-start.3) | collective-permute-done | bytes 131104 | tf_op jit(solution)/shard_map/ppermute | solution.py:42
  30.1 3.4 %collective-permute-done.1.refs_5_ = bf16[2,2,256,256]{3,2,1,0:T(8,128)(2,1)S(1)} collective-permute-done((bf16[2,2,256,256]{3,2,1,0:T(8,128)(2,1)}, bf16[2,2,256,256]{3,2,1,0:T(8,128)(2,1)S(1)}, u32[]{:S(2)}, u32[]{:S(2)}) %collective-permute-start.1) | collective-permute-done | bytes 524320 | tf_op jit(solution)/shard_map/ppermute | solution.py:42
  33.5 6.3 %pattern.1 = (bf16[2,2,256,256]{3,2,1,0:T(8,128)(2,1)S(1)}, bf16[2,8,2,32,128]{4,3,2,1,0:T(8,128)(2,1)S(1)}, bf16[2,8,2,32,128]{4,3,2,1,0:T(8,128)(2,1)S(1)}) custom-call(s32[4,1,16]{2,1,0:T(1,128)S(1)} %copy-done.4, bf16[4,512,512]{2,1,0:T(8,128)(2,1)S(1)} %get-tuple-element.16.refs_1_, f32[2,256,256]{2,1,0:T(8,128)S(1)} %copy-done.5, ...), custom_call_target="tpu_custom_call" | custom-call | flops 3221225472 | bytes 4194304 | tf_op jit(solution)/shard_map/pattern/pallas_call | solution.py:351
  39.9 1.5 %collective-permute-done.8 = bf16[2,8,2,32,128]{4,3,2,1,0:T(8,128)(2,1)S(1)} collective-permute-done((bf16[2,8,2,32,128]{4,3,2,1,0:T(8,128)(2,1)S(1)}, bf16[2,8,2,32,128]{4,3,2,1,0:T(8,128)(2,1)S(1)}, u32[]{:S(2)}, u32[]{:S(2)}) %collective-permute-start.8) | collective-permute-done | bytes 262176 | tf_op jit(solution)/shard_map/ppermute | solution.py:42
  41.8 1.2 %collective-permute-start.7 = (bf16[2,2,256,256]{3,2,1,0:T(8,128)(2,1)S(1)}, bf16[2,2,256,256]{3,2,1,0:T(8,128)(2,1)S(1)}, u32[]{:S(2)}, u32[]{:S(2)}) collective-permute-start(bf16[2,2,256,256]{3,2,1,0:T(8,128)(2,1)S(1)} %get-tuple-element.19.refs_2_), channel_id=1, source_target_pairs={{0,17},{1,18},{2,19},{3,20},{4,21},{5,22},{6,23},{7,16},{8,25},{9,... | collective-permute-start | bytes 1572872 | tf_op jit(solution)/shard_map/ppermute | solution.py:42
  42.9 1.5 %collective-permute-start.6 = (bf16[2,2,256,256]{3,2,1,0:T(8,128)(2,1)S(1)}, bf16[2,2,256,256]{3,2,1,0:T(8,128)(2,1)S(1)}, u32[]{:S(2)}, u32[]{:S(2)}) collective-permute-start(bf16[2,2,256,256]{3,2,1,0:T(8,128)(2,1)S(1)} %get-tuple-element.19.refs_2_), channel_id=1, source_target_pairs={{0,1},{1,2},{2,3},{3,4},{4,5},{5,6},{6,7},{7,0},{8,9},{9,10},{10,1... | collective-permute-start | bytes 1572872 | tf_op jit(solution)/shard_map/ppermute | solution.py:42
  44.6 3.3 %collective-permute-done.9 = bf16[8,2,32,128]{3,2,1,0:T(8,128)(2,1)S(1)} collective-permute-done((bf16[8,2,32,128]{3,2,1,0:T(8,128)(2,1)S(1)}, bf16[8,2,32,128]{3,2,1,0:T(8,128)(2,1)S(1)}, u32[]{:S(2)}, u32[]{:S(2)}) %collective-permute-start.9) | collective-permute-done | bytes 131104 | tf_op jit(solution)/shard_map/ppermute | solution.py:42
  47.9 0.7 fusion
  48.6 15.6 %all-to-all-start.1 = ((bf16[8,2,32,128]{3,2,1,0:T(8,128)(2,1)}), bf16[8,2,32,128]{3,2,1,0:T(8,128)(2,1)S(1)}, u32[]{:S(2)}, u32[]{:S(2)}) async-start(bf16[8,2,32,128]{3,2,1,0:T(8,128)(2,1)} %fusion), calls=%async_computation.1 | async-start | bytes 262144 | tf_op jit(solution)/shard_map/all_to_all | solution.py:432
  64.3 7.8 %collective-permute-done.6.refs_4_ = bf16[2,2,256,256]{3,2,1,0:T(8,128)(2,1)S(1)} collective-permute-done((bf16[2,2,256,256]{3,2,1,0:T(8,128)(2,1)S(1)}, bf16[2,2,256,256]{3,2,1,0:T(8,128)(2,1)S(1)}, u32[]{:S(2)}, u32[]{:S(2)}) %collective-permute-start.6) | collective-permute-done | bytes 524320 | tf_op jit(solution)/shard_map/ppermute | solution.py:42
  72.2 0.8 all-to-all-done.1.refs_1_
  74.1 0.8 %collective-permute-done.12.refs_8_ = bf16[2,2,256,256]{3,2,1,0:T(8,128)(2,1)S(1)} collective-permute-done((bf16[2,2,256,256]{3,2,1,0:T(8,128)(2,1)S(1)}, bf16[2,2,256,256]{3,2,1,0:T(8,128)(2,1)S(1)}, u32[]{:S(2)}, u32[]{:S(2)}) %collective-permute-start.12) | collective-permute-done | bytes 524320 | tf_op jit(solution)/shard_map/ppermute | solution.py:42
  74.9 0.7 collective-permute-done.13.refs_9_
  75.7 0.8 copy-done.13
  76.5 4.3 %place.1 = (f32[2,2,256,512]{3,2,1,0:T(8,128)}, f32[2,2,32,64]{3,2,1,0:T(8,128)}) custom-call(s32[4,1,16]{2,1,0:T(1,128)} %all_to_all.10.info.refs_0_, bf16[8,2,32,128]{3,2,1,0:T(8,128)(2,1)} %copy-done.6, bf16[2,2,256,256]{3,2,1,0:T(8,128)(2,1)} %copy-done.2, bf16[2,2,256,256]{3,2,1,0:T(8,128)(2,1)} %copy-done.9, bf16[2,2,256,256]{3,2,1,0:T(8,128)(2,1)} %copy-done.8, ...), custom_call_target="tpu_custom_call" | custom-call | flops 1048576 | bytes 4194304 | tf_op jit(solution)/shard_map/place/pallas_call | solution.py:351
  (49 shorter events, 2.6 us)
Async XLA Ops:
  2.1 7.5 %collective-permute-start = (s32[8]{0:T(128)S(1)}, s32[8]{0:T(128)S(1)}, u32[]{:S(2)}, u32[]{:S(2)}) collective-permute-start(s32[8]{0:T(128)S(1)} %pad_add_fusion), channel_id=1, source_target_pairs={{0,1},{1,2},{2,3},{3,4},{4,5},{5,6},{6,7},{7,0},{8,9},{9,10},{10,1... | collective-permute-start | bytes 104 | tf_op jit(solution)/shard_map/ppermute | solution.py:42
  16.5 5.3 %copy-start.3 = (bf16[1,1,2,256,256]{4,3,2,1,0:T(8,128)(2,1)S(1)}, bf16[1,1,2,256,256]{4,3,2,1,0:T(8,128)(2,1)}, u32[]{:S(2)}) copy-start(bf16[1,1,2,256,256]{4,3,2,1,0:T(8,128)(2,1)} %param.9) | copy-start | bytes 786436
  16.5 6.4 %copy-start.4 = (s32[4,1,16]{2,1,0:T(1,128)S(1)}, s32[4,1,16]{2,1,0:T(1,128)}, u32[]{:S(2)}) copy-start(s32[4,1,16]{2,1,0:T(1,128)} %all_to_all.10.info.refs_0_) | copy-start | bytes 772
  19.7 13.8 %collective-permute-start.1 = (bf16[2,2,256,256]{3,2,1,0:T(8,128)(2,1)}, bf16[2,2,256,256]{3,2,1,0:T(8,128)(2,1)S(1)}, u32[]{:S(2)}, u32[]{:S(2)}) collective-permute-start(bf16[2,2,256,256]{3,2,1,0:T(8,128)(2,1)} %cut.1), channel_id=1, source_target_pairs={{0,7},{1,0},{2,1},{3,2},{4,3},{5,4},{6,5},{7,6},{8,15},{9,8},{10,9... | collective-permute-start | bytes 1572872 | tf_op jit(solution)/shard_map/ppermute | solution.py:42
  21.8 3.3 %copy-start = (f32[2,2,256,256]{3,2,1,0:T(8,128)S(1)}, f32[2,2,256,256]{3,2,1,0:T(8,128)}, u32[]{:S(2)}) copy-start(f32[2,2,256,256]{3,2,1,0:T(8,128)} %probe_ref.1) | copy-start | bytes 3145732
  21.8 3.3 %copy-start.1 = (f32[2,256,256]{2,1,0:T(8,128)S(1)}, f32[2,256,256]{2,1,0:T(8,128)}, u32[]{:S(2)}) copy-start(f32[2,256,256]{2,1,0:T(8,128)} %constant.6.clone.dft_ref) | copy-start | bytes 1572868
  21.9 11.6 %copy-start.5 = (f32[2,256,256]{2,1,0:T(8,128)S(1)}, f32[2,256,256]{2,1,0:T(8,128)}, u32[]{:S(2)}) copy-start(f32[2,256,256]{2,1,0:T(8,128)} %constant.7.clone.refs_2_) | copy-start | bytes 1572868
  21.9 4.8 %collective-permute-start.4 = (bf16[256,256]{1,0:T(8,128)(2,1)S(1)}, bf16[256,256]{1,0:T(8,128)(2,1)S(1)}, u32[]{:S(2)}, u32[]{:S(2)}) collective-permute-start(bf16[256,256]{1,0:T(8,128)(2,1)S(1)} %slice_bitcast_fusion.2), channel_id=1, source_target_pairs={{0,24},{1,25},{2,26},{3,27},{4,28},{5,29},{6,30},{7,31},{8,0},{9,1... | collective-permute-start | bytes 393224 | tf_op jit(solution)/shard_map/ppermute | solution.py:42
  21.9 7.6 %collective-permute-start.3 = (bf16[256,256]{1,0:T(8,128)(2,1)S(1)}, bf16[256,256]{1,0:T(8,128)(2,1)S(1)}, u32[]{:S(2)}, u32[]{:S(2)}) collective-permute-start(bf16[256,256]{1,0:T(8,128)(2,1)S(1)} %slice_bitcast_fusion.2), channel_id=1, source_target_pairs={{0,16},{1,17},{2,18},{3,19},{4,20},{5,21},{6,22},{7,23},{8,24},{9,... | collective-permute-start | bytes 393224 | tf_op jit(solution)/shard_map/ppermute | solution.py:42
  22.9 7.2 %collective-permute-start.2 = (bf16[256,256]{1,0:T(8,128)(2,1)S(1)}, bf16[256,256]{1,0:T(8,128)(2,1)S(1)}, u32[]{:S(2)}, u32[]{:S(2)}) collective-permute-start(bf16[256,256]{1,0:T(8,128)(2,1)S(1)} %slice_bitcast_fusion.2), channel_id=1, source_target_pairs={{0,8},{1,9},{2,10},{3,11},{4,12},{5,13},{6,14},{7,15},{8,16},{9,17... | collective-permute-start | bytes 393224 | tf_op jit(solution)/shard_map/ppermute | solution.py:42
  39.8 35.8 %copy-start.2 = (bf16[2,2,256,256]{3,2,1,0:T(8,128)(2,1)}, bf16[2,2,256,256]{3,2,1,0:T(8,128)(2,1)S(1)}, u32[]{:S(2)}) copy-start(bf16[2,2,256,256]{3,2,1,0:T(8,128)(2,1)S(1)} %get-tuple-element.19.refs_2_) | copy-start | bytes 1572868
  39.8 1.6 %collective-permute-start.8 = (bf16[2,8,2,32,128]{4,3,2,1,0:T(8,128)(2,1)S(1)}, bf16[2,8,2,32,128]{4,3,2,1,0:T(8,128)(2,1)S(1)}, u32[]{:S(2)}, u32[]{:S(2)}) collective-permute-start(bf16[2,8,2,32,128]{4,3,2,1,0:T(8,128)(2,1)S(1)} %get-tuple-element.21), channel_id=1, source_target_pairs={{0,8},{1,9},{2,10},{3,11},{4,12},{5,13},{6,14},{7,15},{8,0},{9,1},... | collective-permute-start | bytes 786440 | tf_op jit(solution)/shard_map/ppermute | solution.py:42
  41.5 6.4 %collective-permute-start.9 = (bf16[8,2,32,128]{3,2,1,0:T(8,128)(2,1)S(1)}, bf16[8,2,32,128]{3,2,1,0:T(8,128)(2,1)S(1)}, u32[]{:S(2)}, u32[]{:S(2)}) collective-permute-start(bf16[8,2,32,128]{3,2,1,0:T(8,128)(2,1)S(1)} %slice_bitcast_fusion), channel_id=1, source_target_pairs={{0,16},{1,17},{2,18},{3,19},{4,20},{5,21},{6,22},{7,23},{8,24},{9,... | collective-permute-start | bytes 393224 | tf_op jit(solution)/shard_map/ppermute | solution.py:42
  41.8 22.5 %collective-permute-start.7 = (bf16[2,2,256,256]{3,2,1,0:T(8,128)(2,1)S(1)}, bf16[2,2,256,256]{3,2,1,0:T(8,128)(2,1)S(1)}, u32[]{:S(2)}, u32[]{:S(2)}) collective-permute-start(bf16[2,2,256,256]{3,2,1,0:T(8,128)(2,1)S(1)} %get-tuple-element.19.refs_2_), channel_id=1, source_target_pairs={{0,17},{1,18},{2,19},{3,20},{4,21},{5,22},{6,23},{7,16},{8,25},{9,... | collective-permute-start | bytes 1572872 | tf_op jit(solution)/shard_map/ppermute | solution.py:42
  42.9 29.2 %collective-permute-start.6 = (bf16[2,2,256,256]{3,2,1,0:T(8,128)(2,1)S(1)}, bf16[2,2,256,256]{3,2,1,0:T(8,128)(2,1)S(1)}, u32[]{:S(2)}, u32[]{:S(2)}) collective-permute-start(bf16[2,2,256,256]{3,2,1,0:T(8,128)(2,1)S(1)} %get-tuple-element.19.refs_2_), channel_id=1, source_target_pairs={{0,1},{1,2},{2,3},{3,4},{4,5},{5,6},{6,7},{7,0},{8,9},{9,10},{10,1... | collective-permute-start | bytes 1572872 | tf_op jit(solution)/shard_map/ppermute | solution.py:42
  44.5 27.6 %collective-permute-start.5 = (bf16[2,2,256,256]{3,2,1,0:T(8,128)(2,1)S(1)}, bf16[2,2,256,256]{3,2,1,0:T(8,128)(2,1)S(1)}, u32[]{:S(2)}, u32[]{:S(2)}) collective-permute-start(bf16[2,2,256,256]{3,2,1,0:T(8,128)(2,1)S(1)} %get-tuple-element.19.refs_2_), channel_id=1, source_target_pairs={{0,16},{1,17},{2,18},{3,19},{4,20},{5,21},{6,22},{7,23},{8,24},{9,... | collective-permute-start | bytes 1572872 | tf_op jit(solution)/shard_map/ppermute | solution.py:42
  48.6 24.3 %all-to-all-start.1 = ((bf16[8,2,32,128]{3,2,1,0:T(8,128)(2,1)}), bf16[8,2,32,128]{3,2,1,0:T(8,128)(2,1)S(1)}, u32[]{:S(2)}, u32[]{:S(2)}) async-start(bf16[8,2,32,128]{3,2,1,0:T(8,128)(2,1)} %fusion), calls=%async_computation.1 | async-start | bytes 262144 | tf_op jit(solution)/shard_map/all_to_all | solution.py:432
  64.2 9.2 %collective-permute-start.10 = (bf16[2,2,256,256]{3,2,1,0:T(8,128)(2,1)S(1)}, bf16[2,2,256,256]{3,2,1,0:T(8,128)(2,1)S(1)}, u32[]{:S(2)}, u32[]{:S(2)}) collective-permute-start(bf16[2,2,256,256]{3,2,1,0:T(8,128)(2,1)S(1)} %get-tuple-element.19.refs_2_), channel_id=1, source_target_pairs={{0,8},{1,9},{2,10},{3,11},{4,12},{5,13},{6,14},{7,15},{8,0},{9,1},... | collective-permute-start | bytes 1572872 | tf_op jit(solution)/shard_map/ppermute | solution.py:42
  64.3 11.4 %copy-start.7 = (bf16[2,2,256,256]{3,2,1,0:T(8,128)(2,1)}, bf16[2,2,256,256]{3,2,1,0:T(8,128)(2,1)S(1)}, u32[]{:S(2)}) copy-start(bf16[2,2,256,256]{3,2,1,0:T(8,128)(2,1)S(1)} %collective-permute-done.7.refs_5_) | copy-start | bytes 1572868
  72.1 3.5 %copy-start.8 = (bf16[2,2,256,256]{3,2,1,0:T(8,128)(2,1)}, bf16[2,2,256,256]{3,2,1,0:T(8,128)(2,1)S(1)}, u32[]{:S(2)}) copy-start(bf16[2,2,256,256]{3,2,1,0:T(8,128)(2,1)S(1)} %collective-permute-done.6.refs_4_) | copy-start | bytes 1572868
  72.1 3.5 %copy-start.9 = (bf16[2,2,256,256]{3,2,1,0:T(8,128)(2,1)}, bf16[2,2,256,256]{3,2,1,0:T(8,128)(2,1)S(1)}, u32[]{:S(2)}) copy-start(bf16[2,2,256,256]{3,2,1,0:T(8,128)(2,1)S(1)} %collective-permute-done.5.refs_3_) | copy-start | bytes 1572868
  72.1 2.0 %collective-permute-start.11 = (bf16[2,2,256,256]{3,2,1,0:T(8,128)(2,1)S(1)}, bf16[2,2,256,256]{3,2,1,0:T(8,128)(2,1)S(1)}, u32[]{:S(2)}, u32[]{:S(2)}) collective-permute-start(bf16[2,2,256,256]{3,2,1,0:T(8,128)(2,1)S(1)} %collective-permute-done.5.refs_3_), channel_id=1, source_target_pairs={{0,8},{1,9},{2,10},{3,11},{4,12},{5,13},{6,14},{7,15},{8,0},{9,1},... | collective-permute-start | bytes 1572872 | tf_op jit(solution)/shard_map/ppermute | solution.py:42
  73.0 1.9 %collective-permute-start.12 = (bf16[2,2,256,256]{3,2,1,0:T(8,128)(2,1)S(1)}, bf16[2,2,256,256]{3,2,1,0:T(8,128)(2,1)S(1)}, u32[]{:S(2)}, u32[]{:S(2)}) collective-permute-start(bf16[2,2,256,256]{3,2,1,0:T(8,128)(2,1)S(1)} %collective-permute-done.6.refs_4_), channel_id=1, source_target_pairs={{0,8},{1,9},{2,10},{3,11},{4,12},{5,13},{6,14},{7,15},{8,0},{9,1},... | collective-permute-start | bytes 1572872 | tf_op jit(solution)/shard_map/ppermute | solution.py:42
  73.0 2.7 %collective-permute-start.13 = (bf16[2,2,256,256]{3,2,1,0:T(8,128)(2,1)S(1)}, bf16[2,2,256,256]{3,2,1,0:T(8,128)(2,1)S(1)}, u32[]{:S(2)}, u32[]{:S(2)}) collective-permute-start(bf16[2,2,256,256]{3,2,1,0:T(8,128)(2,1)S(1)} %collective-permute-done.7.refs_5_), channel_id=1, source_target_pairs={{0,8},{1,9},{2,10},{3,11},{4,12},{5,13},{6,14},{7,15},{8,0},{9,1},... | collective-permute-start | bytes 1572872 | tf_op jit(solution)/shard_map/ppermute | solution.py:42
  (5 other events, 8.1 us)

commit v9 on v7

--- a/solution.py
+++ b/solution.py
@@ -190,6 +190,7 @@
     grad_ref, keep_ref, give_ref, v_ref, u_ref, s_ref, x_ref, a_ref, meas_ref = refs[6 + n_scan :]
     modes, _, length, _ = p_ref.shape
     me = lax.axis_index("scan")
+    here = lax.axis_index("obj")
     core, chip, chips = lax.rem(me, CORES), lax.div(me, CORES), n_scan // CORES
     source, slot, row, col = assigned(info, OWN, me, n_scan)
     _, off = column_block(col, length, tile_cols)
@@ -272,7 +273,7 @@
                 @pl.when(mine == s % CORES)
                 def _():
                     for o in range(n_obj):
-                        ref[apart, o, m] = both[o * per_row : (o + 1) * per_row].astype(ref.dtype)
+                        ref[apart, o ^ here, m] = both[o * per_row : (o + 1) * per_row].astype(ref.dtype)
 
 
 def place_kernel(sizes, kinds, parts, factor, *refs):
@@ -310,7 +311,7 @@
     out_ref[...] = jnp.zeros(out_ref.shape, jnp.float32)
     per_col = probe_out.shape[3]
     for m in range(probe_out.shape[0]):
-        total = sum(chunks[o, m].astype(jnp.float32) for o in range(n_obj)) * factor
+        total = chunks[0, m].astype(jnp.float32) * factor
         probe_out[m, 0] = total[:, :per_col]
         probe_out[m, 1] = total[:, per_col:]
     lane, line = lanes(length), lines(length)
@@ -426,15 +427,24 @@
         *others,
     )
 
-    here = [grad] + [along(grad, j) for j in range(1, chips)]
-    chunks = (keep.astype(real) + across(give).astype(real)).astype(half)
-    chunks = sum((along(chunks[j], j).astype(real) for j in range(1, chips)), chunks[0].astype(real)).astype(half)
+    def narrow(block):
+        return block.astype(half)
+
+    far = range(1, chips)
+    here = [along(grad, j) for j in far]
+    sums = narrow(keep.astype(real) + across(give).astype(real))
     there = outward(grad, 1)
-    late, chunks = lax.optimization_barrier((here[1:], chunks))
-    here = here[:1] + late
-    x_first = [outward(block[1], 1) for block in late]
-    obj_first = [along(there[0], j) for j in range(1, chips)]
-    held = here + [there] + x_first + obj_first
+    sums = narrow(sum((along(sums[j], j).astype(real) for j in far), sums[0].astype(real)))
+    width = n_obj // 2
+    while width:
+        if width == n_obj // 4:
+            here, there, sums = lax.optimization_barrier((here, there, sums))
+        other = send(sums[width:], lambda s, o: (s, o ^ width))
+        sums = narrow(sums[:width].astype(real) + other.astype(real))
+        width //= 2
+    x_first = [outward(block[1], 1) for block in here]
+    obj_first = [along(there[0], j) for j in far]
+    held = [grad] + here + [there] + x_first + obj_first
     held += [across(block) for block in held]
     kinds, parts = [], []
     for flip in range(2):
@@ -448,7 +458,6 @@
                 parts.append([(start + chips, l) for l in range(layers)])
             else:
                 parts.append([(start + 2 * chips - 1 + j, None), (start + chips + j, None)])
-    chunks = lax.all_to_all(chunks, "obj", 0, 0, tiled=True)
     factor = 1.0 / math.sqrt(n_scan * n_obj * slots // 2)
     object_grad, probe_grad = call(
         (place_kernel, kinds, parts, factor),
@@ -465,7 +474,7 @@
         MIB,
         LARGE,
         info,
-        chunks,
+        sums,
         *held,
     )
     return (object_grad, probe_grad)

time: 87.9 us -> 85.8 us (0.976)
  waiting for transfers between devices: 46 us -> 41.1 us
  starting transfers between devices: 13.4 us -> 16.4 us
    all_to_all x1 -> x0, waiting for transfers between devices: 7.85 us -> none  [body(): chunks = lax.all_to_all(chunks, 'obj', 0, 0, tiled=True)]
    ppermute x16 -> x19, starting transfers between devices: 10 us -> 16.4 us  [send(): return lax.ppermute(block, AXES, route)]
    all_to_all x1 -> x0, starting transfers between devices: 3.37 us -> none  [body(): chunks = lax.all_to_all(chunks, 'obj', 0, 0, tiled=True)]
    ppermute x16 -> x19, waiting for transfers between devices: 38.2 us -> 41.1 us  [send(): return lax.ppermute(block, AXES, route)]
  transfers between devices with their start and end apart: 17 -> 19, of which waited for: 11 -> 12; matrix products, arithmetic and copies ran while one was open for 1% -> 1% of each run, Pallas kernels for 4% -> 4%
where the time goes in v9:
time: 85.8 us; the launch traced here: 85.3 us
  waiting for transfers between devices  41.1 us (48%)
  Pallas kernels  16.8 us (20%)
  starting transfers between devices  16.4 us (19%)
  blocking collectives  6.55 us (8%)
  local copies, waits for them, and re-layouts  1.9 us (2%)
  between operations  1.58 us (2%)
  other arithmetic  0.96 us (1%)
    ppermute x19, waiting for transfers between devices, send(): return lax.ppermute(block, AXES, route)  41.1 us
    pallas_call x5, Pallas kernels, call(): pl.pallas_call(functools.partial(kernel[0], sizes, *kernel[1:]), out_shap...  16.8 us
    ppermute x19, starting transfers between devices, send(): return lax.ppermute(block, AXES, route)  16.4 us
    all_to_all x1, blocking collectives, body(): lax.all_to_all(jnp.broadcast_to(both, (n_scan, 1, 16)), 'scan', 0, 0, til...  6.55 us
  transfers between devices with their start and end apart: 19, of which 12 were waited for; matrix products, arithmetic and copies ran while one was open for 1% of the time, Pallas kernels for 4%

profile of v9, /device:TPU:0, one launch (start us, length us, event | category | flops | bytes accessed | tf_op | source)
XLA Modules:
  0.0 85.3 jit_solution(11237835064654542149)
XLA Ops:
  2.1 3.0 %collective-permute-start = (s32[8]{0:T(128)S(1)}, s32[8]{0:T(128)S(1)}, u32[]{:S(2)}, u32[]{:S(2)}) collective-permute-start(s32[8]{0:T(128)S(1)} %pad_add_fusion), channel_id=1, source_target_pairs={{0,1},{1,2},{2,3},{3,4},{4,5},{5,6},{6,7},{7,0},{8,9},{9,10},{10,1... | collective-permute-start | bytes 104 | tf_op jit(solution)/shard_map/ppermute | solution.py:42
  5.1 4.6 %collective-permute-done = s32[8]{0:T(128)S(1)} collective-permute-done((s32[8]{0:T(128)S(1)}, s32[8]{0:T(128)S(1)}, u32[]{:S(2)}, u32[]{:S(2)}) %collective-permute-start) | collective-permute-done | bytes 64 | tf_op jit(solution)/shard_map/ppermute | solution.py:42
  9.7 6.5 %all_to_all.5.info.refs_0_ = s32[4,1,16]{2,1,0:T(1,128)} all-to-all(s32[4,1,16]{2,1,0:T(1,128)S(1)} %broadcast_in_dim.3), channel_id=1, replica_groups=mesh['scan'=4,'obj'=8] {'scan'}, dimensions={0} | all-to-all | bytes 512 | tf_op jit(solution)/shard_map/all_to_all | solution.py:376
  16.3 3.2 %cut.1 = bf16[2,2,256,256]{3,2,1,0:T(8,128)(2,1)} custom-call(s32[4,1,16]{2,1,0:T(1,128)} %all_to_all.5.info.refs_0_, f32[2,2,256,2048]{3,2,1,0:T(8,128)} %object_ref.3), custom_call_target="tpu_custom_call" | custom-call | flops 1048576 | bytes 4194304 | tf_op jit(solution)/shard_map/cut/pallas_call | solution.py:354
  19.5 2.1 %collective-permute-start.1 = (bf16[2,2,256,256]{3,2,1,0:T(8,128)(2,1)}, bf16[2,2,256,256]{3,2,1,0:T(8,128)(2,1)S(1)}, u32[]{:S(2)}, u32[]{:S(2)}) collective-permute-start(bf16[2,2,256,256]{3,2,1,0:T(8,128)(2,1)} %cut.1), channel_id=1, source_target_pairs={{0,7},{1,0},{2,1},{3,2},{4,3},{5,4},{6,5},{7,6},{8,15},{9,8},{10,9... | collective-permute-start | bytes 1572872 | tf_op jit(solution)/shard_map/ppermute | solution.py:42
  21.7 1.3 %collective-permute-start.3 = (bf16[256,256]{1,0:T(8,128)(2,1)S(1)}, bf16[256,256]{1,0:T(8,128)(2,1)S(1)}, u32[]{:S(2)}, u32[]{:S(2)}) collective-permute-start(bf16[256,256]{1,0:T(8,128)(2,1)S(1)} %slice_bitcast_fusion.4), channel_id=1, source_target_pairs={{0,16},{1,17},{2,18},{3,19},{4,20},{5,21},{6,22},{7,23},{8,24},{9,... | collective-permute-start | bytes 393224 | tf_op jit(solution)/shard_map/ppermute | solution.py:42
  23.0 2.2 %own.1.refs_4_ = f32[2,2,256,256]{3,2,1,0:T(8,128)S(1)} custom-call(s32[4,1,16]{2,1,0:T(1,128)S(1)} %copy-done.4, f32[2,2,256,2048]{3,2,1,0:T(8,128)} %object_ref.3), custom_call_target="tpu_custom_call" | custom-call | flops 1048576 | bytes 4194304 | tf_op jit(solution)/shard_map/own/pallas_call | solution.py:354
  25.3 1.5 %prep.1 = (bf16[4,512,512]{2,1,0:T(8,128)(2,1)S(1)}, f32[2,2,256,256]{3,2,1,0:T(8,128)S(1)}) custom-call(s32[4,1,16]{2,1,0:T(1,128)S(1)} %copy-done.4, f32[2,2,256,256]{3,2,1,0:T(8,128)S(1)} %copy-done, f32[2,256,256]{2,1,0:T(8,128)S(1)} %copy-done.1), custom_call_target="tpu_custom_call" | custom-call | flops 1048576 | bytes 4194304 | tf_op jit(solution)/shard_map/prep/pallas_call | solution.py:354
  26.8 3.1 %collective-permute-done.3.refs_8_ = bf16[256,256]{1,0:T(8,128)(2,1)S(1)} collective-permute-done((bf16[256,256]{1,0:T(8,128)(2,1)S(1)}, bf16[256,256]{1,0:T(8,128)(2,1)S(1)}, u32[]{:S(2)}, u32[]{:S(2)}) %collective-permute-start.3) | collective-permute-done | bytes 131104 | tf_op jit(solution)/shard_map/ppermute | solution.py:42
  30.2 3.4 %collective-permute-done.1.refs_5_ = bf16[2,2,256,256]{3,2,1,0:T(8,128)(2,1)S(1)} collective-permute-done((bf16[2,2,256,256]{3,2,1,0:T(8,128)(2,1)}, bf16[2,2,256,256]{3,2,1,0:T(8,128)(2,1)S(1)}, u32[]{:S(2)}, u32[]{:S(2)}) %collective-permute-start.1) | collective-permute-done | bytes 524320 | tf_op jit(solution)/shard_map/ppermute | solution.py:42
  33.6 6.2 %pattern.1 = (bf16[2,2,256,256]{3,2,1,0:T(8,128)(2,1)S(1)}, bf16[2,8,2,32,128]{4,3,2,1,0:T(8,128)(2,1)S(1)}, bf16[2,8,2,32,128]{4,3,2,1,0:T(8,128)(2,1)S(1)}) custom-call(s32[4,1,16]{2,1,0:T(1,128)S(1)} %copy-done.4, bf16[4,512,512]{2,1,0:T(8,128)(2,1)S(1)} %get-tuple-element.13.refs_1_, f32[2,256,256]{2,1,0:T(8,128)S(1)} %copy-done.5, ...), custom_call_target="tpu_custom_call" | custom-call | flops 3221225472 | bytes 4194304 | tf_op jit(solution)/shard_map/pattern/pallas_call | solution.py:354
  39.9 1.5 %collective-permute-done.7 = bf16[2,8,2,32,128]{4,3,2,1,0:T(8,128)(2,1)S(1)} collective-permute-done((bf16[2,8,2,32,128]{4,3,2,1,0:T(8,128)(2,1)S(1)}, bf16[2,8,2,32,128]{4,3,2,1,0:T(8,128)(2,1)S(1)}, u32[]{:S(2)}, u32[]{:S(2)}) %collective-permute-start.7) | collective-permute-done | bytes 262176 | tf_op jit(solution)/shard_map/ppermute | solution.py:42
  41.7 1.9 %collective-permute-start.5 = (bf16[2,2,256,256]{3,2,1,0:T(8,128)(2,1)S(1)}, bf16[2,2,256,256]{3,2,1,0:T(8,128)(2,1)S(1)}, u32[]{:S(2)}, u32[]{:S(2)}) collective-permute-start(bf16[2,2,256,256]{3,2,1,0:T(8,128)(2,1)S(1)} %get-tuple-element.16.refs_2_), channel_id=1, source_target_pairs={{0,16},{1,17},{2,18},{3,19},{4,20},{5,21},{6,22},{7,23},{8,24},{9,... | collective-permute-start | bytes 1572872 | tf_op jit(solution)/shard_map/ppermute | solution.py:42
  43.6 4.3 %collective-permute-done.8 = bf16[8,2,32,128]{3,2,1,0:T(8,128)(2,1)S(1)} collective-permute-done((bf16[8,2,32,128]{3,2,1,0:T(8,128)(2,1)S(1)}, bf16[8,2,32,128]{3,2,1,0:T(8,128)(2,1)S(1)}, u32[]{:S(2)}, u32[]{:S(2)}) %collective-permute-start.8) | collective-permute-done | bytes 131104 | tf_op jit(solution)/shard_map/ppermute | solution.py:42
  48.0 1.0 %collective-permute-start.9 = (bf16[4,2,32,128]{3,2,1,0:T(8,128)(2,1)S(1)}, bf16[4,2,32,128]{3,2,1,0:T(8,128)(2,1)S(1)}, u32[]{:S(2)}, u32[]{:S(2)}) collective-permute-start(bf16[4,2,32,128]{3,2,1,0:T(8,128)(2,1)S(1)} %slice.47), channel_id=1, source_target_pairs={{0,4},{1,5},{2,6},{3,7},{4,0},{5,1},{6,2},{7,3},{8,12},{9,13},{10,... | collective-permute-start | bytes 196616 | tf_op jit(solution)/shard_map/ppermute | solution.py:42
  49.0 4.3 %collective-permute-done.9 = bf16[4,2,32,128]{3,2,1,0:T(8,128)(2,1)S(1)} collective-permute-done((bf16[4,2,32,128]{3,2,1,0:T(8,128)(2,1)S(1)}, bf16[4,2,32,128]{3,2,1,0:T(8,128)(2,1)S(1)}, u32[]{:S(2)}, u32[]{:S(2)}) %collective-permute-start.9) | collective-permute-done | bytes 65568 | tf_op jit(solution)/shard_map/ppermute | solution.py:42
  53.3 5.9 %collective-permute-done.6.refs_4_ = bf16[2,2,256,256]{3,2,1,0:T(8,128)(2,1)S(1)} collective-permute-done((bf16[2,2,256,256]{3,2,1,0:T(8,128)(2,1)S(1)}, bf16[2,2,256,256]{3,2,1,0:T(8,128)(2,1)S(1)}, u32[]{:S(2)}, u32[]{:S(2)}) %collective-permute-start.6) | collective-permute-done | bytes 524320 | tf_op jit(solution)/shard_map/ppermute | solution.py:42
  59.4 3.8 %collective-permute-done.10 = bf16[2,2,32,128]{3,2,1,0:T(8,128)(2,1)S(1)} collective-permute-done((bf16[2,2,32,128]{3,2,1,0:T(8,128)(2,1)S(1)}, bf16[2,2,32,128]{3,2,1,0:T(8,128)(2,1)S(1)}, u32[]{:S(2)}, u32[]{:S(2)}) %collective-permute-start.10) | collective-permute-done | bytes 32800 | tf_op jit(solution)/shard_map/ppermute | solution.py:42
  63.2 2.9 %collective-permute-start.11 = (bf16[1,2,32,128]{3,2,1,0:T(8,128)(2,1)S(1)}, bf16[1,2,32,128]{3,2,1,0:T(8,128)(2,1)S(1)}, u32[]{:S(2)}, u32[]{:S(2)}) collective-permute-start(bf16[1,2,32,128]{3,2,1,0:T(8,128)(2,1)S(1)} %slice.49), channel_id=1, source_target_pairs={{0,1},{1,0},{2,3},{3,2},{4,5},{5,4},{6,7},{7,6},{8,9},{9,8},{10,11... | collective-permute-start | bytes 49160 | tf_op jit(solution)/shard_map/ppermute | solution.py:42
  66.2 1.7 %collective-permute-start.13 = (bf16[2,256,256]{2,1,0:T(8,128)(2,1)S(1)}, bf16[2,256,256]{2,1,0:T(8,128)(2,1)S(1)}, u32[]{:S(2)}, u32[]{:S(2)}) collective-permute-start(bf16[2,256,256]{2,1,0:T(8,128)(2,1)S(1)} %slice_bitcast_fusion), channel_id=1, source_target_pairs={{0,16},{1,17},{2,18},{3,19},{4,20},{5,21},{6,22},{7,23},{8,24},{9,... | collective-permute-start | bytes 786440 | tf_op jit(solution)/shard_map/ppermute | solution.py:42
  68.0 1.9 %collective-permute-start.12 = (bf16[2,256,256]{2,1,0:T(8,128)(2,1)S(1)}, bf16[2,256,256]{2,1,0:T(8,128)(2,1)S(1)}, u32[]{:S(2)}, u32[]{:S(2)}) collective-permute-start(bf16[2,256,256]{2,1,0:T(8,128)(2,1)S(1)} %slice_bitcast_fusion.1), channel_id=1, source_target_pairs={{0,1},{1,2},{2,3},{3,4},{4,5},{5,6},{6,7},{7,0},{8,9},{9,10},{10,1... | collective-permute-start | bytes 786440 | tf_op jit(solution)/shard_map/ppermute | solution.py:42
  69.9 5.1 %collective-permute-done.13.refs_6_ = bf16[2,256,256]{2,1,0:T(8,128)(2,1)S(1)} collective-permute-done((bf16[2,256,256]{2,1,0:T(8,128)(2,1)S(1)}, bf16[2,256,256]{2,1,0:T(8,128)(2,1)S(1)}, u32[]{:S(2)}, u32[]{:S(2)}) %collective-permute-start.13) | collective-permute-done | bytes 262176 | tf_op jit(solution)/shard_map/ppermute | solution.py:42
  75.0 4.1 %collective-permute-done.12.refs_5_ = bf16[2,256,256]{2,1,0:T(8,128)(2,1)S(1)} collective-permute-done((bf16[2,256,256]{2,1,0:T(8,128)(2,1)S(1)}, bf16[2,256,256]{2,1,0:T(8,128)(2,1)S(1)}, u32[]{:S(2)}, u32[]{:S(2)}) %collective-permute-start.12) | collective-permute-done | bytes 262176 | tf_op jit(solution)/shard_map/ppermute | solution.py:42
  81.7 3.7 %place.1 = (f32[2,2,256,512]{3,2,1,0:T(8,128)}, f32[2,2,32,64]{3,2,1,0:T(8,128)}) custom-call(s32[4,1,16]{2,1,0:T(1,128)} %all_to_all.5.info.refs_0_, bf16[1,2,32,128]{3,2,1,0:T(8,128)(2,1)} %add_convert_fusion.3.refs_1_, bf16[2,2,256,256]{3,2,1,0:T(8,128)(2,1)} %copy-done.2, bf16[2,2,256,256]{3,2,1,0:T(8,128)(2,1)} %copy-done.7, ...), custom_call_target="tpu_custom_call" | custom-call | flops 1048576 | bytes 4194304 | tf_op jit(solution)/shard_map/place/pallas_call | solution.py:354
  (67 shorter events, 4.4 us)
Async XLA Ops:
  2.1 7.5 %collective-permute-start = (s32[8]{0:T(128)S(1)}, s32[8]{0:T(128)S(1)}, u32[]{:S(2)}, u32[]{:S(2)}) collective-permute-start(s32[8]{0:T(128)S(1)} %pad_add_fusion), channel_id=1, source_target_pairs={{0,1},{1,2},{2,3},{3,4},{4,5},{5,6},{6,7},{7,0},{8,9},{9,10},{10,1... | collective-permute-start | bytes 104 | tf_op jit(solution)/shard_map/ppermute | solution.py:42
  16.3 6.8 %copy-start.4 = (s32[4,1,16]{2,1,0:T(1,128)S(1)}, s32[4,1,16]{2,1,0:T(1,128)}, u32[]{:S(2)}) copy-start(s32[4,1,16]{2,1,0:T(1,128)} %all_to_all.5.info.refs_0_) | copy-start | bytes 772
  19.5 14.1 %collective-permute-start.1 = (bf16[2,2,256,256]{3,2,1,0:T(8,128)(2,1)}, bf16[2,2,256,256]{3,2,1,0:T(8,128)(2,1)S(1)}, u32[]{:S(2)}, u32[]{:S(2)}) collective-permute-start(bf16[2,2,256,256]{3,2,1,0:T(8,128)(2,1)} %cut.1), channel_id=1, source_target_pairs={{0,7},{1,0},{2,1},{3,2},{4,3},{5,4},{6,5},{7,6},{8,15},{9,8},{10,9... | collective-permute-start | bytes 1572872 | tf_op jit(solution)/shard_map/ppermute | solution.py:42
  21.6 11.9 %copy-start.5 = (f32[2,256,256]{2,1,0:T(8,128)S(1)}, f32[2,256,256]{2,1,0:T(8,128)}, u32[]{:S(2)}) copy-start(f32[2,256,256]{2,1,0:T(8,128)} %constant.7.clone.refs_2_) | copy-start | bytes 1572868
  21.7 5.1 %collective-permute-start.4 = (bf16[256,256]{1,0:T(8,128)(2,1)S(1)}, bf16[256,256]{1,0:T(8,128)(2,1)S(1)}, u32[]{:S(2)}, u32[]{:S(2)}) collective-permute-start(bf16[256,256]{1,0:T(8,128)(2,1)S(1)} %slice_bitcast_fusion.4), channel_id=1, source_target_pairs={{0,24},{1,25},{2,26},{3,27},{4,28},{5,29},{6,30},{7,31},{8,0},{9,1... | collective-permute-start | bytes 393224 | tf_op jit(solution)/shard_map/ppermute | solution.py:42
  21.7 8.2 %collective-permute-start.3 = (bf16[256,256]{1,0:T(8,128)(2,1)S(1)}, bf16[256,256]{1,0:T(8,128)(2,1)S(1)}, u32[]{:S(2)}, u32[]{:S(2)}) collective-permute-start(bf16[256,256]{1,0:T(8,128)(2,1)S(1)} %slice_bitcast_fusion.4), channel_id=1, source_target_pairs={{0,16},{1,17},{2,18},{3,19},{4,20},{5,21},{6,22},{7,23},{8,24},{9,... | collective-permute-start | bytes 393224 | tf_op jit(solution)/shard_map/ppermute | solution.py:42
  23.0 7.2 %collective-permute-start.2 = (bf16[256,256]{1,0:T(8,128)(2,1)S(1)}, bf16[256,256]{1,0:T(8,128)(2,1)S(1)}, u32[]{:S(2)}, u32[]{:S(2)}) collective-permute-start(bf16[256,256]{1,0:T(8,128)(2,1)S(1)} %slice_bitcast_fusion.4), channel_id=1, source_target_pairs={{0,8},{1,9},{2,10},{3,11},{4,12},{5,13},{6,14},{7,15},{8,16},{9,17... | collective-permute-start | bytes 393224 | tf_op jit(solution)/shard_map/ppermute | solution.py:42
  39.8 40.8 %copy-start.2 = (bf16[2,2,256,256]{3,2,1,0:T(8,128)(2,1)}, bf16[2,2,256,256]{3,2,1,0:T(8,128)(2,1)S(1)}, u32[]{:S(2)}) copy-start(bf16[2,2,256,256]{3,2,1,0:T(8,128)(2,1)S(1)} %get-tuple-element.16.refs_2_) | copy-start | bytes 1572868
  39.8 1.6 %collective-permute-start.7 = (bf16[2,8,2,32,128]{4,3,2,1,0:T(8,128)(2,1)S(1)}, bf16[2,8,2,32,128]{4,3,2,1,0:T(8,128)(2,1)S(1)}, u32[]{:S(2)}, u32[]{:S(2)}) collective-permute-start(bf16[2,8,2,32,128]{4,3,2,1,0:T(8,128)(2,1)S(1)} %get-tuple-element.18), channel_id=1, source_target_pairs={{0,8},{1,9},{2,10},{3,11},{4,12},{5,13},{6,14},{7,15},{8,0},{9,1},... | collective-permute-start | bytes 786440 | tf_op jit(solution)/shard_map/ppermute | solution.py:42
  41.5 6.4 %collective-permute-start.8 = (bf16[8,2,32,128]{3,2,1,0:T(8,128)(2,1)S(1)}, bf16[8,2,32,128]{3,2,1,0:T(8,128)(2,1)S(1)}, u32[]{:S(2)}, u32[]{:S(2)}) collective-permute-start(bf16[8,2,32,128]{3,2,1,0:T(8,128)(2,1)S(1)} %slice_bitcast_fusion.2), channel_id=1, source_target_pairs={{0,16},{1,17},{2,18},{3,19},{4,20},{5,21},{6,22},{7,23},{8,24},{9,... | collective-permute-start | bytes 393224 | tf_op jit(solution)/shard_map/ppermute | solution.py:42
  41.6 17.6 %collective-permute-start.6 = (bf16[2,2,256,256]{3,2,1,0:T(8,128)(2,1)S(1)}, bf16[2,2,256,256]{3,2,1,0:T(8,128)(2,1)S(1)}, u32[]{:S(2)}, u32[]{:S(2)}) collective-permute-start(bf16[2,2,256,256]{3,2,1,0:T(8,128)(2,1)S(1)} %get-tuple-element.16.refs_2_), channel_id=1, source_target_pairs={{0,1},{1,2},{2,3},{3,4},{4,5},{5,6},{6,7},{7,0},{8,9},{9,10},{10,1... | collective-permute-start | bytes 1572872 | tf_op jit(solution)/shard_map/ppermute | solution.py:42
  41.7 17.5 %collective-permute-start.5 = (bf16[2,2,256,256]{3,2,1,0:T(8,128)(2,1)S(1)}, bf16[2,2,256,256]{3,2,1,0:T(8,128)(2,1)S(1)}, u32[]{:S(2)}, u32[]{:S(2)}) collective-permute-start(bf16[2,2,256,256]{3,2,1,0:T(8,128)(2,1)S(1)} %get-tuple-element.16.refs_2_), channel_id=1, source_target_pairs={{0,16},{1,17},{2,18},{3,19},{4,20},{5,21},{6,22},{7,23},{8,24},{9,... | collective-permute-start | bytes 1572872 | tf_op jit(solution)/shard_map/ppermute | solution.py:42
  48.0 5.3 %collective-permute-start.9 = (bf16[4,2,32,128]{3,2,1,0:T(8,128)(2,1)S(1)}, bf16[4,2,32,128]{3,2,1,0:T(8,128)(2,1)S(1)}, u32[]{:S(2)}, u32[]{:S(2)}) collective-permute-start(bf16[4,2,32,128]{3,2,1,0:T(8,128)(2,1)S(1)} %slice.47), channel_id=1, source_target_pairs={{0,4},{1,5},{2,6},{3,7},{4,0},{5,1},{6,2},{7,3},{8,12},{9,13},{10,... | collective-permute-start | bytes 196616 | tf_op jit(solution)/shard_map/ppermute | solution.py:42
  49.0 30.7 %collective-permute-start.14 = (bf16[2,2,256,256]{3,2,1,0:T(8,128)(2,1)S(1)}, bf16[2,2,256,256]{3,2,1,0:T(8,128)(2,1)S(1)}, u32[]{:S(2)}, u32[]{:S(2)}) collective-permute-start(bf16[2,2,256,256]{3,2,1,0:T(8,128)(2,1)S(1)} %get-tuple-element.16.refs_2_), channel_id=1, source_target_pairs={{0,8},{1,9},{2,10},{3,11},{4,12},{5,13},{6,14},{7,15},{8,0},{9,1},... | collective-permute-start | bytes 1572872 | tf_op jit(solution)/shard_map/ppermute | solution.py:42
  59.2 21.4 %copy-start.6 = (bf16[2,2,256,256]{3,2,1,0:T(8,128)(2,1)}, bf16[2,2,256,256]{3,2,1,0:T(8,128)(2,1)S(1)}, u32[]{:S(2)}) copy-start(bf16[2,2,256,256]{3,2,1,0:T(8,128)(2,1)S(1)} %collective-permute-done.6.refs_4_) | copy-start | bytes 1572868
  59.2 21.4 %copy-start.7 = (bf16[2,2,256,256]{3,2,1,0:T(8,128)(2,1)}, bf16[2,2,256,256]{3,2,1,0:T(8,128)(2,1)S(1)}, u32[]{:S(2)}) copy-start(bf16[2,2,256,256]{3,2,1,0:T(8,128)(2,1)S(1)} %collective-permute-done.5.refs_3_) | copy-start | bytes 1572868
  59.2 4.0 %collective-permute-start.10 = (bf16[2,2,32,128]{3,2,1,0:T(8,128)(2,1)S(1)}, bf16[2,2,32,128]{3,2,1,0:T(8,128)(2,1)S(1)}, u32[]{:S(2)}, u32[]{:S(2)}) collective-permute-start(bf16[2,2,32,128]{3,2,1,0:T(8,128)(2,1)S(1)} %slice.39), channel_id=1, source_target_pairs={{0,2},{1,3},{2,0},{3,1},{4,6},{5,7},{6,4},{7,5},{8,10},{9,11},{10,... | collective-permute-start | bytes 98312 | tf_op jit(solution)/shard_map/ppermute | solution.py:42
  59.3 20.4 %collective-permute-start.15 = (bf16[2,2,256,256]{3,2,1,0:T(8,128)(2,1)S(1)}, bf16[2,2,256,256]{3,2,1,0:T(8,128)(2,1)S(1)}, u32[]{:S(2)}, u32[]{:S(2)}) collective-permute-start(bf16[2,2,256,256]{3,2,1,0:T(8,128)(2,1)S(1)} %collective-permute-done.5.refs_3_), channel_id=1, source_target_pairs={{0,8},{1,9},{2,10},{3,11},{4,12},{5,13},{6,14},{7,15},{8,0},{9,1},... | collective-permute-start | bytes 1572872 | tf_op jit(solution)/shard_map/ppermute | solution.py:42
  63.2 4.8 %collective-permute-start.11 = (bf16[1,2,32,128]{3,2,1,0:T(8,128)(2,1)S(1)}, bf16[1,2,32,128]{3,2,1,0:T(8,128)(2,1)S(1)}, u32[]{:S(2)}, u32[]{:S(2)}) collective-permute-start(bf16[1,2,32,128]{3,2,1,0:T(8,128)(2,1)S(1)} %slice.49), channel_id=1, source_target_pairs={{0,1},{1,0},{2,3},{3,2},{4,5},{5,4},{6,7},{7,6},{8,9},{9,8},{10,11... | collective-permute-start | bytes 49160 | tf_op jit(solution)/shard_map/ppermute | solution.py:42
  66.2 13.6 %collective-permute-start.16 = (bf16[2,2,256,256]{3,2,1,0:T(8,128)(2,1)S(1)}, bf16[2,2,256,256]{3,2,1,0:T(8,128)(2,1)S(1)}, u32[]{:S(2)}, u32[]{:S(2)}) collective-permute-start(bf16[2,2,256,256]{3,2,1,0:T(8,128)(2,1)S(1)} %collective-permute-done.6.refs_4_), channel_id=1, source_target_pairs={{0,8},{1,9},{2,10},{3,11},{4,12},{5,13},{6,14},{7,15},{8,0},{9,1},... | collective-permute-start | bytes 1572872 | tf_op jit(solution)/shard_map/ppermute | solution.py:42
  66.2 8.7 %collective-permute-start.13 = (bf16[2,256,256]{2,1,0:T(8,128)(2,1)S(1)}, bf16[2,256,256]{2,1,0:T(8,128)(2,1)S(1)}, u32[]{:S(2)}, u32[]{:S(2)}) collective-permute-start(bf16[2,256,256]{2,1,0:T(8,128)(2,1)S(1)} %slice_bitcast_fusion), channel_id=1, source_target_pairs={{0,16},{1,17},{2,18},{3,19},{4,20},{5,21},{6,22},{7,23},{8,24},{9,... | collective-permute-start | bytes 786440 | tf_op jit(solution)/shard_map/ppermute | solution.py:42
  68.0 11.1 %collective-permute-start.12 = (bf16[2,256,256]{2,1,0:T(8,128)(2,1)S(1)}, bf16[2,256,256]{2,1,0:T(8,128)(2,1)S(1)}, u32[]{:S(2)}, u32[]{:S(2)}) collective-permute-start(bf16[2,256,256]{2,1,0:T(8,128)(2,1)S(1)} %slice_bitcast_fusion.1), channel_id=1, source_target_pairs={{0,1},{1,2},{2,3},{3,4},{4,5},{5,6},{6,7},{7,0},{8,9},{9,10},{10,1... | collective-permute-start | bytes 786440 | tf_op jit(solution)/shard_map/ppermute | solution.py:42
  75.0 4.8 %collective-permute-start.18 = (bf16[2,256,256]{2,1,0:T(8,128)(2,1)S(1)}, bf16[2,256,256]{2,1,0:T(8,128)(2,1)S(1)}, u32[]{:S(2)}, u32[]{:S(2)}) collective-permute-start(bf16[2,256,256]{2,1,0:T(8,128)(2,1)S(1)} %collective-permute-done.13.refs_6_), channel_id=1, source_target_pairs={{0,8},{1,9},{2,10},{3,11},{4,12},{5,13},{6,14},{7,15},{8,0},{9,1},... | collective-permute-start | bytes 786440 | tf_op jit(solution)/shard_map/ppermute | solution.py:42
  79.1 1.5 %collective-permute-start.17 = (bf16[2,256,256]{2,1,0:T(8,128)(2,1)S(1)}, bf16[2,256,256]{2,1,0:T(8,128)(2,1)S(1)}, u32[]{:S(2)}, u32[]{:S(2)}) collective-permute-start(bf16[2,256,256]{2,1,0:T(8,128)(2,1)S(1)} %collective-permute-done.12.refs_5_), channel_id=1, source_target_pairs={{0,8},{1,9},{2,10},{3,11},{4,12},{5,13},{6,14},{7,15},{8,0},{9,1},... | collective-permute-start | bytes 786440 | tf_op jit(solution)/shard_map/ppermute | solution.py:42
  (10 other events, 24.7 us)

commit v10 on v6

--- a/solution.py
+++ b/solution.py
@@ -13,7 +13,7 @@
 AXES = ("scan", "obj")
 CORES = 2
 MIB = 1 << 20
-SMALL, LARGE = 20, 56
+SMALL, MIDDLE, LARGE = 20, 48, 56
 
 
 def dft_tables(length):
@@ -387,7 +387,7 @@
     )
     piece = outward(piece, -1)
     (own_part,) = call(
-        (pick_kernel, True), [(patch_shape, real)], [smem, hbm], wide, "own", MIB, LARGE, info, object_slices
+        (pick_kernel, True), [(patch_shape, real)], [smem, hbm], wide, "own", MIB, MIDDLE, info, object_slices
     )
     mats, turned = call(
         (prep_kernel,),

time: 80.6 us -> 79.5 us (0.986)
  local copies, waits for them, and re-layouts: 3.6 us -> 2.36 us
  waiting for transfers between devices: 34.2 us -> 35.4 us
    unnamed x26 -> x24, local copies, waits for them, and re-layouts: 2.19 us -> 0.95 us
    ppermute x16, waiting for transfers between devices: 34.2 us -> 35.4 us  [send(): return lax.ppermute(block, AXES, route)]
    pallas_call x5, Pallas kernels: 18.2 us -> 17.4 us  [call(): pl.pallas_call(functools.partial(kernel[0], sizes, *kernel[1:]), out_shap...]
  transfers between devices with their start and end apart: 17 -> 17, of which waited for: 9 -> 9; matrix products, arithmetic and copies ran while one was open for 2% -> 2% of each run, Pallas kernels for 6% -> 5%
where the time goes in v10:
time: 79.5 us; the launch traced here: 79.2 us
  waiting for transfers between devices  35.4 us (45%)
  Pallas kernels  17.4 us (22%)
  starting transfers between devices  14.8 us (19%)
  blocking collectives  6.76 us (9%)
  local copies, waits for them, and re-layouts  2.36 us (3%)
  between operations  1.49 us (2%)
  other arithmetic  0.98 us (1%)
    ppermute x16, waiting for transfers between devices, send(): return lax.ppermute(block, AXES, route)  35.4 us
    pallas_call x5, Pallas kernels, call(): pl.pallas_call(functools.partial(kernel[0], sizes, *kernel[1:]), out_shap...  17.4 us
    ppermute x16, starting transfers between devices, send(): return lax.ppermute(block, AXES, route)  8.42 us
    all_to_all x1, blocking collectives, body(): lax.all_to_all(jnp.broadcast_to(both, (n_scan, 1, 16)), 'scan', 0, 0, til...  6.76 us
    all_to_all x1, starting transfers between devices, body(): chunks = lax.all_to_all(chunks, 'obj', 0, 0, tiled=True)  6.42 us
  transfers between devices with their start and end apart: 17, of which 9 were waited for; matrix products, arithmetic and copies ran while one was open for 2% of the time, Pallas kernels for 5%

profile of v10, /device:TPU:0, one launch (start us, length us, event | category | flops | bytes accessed | tf_op | source)
XLA Modules:
  0.0 79.2 jit_solution(13593061431716290592)
XLA Ops:
  1.3 0.8 reshape_squeeze.3
  2.1 3.0 %collective-permute-start = (s32[8]{0:T(128)S(1)}, s32[8]{0:T(128)S(1)}, u32[]{:S(2)}, u32[]{:S(2)}) collective-permute-start(s32[8]{0:T(128)S(1)} %pad_add_fusion), channel_id=1, source_target_pairs={{0,1},{1,2},{2,3},{3,4},{4,5},{5,6},{6,7},{7,0},{8,9},{9,10},{10,1... | collective-permute-start | bytes 104 | tf_op jit(solution)/shard_map/ppermute | solution.py:42
  5.1 4.6 %collective-permute-done = s32[8]{0:T(128)S(1)} collective-permute-done((s32[8]{0:T(128)S(1)}, s32[8]{0:T(128)S(1)}, u32[]{:S(2)}, u32[]{:S(2)}) %collective-permute-start) | collective-permute-done | bytes 64 | tf_op jit(solution)/shard_map/ppermute | solution.py:42
  9.7 6.8 %all_to_all.10.info.refs_0_ = s32[4,1,16]{2,1,0:T(1,128)} all-to-all(s32[4,1,16]{2,1,0:T(1,128)S(1)} %broadcast_in_dim.3), channel_id=1, replica_groups=mesh['scan'=4,'obj'=8] {'scan'}, dimensions={0} | all-to-all | bytes 512 | tf_op jit(solution)/shard_map/all_to_all | solution.py:376
  16.5 3.2 %cut.1 = bf16[2,2,256,256]{3,2,1,0:T(8,128)(2,1)} custom-call(s32[4,1,16]{2,1,0:T(1,128)} %all_to_all.10.info.refs_0_, f32[2,2,256,2048]{3,2,1,0:T(8,128)} %object_ref.3), custom_call_target="tpu_custom_call" | custom-call | flops 1048576 | bytes 4194304 | tf_op jit(solution)/shard_map/cut/pallas_call | solution.py:354
  19.7 2.1 %collective-permute-start.1 = (bf16[2,2,256,256]{3,2,1,0:T(8,128)(2,1)}, bf16[2,2,256,256]{3,2,1,0:T(8,128)(2,1)S(1)}, u32[]{:S(2)}, u32[]{:S(2)}) collective-permute-start(bf16[2,2,256,256]{3,2,1,0:T(8,128)(2,1)} %cut.1), channel_id=1, source_target_pairs={{0,7},{1,0},{2,1},{3,2},{4,3},{5,4},{6,5},{7,6},{8,15},{9,8},{10,9... | collective-permute-start | bytes 1572872 | tf_op jit(solution)/shard_map/ppermute | solution.py:42
  21.9 1.0 %collective-permute-start.3 = (bf16[256,256]{1,0:T(8,128)(2,1)S(1)}, bf16[256,256]{1,0:T(8,128)(2,1)S(1)}, u32[]{:S(2)}, u32[]{:S(2)}) collective-permute-start(bf16[256,256]{1,0:T(8,128)(2,1)S(1)} %slice_bitcast_fusion.2), channel_id=1, source_target_pairs={{0,16},{1,17},{2,18},{3,19},{4,20},{5,21},{6,22},{7,23},{8,24},{9,... | collective-permute-start | bytes 393224 | tf_op jit(solution)/shard_map/ppermute | solution.py:42
  22.9 2.2 %own.1.refs_4_ = f32[2,2,256,256]{3,2,1,0:T(8,128)S(1)} custom-call(s32[4,1,16]{2,1,0:T(1,128)S(1)} %copy-done.4, f32[2,2,256,2048]{3,2,1,0:T(8,128)} %object_ref.3), custom_call_target="tpu_custom_call" | custom-call | flops 1048576 | bytes 4194304 | tf_op jit(solution)/shard_map/own/pallas_call | solution.py:354
  25.2 1.5 %prep.1 = (bf16[4,512,512]{2,1,0:T(8,128)(2,1)S(1)}, f32[2,2,256,256]{3,2,1,0:T(8,128)S(1)}) custom-call(s32[4,1,16]{2,1,0:T(1,128)S(1)} %copy-done.4, f32[2,2,256,256]{3,2,1,0:T(8,128)S(1)} %copy-done, f32[2,256,256]{2,1,0:T(8,128)S(1)} %copy-done.1), custom_call_target="tpu_custom_call" | custom-call | flops 1048576 | bytes 4194304 | tf_op jit(solution)/shard_map/prep/pallas_call | solution.py:354
  26.7 2.9 %collective-permute-done.3.refs_8_ = bf16[256,256]{1,0:T(8,128)(2,1)S(1)} collective-permute-done((bf16[256,256]{1,0:T(8,128)(2,1)S(1)}, bf16[256,256]{1,0:T(8,128)(2,1)S(1)}, u32[]{:S(2)}, u32[]{:S(2)}) %collective-permute-start.3) | collective-permute-done | bytes 131104 | tf_op jit(solution)/shard_map/ppermute | solution.py:42
  30.1 3.4 %collective-permute-done.1.refs_5_ = bf16[2,2,256,256]{3,2,1,0:T(8,128)(2,1)S(1)} collective-permute-done((bf16[2,2,256,256]{3,2,1,0:T(8,128)(2,1)}, bf16[2,2,256,256]{3,2,1,0:T(8,128)(2,1)S(1)}, u32[]{:S(2)}, u32[]{:S(2)}) %collective-permute-start.1) | collective-permute-done | bytes 524320 | tf_op jit(solution)/shard_map/ppermute | solution.py:42
  33.5 6.3 %pattern.1 = (bf16[2,2,256,256]{3,2,1,0:T(8,128)(2,1)S(1)}, bf16[8,2,2,32,128]{4,3,2,1,0:T(8,128)(2,1)S(1)}, bf16[8,2,2,32,128]{4,3,2,1,0:T(8,128)(2,1)S(1)}) custom-call(s32[4,1,16]{2,1,0:T(1,128)S(1)} %copy-done.4, bf16[4,512,512]{2,1,0:T(8,128)(2,1)S(1)} %get-tuple-element.12.refs_1_, f32[2,256,256]{2,1,0:T(8,128)S(1)} %copy-done.5, ...), custom_call_target="tpu_custom_call" | custom-call | flops 3221225472 | bytes 4194304 | tf_op jit(solution)/shard_map/pattern/pallas_call | solution.py:354
  40.2 1.3 %collective-permute-done.5 = bf16[8,2,2,32,128]{4,3,2,1,0:T(8,128)(2,1)S(1)} collective-permute-done((bf16[8,2,2,32,128]{4,3,2,1,0:T(8,128)(2,1)S(1)}, bf16[8,2,2,32,128]{4,3,2,1,0:T(8,128)(2,1)S(1)}, u32[]{:S(2)}, u32[]{:S(2)}) %collective-permute-start.5) | collective-permute-done | bytes 262176 | tf_op jit(solution)/shard_map/ppermute | solution.py:42
  41.4 0.8 add_convert_fusion
  42.4 6.4 %all-to-all-start.1 = ((bf16[8,2,2,32,128]{4,3,2,1,0:T(8,128)(2,1)}), bf16[8,2,2,32,128]{4,3,2,1,0:T(8,128)(2,1)S(1)}, u32[]{:S(2)}, u32[]{:S(2)}) async-start(bf16[8,2,2,32,128]{4,3,2,1,0:T(8,128)(2,1)} %add_convert_fusion), calls=%async_computation.1 | async-start | bytes 524288 | tf_op jit(solution)/shard_map/all_to_all | solution.py:450
  48.8 5.5 %collective-permute-done.7.refs_4_ = bf16[2,2,256,256]{3,2,1,0:T(8,128)(2,1)S(1)} collective-permute-done((bf16[2,2,256,256]{3,2,1,0:T(8,128)(2,1)S(1)}, bf16[2,2,256,256]{3,2,1,0:T(8,128)(2,1)S(1)}, u32[]{:S(2)}, u32[]{:S(2)}) %collective-permute-start.7) | collective-permute-done | bytes 524320 | tf_op jit(solution)/shard_map/ppermute | solution.py:42
  54.4 5.3 %collective-permute-done.8.refs_5_ = bf16[2,2,256,256]{3,2,1,0:T(8,128)(2,1)S(1)} collective-permute-done((bf16[2,2,256,256]{3,2,1,0:T(8,128)(2,1)S(1)}, bf16[2,2,256,256]{3,2,1,0:T(8,128)(2,1)S(1)}, u32[]{:S(2)}, u32[]{:S(2)}) %collective-permute-start.8) | collective-permute-done | bytes 524320 | tf_op jit(solution)/shard_map/ppermute | solution.py:42
  59.8 0.6 collective-permute-start.10
  60.4 8.8 %collective-permute-done.9.refs_6_ = bf16[2,256,256]{2,1,0:T(8,128)(2,1)} collective-permute-done((bf16[2,256,256]{2,1,0:T(8,128)(2,1)S(1)}, bf16[2,256,256]{2,1,0:T(8,128)(2,1)}, u32[]{:S(2)}, u32[]{:S(2)}) %collective-permute-start.9) | collective-permute-done | bytes 262176 | tf_op jit(solution)/shard_map/ppermute | solution.py:42
  69.7 0.6 slice_bitcast_fusion.3
  70.4 0.6 collective-permute-start.6
  71.0 3.1 %collective-permute-done.6.refs_2_ = bf16[2,32,128]{2,1,0:T(8,128)(2,1)S(1)} collective-permute-done((bf16[2,32,128]{2,1,0:T(8,128)(2,1)S(1)}, bf16[2,32,128]{2,1,0:T(8,128)(2,1)S(1)}, u32[]{:S(2)}, u32[]{:S(2)}) %collective-permute-start.6) | collective-permute-done | bytes 16416 | tf_op jit(solution)/shard_map/ppermute | solution.py:42
  74.2 0.5 copy-done.11
  75.1 4.1 %place.1 = (f32[2,2,256,512]{3,2,1,0:T(8,128)}, f32[2,2,32,64]{3,2,1,0:T(8,128)}) custom-call(s32[4,1,16]{2,1,0:T(1,128)} %all_to_all.10.info.refs_0_, bf16[2,32,128]{2,1,0:T(8,128)(2,1)} %get-tuple-element.21.refs_1_, bf16[2,32,128]{2,1,0:T(8,128)(2,1)} %copy-done.11, bf16[2,2,256,256]{3,2,1,0:T(8,128)(2,1)} %copy-done.2, ...), custom_call_target="tpu_custom_call" | custom-call | flops 1048576 | bytes 4194304 | tf_op jit(solution)/shard_map/place/pallas_call | solution.py:354
  (51 shorter events, 2.4 us)
Async XLA Ops:
  2.1 7.5 %collective-permute-start = (s32[8]{0:T(128)S(1)}, s32[8]{0:T(128)S(1)}, u32[]{:S(2)}, u32[]{:S(2)}) collective-permute-start(s32[8]{0:T(128)S(1)} %pad_add_fusion), channel_id=1, source_target_pairs={{0,1},{1,2},{2,3},{3,4},{4,5},{5,6},{6,7},{7,0},{8,9},{9,10},{10,1... | collective-permute-start | bytes 104 | tf_op jit(solution)/shard_map/ppermute | solution.py:42
  16.5 5.3 %copy-start.3 = (bf16[1,1,2,256,256]{4,3,2,1,0:T(8,128)(2,1)S(1)}, bf16[1,1,2,256,256]{4,3,2,1,0:T(8,128)(2,1)}, u32[]{:S(2)}) copy-start(bf16[1,1,2,256,256]{4,3,2,1,0:T(8,128)(2,1)} %param.9) | copy-start | bytes 786436
  16.5 6.4 %copy-start.4 = (s32[4,1,16]{2,1,0:T(1,128)S(1)}, s32[4,1,16]{2,1,0:T(1,128)}, u32[]{:S(2)}) copy-start(s32[4,1,16]{2,1,0:T(1,128)} %all_to_all.10.info.refs_0_) | copy-start | bytes 772
  19.7 13.8 %collective-permute-start.1 = (bf16[2,2,256,256]{3,2,1,0:T(8,128)(2,1)}, bf16[2,2,256,256]{3,2,1,0:T(8,128)(2,1)S(1)}, u32[]{:S(2)}, u32[]{:S(2)}) collective-permute-start(bf16[2,2,256,256]{3,2,1,0:T(8,128)(2,1)} %cut.1), channel_id=1, source_target_pairs={{0,7},{1,0},{2,1},{3,2},{4,3},{5,4},{6,5},{7,6},{8,15},{9,8},{10,9... | collective-permute-start | bytes 1572872 | tf_op jit(solution)/shard_map/ppermute | solution.py:42
  21.9 11.6 %copy-start.5 = (f32[2,256,256]{2,1,0:T(8,128)S(1)}, f32[2,256,256]{2,1,0:T(8,128)}, u32[]{:S(2)}) copy-start(f32[2,256,256]{2,1,0:T(8,128)} %constant.10.clone.refs_2_) | copy-start | bytes 1572868
  21.9 4.8 %collective-permute-start.4 = (bf16[256,256]{1,0:T(8,128)(2,1)S(1)}, bf16[256,256]{1,0:T(8,128)(2,1)S(1)}, u32[]{:S(2)}, u32[]{:S(2)}) collective-permute-start(bf16[256,256]{1,0:T(8,128)(2,1)S(1)} %slice_bitcast_fusion.2), channel_id=1, source_target_pairs={{0,24},{1,25},{2,26},{3,27},{4,28},{5,29},{6,30},{7,31},{8,0},{9,1... | collective-permute-start | bytes 393224 | tf_op jit(solution)/shard_map/ppermute | solution.py:42
  21.9 7.6 %collective-permute-start.3 = (bf16[256,256]{1,0:T(8,128)(2,1)S(1)}, bf16[256,256]{1,0:T(8,128)(2,1)S(1)}, u32[]{:S(2)}, u32[]{:S(2)}) collective-permute-start(bf16[256,256]{1,0:T(8,128)(2,1)S(1)} %slice_bitcast_fusion.2), channel_id=1, source_target_pairs={{0,16},{1,17},{2,18},{3,19},{4,20},{5,21},{6,22},{7,23},{8,24},{9,... | collective-permute-start | bytes 393224 | tf_op jit(solution)/shard_map/ppermute | solution.py:42
  22.9 7.2 %collective-permute-start.2 = (bf16[256,256]{1,0:T(8,128)(2,1)S(1)}, bf16[256,256]{1,0:T(8,128)(2,1)S(1)}, u32[]{:S(2)}, u32[]{:S(2)}) collective-permute-start(bf16[256,256]{1,0:T(8,128)(2,1)S(1)} %slice_bitcast_fusion.2), channel_id=1, source_target_pairs={{0,8},{1,9},{2,10},{3,11},{4,12},{5,13},{6,14},{7,15},{8,16},{9,17... | collective-permute-start | bytes 393224 | tf_op jit(solution)/shard_map/ppermute | solution.py:42
  39.8 34.3 %copy-start.2 = (bf16[2,2,256,256]{3,2,1,0:T(8,128)(2,1)}, bf16[2,2,256,256]{3,2,1,0:T(8,128)(2,1)S(1)}, u32[]{:S(2)}) copy-start(bf16[2,2,256,256]{3,2,1,0:T(8,128)(2,1)S(1)} %get-tuple-element.19.refs_3_) | copy-start | bytes 1572868
  39.8 1.6 %collective-permute-start.5 = (bf16[8,2,2,32,128]{4,3,2,1,0:T(8,128)(2,1)S(1)}, bf16[8,2,2,32,128]{4,3,2,1,0:T(8,128)(2,1)S(1)}, u32[]{:S(2)}, u32[]{:S(2)}) collective-permute-start(bf16[8,2,2,32,128]{4,3,2,1,0:T(8,128)(2,1)S(1)} %get-tuple-element.17), channel_id=1, source_target_pairs={{0,8},{1,9},{2,10},{3,11},{4,12},{5,13},{6,14},{7,15},{8,0},{9,1},... | collective-permute-start | bytes 786440 | tf_op jit(solution)/shard_map/ppermute | solution.py:42
  39.9 14.3 %collective-permute-start.7 = (bf16[2,2,256,256]{3,2,1,0:T(8,128)(2,1)S(1)}, bf16[2,2,256,256]{3,2,1,0:T(8,128)(2,1)S(1)}, u32[]{:S(2)}, u32[]{:S(2)}) collective-permute-start(bf16[2,2,256,256]{3,2,1,0:T(8,128)(2,1)S(1)} %get-tuple-element.19.refs_3_), channel_id=1, source_target_pairs={{0,16},{1,17},{2,18},{3,19},{4,20},{5,21},{6,22},{7,23},{8,24},{9,... | collective-permute-start | bytes 1572872 | tf_op jit(solution)/shard_map/ppermute | solution.py:42
  42.2 17.5 %collective-permute-start.8 = (bf16[2,2,256,256]{3,2,1,0:T(8,128)(2,1)S(1)}, bf16[2,2,256,256]{3,2,1,0:T(8,128)(2,1)S(1)}, u32[]{:S(2)}, u32[]{:S(2)}) collective-permute-start(bf16[2,2,256,256]{3,2,1,0:T(8,128)(2,1)S(1)} %get-tuple-element.19.refs_3_), channel_id=1, source_target_pairs={{0,1},{1,2},{2,3},{3,4},{4,5},{5,6},{6,7},{7,0},{8,9},{9,10},{10,1... | collective-permute-start | bytes 1572872 | tf_op jit(solution)/shard_map/ppermute | solution.py:42
  42.2 28.1 %collective-permute-start.11 = (bf16[2,2,256,256]{3,2,1,0:T(8,128)(2,1)S(1)}, bf16[2,2,256,256]{3,2,1,0:T(8,128)(2,1)S(1)}, u32[]{:S(2)}, u32[]{:S(2)}) collective-permute-start(bf16[2,2,256,256]{3,2,1,0:T(8,128)(2,1)S(1)} %get-tuple-element.19.refs_3_), channel_id=1, source_target_pairs={{0,8},{1,9},{2,10},{3,11},{4,12},{5,13},{6,14},{7,15},{8,0},{9,1},... | collective-permute-start | bytes 1572872 | tf_op jit(solution)/shard_map/ppermute | solution.py:42
  42.4 27.3 %all-to-all-start.1 = ((bf16[8,2,2,32,128]{4,3,2,1,0:T(8,128)(2,1)}), bf16[8,2,2,32,128]{4,3,2,1,0:T(8,128)(2,1)S(1)}, u32[]{:S(2)}, u32[]{:S(2)}) async-start(bf16[8,2,2,32,128]{4,3,2,1,0:T(8,128)(2,1)} %add_convert_fusion), calls=%async_computation.1 | async-start | bytes 524288 | tf_op jit(solution)/shard_map/all_to_all | solution.py:450
  54.2 19.9 %copy-start.6 = (bf16[2,2,256,256]{3,2,1,0:T(8,128)(2,1)}, bf16[2,2,256,256]{3,2,1,0:T(8,128)(2,1)S(1)}, u32[]{:S(2)}) copy-start(bf16[2,2,256,256]{3,2,1,0:T(8,128)(2,1)S(1)} %collective-permute-done.7.refs_4_) | copy-start | bytes 1572868
  54.3 14.9 %collective-permute-start.9 = (bf16[2,256,256]{2,1,0:T(8,128)(2,1)S(1)}, bf16[2,256,256]{2,1,0:T(8,128)(2,1)}, u32[]{:S(2)}, u32[]{:S(2)}) collective-permute-start(bf16[2,256,256]{2,1,0:T(8,128)(2,1)S(1)} %slice_bitcast_fusion.1), channel_id=1, source_target_pairs={{0,1},{1,2},{2,3},{3,4},{4,5},{5,6},{6,7},{7,0},{8,9},{9,10},{10,1... | collective-permute-start | bytes 786440 | tf_op jit(solution)/shard_map/ppermute | solution.py:42
  54.3 19.8 %collective-permute-start.12 = (bf16[2,2,256,256]{3,2,1,0:T(8,128)(2,1)S(1)}, bf16[2,2,256,256]{3,2,1,0:T(8,128)(2,1)S(1)}, u32[]{:S(2)}, u32[]{:S(2)}) collective-permute-start(bf16[2,2,256,256]{3,2,1,0:T(8,128)(2,1)S(1)} %collective-permute-done.7.refs_4_), channel_id=1, source_target_pairs={{0,8},{1,9},{2,10},{3,11},{4,12},{5,13},{6,14},{7,15},{8,0},{9,1},... | collective-permute-start | bytes 1572872 | tf_op jit(solution)/shard_map/ppermute | solution.py:42
  59.8 14.4 %copy-start.7 = (bf16[2,2,256,256]{3,2,1,0:T(8,128)(2,1)}, bf16[2,2,256,256]{3,2,1,0:T(8,128)(2,1)S(1)}, u32[]{:S(2)}) copy-start(bf16[2,2,256,256]{3,2,1,0:T(8,128)(2,1)S(1)} %collective-permute-done.8.refs_5_) | copy-start | bytes 1572868
  59.8 9.4 %collective-permute-start.10 = (bf16[2,256,256]{2,1,0:T(8,128)(2,1)S(1)}, bf16[2,256,256]{2,1,0:T(8,128)(2,1)}, u32[]{:S(2)}, u32[]{:S(2)}) collective-permute-start(bf16[2,256,256]{2,1,0:T(8,128)(2,1)S(1)} %slice_bitcast_fusion), channel_id=1, source_target_pairs={{0,16},{1,17},{2,18},{3,19},{4,20},{5,21},{6,22},{7,23},{8,24},{9,... | collective-permute-start | bytes 786440 | tf_op jit(solution)/shard_map/ppermute | solution.py:42
  60.4 13.7 %collective-permute-start.13 = (bf16[2,2,256,256]{3,2,1,0:T(8,128)(2,1)S(1)}, bf16[2,2,256,256]{3,2,1,0:T(8,128)(2,1)S(1)}, u32[]{:S(2)}, u32[]{:S(2)}) collective-permute-start(bf16[2,2,256,256]{3,2,1,0:T(8,128)(2,1)S(1)} %collective-permute-done.8.refs_5_), channel_id=1, source_target_pairs={{0,8},{1,9},{2,10},{3,11},{4,12},{5,13},{6,14},{7,15},{8,0},{9,1},... | collective-permute-start | bytes 1572872 | tf_op jit(solution)/shard_map/ppermute | solution.py:42
  69.2 4.9 %collective-permute-start.14 = (bf16[2,256,256]{2,1,0:T(8,128)(2,1)}, bf16[2,256,256]{2,1,0:T(8,128)(2,1)}, u32[]{:S(2)}, u32[]{:S(2)}) collective-permute-start(bf16[2,256,256]{2,1,0:T(8,128)(2,1)} %collective-permute-done.9.refs_6_), channel_id=1, source_target_pairs={{0,8},{1,9},{2,10},{3,11},{4,12},{5,13},{6,14},{7,15},{8,0},{9,1},... | collective-permute-start | bytes 786440 | tf_op jit(solution)/shard_map/ppermute | solution.py:42
  69.2 4.9 %collective-permute-start.15 = (bf16[2,256,256]{2,1,0:T(8,128)(2,1)}, bf16[2,256,256]{2,1,0:T(8,128)(2,1)}, u32[]{:S(2)}, u32[]{:S(2)}) collective-permute-start(bf16[2,256,256]{2,1,0:T(8,128)(2,1)} %collective-permute-done.10.refs_7_), channel_id=1, source_target_pairs={{0,8},{1,9},{2,10},{3,11},{4,12},{5,13},{6,14},{7,15},{8,0},{9,1},... | collective-permute-start | bytes 786440 | tf_op jit(solution)/shard_map/ppermute | solution.py:42
  70.4 3.8 %copy-start.8 = (bf16[2,2,256,256]{3,2,1,0:T(8,128)(2,1)}, bf16[2,2,256,256]{3,2,1,0:T(8,128)(2,1)S(1)}, u32[]{:S(2)}) copy-start(bf16[2,2,256,256]{3,2,1,0:T(8,128)(2,1)S(1)} %collective-permute-done.11.refs_8_) | copy-start | bytes 1572868
  70.4 3.7 %collective-permute-start.6 = (bf16[2,32,128]{2,1,0:T(8,128)(2,1)S(1)}, bf16[2,32,128]{2,1,0:T(8,128)(2,1)S(1)}, u32[]{:S(2)}, u32[]{:S(2)}) collective-permute-start(bf16[2,32,128]{2,1,0:T(8,128)(2,1)S(1)} %get-tuple-element.20), channel_id=1, source_target_pairs={{0,16},{1,17},{2,18},{3,19},{4,20},{5,21},{6,22},{7,23},{8,24},{9,... | collective-permute-start | bytes 49160 | tf_op jit(solution)/shard_map/ppermute | solution.py:42
  (5 other events, 9.0 us)

commit v11 on v10

--- a/solution.py
+++ b/solution.py
@@ -427,10 +427,10 @@
         *others,
     )
 
-    here = [grad] + [along(grad, j) for j in range(1, chips)]
+    there = outward(grad, 1)
     chunks = (keep.astype(real) + across(give).astype(real)).astype(half)
     first, chunks = lax.optimization_barrier((grad, chunks))
-    there = outward(first, 1)
+    here = [grad] + [along(first, j) for j in range(1, chips)]
     x_first = [outward(block[1], 1) for block in here[1:]]
     obj_first = [along(there[0], j) for j in range(1, chips)]
     held = here + [there] + x_first + obj_first

time: 79.5 us -> 79.6 us (level)
  no operation moved by 1% of the time
where the time goes in v11:
time: 79.6 us; the launch traced here: 79.2 us
  waiting for transfers between devices  34.9 us (44%)
  Pallas kernels  17.6 us (22%)
  starting transfers between devices  15.1 us (19%)
  blocking collectives  6.76 us (8%)
  local copies, waits for them, and re-layouts  2.38 us (3%)
  between operations  1.5 us (2%)
  other arithmetic  0.98 us (1%)
    ppermute x16, waiting for transfers between devices, send(): return lax.ppermute(block, AXES, route)  34.8 us
    pallas_call x5, Pallas kernels, call(): pl.pallas_call(functools.partial(kernel[0], sizes, *kernel[1:]), out_shap...  17.6 us
    ppermute x16, starting transfers between devices, send(): return lax.ppermute(block, AXES, route)  9.13 us
    all_to_all x1, blocking collectives, body(): lax.all_to_all(jnp.broadcast_to(both, (n_scan, 1, 16)), 'scan', 0, 0, til...  6.76 us
    all_to_all x1, starting transfers between devices, body(): chunks = lax.all_to_all(chunks, 'obj', 0, 0, tiled=True)  6 us
  transfers between devices with their start and end apart: 17, of which 9 were waited for; matrix products, arithmetic and copies ran while one was open for 2% of the time, Pallas kernels for 5%

profile of v11, /device:TPU:0, one launch (start us, length us, event | category | flops | bytes accessed | tf_op | source)
XLA Modules:
  0.0 79.2 jit_solution(4506724555450807613)
XLA Ops:
  1.3 0.8 reshape_squeeze.3
  2.1 3.0 %collective-permute-start = (s32[8]{0:T(128)S(1)}, s32[8]{0:T(128)S(1)}, u32[]{:S(2)}, u32[]{:S(2)}) collective-permute-start(s32[8]{0:T(128)S(1)} %pad_add_fusion), channel_id=1, source_target_pairs={{0,1},{1,2},{2,3},{3,4},{4,5},{5,6},{6,7},{7,0},{8,9},{9,10},{10,1... | collective-permute-start | bytes 104 | tf_op jit(solution)/shard_map/ppermute | solution.py:42
  5.1 4.6 %collective-permute-done = s32[8]{0:T(128)S(1)} collective-permute-done((s32[8]{0:T(128)S(1)}, s32[8]{0:T(128)S(1)}, u32[]{:S(2)}, u32[]{:S(2)}) %collective-permute-start) | collective-permute-done | bytes 64 | tf_op jit(solution)/shard_map/ppermute | solution.py:42
  9.7 6.8 %all_to_all.10.info.refs_0_ = s32[4,1,16]{2,1,0:T(1,128)} all-to-all(s32[4,1,16]{2,1,0:T(1,128)S(1)} %broadcast_in_dim.3), channel_id=1, replica_groups=mesh['scan'=4,'obj'=8] {'scan'}, dimensions={0} | all-to-all | bytes 512 | tf_op jit(solution)/shard_map/all_to_all | solution.py:376
  16.5 3.2 %cut.1 = bf16[2,2,256,256]{3,2,1,0:T(8,128)(2,1)} custom-call(s32[4,1,16]{2,1,0:T(1,128)} %all_to_all.10.info.refs_0_, f32[2,2,256,2048]{3,2,1,0:T(8,128)} %object_ref.3), custom_call_target="tpu_custom_call" | custom-call | flops 1048576 | bytes 4194304 | tf_op jit(solution)/shard_map/cut/pallas_call | solution.py:354
  19.7 2.1 %collective-permute-start.1 = (bf16[2,2,256,256]{3,2,1,0:T(8,128)(2,1)}, bf16[2,2,256,256]{3,2,1,0:T(8,128)(2,1)S(1)}, u32[]{:S(2)}, u32[]{:S(2)}) collective-permute-start(bf16[2,2,256,256]{3,2,1,0:T(8,128)(2,1)} %cut.1), channel_id=1, source_target_pairs={{0,7},{1,0},{2,1},{3,2},{4,3},{5,4},{6,5},{7,6},{8,15},{9,8},{10,9... | collective-permute-start | bytes 1572872 | tf_op jit(solution)/shard_map/ppermute | solution.py:42
  21.9 1.0 %collective-permute-start.3 = (bf16[256,256]{1,0:T(8,128)(2,1)S(1)}, bf16[256,256]{1,0:T(8,128)(2,1)S(1)}, u32[]{:S(2)}, u32[]{:S(2)}) collective-permute-start(bf16[256,256]{1,0:T(8,128)(2,1)S(1)} %slice_bitcast_fusion.2), channel_id=1, source_target_pairs={{0,16},{1,17},{2,18},{3,19},{4,20},{5,21},{6,22},{7,23},{8,24},{9,... | collective-permute-start | bytes 393224 | tf_op jit(solution)/shard_map/ppermute | solution.py:42
  22.9 2.2 %own.1.refs_4_ = f32[2,2,256,256]{3,2,1,0:T(8,128)S(1)} custom-call(s32[4,1,16]{2,1,0:T(1,128)S(1)} %copy-done.4, f32[2,2,256,2048]{3,2,1,0:T(8,128)} %object_ref.3), custom_call_target="tpu_custom_call" | custom-call | flops 1048576 | bytes 4194304 | tf_op jit(solution)/shard_map/own/pallas_call | solution.py:354
  25.2 1.5 %prep.1 = (bf16[4,512,512]{2,1,0:T(8,128)(2,1)S(1)}, f32[2,2,256,256]{3,2,1,0:T(8,128)S(1)}) custom-call(s32[4,1,16]{2,1,0:T(1,128)S(1)} %copy-done.4, f32[2,2,256,256]{3,2,1,0:T(8,128)S(1)} %copy-done, f32[2,256,256]{2,1,0:T(8,128)S(1)} %copy-done.1), custom_call_target="tpu_custom_call" | custom-call | flops 1048576 | bytes 4194304 | tf_op jit(solution)/shard_map/prep/pallas_call | solution.py:354
  26.7 2.9 %collective-permute-done.3.refs_8_ = bf16[256,256]{1,0:T(8,128)(2,1)S(1)} collective-permute-done((bf16[256,256]{1,0:T(8,128)(2,1)S(1)}, bf16[256,256]{1,0:T(8,128)(2,1)S(1)}, u32[]{:S(2)}, u32[]{:S(2)}) %collective-permute-start.3) | collective-permute-done | bytes 131104 | tf_op jit(solution)/shard_map/ppermute | solution.py:42
  30.1 3.4 %collective-permute-done.1.refs_5_ = bf16[2,2,256,256]{3,2,1,0:T(8,128)(2,1)S(1)} collective-permute-done((bf16[2,2,256,256]{3,2,1,0:T(8,128)(2,1)}, bf16[2,2,256,256]{3,2,1,0:T(8,128)(2,1)S(1)}, u32[]{:S(2)}, u32[]{:S(2)}) %collective-permute-start.1) | collective-permute-done | bytes 524320 | tf_op jit(solution)/shard_map/ppermute | solution.py:42
  33.5 6.3 %pattern.1 = (bf16[2,2,256,256]{3,2,1,0:T(8,128)(2,1)S(1)}, bf16[8,2,2,32,128]{4,3,2,1,0:T(8,128)(2,1)S(1)}, bf16[8,2,2,32,128]{4,3,2,1,0:T(8,128)(2,1)S(1)}) custom-call(s32[4,1,16]{2,1,0:T(1,128)S(1)} %copy-done.4, bf16[4,512,512]{2,1,0:T(8,128)(2,1)S(1)} %get-tuple-element.12.refs_1_, f32[2,256,256]{2,1,0:T(8,128)S(1)} %copy-done.5, ...), custom_call_target="tpu_custom_call" | custom-call | flops 3221225472 | bytes 4194304 | tf_op jit(solution)/shard_map/pattern/pallas_call | solution.py:354
  40.0 1.5 %collective-permute-done.5 = bf16[8,2,2,32,128]{4,3,2,1,0:T(8,128)(2,1)S(1)} collective-permute-done((bf16[8,2,2,32,128]{4,3,2,1,0:T(8,128)(2,1)S(1)}, bf16[8,2,2,32,128]{4,3,2,1,0:T(8,128)(2,1)S(1)}, u32[]{:S(2)}, u32[]{:S(2)}) %collective-permute-start.5) | collective-permute-done | bytes 262176 | tf_op jit(solution)/shard_map/ppermute | solution.py:42
  41.4 0.8 add_convert_fusion
  42.4 6.0 %all-to-all-start.1 = ((bf16[8,2,2,32,128]{4,3,2,1,0:T(8,128)(2,1)}), bf16[8,2,2,32,128]{4,3,2,1,0:T(8,128)(2,1)S(1)}, u32[]{:S(2)}, u32[]{:S(2)}) async-start(bf16[8,2,2,32,128]{4,3,2,1,0:T(8,128)(2,1)} %add_convert_fusion), calls=%async_computation.1 | async-start | bytes 524288 | tf_op jit(solution)/shard_map/all_to_all | solution.py:450
  48.4 9.2 %collective-permute-done.8.refs_5_ = bf16[2,2,256,256]{3,2,1,0:T(8,128)(2,1)S(1)} collective-permute-done((bf16[2,2,256,256]{3,2,1,0:T(8,128)(2,1)S(1)}, bf16[2,2,256,256]{3,2,1,0:T(8,128)(2,1)S(1)}, u32[]{:S(2)}, u32[]{:S(2)}) %collective-permute-start.8) | collective-permute-done | bytes 524320 | tf_op jit(solution)/shard_map/ppermute | solution.py:42
  58.0 0.6 collective-permute-start.12
  58.5 7.0 %collective-permute-done.10.refs_7_ = bf16[2,256,256]{2,1,0:T(8,128)(2,1)} collective-permute-done((bf16[2,256,256]{2,1,0:T(8,128)(2,1)S(1)}, bf16[2,256,256]{2,1,0:T(8,128)(2,1)}, u32[]{:S(2)}, u32[]{:S(2)}) %collective-permute-start.10) | collective-permute-done | bytes 262176 | tf_op jit(solution)/shard_map/ppermute | solution.py:42
  65.6 3.9 %collective-permute-done.9.refs_6_ = bf16[2,256,256]{2,1,0:T(8,128)(2,1)} collective-permute-done((bf16[2,256,256]{2,1,0:T(8,128)(2,1)S(1)}, bf16[2,256,256]{2,1,0:T(8,128)(2,1)}, u32[]{:S(2)}, u32[]{:S(2)}) %collective-permute-start.9) | collective-permute-done | bytes 262176 | tf_op jit(solution)/shard_map/ppermute | solution.py:42
  69.5 0.6 slice_bitcast_fusion.3
  70.1 1.8 %collective-permute-start.6 = (bf16[2,32,128]{2,1,0:T(8,128)(2,1)S(1)}, bf16[2,32,128]{2,1,0:T(8,128)(2,1)S(1)}, u32[]{:S(2)}, u32[]{:S(2)}) collective-permute-start(bf16[2,32,128]{2,1,0:T(8,128)(2,1)S(1)} %get-tuple-element.20), channel_id=1, source_target_pairs={{0,16},{1,17},{2,18},{3,19},{4,20},{5,21},{6,22},{7,23},{8,24},{9,... | collective-permute-start | bytes 49160 | tf_op jit(solution)/shard_map/ppermute | solution.py:42
  72.0 1.9 %collective-permute-done.6.refs_2_ = bf16[2,32,128]{2,1,0:T(8,128)(2,1)S(1)} collective-permute-done((bf16[2,32,128]{2,1,0:T(8,128)(2,1)S(1)}, bf16[2,32,128]{2,1,0:T(8,128)(2,1)S(1)}, u32[]{:S(2)}, u32[]{:S(2)}) %collective-permute-start.6) | collective-permute-done | bytes 16416 | tf_op jit(solution)/shard_map/ppermute | solution.py:42
  74.0 0.5 copy-done.11
  74.9 4.3 %place.1 = (f32[2,2,256,512]{3,2,1,0:T(8,128)}, f32[2,2,32,64]{3,2,1,0:T(8,128)}) custom-call(s32[4,1,16]{2,1,0:T(1,128)} %all_to_all.10.info.refs_0_, bf16[2,32,128]{2,1,0:T(8,128)(2,1)} %get-tuple-element.21.refs_1_, bf16[2,32,128]{2,1,0:T(8,128)(2,1)} %copy-done.11, bf16[2,2,256,256]{3,2,1,0:T(8,128)(2,1)} %copy-done.2, ...), custom_call_target="tpu_custom_call" | custom-call | flops 1048576 | bytes 4194304 | tf_op jit(solution)/shard_map/place/pallas_call | solution.py:354
  (51 shorter events, 1.9 us)
Async XLA Ops:
  2.1 7.5 %collective-permute-start = (s32[8]{0:T(128)S(1)}, s32[8]{0:T(128)S(1)}, u32[]{:S(2)}, u32[]{:S(2)}) collective-permute-start(s32[8]{0:T(128)S(1)} %pad_add_fusion), channel_id=1, source_target_pairs={{0,1},{1,2},{2,3},{3,4},{4,5},{5,6},{6,7},{7,0},{8,9},{9,10},{10,1... | collective-permute-start | bytes 104 | tf_op jit(solution)/shard_map/ppermute | solution.py:42
  16.5 5.3 %copy-start.3 = (bf16[1,1,2,256,256]{4,3,2,1,0:T(8,128)(2,1)S(1)}, bf16[1,1,2,256,256]{4,3,2,1,0:T(8,128)(2,1)}, u32[]{:S(2)}) copy-start(bf16[1,1,2,256,256]{4,3,2,1,0:T(8,128)(2,1)} %param.9) | copy-start | bytes 786436
  16.5 6.4 %copy-start.4 = (s32[4,1,16]{2,1,0:T(1,128)S(1)}, s32[4,1,16]{2,1,0:T(1,128)}, u32[]{:S(2)}) copy-start(s32[4,1,16]{2,1,0:T(1,128)} %all_to_all.10.info.refs_0_) | copy-start | bytes 772
  19.7 13.8 %collective-permute-start.1 = (bf16[2,2,256,256]{3,2,1,0:T(8,128)(2,1)}, bf16[2,2,256,256]{3,2,1,0:T(8,128)(2,1)S(1)}, u32[]{:S(2)}, u32[]{:S(2)}) collective-permute-start(bf16[2,2,256,256]{3,2,1,0:T(8,128)(2,1)} %cut.1), channel_id=1, source_target_pairs={{0,7},{1,0},{2,1},{3,2},{4,3},{5,4},{6,5},{7,6},{8,15},{9,8},{10,9... | collective-permute-start | bytes 1572872 | tf_op jit(solution)/shard_map/ppermute | solution.py:42
  21.9 11.6 %copy-start.5 = (f32[2,256,256]{2,1,0:T(8,128)S(1)}, f32[2,256,256]{2,1,0:T(8,128)}, u32[]{:S(2)}) copy-start(f32[2,256,256]{2,1,0:T(8,128)} %constant.10.clone.refs_2_) | copy-start | bytes 1572868
  21.9 4.8 %collective-permute-start.4 = (bf16[256,256]{1,0:T(8,128)(2,1)S(1)}, bf16[256,256]{1,0:T(8,128)(2,1)S(1)}, u32[]{:S(2)}, u32[]{:S(2)}) collective-permute-start(bf16[256,256]{1,0:T(8,128)(2,1)S(1)} %slice_bitcast_fusion.2), channel_id=1, source_target_pairs={{0,24},{1,25},{2,26},{3,27},{4,28},{5,29},{6,30},{7,31},{8,0},{9,1... | collective-permute-start | bytes 393224 | tf_op jit(solution)/shard_map/ppermute | solution.py:42
  21.9 7.6 %collective-permute-start.3 = (bf16[256,256]{1,0:T(8,128)(2,1)S(1)}, bf16[256,256]{1,0:T(8,128)(2,1)S(1)}, u32[]{:S(2)}, u32[]{:S(2)}) collective-permute-start(bf16[256,256]{1,0:T(8,128)(2,1)S(1)} %slice_bitcast_fusion.2), channel_id=1, source_target_pairs={{0,16},{1,17},{2,18},{3,19},{4,20},{5,21},{6,22},{7,23},{8,24},{9,... | collective-permute-start | bytes 393224 | tf_op jit(solution)/shard_map/ppermute | solution.py:42
  22.9 7.2 %collective-permute-start.2 = (bf16[256,256]{1,0:T(8,128)(2,1)S(1)}, bf16[256,256]{1,0:T(8,128)(2,1)S(1)}, u32[]{:S(2)}, u32[]{:S(2)}) collective-permute-start(bf16[256,256]{1,0:T(8,128)(2,1)S(1)} %slice_bitcast_fusion.2), channel_id=1, source_target_pairs={{0,8},{1,9},{2,10},{3,11},{4,12},{5,13},{6,14},{7,15},{8,16},{9,17... | collective-permute-start | bytes 393224 | tf_op jit(solution)/shard_map/ppermute | solution.py:42
  39.8 34.1 %copy-start.2 = (bf16[2,2,256,256]{3,2,1,0:T(8,128)(2,1)}, bf16[2,2,256,256]{3,2,1,0:T(8,128)(2,1)S(1)}, u32[]{:S(2)}) copy-start(bf16[2,2,256,256]{3,2,1,0:T(8,128)(2,1)S(1)} %get-tuple-element.19.refs_3_) | copy-start | bytes 1572868
  39.8 1.6 %collective-permute-start.5 = (bf16[8,2,2,32,128]{4,3,2,1,0:T(8,128)(2,1)S(1)}, bf16[8,2,2,32,128]{4,3,2,1,0:T(8,128)(2,1)S(1)}, u32[]{:S(2)}, u32[]{:S(2)}) collective-permute-start(bf16[8,2,2,32,128]{4,3,2,1,0:T(8,128)(2,1)S(1)} %get-tuple-element.17), channel_id=1, source_target_pairs={{0,8},{1,9},{2,10},{3,11},{4,12},{5,13},{6,14},{7,15},{8,0},{9,1},... | collective-permute-start | bytes 786440 | tf_op jit(solution)/shard_map/ppermute | solution.py:42
  39.9 17.7 %collective-permute-start.8 = (bf16[2,2,256,256]{3,2,1,0:T(8,128)(2,1)S(1)}, bf16[2,2,256,256]{3,2,1,0:T(8,128)(2,1)S(1)}, u32[]{:S(2)}, u32[]{:S(2)}) collective-permute-start(bf16[2,2,256,256]{3,2,1,0:T(8,128)(2,1)S(1)} %get-tuple-element.19.refs_3_), channel_id=1, source_target_pairs={{0,1},{1,2},{2,3},{3,4},{4,5},{5,6},{6,7},{7,0},{8,9},{9,10},{10,1... | collective-permute-start | bytes 1572872 | tf_op jit(solution)/shard_map/ppermute | solution.py:42
  42.2 15.7 %collective-permute-start.7 = (bf16[2,2,256,256]{3,2,1,0:T(8,128)(2,1)S(1)}, bf16[2,2,256,256]{3,2,1,0:T(8,128)(2,1)S(1)}, u32[]{:S(2)}, u32[]{:S(2)}) collective-permute-start(bf16[2,2,256,256]{3,2,1,0:T(8,128)(2,1)S(1)} %get-tuple-element.19.refs_3_), channel_id=1, source_target_pairs={{0,16},{1,17},{2,18},{3,19},{4,20},{5,21},{6,22},{7,23},{8,24},{9,... | collective-permute-start | bytes 1572872 | tf_op jit(solution)/shard_map/ppermute | solution.py:42
  42.4 27.7 %collective-permute-start.11 = (bf16[2,2,256,256]{3,2,1,0:T(8,128)(2,1)S(1)}, bf16[2,2,256,256]{3,2,1,0:T(8,128)(2,1)S(1)}, u32[]{:S(2)}, u32[]{:S(2)}) collective-permute-start(bf16[2,2,256,256]{3,2,1,0:T(8,128)(2,1)S(1)} %get-tuple-element.19.refs_3_), channel_id=1, source_target_pairs={{0,8},{1,9},{2,10},{3,11},{4,12},{5,13},{6,14},{7,15},{8,0},{9,1},... | collective-permute-start | bytes 1572872 | tf_op jit(solution)/shard_map/ppermute | solution.py:42
  42.4 27.1 %all-to-all-start.1 = ((bf16[8,2,2,32,128]{4,3,2,1,0:T(8,128)(2,1)}), bf16[8,2,2,32,128]{4,3,2,1,0:T(8,128)(2,1)S(1)}, u32[]{:S(2)}, u32[]{:S(2)}) async-start(bf16[8,2,2,32,128]{4,3,2,1,0:T(8,128)(2,1)} %add_convert_fusion), calls=%async_computation.1 | async-start | bytes 524288 | tf_op jit(solution)/shard_map/all_to_all | solution.py:450
  57.6 16.3 %copy-start.6 = (bf16[2,2,256,256]{3,2,1,0:T(8,128)(2,1)}, bf16[2,2,256,256]{3,2,1,0:T(8,128)(2,1)S(1)}, u32[]{:S(2)}) copy-start(bf16[2,2,256,256]{3,2,1,0:T(8,128)(2,1)S(1)} %collective-permute-done.8.refs_5_) | copy-start | bytes 1572868
  57.6 7.9 %collective-permute-start.10 = (bf16[2,256,256]{2,1,0:T(8,128)(2,1)S(1)}, bf16[2,256,256]{2,1,0:T(8,128)(2,1)}, u32[]{:S(2)}, u32[]{:S(2)}) collective-permute-start(bf16[2,256,256]{2,1,0:T(8,128)(2,1)S(1)} %slice_bitcast_fusion), channel_id=1, source_target_pairs={{0,16},{1,17},{2,18},{3,19},{4,20},{5,21},{6,22},{7,23},{8,24},{9,... | collective-permute-start | bytes 786440 | tf_op jit(solution)/shard_map/ppermute | solution.py:42
  57.9 16.0 %collective-permute-start.13 = (bf16[2,2,256,256]{3,2,1,0:T(8,128)(2,1)S(1)}, bf16[2,2,256,256]{3,2,1,0:T(8,128)(2,1)S(1)}, u32[]{:S(2)}, u32[]{:S(2)}) collective-permute-start(bf16[2,2,256,256]{3,2,1,0:T(8,128)(2,1)S(1)} %collective-permute-done.8.refs_5_), channel_id=1, source_target_pairs={{0,8},{1,9},{2,10},{3,11},{4,12},{5,13},{6,14},{7,15},{8,0},{9,1},... | collective-permute-start | bytes 1572872 | tf_op jit(solution)/shard_map/ppermute | solution.py:42
  57.9 16.1 %copy-start.7 = (bf16[2,2,256,256]{3,2,1,0:T(8,128)(2,1)}, bf16[2,2,256,256]{3,2,1,0:T(8,128)(2,1)S(1)}, u32[]{:S(2)}) copy-start(bf16[2,2,256,256]{3,2,1,0:T(8,128)(2,1)S(1)} %collective-permute-done.7.refs_4_) | copy-start | bytes 1572868
  57.9 11.6 %collective-permute-start.9 = (bf16[2,256,256]{2,1,0:T(8,128)(2,1)S(1)}, bf16[2,256,256]{2,1,0:T(8,128)(2,1)}, u32[]{:S(2)}, u32[]{:S(2)}) collective-permute-start(bf16[2,256,256]{2,1,0:T(8,128)(2,1)S(1)} %slice_bitcast_fusion.1), channel_id=1, source_target_pairs={{0,1},{1,2},{2,3},{3,4},{4,5},{5,6},{6,7},{7,0},{8,9},{9,10},{10,1... | collective-permute-start | bytes 786440 | tf_op jit(solution)/shard_map/ppermute | solution.py:42
  58.0 15.9 %collective-permute-start.12 = (bf16[2,2,256,256]{3,2,1,0:T(8,128)(2,1)S(1)}, bf16[2,2,256,256]{3,2,1,0:T(8,128)(2,1)S(1)}, u32[]{:S(2)}, u32[]{:S(2)}) collective-permute-start(bf16[2,2,256,256]{3,2,1,0:T(8,128)(2,1)S(1)} %collective-permute-done.7.refs_4_), channel_id=1, source_target_pairs={{0,8},{1,9},{2,10},{3,11},{4,12},{5,13},{6,14},{7,15},{8,0},{9,1},... | collective-permute-start | bytes 1572872 | tf_op jit(solution)/shard_map/ppermute | solution.py:42
  65.6 8.3 %collective-permute-start.15 = (bf16[2,256,256]{2,1,0:T(8,128)(2,1)}, bf16[2,256,256]{2,1,0:T(8,128)(2,1)}, u32[]{:S(2)}, u32[]{:S(2)}) collective-permute-start(bf16[2,256,256]{2,1,0:T(8,128)(2,1)} %collective-permute-done.10.refs_7_), channel_id=1, source_target_pairs={{0,8},{1,9},{2,10},{3,11},{4,12},{5,13},{6,14},{7,15},{8,0},{9,1},... | collective-permute-start | bytes 786440 | tf_op jit(solution)/shard_map/ppermute | solution.py:42
  69.5 4.4 %collective-permute-start.14 = (bf16[2,256,256]{2,1,0:T(8,128)(2,1)}, bf16[2,256,256]{2,1,0:T(8,128)(2,1)}, u32[]{:S(2)}, u32[]{:S(2)}) collective-permute-start(bf16[2,256,256]{2,1,0:T(8,128)(2,1)} %collective-permute-done.9.refs_6_), channel_id=1, source_target_pairs={{0,8},{1,9},{2,10},{3,11},{4,12},{5,13},{6,14},{7,15},{8,0},{9,1},... | collective-permute-start | bytes 786440 | tf_op jit(solution)/shard_map/ppermute | solution.py:42
  70.1 3.8 %copy-start.8 = (bf16[2,2,256,256]{3,2,1,0:T(8,128)(2,1)}, bf16[2,2,256,256]{3,2,1,0:T(8,128)(2,1)S(1)}, u32[]{:S(2)}) copy-start(bf16[2,2,256,256]{3,2,1,0:T(8,128)(2,1)S(1)} %collective-permute-done.11.refs_8_) | copy-start | bytes 1572868
  70.1 3.7 %collective-permute-start.6 = (bf16[2,32,128]{2,1,0:T(8,128)(2,1)S(1)}, bf16[2,32,128]{2,1,0:T(8,128)(2,1)S(1)}, u32[]{:S(2)}, u32[]{:S(2)}) collective-permute-start(bf16[2,32,128]{2,1,0:T(8,128)(2,1)S(1)} %get-tuple-element.20), channel_id=1, source_target_pairs={{0,16},{1,17},{2,18},{3,19},{4,20},{5,21},{6,22},{7,23},{8,24},{9,... | collective-permute-start | bytes 49160 | tf_op jit(solution)/shard_map/ppermute | solution.py:42
  (5 other events, 9.0 us)

commit v12 on v11

--- a/solution.py
+++ b/solution.py
@@ -464,7 +464,7 @@
         ],
         "place",
         MIB,
-        LARGE,
+        MIDDLE,
         info,
         *shares,
         *held,

time: 79.6 us -> 77.9 us (0.979)
  Pallas kernels: 17.6 us -> 16 us
  local copies, waits for them, and re-layouts: 2.38 us -> 0.85 us
  other arithmetic: 0.98 us -> 1.93 us
    pallas_call x5, Pallas kernels: 17.6 us -> 16 us  [call(): pl.pallas_call(functools.partial(kernel[0], sizes, *kernel[1:]), out_shap...]
    reduce_sum x1, other arithmetic: 0.04 us -> 0.99 us  [body(): chunks = jnp.sum(chunks.astype(real), axis=0).astype(half)]
    unnamed x24 -> x10, local copies, waits for them, and re-layouts: 0.96 us -> 0.03 us
where the time goes in v12:
time: 77.9 us; the launch traced here: 77.1 us
  waiting for transfers between devices  34.9 us (45%)
  Pallas kernels  16 us (21%)
  starting transfers between devices  15.2 us (20%)
  blocking collectives  6.76 us (9%)
  other arithmetic  1.93 us (2%)
  between operations  1.45 us (2%)
  local copies, waits for them, and re-layouts  0.85 us (1%)
    ppermute x16, waiting for transfers between devices, send(): return lax.ppermute(block, AXES, route)  34.9 us
    pallas_call x5, Pallas kernels, call(): pl.pallas_call(functools.partial(kernel[0], sizes, *kernel[1:]), out_shap...  16 us
    ppermute x16, starting transfers between devices, send(): return lax.ppermute(block, AXES, route)  9.22 us
    all_to_all x1, blocking collectives, body(): lax.all_to_all(jnp.broadcast_to(both, (n_scan, 1, 16)), 'scan', 0, 0, til...  6.76 us
    all_to_all x1, starting transfers between devices, body(): chunks = lax.all_to_all(chunks, 'obj', 0, 0, tiled=True)  5.98 us
  transfers between devices with their start and end apart: 17, of which 9 were waited for; matrix products, arithmetic and copies ran while one was open for 2% of the time, Pallas kernels for 5%

profile of v12, /device:TPU:0, one launch (start us, length us, event | category | flops | bytes accessed | tf_op | source)
XLA Modules:
  0.0 77.1 jit_solution(771354150338921983)
XLA Ops:
  1.3 0.8 reshape_squeeze.3
  2.1 3.0 %collective-permute-start = (s32[8]{0:T(128)S(1)}, s32[8]{0:T(128)S(1)}, u32[]{:S(2)}, u32[]{:S(2)}) collective-permute-start(s32[8]{0:T(128)S(1)} %pad_add_fusion), channel_id=1, source_target_pairs={{0,1},{1,2},{2,3},{3,4},{4,5},{5,6},{6,7},{7,0},{8,9},{9,10},{10,1... | collective-permute-start | bytes 104 | tf_op jit(solution)/shard_map/ppermute | solution.py:42
  5.1 4.6 %collective-permute-done = s32[8]{0:T(128)S(1)} collective-permute-done((s32[8]{0:T(128)S(1)}, s32[8]{0:T(128)S(1)}, u32[]{:S(2)}, u32[]{:S(2)}) %collective-permute-start) | collective-permute-done | bytes 64 | tf_op jit(solution)/shard_map/ppermute | solution.py:42
  9.7 6.8 %all_to_all.10.info.refs_0_ = s32[4,1,16]{2,1,0:T(1,128)} all-to-all(s32[4,1,16]{2,1,0:T(1,128)S(1)} %broadcast_in_dim.3), channel_id=1, replica_groups=mesh['scan'=4,'obj'=8] {'scan'}, dimensions={0} | all-to-all | bytes 512 | tf_op jit(solution)/shard_map/all_to_all | solution.py:376
  16.5 3.2 %cut.1 = bf16[2,2,256,256]{3,2,1,0:T(8,128)(2,1)} custom-call(s32[4,1,16]{2,1,0:T(1,128)} %all_to_all.10.info.refs_0_, f32[2,2,256,2048]{3,2,1,0:T(8,128)} %object_ref.3), custom_call_target="tpu_custom_call" | custom-call | flops 1048576 | bytes 4194304 | tf_op jit(solution)/shard_map/cut/pallas_call | solution.py:354
  19.7 2.1 %collective-permute-start.1 = (bf16[2,2,256,256]{3,2,1,0:T(8,128)(2,1)}, bf16[2,2,256,256]{3,2,1,0:T(8,128)(2,1)S(1)}, u32[]{:S(2)}, u32[]{:S(2)}) collective-permute-start(bf16[2,2,256,256]{3,2,1,0:T(8,128)(2,1)} %cut.1), channel_id=1, source_target_pairs={{0,7},{1,0},{2,1},{3,2},{4,3},{5,4},{6,5},{7,6},{8,15},{9,8},{10,9... | collective-permute-start | bytes 1572872 | tf_op jit(solution)/shard_map/ppermute | solution.py:42
  21.9 1.0 %collective-permute-start.3 = (bf16[256,256]{1,0:T(8,128)(2,1)S(1)}, bf16[256,256]{1,0:T(8,128)(2,1)S(1)}, u32[]{:S(2)}, u32[]{:S(2)}) collective-permute-start(bf16[256,256]{1,0:T(8,128)(2,1)S(1)} %slice_bitcast_fusion.2), channel_id=1, source_target_pairs={{0,16},{1,17},{2,18},{3,19},{4,20},{5,21},{6,22},{7,23},{8,24},{9,... | collective-permute-start | bytes 393224 | tf_op jit(solution)/shard_map/ppermute | solution.py:42
  22.9 2.2 %own.1.refs_4_ = f32[2,2,256,256]{3,2,1,0:T(8,128)S(1)} custom-call(s32[4,1,16]{2,1,0:T(1,128)S(1)} %copy-done.3, f32[2,2,256,2048]{3,2,1,0:T(8,128)} %object_ref.3), custom_call_target="tpu_custom_call" | custom-call | flops 1048576 | bytes 4194304 | tf_op jit(solution)/shard_map/own/pallas_call | solution.py:354
  25.2 1.5 %prep.1 = (bf16[4,512,512]{2,1,0:T(8,128)(2,1)S(1)}, f32[2,2,256,256]{3,2,1,0:T(8,128)S(1)}) custom-call(s32[4,1,16]{2,1,0:T(1,128)S(1)} %copy-done.3, f32[2,2,256,256]{3,2,1,0:T(8,128)S(1)} %copy-done, f32[2,256,256]{2,1,0:T(8,128)S(1)} %copy-done.1), custom_call_target="tpu_custom_call" | custom-call | flops 1048576 | bytes 4194304 | tf_op jit(solution)/shard_map/prep/pallas_call | solution.py:354
  26.7 2.9 %collective-permute-done.3.refs_8_ = bf16[256,256]{1,0:T(8,128)(2,1)S(1)} collective-permute-done((bf16[256,256]{1,0:T(8,128)(2,1)S(1)}, bf16[256,256]{1,0:T(8,128)(2,1)S(1)}, u32[]{:S(2)}, u32[]{:S(2)}) %collective-permute-start.3) | collective-permute-done | bytes 131104 | tf_op jit(solution)/shard_map/ppermute | solution.py:42
  29.6 0.5 collective-permute-done.2.refs_7_
  30.1 3.4 %collective-permute-done.1.refs_5_ = bf16[2,2,256,256]{3,2,1,0:T(8,128)(2,1)S(1)} collective-permute-done((bf16[2,2,256,256]{3,2,1,0:T(8,128)(2,1)}, bf16[2,2,256,256]{3,2,1,0:T(8,128)(2,1)S(1)}, u32[]{:S(2)}, u32[]{:S(2)}) %collective-permute-start.1) | collective-permute-done | bytes 524320 | tf_op jit(solution)/shard_map/ppermute | solution.py:42
  33.5 6.2 %pattern.1 = (bf16[2,2,256,256]{3,2,1,0:T(8,128)(2,1)S(1)}, bf16[8,2,2,32,128]{4,3,2,1,0:T(8,128)(2,1)S(1)}, bf16[8,2,2,32,128]{4,3,2,1,0:T(8,128)(2,1)S(1)}) custom-call(s32[4,1,16]{2,1,0:T(1,128)S(1)} %copy-done.3, bf16[4,512,512]{2,1,0:T(8,128)(2,1)S(1)} %get-tuple-element.12.refs_1_, f32[2,256,256]{2,1,0:T(8,128)S(1)} %copy-done.4, ...), custom_call_target="tpu_custom_call" | custom-call | flops 3221225472 | bytes 4194304 | tf_op jit(solution)/shard_map/pattern/pallas_call | solution.py:354
  39.8 1.5 %collective-permute-done.5 = bf16[8,2,2,32,128]{4,3,2,1,0:T(8,128)(2,1)S(1)} collective-permute-done((bf16[8,2,2,32,128]{4,3,2,1,0:T(8,128)(2,1)S(1)}, bf16[8,2,2,32,128]{4,3,2,1,0:T(8,128)(2,1)S(1)}, u32[]{:S(2)}, u32[]{:S(2)}) %collective-permute-start.5) | collective-permute-done | bytes 262176 | tf_op jit(solution)/shard_map/ppermute | solution.py:42
  41.3 0.8 %add_convert_fusion = bf16[8,2,2,32,128]{4,3,2,1,0:T(8,128)(2,1)} fusion(bf16[8,2,2,32,128]{4,3,2,1,0:T(8,128)(2,1)S(1)} %collective-permute-done.5, bf16[8,2,2,32,128]{4,3,2,1,0:T(8,128)(2,1)S(1)} %get-tuple-element.16), kind=kLoop, calls=%fused_computation | loop fusion | flops 524288 | bytes 786432 | tf_op jit(solution)/shard_map/convert_element_type | solution.py:431
  42.3 6.0 %all-to-all-start.1 = ((bf16[8,2,2,32,128]{4,3,2,1,0:T(8,128)(2,1)}), bf16[8,2,2,32,128]{4,3,2,1,0:T(8,128)(2,1)}, u32[]{:S(2)}, u32[]{:S(2)}) async-start(bf16[8,2,2,32,128]{4,3,2,1,0:T(8,128)(2,1)} %add_convert_fusion), calls=%async_computation.1 | async-start | bytes 524288 | tf_op jit(solution)/shard_map/all_to_all | solution.py:450
  48.3 9.2 %collective-permute-done.8.refs_5_ = bf16[2,2,256,256]{3,2,1,0:T(8,128)(2,1)S(1)} collective-permute-done((bf16[2,2,256,256]{3,2,1,0:T(8,128)(2,1)S(1)}, bf16[2,2,256,256]{3,2,1,0:T(8,128)(2,1)S(1)}, u32[]{:S(2)}, u32[]{:S(2)}) %collective-permute-start.8) | collective-permute-done | bytes 524320 | tf_op jit(solution)/shard_map/ppermute | solution.py:42
  57.8 0.6 collective-permute-start.12
  58.4 6.9 %collective-permute-done.10.refs_7_ = bf16[2,256,256]{2,1,0:T(8,128)(2,1)S(1)} collective-permute-done((bf16[2,256,256]{2,1,0:T(8,128)(2,1)S(1)}, bf16[2,256,256]{2,1,0:T(8,128)(2,1)S(1)}, u32[]{:S(2)}, u32[]{:S(2)}) %collective-permute-start.10) | collective-permute-done | bytes 262176 | tf_op jit(solution)/shard_map/ppermute | solution.py:42
  65.3 4.0 %collective-permute-done.9.refs_6_ = bf16[2,256,256]{2,1,0:T(8,128)(2,1)} collective-permute-done((bf16[2,256,256]{2,1,0:T(8,128)(2,1)S(1)}, bf16[2,256,256]{2,1,0:T(8,128)(2,1)}, u32[]{:S(2)}, u32[]{:S(2)}) %collective-permute-start.9) | collective-permute-done | bytes 262176 | tf_op jit(solution)/shard_map/ppermute | solution.py:42
  69.3 1.0 %reduce_sum.12 = bf16[2,2,32,128]{3,2,1,0:T(8,128)(2,1)S(1)} reduce(bf16[8,2,2,32,128]{4,3,2,1,0:T(8,128)(2,1)} %all-to-all-done.1, bf16[]{:T(256)} %constant.8.clone.1), dimensions={0}, to_apply=%region_0.0 | reduce | flops 114688 | bytes 294914 | tf_op jit(solution)/shard_map/reduce_sum | solution.py:451
  70.4 1.9 %collective-permute-start.6 = (bf16[2,32,128]{2,1,0:T(8,128)(2,1)S(1)}, bf16[2,32,128]{2,1,0:T(8,128)(2,1)S(1)}, u32[]{:S(2)}, u32[]{:S(2)}) collective-permute-start(bf16[2,32,128]{2,1,0:T(8,128)(2,1)S(1)} %get-tuple-element.20), channel_id=1, source_target_pairs={{0,16},{1,17},{2,18},{3,19},{4,20},{5,21},{6,22},{7,23},{8,24},{9,... | collective-permute-start | bytes 49160 | tf_op jit(solution)/shard_map/ppermute | solution.py:42
  72.3 1.9 %collective-permute-done.6.refs_2_ = bf16[2,32,128]{2,1,0:T(8,128)(2,1)S(1)} collective-permute-done((bf16[2,32,128]{2,1,0:T(8,128)(2,1)S(1)}, bf16[2,32,128]{2,1,0:T(8,128)(2,1)S(1)}, u32[]{:S(2)}, u32[]{:S(2)}) %collective-permute-start.6) | collective-permute-done | bytes 16416 | tf_op jit(solution)/shard_map/ppermute | solution.py:42
  74.2 2.9 %place.1 = (f32[2,2,256,512]{3,2,1,0:T(8,128)}, f32[2,2,32,64]{3,2,1,0:T(8,128)}) custom-call(s32[4,1,16]{2,1,0:T(1,128)S(1)} %copy-done.3, bf16[2,32,128]{2,1,0:T(8,128)(2,1)S(1)} %get-tuple-element.21.refs_1_, bf16[2,32,128]{2,1,0:T(8,128)(2,1)S(1)} %collective-permute-done.6.refs_2_, bf16[2,2,256,256]{3,2,1,0:T(8,128)(2,1)S(1)} %get-tuple-element.19.refs_3_, ...), custom_call_target="tpu_custom_call" | custom-call | flops 1048576 | bytes 4194304 | tf_op jit(solution)/shard_map/place/pallas_call | solution.py:354
  (37 shorter events, 1.0 us)
Async XLA Ops:
  2.1 7.5 %collective-permute-start = (s32[8]{0:T(128)S(1)}, s32[8]{0:T(128)S(1)}, u32[]{:S(2)}, u32[]{:S(2)}) collective-permute-start(s32[8]{0:T(128)S(1)} %pad_add_fusion), channel_id=1, source_target_pairs={{0,1},{1,2},{2,3},{3,4},{4,5},{5,6},{6,7},{7,0},{8,9},{9,10},{10,1... | collective-permute-start | bytes 104 | tf_op jit(solution)/shard_map/ppermute | solution.py:42
  16.5 5.3 %copy-start.2 = (bf16[1,1,2,256,256]{4,3,2,1,0:T(8,128)(2,1)S(1)}, bf16[1,1,2,256,256]{4,3,2,1,0:T(8,128)(2,1)}, u32[]{:S(2)}) copy-start(bf16[1,1,2,256,256]{4,3,2,1,0:T(8,128)(2,1)} %param.9) | copy-start | bytes 786436
  16.5 6.4 %copy-start.3 = (s32[4,1,16]{2,1,0:T(1,128)S(1)}, s32[4,1,16]{2,1,0:T(1,128)}, u32[]{:S(2)}) copy-start(s32[4,1,16]{2,1,0:T(1,128)} %all_to_all.10.info.refs_0_) | copy-start | bytes 772
  19.7 13.8 %collective-permute-start.1 = (bf16[2,2,256,256]{3,2,1,0:T(8,128)(2,1)}, bf16[2,2,256,256]{3,2,1,0:T(8,128)(2,1)S(1)}, u32[]{:S(2)}, u32[]{:S(2)}) collective-permute-start(bf16[2,2,256,256]{3,2,1,0:T(8,128)(2,1)} %cut.1), channel_id=1, source_target_pairs={{0,7},{1,0},{2,1},{3,2},{4,3},{5,4},{6,5},{7,6},{8,15},{9,8},{10,9... | collective-permute-start | bytes 1572872 | tf_op jit(solution)/shard_map/ppermute | solution.py:42
  21.8 3.3 %copy-start = (f32[2,2,256,256]{3,2,1,0:T(8,128)S(1)}, f32[2,2,256,256]{3,2,1,0:T(8,128)}, u32[]{:S(2)}) copy-start(f32[2,2,256,256]{3,2,1,0:T(8,128)} %probe_ref.1) | copy-start | bytes 3145732
  21.8 3.3 %copy-start.1 = (f32[2,256,256]{2,1,0:T(8,128)S(1)}, f32[2,256,256]{2,1,0:T(8,128)}, u32[]{:S(2)}) copy-start(f32[2,256,256]{2,1,0:T(8,128)} %constant.9.clone.dft_ref) | copy-start | bytes 1572868
  21.8 11.6 %copy-start.4 = (f32[2,256,256]{2,1,0:T(8,128)S(1)}, f32[2,256,256]{2,1,0:T(8,128)}, u32[]{:S(2)}) copy-start(f32[2,256,256]{2,1,0:T(8,128)} %constant.10.clone.refs_2_) | copy-start | bytes 1572868
  21.9 4.8 %collective-permute-start.4 = (bf16[256,256]{1,0:T(8,128)(2,1)S(1)}, bf16[256,256]{1,0:T(8,128)(2,1)S(1)}, u32[]{:S(2)}, u32[]{:S(2)}) collective-permute-start(bf16[256,256]{1,0:T(8,128)(2,1)S(1)} %slice_bitcast_fusion.2), channel_id=1, source_target_pairs={{0,24},{1,25},{2,26},{3,27},{4,28},{5,29},{6,30},{7,31},{8,0},{9,1... | collective-permute-start | bytes 393224 | tf_op jit(solution)/shard_map/ppermute | solution.py:42
  21.9 7.6 %collective-permute-start.3 = (bf16[256,256]{1,0:T(8,128)(2,1)S(1)}, bf16[256,256]{1,0:T(8,128)(2,1)S(1)}, u32[]{:S(2)}, u32[]{:S(2)}) collective-permute-start(bf16[256,256]{1,0:T(8,128)(2,1)S(1)} %slice_bitcast_fusion.2), channel_id=1, source_target_pairs={{0,16},{1,17},{2,18},{3,19},{4,20},{5,21},{6,22},{7,23},{8,24},{9,... | collective-permute-start | bytes 393224 | tf_op jit(solution)/shard_map/ppermute | solution.py:42
  22.9 7.2 %collective-permute-start.2 = (bf16[256,256]{1,0:T(8,128)(2,1)S(1)}, bf16[256,256]{1,0:T(8,128)(2,1)S(1)}, u32[]{:S(2)}, u32[]{:S(2)}) collective-permute-start(bf16[256,256]{1,0:T(8,128)(2,1)S(1)} %slice_bitcast_fusion.2), channel_id=1, source_target_pairs={{0,8},{1,9},{2,10},{3,11},{4,12},{5,13},{6,14},{7,15},{8,16},{9,17... | collective-permute-start | bytes 393224 | tf_op jit(solution)/shard_map/ppermute | solution.py:42
  39.7 1.6 %collective-permute-start.5 = (bf16[8,2,2,32,128]{4,3,2,1,0:T(8,128)(2,1)S(1)}, bf16[8,2,2,32,128]{4,3,2,1,0:T(8,128)(2,1)S(1)}, u32[]{:S(2)}, u32[]{:S(2)}) collective-permute-start(bf16[8,2,2,32,128]{4,3,2,1,0:T(8,128)(2,1)S(1)} %get-tuple-element.17), channel_id=1, source_target_pairs={{0,8},{1,9},{2,10},{3,11},{4,12},{5,13},{6,14},{7,15},{8,0},{9,1},... | collective-permute-start | bytes 786440 | tf_op jit(solution)/shard_map/ppermute | solution.py:42
  39.8 17.7 %collective-permute-start.8 = (bf16[2,2,256,256]{3,2,1,0:T(8,128)(2,1)S(1)}, bf16[2,2,256,256]{3,2,1,0:T(8,128)(2,1)S(1)}, u32[]{:S(2)}, u32[]{:S(2)}) collective-permute-start(bf16[2,2,256,256]{3,2,1,0:T(8,128)(2,1)S(1)} %get-tuple-element.19.refs_3_), channel_id=1, source_target_pairs={{0,1},{1,2},{2,3},{3,4},{4,5},{5,6},{6,7},{7,0},{8,9},{9,10},{10,1... | collective-permute-start | bytes 1572872 | tf_op jit(solution)/shard_map/ppermute | solution.py:42
  42.1 15.7 %collective-permute-start.7 = (bf16[2,2,256,256]{3,2,1,0:T(8,128)(2,1)S(1)}, bf16[2,2,256,256]{3,2,1,0:T(8,128)(2,1)S(1)}, u32[]{:S(2)}, u32[]{:S(2)}) collective-permute-start(bf16[2,2,256,256]{3,2,1,0:T(8,128)(2,1)S(1)} %get-tuple-element.19.refs_3_), channel_id=1, source_target_pairs={{0,16},{1,17},{2,18},{3,19},{4,20},{5,21},{6,22},{7,23},{8,24},{9,... | collective-permute-start | bytes 1572872 | tf_op jit(solution)/shard_map/ppermute | solution.py:42
  42.3 28.1 %collective-permute-start.11 = (bf16[2,2,256,256]{3,2,1,0:T(8,128)(2,1)S(1)}, bf16[2,2,256,256]{3,2,1,0:T(8,128)(2,1)S(1)}, u32[]{:S(2)}, u32[]{:S(2)}) collective-permute-start(bf16[2,2,256,256]{3,2,1,0:T(8,128)(2,1)S(1)} %get-tuple-element.19.refs_3_), channel_id=1, source_target_pairs={{0,8},{1,9},{2,10},{3,11},{4,12},{5,13},{6,14},{7,15},{8,0},{9,1},... | collective-permute-start | bytes 1572872 | tf_op jit(solution)/shard_map/ppermute | solution.py:42
  42.3 27.1 %all-to-all-start.1 = ((bf16[8,2,2,32,128]{4,3,2,1,0:T(8,128)(2,1)}), bf16[8,2,2,32,128]{4,3,2,1,0:T(8,128)(2,1)}, u32[]{:S(2)}, u32[]{:S(2)}) async-start(bf16[8,2,2,32,128]{4,3,2,1,0:T(8,128)(2,1)} %add_convert_fusion), calls=%async_computation.1 | async-start | bytes 524288 | tf_op jit(solution)/shard_map/all_to_all | solution.py:450
  57.5 7.8 %collective-permute-start.10 = (bf16[2,256,256]{2,1,0:T(8,128)(2,1)S(1)}, bf16[2,256,256]{2,1,0:T(8,128)(2,1)S(1)}, u32[]{:S(2)}, u32[]{:S(2)}) collective-permute-start(bf16[2,256,256]{2,1,0:T(8,128)(2,1)S(1)} %slice_bitcast_fusion), channel_id=1, source_target_pairs={{0,16},{1,17},{2,18},{3,19},{4,20},{5,21},{6,22},{7,23},{8,24},{9,... | collective-permute-start | bytes 786440 | tf_op jit(solution)/shard_map/ppermute | solution.py:42
  57.7 16.4 %collective-permute-start.13 = (bf16[2,2,256,256]{3,2,1,0:T(8,128)(2,1)S(1)}, bf16[2,2,256,256]{3,2,1,0:T(8,128)(2,1)S(1)}, u32[]{:S(2)}, u32[]{:S(2)}) collective-permute-start(bf16[2,2,256,256]{3,2,1,0:T(8,128)(2,1)S(1)} %collective-permute-done.8.refs_5_), channel_id=1, source_target_pairs={{0,8},{1,9},{2,10},{3,11},{4,12},{5,13},{6,14},{7,15},{8,0},{9,1},... | collective-permute-start | bytes 1572872 | tf_op jit(solution)/shard_map/ppermute | solution.py:42
  57.8 11.6 %collective-permute-start.9 = (bf16[2,256,256]{2,1,0:T(8,128)(2,1)S(1)}, bf16[2,256,256]{2,1,0:T(8,128)(2,1)}, u32[]{:S(2)}, u32[]{:S(2)}) collective-permute-start(bf16[2,256,256]{2,1,0:T(8,128)(2,1)S(1)} %slice_bitcast_fusion.1), channel_id=1, source_target_pairs={{0,1},{1,2},{2,3},{3,4},{4,5},{5,6},{6,7},{7,0},{8,9},{9,10},{10,1... | collective-permute-start | bytes 786440 | tf_op jit(solution)/shard_map/ppermute | solution.py:42
  57.8 16.3 %collective-permute-start.12 = (bf16[2,2,256,256]{3,2,1,0:T(8,128)(2,1)S(1)}, bf16[2,2,256,256]{3,2,1,0:T(8,128)(2,1)S(1)}, u32[]{:S(2)}, u32[]{:S(2)}) collective-permute-start(bf16[2,2,256,256]{3,2,1,0:T(8,128)(2,1)S(1)} %collective-permute-done.7.refs_4_), channel_id=1, source_target_pairs={{0,8},{1,9},{2,10},{3,11},{4,12},{5,13},{6,14},{7,15},{8,0},{9,1},... | collective-permute-start | bytes 1572872 | tf_op jit(solution)/shard_map/ppermute | solution.py:42
  65.3 8.9 %collective-permute-start.15 = (bf16[2,256,256]{2,1,0:T(8,128)(2,1)S(1)}, bf16[2,256,256]{2,1,0:T(8,128)(2,1)}, u32[]{:S(2)}, u32[]{:S(2)}) collective-permute-start(bf16[2,256,256]{2,1,0:T(8,128)(2,1)S(1)} %collective-permute-done.10.refs_7_), channel_id=1, source_target_pairs={{0,8},{1,9},{2,10},{3,11},{4,12},{5,13},{6,14},{7,15},{8,0},{9,1},... | collective-permute-start | bytes 786440 | tf_op jit(solution)/shard_map/ppermute | solution.py:42
  69.3 4.8 %collective-permute-start.14 = (bf16[2,256,256]{2,1,0:T(8,128)(2,1)}, bf16[2,256,256]{2,1,0:T(8,128)(2,1)}, u32[]{:S(2)}, u32[]{:S(2)}) collective-permute-start(bf16[2,256,256]{2,1,0:T(8,128)(2,1)} %collective-permute-done.9.refs_6_), channel_id=1, source_target_pairs={{0,8},{1,9},{2,10},{3,11},{4,12},{5,13},{6,14},{7,15},{8,0},{9,1},... | collective-permute-start | bytes 786440 | tf_op jit(solution)/shard_map/ppermute | solution.py:42
  70.4 3.8 %collective-permute-start.6 = (bf16[2,32,128]{2,1,0:T(8,128)(2,1)S(1)}, bf16[2,32,128]{2,1,0:T(8,128)(2,1)S(1)}, u32[]{:S(2)}, u32[]{:S(2)}) collective-permute-start(bf16[2,32,128]{2,1,0:T(8,128)(2,1)S(1)} %get-tuple-element.20), channel_id=1, source_target_pairs={{0,16},{1,17},{2,18},{3,19},{4,20},{5,21},{6,22},{7,23},{8,24},{9,... | collective-permute-start | bytes 49160 | tf_op jit(solution)/shard_map/ppermute | solution.py:42
